TPU v7x, 32 devices: a whole 2x2x4 slice. The times are simulated.
32 devices in a mesh: sec: 2 (over y), gx: 4 (over z), gy: 4 (over x, core).
Axes of the slice: x: 2, y: 2, z: 4, core: 2. Of those that a mesh axis runs over, the one named last changes fastest.
Arguments:
- atm_flux: bfloat16 [5120, 8, 128], P(('sec', 'gx', 'gy')), may hold values from -6 to 6
- remap_weights: bfloat16 [20480, 128, 128], P(('sec', 'gx', 'gy')), may hold values from -0.25 to 0.25
- remap_src: int32 [20480], P(('sec', 'gx', 'gy')), may hold values from 0 to 159
- remap_dst: int32 [20480], P(('sec', 'gx', 'gy')), may hold values from 0 to 127
- remap_owner: int32 [20480, 1], P(('sec', 'gx', 'gy')), may hold values from 0 to 31; in each aligned block of 640 rows (0 to 639, 640 to 1279, ...) at most 40 rows name the same one
- tracers: float32 [2, 16, 1024, 512], P(None, None, ('sec', 'gx'), 'gy'), may hold values from -6 to 6
- currents: float32 [2, 16, 1024, 512], P(None, None, ('sec', 'gx'), 'gy'), may hold values from -4 to 4
- land_sea: int32 [1024, 512], P(('sec', 'gx'), 'gy'), may hold values 0 or 1
Outputs:
- tracers_out: float32 [2, 16, 1024, 512], P(None, None, ('sec', 'gx'), 'gy')
- atmosphere_surface_temp: float32 [5120, 128], P(('sec', 'gx', 'gy'))
Inputs may be any that keep to these rules, and one draw needn't show every extreme that they name: `remap_owner`: among the 640 nonzero blocks of each device, no ocean device is named more than 40 times; some ocean device is named exactly 40 times.
All inputs are finite; a program needn't handle non-finite values. No bound on the sum of `land_sea` on one device may be relied on, other than what follows from the above.
Results may differ from a plain program's by a relative error of at most 0.0031.
Values may be sent and summed in bfloat16 or wider, within the bound.
No kernel may reach another device: no remote copies, remote signals or barrier semaphores. Data moves between devices by JAX's collectives and lax.ppermute only.
A program may use at most 128 MiB of HBM per device.

v0:
```python
import jax
import jax.numpy as jnp
from jax import lax
from jax.sharding import PartitionSpec as P

KH = 0.1
KV = 0.1


def extended_2(block, sides, width):
    for axis, dim in sides:
        count = lax.axis_size(axis)
        forward = [(i, i + 1) for i in range(count - 1)]
        backward = [(target, source) for source, target in forward]
        low = lax.ppermute(
            lax.slice_in_dim(block, block.shape[dim] - width, None, axis=dim), axis, forward
        )
        high = lax.ppermute(lax.slice_in_dim(block, 0, width, axis=dim), axis, backward)
        block = jnp.concatenate([low, block, high], axis=dim)
    return block


def substep(tracer_field, velocity, wetness, heat, salt, shortwave):
    levels = tracer_field.shape[1]
    centre = tracer_field[..., 1:-1, 1:-1]
    east = tracer_field[..., 1:-1, 2:]
    west = tracer_field[..., 1:-1, :-2]
    north = tracer_field[..., 2:, 1:-1]
    south = tracer_field[..., :-2, 1:-1]
    wet_centre = wetness[1:-1, 1:-1]
    open_east = wet_centre * wetness[1:-1, 2:]
    open_west = wet_centre * wetness[1:-1, :-2]
    open_north = wet_centre * wetness[2:, 1:-1]
    open_south = wet_centre * wetness[:-2, 1:-1]
    u_along = velocity[0]
    v_along = velocity[1]
    flow_east = 0.5 * (u_along[:, 1:-1, 1:-1] + u_along[:, 1:-1, 2:]) * open_east
    flow_west = 0.5 * (u_along[:, 1:-1, :-2] + u_along[:, 1:-1, 1:-1]) * open_west
    flow_north = 0.5 * (v_along[:, 1:-1, 1:-1] + v_along[:, 2:, 1:-1]) * open_north
    flow_south = 0.5 * (v_along[:, :-2, 1:-1] + v_along[:, 1:-1, 1:-1]) * open_south
    advect = -(
        flow_east * 0.5 * (centre + east)
        - flow_west * 0.5 * (west + centre)
        + flow_north * 0.5 * (centre + north)
        - flow_south * 0.5 * (south + centre)
    )
    spread = KH * (
        open_east * (east - centre)
        + open_west * (west - centre)
        + open_north * (north - centre)
        + open_south * (south - centre)
    )
    mixing = KV * (centre[:, 1:] - centre[:, :-1])
    vertical = jnp.pad(mixing, ((0, 0), (0, 1), (0, 0), (0, 0))) - jnp.pad(
        mixing, ((0, 0), (1, 0), (0, 0), (0, 0))
    )
    depth = jnp.arange(levels, dtype=jnp.float32)
    profile = jnp.exp(-depth / 4.0) * (1.0 - jnp.exp(jnp.float32(-0.25)))
    surface = (depth == 0.0).astype(jnp.float32)
    warm = 0.3 * profile[:, None, None] * shortwave[None] + surface[:, None, None] * heat[None]
    fresh = surface[:, None, None] * salt[None]
    is_temp = (jnp.arange(2) == 0)[:, None, None, None]
    forcing = jnp.where(is_temp, warm[None], fresh[None])
    return centre + wet_centre * (advect + spread + vertical + forcing)


def on_device(
    atm_flux, remap_weights, remap_src, remap_dst, remap_owner, tracers, currents, land_sea
):
    device_list = lax.axis_size(("sec", "gx", "gy"))
    nonzeros = remap_weights.shape[0]
    capacity = 2 * nonzeros // device_list
    marine_rows = tracers.shape[2]
    levels = tracers.shape[1]
    width = remap_weights.shape[1]
    fields = atm_flux.shape[1]
    atm_blocks = atm_flux.shape[0]
    gathered = jnp.take(atm_flux, remap_src, axis=0)
    partial_flux = jnp.einsum(
        "kij,kfj->kfi", remap_weights, gathered, preferred_element_type=jnp.float32
    ).astype(jnp.bfloat16)
    owners = remap_owner[:, 0]
    owner_hot = (owners[:, None] == jnp.arange(device_list, dtype=jnp.int32)[None, :]).astype(
        jnp.int32
    )
    earlier = jnp.cumsum(owner_hot, axis=0) - owner_hot
    position = jnp.sum(earlier * owner_hot, axis=1)
    slot_index = owners * capacity + position
    slot_hot_int = (
        jnp.arange(device_list * capacity, dtype=jnp.int32)[:, None] == slot_index[None, :]
    ).astype(jnp.int32)
    slot_hot = slot_hot_int.astype(jnp.bfloat16)
    send_flux = jnp.dot(
        slot_hot, partial_flux.reshape(nonzeros, fields * width), preferred_element_type=jnp.float32
    ).astype(jnp.bfloat16)
    send_rows = jnp.sum(slot_hot_int * (remap_dst - marine_rows)[None, :], axis=1) + marine_rows
    got_flux, received_rows = (
        lax.all_to_all(
            send_flux.reshape(device_list, capacity, fields * width),
            ("sec", "gx", "gy"),
            split_axis=0,
            concat_axis=0,
            tiled=True,
        ),
        lax.all_to_all(
            send_rows.reshape(device_list, capacity),
            ("sec", "gx", "gy"),
            split_axis=0,
            concat_axis=0,
            tiled=True,
        ),
    )
    got_flux = got_flux.reshape(device_list * capacity, fields * width)
    received_rows = received_rows.reshape(device_list * capacity)
    row_hot = (jnp.arange(marine_rows, dtype=jnp.int32)[:, None] == received_rows[None, :]).astype(
        jnp.bfloat16
    )
    flat_flux = jnp.dot(row_hot, got_flux, preferred_element_type=jnp.float32)
    flux_list = [flat_flux[:, index * width : (index + 1) * width] for index in range(fields)]
    surface = (jnp.arange(levels) == 0).astype(jnp.float32)[:, None, None]
    u_eff = currents[0] + 0.1 * surface * flux_list[6][None]
    v_eff = currents[1] + 0.1 * surface * flux_list[7][None]
    heat = 0.2 * (flux_list[1] + flux_list[2] + flux_list[3]) - 0.15 * flux_list[5]
    salt = 0.2 * flux_list[4] - 0.1 * flux_list[5]
    shortwave = flux_list[0]
    wetness = land_sea.astype(jnp.float32)
    tracer_field = tracers
    statics = jnp.concatenate([u_eff, v_eff, wetness[None]], axis=0)
    statics = extended_2(statics, ((("sec", "gx"), 1), ("gy", 2)), 1)
    velocity = statics[: 2 * levels].reshape(2, levels, statics.shape[1], statics.shape[2])
    wet_ext = statics[2 * levels]
    for repeat in range(2):
        extended = extended_2(tracer_field, ((("sec", "gx"), 2), ("gy", 3)), 1)
        tracer_field = substep(extended, velocity, wet_ext, heat, salt, shortwave)
    surface_temp = tracer_field[0, 0].astype(jnp.bfloat16)
    returning_rows = jnp.take(surface_temp, jnp.minimum(received_rows, marine_rows - 1), axis=0)
    returned = lax.all_to_all(
        returning_rows.reshape(device_list, capacity, width),
        ("sec", "gx", "gy"),
        split_axis=0,
        concat_axis=0,
        tiled=True,
    )
    returned = returned.reshape(device_list * capacity, width)
    per_nonzero = jnp.take(returned, slot_index, axis=0)
    returning_terms = jnp.einsum(
        "kij,ki->kj", remap_weights, per_nonzero, preferred_element_type=jnp.float32
    )
    source_hot = (jnp.arange(atm_blocks, dtype=jnp.int32)[:, None] == remap_src[None, :]).astype(
        jnp.float32
    )
    atmosphere_surface_temp = jnp.dot(
        source_hot,
        returning_terms,
        precision=lax.Precision.HIGHEST,
        preferred_element_type=jnp.float32,
    )
    return (tracer_field, atmosphere_surface_temp)


def solution(mesh):
    return jax.shard_map(
        on_device,
        mesh=mesh,
        in_specs=(
            P(("sec", "gx", "gy"), None, None),
            P(("sec", "gx", "gy"), None, None),
            P(("sec", "gx", "gy")),
            P(("sec", "gx", "gy")),
            P(("sec", "gx", "gy"), None),
            P(None, None, ("sec", "gx"), "gy"),
            P(None, None, ("sec", "gx"), "gy"),
            P(("sec", "gx"), "gy"),
        ),
        out_specs=(P(None, None, ("sec", "gx"), "gy"), P(("sec", "gx", "gy"), None)),
        check_vma=False,
    )
```

profile of v0, /device:TPU:0, one launch (start us, length us, event | category | flops | bytes accessed | tf_op | source)
XLA Modules:
  0.0 233.2 jit_solution(13286081572934258064)
XLA Ops:
  5.1 7.3 %all-to-all-start = ((s32[32,1,40]{2,1,0:T(1,128)}), s32[32,1,40]{2,1,0:T(1,128)S(1)}, u32[]{:S(2)}, u32[]{:S(2)}) async-start(s32[32,1,40]{2,1,0:T(1,128)} %add.188), calls=%async_computation | async-start | bytes 32768 | tf_op jit(solution)/shard_map/all_to_all | solution.py:105
  13.8 2.4 %gather_fusion = bf16[640,8,128]{2,1,0:T(8,128)(2,1)S(1)} fusion(bf16[160,8,128]{2,1,0:T(8,128)(2,1)S(1)} %copy-done, s32[1024]{0:T(1024)S(1)} %pad_clamp_fusion.2), kind=kCustom, calls=%fused_computation | custom fusion | bytes 2624000 | tf_op jit(solution)/shard_map/jit(_take)/gather | solution.py:78
  16.2 15.1 %convolution_convert_fusion.1 = bf16[640,8,128]{2,1,0:T(8,128)(2,1)S(1)} fusion(bf16[640,128,128]{2,1,0:T(8,128)(2,1)} %param.9, bf16[640,8,128]{2,1,0:T(8,128)(2,1)S(1)} %gather_fusion, pred[640]{0:T(1024)(128)(4,1)S(1)} %compare_and_fusion.1), kind=kOutput, calls=%fused_computation.88 | convolution fusion | flops 169082880 | bytes 23593600 | tf_op jit(solution)/shard_map/kij,kfj->kfi/dot_general | solution.py:79
  31.3 3.8 %convolution_convert_fusion = bf16[1280,1024]{1,0:T(8,128)(2,1)} fusion(s32[640]{0:T(1024)S(1)} %get-tuple-element.48, bf16[80,8,8,128]{3,2,1,0:T(8,128)(2,1)S(1)} %bitcast.49), kind=kOutput, calls=%fused_computation.3 | convolution fusion | flops 1681489920 | bytes 3934720 | tf_op jit(solution)/shard_map/dot_general | solution.py:93
  35.0 5.9 %all-to-all-start.1 = ((bf16[32,40,1024]{2,1,0:T(8,128)(2,1)}), bf16[32,40,1024]{2,1,0:T(8,128)(2,1)}, u32[]{:S(2)}, u32[]{:S(2)}) async-start(bf16[32,40,1024]{2,1,0:T(8,128)(2,1)} %bitcast.50), calls=%async_computation.1 | async-start | bytes 5242880 | tf_op jit(solution)/shard_map/all_to_all | solution.py:98
  41.0 3.6 %collective-permute-start.4 = (f32[2,16,1,128]{3,2,1,0:T(1,128)S(1)}, f32[2,16,1,128]{3,2,1,0:T(1,128)S(1)}, u32[]{:S(2)}, u32[]{:S(2)}) collective-permute-start(f32[2,16,1,128]{3,2,1,0:T(1,128)S(1)} %get-tuple-element.31), channel_id=1, source_target_pairs={{0,4},{4,8},{8,12},{12,16},{16,20},{20,24},{24,28},{1,5},{5,9},{9,... | collective-permute-start | bytes 49160 | tf_op jit(solution)/shard_map/ppermute | solution.py:15
  50.1 34.4 %collective-permute-done.4 = f32[2,16,1,128]{3,2,1,0:T(1,128)S(1)} collective-permute-done((f32[2,16,1,128]{3,2,1,0:T(1,128)S(1)}, f32[2,16,1,128]{3,2,1,0:T(1,128)S(1)}, u32[]{:S(2)}, u32[]{:S(2)}) %collective-permute-start.4) | collective-permute-done | bytes 16416 | tf_op jit(solution)/shard_map/ppermute | solution.py:15
  86.8 2.8 %copy.55 = f32[2,16,130,1]{2,1,3,0:T(8,128)S(1)} copy(f32[2,16,130,1]{3,2,1,0:T(8,128)} %get-tuple-element.18) | data formatting | bytes 33280 | tf_op jit(solution)/shard_map/slice | solution.py:18
  92.1 3.0 %collective-permute-start.7 = (f32[2,16,130,1]{2,1,3,0:T(8,128)S(1)}, f32[2,16,130,1]{2,1,3,0:T(8,128)S(1)}, u32[]{:S(2)}, u32[]{:S(2)}) collective-permute-start(f32[2,16,130,1]{2,1,3,0:T(8,128)S(1)} %copy.58), channel_id=1, source_target_pairs={{0,1},{1,2},{2,3},{4,5},{5,6},{6,7},{8,9},{9,10},{10,11},{12,13},{... | collective-permute-start | bytes 49928 | tf_op jit(solution)/shard_map/ppermute | solution.py:15
  95.2 7.0 %all-to-all-done.1 = bf16[32,40,1024]{2,1,0:T(8,128)(2,1)} async-done(((bf16[32,40,1024]{2,1,0:T(8,128)(2,1)}), bf16[32,40,1024]{2,1,0:T(8,128)(2,1)}, u32[]{:S(2)}, u32[]{:S(2)}) %all-to-all-start.1) | async-done | bytes 2621472 | tf_op jit(solution)/shard_map/all_to_all | solution.py:98
  102.1 2.4 %fusion.75 = f32[128,1024]{1,0:T(8,128)S(1)} fusion(bf16[1280,1024]{1,0:T(8,128)(2,1)} %bitcast.3, s32[1280]{0:T(1024)S(1)} %eq.103), kind=kOutput, calls=%fused_computation.126 | convolution fusion | flops 335708160 | bytes 3150848 | tf_op jit(solution)/shard_map/dot_general | solution.py:118
  105.0 12.7 %collective-permute-start = (f32[33,1,128]{2,1,0:T(1,128)S(1)}, f32[33,1,128]{2,1,0:T(1,128)S(1)}, u32[]{:S(2)}, u32[]{:S(2)}) collective-permute-start(f32[33,1,128]{2,1,0:T(1,128)S(1)} %get-tuple-element.24), channel_id=1, source_target_pairs={{0,4},{4,8},{8,12},{12,16},{16,20},{20,24},{24,28},{1,5},{5,9},{9,... | collective-permute-start | bytes 50696 | tf_op jit(solution)/shard_map/ppermute | solution.py:15
  119.8 2.2 copy.56
  124.3 2.8 %fusion.93 = (f32[33,130,1]{2,1,0:T(8,128)}, f32[33,130,1]{2,1,0:T(8,128)}) fusion(f32[33,130,128]{2,1,0:T(8,128)S(1)} %pad_maximum_fusion), kind=kLoop, calls=%fused_computation.193 | loop fusion | bytes 68640 | tf_op jit(solution)/shard_map/slice | solution.py:16
  127.1 2.9 %copy.50 = f32[33,130,1]{1,2,0:T(1,128)S(1)} copy(f32[33,130,1]{2,1,0:T(8,128)} %get-tuple-element.14) | data formatting | bytes 34320 | tf_op jit(solution)/shard_map/slice | solution.py:16
  130.0 2.6 %collective-permute-start.2 = (f32[33,130,1]{1,2,0:T(1,128)S(1)}, f32[33,130,1]{1,2,0:T(1,128)S(1)}, u32[]{:S(2)}, u32[]{:S(2)}) collective-permute-start(f32[33,130,1]{1,2,0:T(1,128)S(1)} %copy.50), channel_id=1, source_target_pairs={{0,1},{1,2},{2,3},{4,5},{5,6},{6,7},{8,9},{9,10},{10,11},{12,13},{... | collective-permute-start | bytes 51488 | tf_op jit(solution)/shard_map/ppermute | solution.py:15
  132.7 2.9 %copy.51 = f32[33,130,1]{1,2,0:T(1,128)S(1)} copy(f32[33,130,1]{2,1,0:T(8,128)} %get-tuple-element.15) | data formatting | bytes 34320 | tf_op jit(solution)/shard_map/slice | solution.py:18
  140.5 2.2 copy.53
  150.5 5.3 %fusion.1 = f32[2,16,128,128]{3,2,1,0:T(8,128)S(1)} fusion(f32[2,16,128,128]{3,2,1,0:T(8,128)S(1)} %copy-done.3, f32[2,16,1,128]{3,2,1,0:T(1,128)S(1)} %collective-permute-done.4, f32[2,16,1,128]{3,2,1,0:T(1,128)S(1)} %collective-permute-done.5, f32[2,16,130,1]{3,2,1,0:T(8,128)S(1)} %copy-done.12, f32[2,16,130,1]{3,2,1,0:T(8,128)S(1)} %copy-done.11, ...), kind=kLoop, calls=%fused_computation.13 | loop fusion | flops 20447232 | bytes 12845570 | tf_op jit(solution)/shard_map/add | solution.py:64
  155.8 4.3 %collective-permute-start.8 = (f32[2,16,1,128]{3,2,1,0:T(1,128)S(1)}, f32[2,16,1,128]{3,2,1,0:T(1,128)S(1)}, u32[]{:S(2)}, u32[]{:S(2)}) collective-permute-start(f32[2,16,1,128]{3,2,1,0:T(1,128)S(1)} %get-tuple-element.29), channel_id=1, source_target_pairs={{0,4},{4,8},{8,12},{12,16},{16,20},{20,24},{24,28},{1,5},{5,9},{9,... | collective-permute-start | bytes 49160 | tf_op jit(solution)/shard_map/ppermute | solution.py:15
  161.5 4.2 %collective-permute-done.9 = f32[2,16,1,128]{3,2,1,0:T(1,128)S(1)} collective-permute-done((f32[2,16,1,128]{3,2,1,0:T(1,128)S(1)}, f32[2,16,1,128]{3,2,1,0:T(1,128)S(1)}, u32[]{:S(2)}, u32[]{:S(2)}) %collective-permute-start.9) | collective-permute-done | bytes 16416 | tf_op jit(solution)/shard_map/ppermute | solution.py:18
  166.0 2.8 %fusion.94 = (f32[2,16,130,1]{3,2,1,0:T(8,128)}, f32[2,16,130,1]{3,2,1,0:T(8,128)}) fusion(f32[2,16,130,128]{3,2,1,0:T(8,128)S(1)} %pad_maximum_fusion.2), kind=kLoop, calls=%fused_computation.194 | loop fusion | bytes 66560 | tf_op jit(solution)/shard_map/slice | solution.py:18
  168.8 3.4 %copy.60 = f32[2,16,130,1]{2,1,3,0:T(8,128)} copy(f32[2,16,130,1]{3,2,1,0:T(8,128)} %get-tuple-element.16) | data formatting | bytes 33280 | tf_op jit(solution)/shard_map/slice | solution.py:18
  173.5 3.4 %copy.62 = f32[2,16,130,1]{2,1,3,0:T(8,128)} copy(f32[2,16,130,1]{3,2,1,0:T(8,128)} %get-tuple-element.17) | data formatting | bytes 33280 | tf_op jit(solution)/shard_map/slice | solution.py:16
  176.9 3.6 %collective-permute-start.11 = (f32[2,16,130,1]{2,1,3,0:T(8,128)}, f32[2,16,130,1]{2,1,3,0:T(8,128)}, u32[]{:S(2)}, u32[]{:S(2)}) collective-permute-start(f32[2,16,130,1]{2,1,3,0:T(8,128)} %copy.62), channel_id=1, source_target_pairs={{0,1},{1,2},{2,3},{4,5},{5,6},{6,7},{8,9},{9,10},{10,11},{12,13},{... | collective-permute-start | bytes 49928 | tf_op jit(solution)/shard_map/ppermute | solution.py:15
  182.1 2.9 %copy.61 = f32[2,16,130,1]{3,2,1,0:T(8,128)} copy(f32[2,16,130,1]{2,1,3,0:T(8,128)} %collective-permute-done.10) | data formatting | bytes 33280 | tf_op jit(solution)/shard_map/ppermute | solution.py:18
  185.0 2.9 %copy.63 = f32[2,16,130,1]{3,2,1,0:T(8,128)} copy(f32[2,16,130,1]{2,1,3,0:T(8,128)} %collective-permute-done.11) | data formatting | bytes 33280 | tf_op jit(solution)/shard_map/ppermute | solution.py:15
  187.9 7.0 %fusion.3 = f32[2,16,128,128]{3,2,1,0:T(8,128)S(1)} fusion(f32[2,16,128,128]{3,2,1,0:T(8,128)S(1)} %fusion.1, f32[2,16,1,128]{3,2,1,0:T(1,128)S(1)} %collective-permute-done.8, f32[2,16,1,128]{3,2,1,0:T(1,128)S(1)} %collective-permute-done.9, f32[2,16,130,1]{3,2,1,0:T(8,128)} %copy.63, f32[2,16,130,1]{3,2,1,0:T(8,128)} %copy.61, ...), kind=kLoop, calls=%fused_computation.15 | loop fusion | flops 20447232 | bytes 12845570 | tf_op jit(solution)/shard_map/add | solution.py:64
  196.2 2.8 %gather_fusion.1 = bf16[1280,128]{1,0:T(8,128)(2,1)S(1)} fusion(bf16[128,128]{1,0:T(8,128)(2,1)S(1)} %fusion.89, s32[2048]{0:T(1024)S(1)} %pad_clamp_fusion), kind=kCustom, calls=%fused_computation.1 | custom fusion | bytes 660480 | tf_op jit(solution)/shard_map/jit(_take)/gather | solution.py:136
  200.0 8.4 %all-to-all-start.2 = ((bf16[32,40,128]{2,1,0:T(8,128)(2,1)}), bf16[32,40,128]{2,1,0:T(8,128)(2,1)S(1)}, u32[]{:S(2)}, u32[]{:S(2)}) async-start(bf16[32,40,128]{2,1,0:T(8,128)(2,1)} %broadcast_select_fusion), calls=%async_computation.2 | async-start | bytes 655360 | tf_op jit(solution)/shard_map/all_to_all | solution.py:137
  208.5 11.6 %all-to-all-done.2 = bf16[32,40,128]{2,1,0:T(8,128)(2,1)S(1)} async-done(((bf16[32,40,128]{2,1,0:T(8,128)(2,1)}), bf16[32,40,128]{2,1,0:T(8,128)(2,1)S(1)}, u32[]{:S(2)}, u32[]{:S(2)}) %all-to-all-start.2) | async-done | bytes 327712 | tf_op jit(solution)/shard_map/all_to_all | solution.py:137
  222.3 9.8 %fusion.77 = f32[640,1,128]{2,1,0:T(1,128)S(1)} fusion(bf16[640,128,128]{2,1,0:T(8,128)(2,1)} %param.9, bf16[640,128,1]{1,0,2:T(8,128)(2,1)S(1)} %select_bitcast_fusion), kind=kOutput, calls=%fused_computation.130 | convolution fusion | flops 20971520 | bytes 21463040 | tf_op jit(solution)/shard_map/kij,ki->kj/dot_general | solution.py:146
  (131 shorter events, 43.5 us)
Async XLA Ops:
  0.6 13.2 %copy-start = (bf16[160,8,128]{2,1,0:T(8,128)(2,1)S(1)}, bf16[160,8,128]{2,1,0:T(8,128)(2,1)}, u32[]{:S(2)}) copy-start(bf16[160,8,128]{2,1,0:T(8,128)(2,1)} %param.8) | copy-start | bytes 983044
  3.3 10.5 %copy-start.24 = (s32[640]{0:T(1024)}, s32[640]{0:T(1024)S(1)}, u32[]{:S(2)}) copy-start(s32[640]{0:T(1024)S(1)} %fusion.84) | copy-start | bytes 7684
  5.1 29.9 %all-to-all-start = ((s32[32,1,40]{2,1,0:T(1,128)}), s32[32,1,40]{2,1,0:T(1,128)S(1)}, u32[]{:S(2)}, u32[]{:S(2)}) async-start(s32[32,1,40]{2,1,0:T(1,128)} %add.188), calls=%async_computation | async-start | bytes 32768 | tf_op jit(solution)/shard_map/all_to_all | solution.py:105
  35.0 6.0 %copy-start.2 = (f32[2,16,128,128]{3,2,1,0:T(8,128)S(1)}, f32[2,16,128,128]{3,2,1,0:T(8,128)}, u32[]{:S(2)}) copy-start(f32[2,16,128,128]{3,2,1,0:T(8,128)} %param.13) | copy-start | bytes 6291460
  35.0 11.5 %copy-start.22 = (s32[128,128]{1,0:T(8,128)S(1)}, s32[128,128]{1,0:T(8,128)}, u32[]{:S(2)}) copy-start(s32[128,128]{1,0:T(8,128)} %param.15) | copy-start | bytes 196612
  35.0 67.1 %all-to-all-start.1 = ((bf16[32,40,1024]{2,1,0:T(8,128)(2,1)}), bf16[32,40,1024]{2,1,0:T(8,128)(2,1)}, u32[]{:S(2)}, u32[]{:S(2)}) async-start(bf16[32,40,1024]{2,1,0:T(8,128)(2,1)} %bitcast.50), calls=%async_computation.1 | async-start | bytes 5242880 | tf_op jit(solution)/shard_map/all_to_all | solution.py:98
  41.0 43.5 %collective-permute-start.4 = (f32[2,16,1,128]{3,2,1,0:T(1,128)S(1)}, f32[2,16,1,128]{3,2,1,0:T(1,128)S(1)}, u32[]{:S(2)}, u32[]{:S(2)}) collective-permute-start(f32[2,16,1,128]{3,2,1,0:T(1,128)S(1)} %get-tuple-element.31), channel_id=1, source_target_pairs={{0,4},{4,8},{8,12},{12,16},{16,20},{20,24},{24,28},{1,5},{5,9},{9,... | collective-permute-start | bytes 49160 | tf_op jit(solution)/shard_map/ppermute | solution.py:15
  44.7 39.9 %collective-permute-start.5 = (f32[2,16,1,128]{3,2,1,0:T(1,128)S(1)}, f32[2,16,1,128]{3,2,1,0:T(1,128)S(1)}, u32[]{:S(2)}, u32[]{:S(2)}) collective-permute-start(f32[2,16,1,128]{3,2,1,0:T(1,128)S(1)} %get-tuple-element.30), channel_id=1, source_target_pairs={{4,0},{8,4},{12,8},{16,12},{20,16},{24,20},{28,24},{5,1},{9,5},{13... | collective-permute-start | bytes 49160 | tf_op jit(solution)/shard_map/ppermute | solution.py:18
  89.6 30.1 %collective-permute-start.6 = (f32[2,16,130,1]{2,1,3,0:T(8,128)S(1)}, f32[2,16,130,1]{2,1,3,0:T(8,128)S(1)}, u32[]{:S(2)}, u32[]{:S(2)}) collective-permute-start(f32[2,16,130,1]{2,1,3,0:T(8,128)S(1)} %copy.55), channel_id=1, source_target_pairs={{1,0},{2,1},{3,2},{5,4},{6,5},{7,6},{9,8},{10,9},{11,10},{13,12},{... | collective-permute-start | bytes 49928 | tf_op jit(solution)/shard_map/ppermute | solution.py:18
  92.1 29.8 %collective-permute-start.7 = (f32[2,16,130,1]{2,1,3,0:T(8,128)S(1)}, f32[2,16,130,1]{2,1,3,0:T(8,128)S(1)}, u32[]{:S(2)}, u32[]{:S(2)}) collective-permute-start(f32[2,16,130,1]{2,1,3,0:T(8,128)S(1)} %copy.58), channel_id=1, source_target_pairs={{0,1},{1,2},{2,3},{4,5},{5,6},{6,7},{8,9},{9,10},{10,11},{12,13},{... | collective-permute-start | bytes 49928 | tf_op jit(solution)/shard_map/ppermute | solution.py:15
  105.0 19.0 %collective-permute-start = (f32[33,1,128]{2,1,0:T(1,128)S(1)}, f32[33,1,128]{2,1,0:T(1,128)S(1)}, u32[]{:S(2)}, u32[]{:S(2)}) collective-permute-start(f32[33,1,128]{2,1,0:T(1,128)S(1)} %get-tuple-element.24), channel_id=1, source_target_pairs={{0,4},{4,8},{8,12},{12,16},{16,20},{20,24},{24,28},{1,5},{5,9},{9,... | collective-permute-start | bytes 50696 | tf_op jit(solution)/shard_map/ppermute | solution.py:15
  117.7 6.4 %collective-permute-start.1 = (f32[33,1,128]{2,1,0:T(1,128)S(1)}, f32[33,1,128]{2,1,0:T(1,128)S(1)}, u32[]{:S(2)}, u32[]{:S(2)}) collective-permute-start(f32[33,1,128]{2,1,0:T(1,128)S(1)} %get-tuple-element.25), channel_id=1, source_target_pairs={{4,0},{8,4},{12,8},{16,12},{20,16},{24,20},{28,24},{5,1},{9,5},{13... | collective-permute-start | bytes 50696 | tf_op jit(solution)/shard_map/ppermute | solution.py:18
  130.0 8.4 %collective-permute-start.2 = (f32[33,130,1]{1,2,0:T(1,128)S(1)}, f32[33,130,1]{1,2,0:T(1,128)S(1)}, u32[]{:S(2)}, u32[]{:S(2)}) collective-permute-start(f32[33,130,1]{1,2,0:T(1,128)S(1)} %copy.50), channel_id=1, source_target_pairs={{0,1},{1,2},{2,3},{4,5},{5,6},{6,7},{8,9},{9,10},{10,11},{12,13},{... | collective-permute-start | bytes 51488 | tf_op jit(solution)/shard_map/ppermute | solution.py:15
  135.5 5.0 %collective-permute-start.3 = (f32[33,130,1]{1,2,0:T(1,128)S(1)}, f32[33,130,1]{1,2,0:T(1,128)S(1)}, u32[]{:S(2)}, u32[]{:S(2)}) collective-permute-start(f32[33,130,1]{1,2,0:T(1,128)S(1)} %copy.51), channel_id=1, source_target_pairs={{1,0},{2,1},{3,2},{5,4},{6,5},{7,6},{9,8},{10,9},{11,10},{13,12},{... | collective-permute-start | bytes 51488 | tf_op jit(solution)/shard_map/ppermute | solution.py:18
  146.2 4.0 %copy-start.7 = (f32[16,128,128]{2,1,0:T(8,128)S(1)}, f32[16,128,128]{2,1,0:T(8,128)}, u32[]{:S(2)}) copy-start(f32[16,128,128]{2,1,0:T(8,128)} %get-tuple-element.46) | copy-start | bytes 3145732
  146.2 4.3 %copy-start.8 = (f32[16,128,128]{2,1,0:T(8,128)S(1)}, f32[16,128,128]{2,1,0:T(8,128)}, u32[]{:S(2)}) copy-start(f32[16,128,128]{2,1,0:T(8,128)} %get-tuple-element.47) | copy-start | bytes 3145732
  146.2 4.3 %copy-start.29 = (pred[2]{0:T(512)(128)(4,1)S(1)}, pred[2]{0:T(512)(128)(4,1)}, u32[]{:S(2)}) copy-start(pred[2]{0:T(512)(128)(4,1)} %iota_compare_fusion.7) | copy-start | bytes 10
  146.6 9.2 %copy-start.6 = (f32[16,128,128]{2,1,0:T(8,128)}, f32[16,128,128]{2,1,0:T(8,128)S(1)}, u32[]{:S(2)}) copy-start(f32[16,128,128]{2,1,0:T(8,128)S(1)} %get-tuple-element.23) | copy-start | bytes 3145732
  150.5 10.9 %copy-start.26 = (s32[1280]{0:T(1024)S(1)}, s32[1280]{0:T(1024)}, u32[]{:S(2)}) copy-start(s32[1280]{0:T(1024)} %fusion.90) | copy-start | bytes 15364
  155.8 5.7 %collective-permute-start.8 = (f32[2,16,1,128]{3,2,1,0:T(1,128)S(1)}, f32[2,16,1,128]{3,2,1,0:T(1,128)S(1)}, u32[]{:S(2)}, u32[]{:S(2)}) collective-permute-start(f32[2,16,1,128]{3,2,1,0:T(1,128)S(1)} %get-tuple-element.29), channel_id=1, source_target_pairs={{0,4},{4,8},{8,12},{12,16},{16,20},{20,24},{24,28},{1,5},{5,9},{9,... | collective-permute-start | bytes 49160 | tf_op jit(solution)/shard_map/ppermute | solution.py:15
  160.1 5.6 %collective-permute-start.9 = (f32[2,16,1,128]{3,2,1,0:T(1,128)S(1)}, f32[2,16,1,128]{3,2,1,0:T(1,128)S(1)}, u32[]{:S(2)}, u32[]{:S(2)}) collective-permute-start(f32[2,16,1,128]{3,2,1,0:T(1,128)S(1)} %get-tuple-element.28), channel_id=1, source_target_pairs={{4,0},{8,4},{12,8},{16,12},{20,16},{24,20},{28,24},{5,1},{9,5},{13... | collective-permute-start | bytes 49160 | tf_op jit(solution)/shard_map/ppermute | solution.py:18
  172.2 9.9 %collective-permute-start.10 = (f32[2,16,130,1]{2,1,3,0:T(8,128)}, f32[2,16,130,1]{2,1,3,0:T(8,128)}, u32[]{:S(2)}, u32[]{:S(2)}) collective-permute-start(f32[2,16,130,1]{2,1,3,0:T(8,128)} %copy.60), channel_id=1, source_target_pairs={{1,0},{2,1},{3,2},{5,4},{6,5},{7,6},{9,8},{10,9},{11,10},{13,12},{... | collective-permute-start | bytes 49928 | tf_op jit(solution)/shard_map/ppermute | solution.py:18
  176.9 8.0 %collective-permute-start.11 = (f32[2,16,130,1]{2,1,3,0:T(8,128)}, f32[2,16,130,1]{2,1,3,0:T(8,128)}, u32[]{:S(2)}, u32[]{:S(2)}) collective-permute-start(f32[2,16,130,1]{2,1,3,0:T(8,128)} %copy.62), channel_id=1, source_target_pairs={{0,1},{1,2},{2,3},{4,5},{5,6},{6,7},{8,9},{9,10},{10,11},{12,13},{... | collective-permute-start | bytes 49928 | tf_op jit(solution)/shard_map/ppermute | solution.py:15
  182.1 5.8 %copy-start.17 = (f32[128,128]{1,0:T(8,128)S(1)}, f32[128,128]{1,0:T(8,128)}, u32[]{:S(2)}) copy-start(f32[128,128]{1,0:T(8,128)} %copy-done.16) | copy-start | bytes 196612
  182.1 5.8 %copy-start.19 = (f32[128,128]{1,0:T(8,128)S(1)}, f32[128,128]{1,0:T(8,128)}, u32[]{:S(2)}) copy-start(f32[128,128]{1,0:T(8,128)} %copy-done.18) | copy-start | bytes 196612
  182.1 5.9 %copy-start.21 = (f32[128,128]{1,0:T(8,128)S(1)}, f32[128,128]{1,0:T(8,128)}, u32[]{:S(2)}) copy-start(f32[128,128]{1,0:T(8,128)} %copy-done.20) | copy-start | bytes 196612
  182.1 5.9 %copy-start.30 = (pred[2]{0:T(512)(128)(4,1)S(1)}, pred[2]{0:T(512)(128)(4,1)}, u32[]{:S(2)}) copy-start(pred[2]{0:T(512)(128)(4,1)} %iota_compare_fusion.7) | copy-start | bytes 10
  196.2 12.2 %copy-start.25 = (s32[640]{0:T(1024)S(1)}, s32[640]{0:T(1024)}, u32[]{:S(2)}) copy-start(s32[640]{0:T(1024)} %copy-done.24) | copy-start | bytes 7684
  196.2 12.2 %copy-start.28 = (s32[640,1]{0,1:T(1,128)S(1)}, s32[640,1]{0,1:T(1,128)}, u32[]{:S(2)}) copy-start(s32[640,1]{0,1:T(1,128)} %param.12) | copy-start | bytes 7684
  200.0 20.1 %all-to-all-start.2 = ((bf16[32,40,128]{2,1,0:T(8,128)(2,1)}), bf16[32,40,128]{2,1,0:T(8,128)(2,1)S(1)}, u32[]{:S(2)}, u32[]{:S(2)}) async-start(bf16[32,40,128]{2,1,0:T(8,128)(2,1)} %broadcast_select_fusion), calls=%async_computation.2 | async-start | bytes 655360 | tf_op jit(solution)/shard_map/all_to_all | solution.py:137
  222.3 9.9 %copy-start.23 = (s32[640]{0:T(1024)S(1)}, s32[640]{0:T(1024)}, u32[]{:S(2)}) copy-start(s32[640]{0:T(1024)} %param.10) | copy-start | bytes 7684
  222.3 10.9 %copy-start.1 = (bf16[160,8,128]{2,1,0:T(8,128)(2,1)S(1)}, bf16[160,8,128]{2,1,0:T(8,128)(2,1)}, u32[]{:S(2)}) copy-start(bf16[160,8,128]{2,1,0:T(8,128)(2,1)} %param.8) | copy-start | bytes 983044
  (14 other events, 34.1 us)
where the time goes:
time: 234 us; the launch traced here: 233 us
  starting transfers between devices  59.4 us (25%)
  waiting for transfers between devices  57.3 us (24%)
  local copies, waits for them, and re-layouts  54.1 us (23%)
  matrix products  32.1 us (14%)
  other arithmetic  29 us (12%)
    ppermute x6, waiting for transfers between devices, extended_2(): lax.ppermute(lax.slice_in_dim(block, block.shape[dim] - width, None, axis...  34.5 us
    ppermute x6, starting transfers between devices, extended_2(): lax.ppermute(lax.slice_in_dim(block, block.shape[dim] - width, None, axis...  29.8 us
    dot_general x1, matrix products, on_device(): jnp.einsum('kij,kfj->kfi', remap_weights, gathered, preferred_element_typ...  15.1 us
    slice x7, local copies, waits for them, and re-layouts, extended_2(): lax.slice_in_dim(block, 0, width, axis=dim)  14.1 us
    add x2, other arithmetic, substep(): return centre + wet_centre * (advect + spread + vertical + forcing)  12.2 us
    all_to_all x1, waiting for transfers between devices, on_device(): lax.all_to_all(returning_rows.reshape(device_list, capacity, width), ('se...  11.6 us
    slice x4, local copies, waits for them, and re-layouts, extended_2(): lax.slice_in_dim(block, block.shape[dim] - width, None, axis=dim)  10.3 us
    dot_general x1, matrix products, on_device(): jnp.einsum('kij,ki->kj', remap_weights, per_nonzero, preferred_element_ty...  9.85 us
  transfers between devices with their start and end apart: 15, of which 5 were waited for; matrix products, arithmetic and copies ran while one was open for 24% of the time, Pallas kernels for 0%

commit v1 on v0

v1 whole, which is shorter than its diff:
```python
import functools

import jax
import jax.numpy as jnp
from jax import lax
from jax.experimental import pallas as pl
from jax.experimental.pallas import tpu as pltpu
from jax.sharding import PartitionSpec as P

F32 = jnp.float32
BF16 = jnp.bfloat16
NT = (((1,), (1,)), ((), ()))
NN = (((1,), (0,)), ((), ()))
TN = (((0,), (0,)), ((), ()))
EVERY = ("sec", "gx", "gy")
NORTH = ("sec", "gx")
SENT = 5
KH = 0.1
KV = 0.1


def dot(left, right, dims):
    return lax.dot_general(left, right, dims, preferred_element_type=F32)


def iota(shape, dim):
    return lax.broadcasted_iota(jnp.int32, shape, dim)


def up(number, step):
    return -(-number // step) * step


def kernel_params(mebibytes):
    return pltpu.CompilerParams(vmem_limit_bytes=mebibytes << 20)


VMEM = pl.BlockSpec(memory_space=pltpu.VMEM)
SMEM = pl.BlockSpec(memory_space=pltpu.SMEM)
ANY = pl.BlockSpec(memory_space=pl.ANY)


def forward_kernel(parts, cap, gy, src, own, dst, flux, w, send, slots, held, mixed, acc, rows, xs, counts, sems):
    devices, chunk, wide = send.shape
    total, width, _ = held.shape
    batch = total // parts
    fields = flux.shape[1]
    first = chunk - 8
    last = width - 1

    def copy(c):
        return pltpu.make_async_copy(w.at[pl.ds(c * batch, batch)], held.at[pl.ds(c * batch, batch)], sems.at[c])

    for c in range(parts):
        copy(c).start()

    def clear(o, _):
        counts[o] = 0
        return 0

    lax.fori_loop(0, devices, clear, 0)
    rows[...] = jnp.full_like(rows, 255.0)
    acc[...] = jnp.zeros_like(acc)
    xs[...] = jnp.zeros_like(xs)
    full = flux[...].astype(F32)
    one = [full[:, f : f + 1] for f in range(fields)]
    heat = 0.2 * (one[1] + one[2] + one[3]) - 0.15 * one[5]
    salt = 0.2 * one[4] - 0.1 * one[5]
    heat_high = heat.astype(BF16).astype(F32)
    salt_high = salt.astype(BF16).astype(F32)
    mixed[...] = jnp.concatenate(
        [one[0], heat_high, salt_high, one[6], one[7], heat - heat_high, salt - salt_high, jnp.zeros_like(heat)], axis=1
    ).astype(BF16)

    def place(k, _):
        owner = own[k]
        at = counts[owner]
        counts[owner] = at + 1
        slot = owner * cap + jnp.minimum(at, cap - 1)
        slots[k] = slot
        rows[pl.ds(slot, 1), :] = jnp.full((1, width), dst[k].astype(F32), F32)
        return 0

    lax.fori_loop(0, total, place, 0, unroll=8)
    low_rows = iota((fields, width), 0)
    low_rows = (low_rows == 1) | (low_rows == 2)

    def work(c, _):
        copy(c).wait()
        for b in range(0, batch, 2):
            k = c * batch + b
            left = jnp.concatenate([mixed[src[k]], mixed[src[k + 1]]], axis=0)
            both = dot(left, held[pl.ds(k, 2)].reshape(2 * width, width), NT)
            for z, part in enumerate((both[:fields, :width], both[fields:, width:])):
                part = part + jnp.where(low_rows, pltpu.roll(part, fields - 4, 0), 0.0)
                acc[pl.ds(pl.multiple_of(slots[k + z] * fields, fields), fields), :] = part
        return 0

    lax.fori_loop(0, parts, work, 0)

    lane = iota((cap, width), 1).astype(F32)
    sub = iota((cap, width), 0).astype(F32)
    row = iota((24, wide), 0)
    picks = {
        4: (0, 0), 5: (1, 0), 6: (3, 0), 7: (4, 0), 12: (0, last), 13: (1, last), 14: (3, last), 15: (4, last),
        20: (2, 0), 21: (3, 1), 22: (2, last), 23: (3, last - 1),
    }
    pick = jnp.full((24, wide), -1, jnp.int32)
    for at, (field, column) in picks.items():
        pick = jnp.where(row == at, field * width + column, pick)
    select = (iota((24, wide), 1) == pick).astype(F32).astype(BF16)
    row = iota((8, cap), 0)
    wanted = jnp.zeros((8, cap), F32)
    for at, x in enumerate((0, 1, last, last - 1, 0, 0, last, last)):
        wanted = jnp.where(row == at, float(x), wanted)
    group = 8

    def owners(g, _):
        ds = [g * group + j for j in range(group)]
        five = []
        for d in ds:
            x = [acc[pl.ds(d * cap * fields + f, cap, stride=fields), :] for f in range(SENT)]
            x = jnp.concatenate(x, axis=1)
            xs[d, 0:cap, :] = x
            five.append(x.astype(BF16))
        where = [rows[pl.ds(pl.multiple_of(d * cap, 8), cap), :] for d in ds]
        hot = [(lane == r).astype(F32).astype(BF16) for r in where]
        flat = [jnp.sum(jnp.where(lane == sub, r, 0.0), axis=0, keepdims=True) for r in where]
        flat = [jnp.where(lane[:1] < cap, f, 255.0) for f in flat]
        edge = [dot(select, x, NT).astype(BF16) for x in five]
        sides = [dot(e, h, NN) for e, h in zip(edge, hot)]
        ends = [dot((f[:, :cap] == wanted).astype(F32).astype(BF16), x, NN) for f, x in zip(flat, five)]
        for d, f, side, end in zip(ds, flat, sides, ends):

            def at(offset):
                return lax.rem(d + offset + 2 * devices, devices)

            xs[at(-gy), first : first + 1, :] = end[0:1]
            xs[at(-gy), first + 1 : first + 2, 4 * width :] = end[1:2, 4 * width :]
            xs[at(gy), first + 2 : first + 3, :] = end[2:3]
            xs[at(gy), first + 3 : first + 4, 4 * width :] = end[3:4, 4 * width :]
            xs[at(-gy - 1), first + 4 : first + 5, 3 * width :] = end[4:5, 3 * width :]
            xs[at(-gy + 1), first + 5 : first + 6, 3 * width :] = end[5:6, 3 * width :]
            xs[at(gy - 1), first + 6 : first + 7, 3 * width :] = end[6:7, 3 * width :]
            xs[at(gy + 1), first + 7 : first + 8, 3 * width :] = end[7:8, 3 * width :]
            xs[at(-1), first + 4 : first + 8, 0:width] = side[4:8]
            xs[at(1), first + 4 : first + 8, width : 2 * width] = side[12:16]
            xs[at(-1), first + 4 : first + 6, 2 * width : 3 * width] = side[20:22]
            xs[at(1), first + 6 : first + 8, 2 * width : 3 * width] = side[22:24]
            xs[d, first + 1 : first + 2, 0:width] = f
        return 0

    lax.fori_loop(0, devices // group, owners, 0)

    def out(d, _):
        send[d] = xs[d].astype(BF16)
        return 0

    lax.fori_loop(0, devices, out, 0, unroll=8)


def forward(flux, w, src, own, dst, devices, cap, gy, parts=20):
    total, width, _ = w.shape
    chunk = up(cap + 8, 16)
    fields = flux.shape[1]
    wide = SENT * width
    return pl.pallas_call(
        functools.partial(forward_kernel, parts, cap, gy),
        in_specs=[SMEM, SMEM, SMEM, VMEM, ANY],
        out_specs=[VMEM, SMEM],
        scratch_shapes=[
            pltpu.VMEM(w.shape, BF16),
            pltpu.VMEM(flux.shape, BF16),
            pltpu.VMEM((devices * cap * fields, width), F32),
            pltpu.VMEM((devices * cap, width), F32),
            pltpu.VMEM((devices, chunk, wide), F32),
            pltpu.SMEM((devices,), jnp.int32),
            pltpu.SemaphoreType.DMA((parts,)),
        ],
        out_shape=[jax.ShapeDtypeStruct((devices, chunk, wide), BF16), jax.ShapeDtypeStruct((total,), jnp.int32)],
        compiler_params=kernel_params(58),
        cost_estimate=pl.CostEstimate(flops=2 * total * 8 * width * width, bytes_accessed=total * width * width * 2, transcendentals=0),
        name="forward_remap",
    )(src, own, dst, flux, w)


def columns_kernel(tracers, currents, land, west, east):
    levels = tracers.shape[1]
    width = tracers.shape[3]
    last = width - 1
    lane = iota((width, width), 1)

    def put(held, plane, row, column):
        return jnp.where(lane == row, pltpu.roll(plane, lax.rem(row - column + width, width), 1), held)

    def level(l, held):
        w, e = held
        for t in range(2):
            q = tracers[t, l]
            w = put(put(w, q, t * levels + l, 0), q, (2 + t) * levels + l, 1)
            e = put(put(e, q, t * levels + l, last), q, (2 + t) * levels + l, last - 1)
        u = currents[0, l]
        w = put(put(w, u, 4 * levels + l, 0), u, 6 * levels + l, 1)
        e = put(put(e, u, 4 * levels + l, last), u, 6 * levels + l, last - 1)
        v = currents[1, l]
        return put(w, v, 5 * levels + l, 0), put(e, v, 5 * levels + l, last)

    zero = jnp.zeros((width, width), F32)
    w, e = lax.fori_loop(0, levels, level, (zero, zero))
    wet = land[...].astype(F32)
    w = put(put(w, wet, 7 * levels, 0), wet, 7 * levels + 1, 1)
    e = put(put(e, wet, 7 * levels, last), wet, 7 * levels + 1, last - 1)
    west[...] = w.T
    east[...] = e.T


def rows_kernel(tracers, currents, land, from_west, from_east, south, north):
    levels = tracers.shape[0] // 2 // land.shape[0]
    height, width = land.shape
    lane = iota((1, width), 1)
    for out, edge, second in ((south, 0, 1), (north, height - 1, height - 2)):
        out[0 : 2 * levels] = tracers[pl.ds(edge, 2 * levels, stride=height), :]
        out[2 * levels : 4 * levels] = tracers[pl.ds(second, 2 * levels, stride=height), :]
        out[4 * levels : 6 * levels] = currents[pl.ds(edge, 2 * levels, stride=height), :]
        out[6 * levels : 7 * levels] = currents[pl.ds(levels * height + second, levels, stride=height), :]
        wet = [land[x : x + 1, :].astype(F32) for x in (edge, second)]
        out[7 * levels : 7 * levels + 8] = jnp.concatenate(wet + [jnp.zeros((6, width), F32)], axis=0)
    base = 7 * levels + 8
    for start, stop, at in ((0, 2 * levels, 0), (4 * levels, 6 * levels, 2 * levels), (7 * levels, 7 * levels + 8, 4 * levels)):
        w, e = from_west[start:stop], from_east[start:stop]
        there = slice(base + at, base + at + stop - start)
        south[there] = jnp.where(lane == 0, w, pltpu.roll(e, width - 1, 1))
        north[there] = jnp.where(lane == width - 1, e, pltpu.roll(w, 1, 1))


def plus_side(q, other, speed, speed_other, passable):
    return KH * passable * (other - q) - 0.25 * (speed + speed_other) * passable * (q + other)


def minus_side(q, other, speed, speed_other, passable):
    return KH * passable * (other - q) + 0.25 * (speed_other + speed) * passable * (other + q)


def level_profile(levels, width):
    depth = iota((levels, width), 0).astype(F32)
    return jnp.exp(-depth / 4.0) * (1.0 - jnp.exp(jnp.full((levels, width), -0.25, F32)))


def strip_step(q, q_plus, q_minus, across, across_plus, across_minus, along, corner_q, corner_along, wet, wet_plus, wet_minus, corner_wet, forcing):
    levels, width = q.shape
    lane = iota((1, width), 1)
    row = iota((levels, 1), 0)

    def ahead(x, corner):
        return jnp.where(lane == width - 1, corner, pltpu.roll(x, width - 1, 1))

    def behind(x, corner):
        return jnp.where(lane == 0, corner, pltpu.roll(x, 1, 1))

    total = plus_side(q, q_plus, across, across_plus, wet * wet_plus)
    total += minus_side(q, q_minus, across, across_minus, wet * wet_minus)
    total += plus_side(q, ahead(q, corner_q), along, ahead(along, corner_along), wet * ahead(wet, corner_wet))
    total += minus_side(q, behind(q, corner_q), along, behind(along, corner_along), wet * behind(wet, corner_wet))
    below = jnp.where(row < levels - 1, pltpu.roll(q, levels - 1, 0) - q, 0.0)
    above = jnp.where(row > 0, q - pltpu.roll(q, 1, 0), 0.0)
    return q + total + wet * (KV * (below - above) + forcing)


def strips(tracer, levels, inner, outer, flux):
    width = outer[0].shape[1]
    lane = iota((1, width), 1)
    base = 7 * levels + 8
    north, south, east, west = outer

    def part(x, at, count=levels):
        return x[at : at + count]

    def corners(at, count):
        n, s = part(north, base + at, count), part(south, base + at, count)
        e = jnp.where(lane == width - 1, n, pltpu.roll(s, 1, 1))
        w = jnp.where(lane == width - 1, pltpu.roll(n, width - 1, 1), s)
        return n, s, e, w

    corner_q = corners(tracer * levels, levels)
    corner_u = corners(2 * levels, levels)
    corner_v = corners(3 * levels, levels)
    corner_wet = corners(4 * levels, 1)
    top = (iota((levels, 1), 0) == 0).astype(F32)
    profile = level_profile(levels, width)
    results = []
    for side in range(4):
        near, far = inner[side], outer[side]
        beside, out = part(near, tracer * levels), part(far, (2 + tracer) * levels)
        mid = part(far, tracer * levels)
        speed = 5 if side < 2 else 4
        along = part(far, (9 - speed) * levels)
        corner_along = (corner_u if side < 2 else corner_v)[side]
        across, across_in, across_out = part(far, speed * levels), part(near, speed * levels), part(far, 6 * levels)
        wet, wet_in, wet_out = part(far, 7 * levels, 1), part(near, 7 * levels, 1), part(far, 7 * levels + 1, 1)
        shortwave, heat, salt = flux[side]
        forcing = 0.3 * profile * shortwave + top * heat if tracer == 0 else top * salt
        if side % 2 == 0:
            pairs = (out, beside, across, across_out, across_in)
            wets = (wet, wet_out, wet_in)
        else:
            pairs = (beside, out, across, across_in, across_out)
            wets = (wet, wet_in, wet_out)
        results.append(strip_step(mid, *pairs, along, corner_q[side], corner_along, *wets, corner_wet[side], forcing))
    return results


def shifts(plane, north, south, east, west):
    height, width = plane.shape
    lane, row = iota(plane.shape, 1), iota(plane.shape, 0)
    return (
        jnp.where(lane == width - 1, east, pltpu.roll(plane, width - 1, 1)),
        jnp.where(lane == 0, west, pltpu.roll(plane, 1, 1)),
        jnp.where(row == height - 1, north, pltpu.roll(plane, height - 1, 0)),
        jnp.where(row == 0, south, pltpu.roll(plane, 1, 0)),
    )


def wet_products(wet, north, south, east, west):
    return [wet * other for other in shifts(wet, north, south, east, west)]


def coefficients(u, v, u_east, u_west, v_north, v_south, passable):
    east, west, north, south = passable
    height, width = u.shape
    lane, row = iota(u.shape, 1), iota(u.shape, 0)
    e = jnp.where(lane == width - 1, u_east, pltpu.roll(u, width - 1, 1))
    w = jnp.where(lane == 0, u_west, pltpu.roll(u, 1, 1))
    n = jnp.where(row == height - 1, v_north, pltpu.roll(v, height - 1, 0))
    s = jnp.where(row == 0, v_south, pltpu.roll(v, 1, 0))
    flow_e, flow_w = 0.25 * (u + e) * east, 0.25 * (w + u) * west
    flow_n, flow_s = 0.25 * (v + n) * north, 0.25 * (s + v) * south
    own = 1.0 + (flow_w - flow_e) + (flow_s - flow_n) - KH * (east + west + north + south)
    return own, KH * east - flow_e, KH * west + flow_w, KH * north - flow_n, KH * south + flow_s


def column(turned, index, lane):
    return pltpu.roll(turned, lax.rem(lane - index + 2 * turned.shape[1], turned.shape[1]), 1)


def corrected(edge, x_rows):
    row = iota((edge.shape[0], 1), 0)
    for at, x in x_rows:
        edge = edge + jnp.where(row == at, 0.1 * x, 0.0)
    return edge


def surface_kernel(
    cap, levels, got, tracers, currents, land, own_n, own_s, own_e, own_w, from_n, from_s, from_e, from_w,
    back, flux, rim, in_n, in_s, in_e, in_w, out_n, out_s, out_e, out_w,
):
    devices, chunk, wide = got.shape
    height, width = land.shape
    first = chunk - 8
    last = width - 1
    lane = iota((1, width), 1)
    ext = got[0, first:chunk, :].astype(F32)
    lines = [ext[1:2, :chunk]]
    for d in range(1, devices):
        piece = got[d, first:chunk, :].astype(F32)
        lines.append(piece[1:2, :chunk])
        ext = ext + piece
    where = jnp.concatenate(lines, axis=1)
    hot = (iota((height, devices * chunk), 0).astype(F32) == where).astype(F32)
    sums = dot(hot.astype(BF16), got[...].reshape(devices * chunk, wide), NN)
    shortwave, heat, salt, stress_u, stress_v = [sums[:, f * width : (f + 1) * width] for f in range(SENT)]
    wet = land[...].astype(F32)
    u0 = currents[0, 0] + 0.1 * stress_u
    v0 = currents[1, 0] + 0.1 * stress_v
    flux[0], flux[1], flux[2], flux[3], flux[4] = shortwave, heat, salt, u0, v0
    rim[...] = ext

    def block(r, b):
        return ext[r : r + 1, b * width : (b + 1) * width]

    n_flux, s_flux = [[block(r, b) for b in range(SENT)] for r in (0, 2)]
    ne, nw, se, sw = [[block(r, b) for b in (3, 4)] for r in (4, 5, 6, 7)]
    level0_u, level0_v, second = 4 * levels, 5 * levels, 6 * levels
    base = 7 * levels + 8
    corner_n = jnp.where(lane == last, pltpu.roll(ne[0], last, 1), pltpu.roll(nw[0], 1, 1))
    corner_s = jnp.where(lane == last, pltpu.roll(se[0], last, 1), pltpu.roll(sw[0], 1, 1))
    corner_n_v = jnp.where(lane == last, pltpu.roll(ne[1], last, 1), pltpu.roll(nw[1], 1, 1))
    corner_s_v = jnp.where(lane == last, pltpu.roll(se[1], last, 1), pltpu.roll(sw[1], 1, 1))
    far_n = corrected(
        from_n[...],
        [(level0_u, n_flux[3]), (level0_v, n_flux[4]), (second, block(1, 4)), (base + 2 * levels, corner_n), (base + 3 * levels, corner_n_v)],
    )
    far_s = corrected(
        from_s[...],
        [(level0_u, s_flux[3]), (level0_v, s_flux[4]), (second, block(3, 4)), (base + 2 * levels, corner_s), (base + 3 * levels, corner_s_v)],
    )
    far_e = corrected(from_e[...], [(level0_u, block(6, 0)), (level0_v, block(7, 0)), (second, block(5, 2))])
    far_w = corrected(from_w[...], [(level0_u, block(6, 1)), (level0_v, block(7, 1)), (second, block(7, 2))])
    turned = stress_u.T
    near_n = corrected(own_n[...], [(level0_v, stress_v[height - 1 : height])])
    near_s = corrected(own_s[...], [(level0_v, stress_v[0:1])])
    near_e = corrected(own_e[...], [(level0_u, turned[last : last + 1])])
    near_w = corrected(own_w[...], [(level0_u, turned[0:1])])
    in_n[...], in_s[...], in_e[...], in_w[...] = near_n, near_s, near_e, near_w
    out_n[...], out_s[...], out_e[...], out_w[...] = far_n, far_s, far_e, far_w

    e_turned, w_turned = far_e.T, far_w.T
    east = lambda index: column(e_turned, index, last)
    west = lambda index: column(w_turned, index, 0)
    passable = wet_products(
        wet, far_n[7 * levels : 7 * levels + 1], far_s[7 * levels : 7 * levels + 1], east(7 * levels), west(7 * levels)
    )
    lines = strips(0, levels, (near_n, near_s, near_e, near_w), (far_n, far_s, far_e, far_w), rim_flux(ext, width))
    profile = level_profile(levels, width)
    mix = KV * wet
    warm = 0.3 * wet * shortwave

    def weights(l, u, v):
        v_n, v_s = [x[5 * levels + l : 5 * levels + l + 1] for x in (far_n, far_s)]
        return coefficients(u, v, east(4 * levels + l), west(4 * levels + l), v_n, v_s, passable)

    def horizontal(c, q, halo):
        e, w, n, s = shifts(q, *halo)
        return c[0] * q + c[1] * e + c[2] * w + c[3] * n + c[4] * s

    def start(l):
        return far_n[l : l + 1], far_s[l : l + 1], east(l), west(l)

    q0, q1, q2 = tracers[0, 0], tracers[0, 1], tracers[0, 2]
    c0 = weights(0, u0, v0)
    c1 = weights(1, currents[0, 1], currents[1, 1])
    t0 = horizontal(c0, q0, start(0)) + mix * (q1 - q0) + warm * profile[0:1] + wet * heat
    t1 = horizontal(c1, q1, start(1)) + mix * ((q2 - q1) - (q1 - q0)) + warm * profile[1:2]
    sides = jnp.concatenate([lines[2][0:8], lines[3][0:8], jnp.zeros((width - 16, width), F32)], axis=0).T
    halo = lines[0][0:1], lines[1][0:1], column(sides, 0, last), column(sides, 8, 0)
    t0 = horizontal(c0, t0, halo) + mix * (t1 - t0) + warm * profile[0:1] + wet * heat
    sst = t0.astype(BF16)
    picked = dot(hot.T.astype(BF16), sst, NN).reshape(devices, chunk, width)
    back[...] = picked[:, :cap].astype(BF16)


def rim_flux(ext, width):
    def block(r, b):
        return ext[r : r + 1, b * width : (b + 1) * width]

    return (
        (block(0, 0), block(0, 1), block(0, 2)),
        (block(2, 0), block(2, 1), block(2, 2)),
        (block(4, 0), block(5, 0), block(4, 2)),
        (block(4, 1), block(5, 1), block(6, 2)),
    )


def stencil_kernel(
    tracers, currents, land, flux, rim, in_n, in_s, in_e, in_w, out_n, out_s, out_e, out_w,
    out, held, weights, line_n, line_s, depth, forced, passing,
):
    levels = tracers.shape[1]
    height, width = land.shape
    last = width - 1
    wet = land[...].astype(F32)
    far_n, far_s, far_e, far_w = out_n[...], out_s[...], out_e[...], out_w[...]
    e_turned, w_turned = far_e.T, far_w.T
    at = 7 * levels
    for i, x in enumerate(
        wet_products(wet, far_n[at : at + 1], far_s[at : at + 1], column(e_turned, at, last), column(w_turned, at, 0))
    ):
        passing[i] = x
    forced[0], forced[1], forced[2] = 0.3 * wet * flux[0], wet * flux[1], wet * flux[2]
    depth[...] = level_profile(levels, width)
    columns = []
    for tracer in range(2):
        lines = strips(
            tracer, levels, (in_n[...], in_s[...], in_e[...], in_w[...]), (far_n, far_s, far_e, far_w), rim_flux(rim[...], width)
        )
        line_n[tracer * levels : (tracer + 1) * levels] = lines[0]
        line_s[tracer * levels : (tracer + 1) * levels] = lines[1]
        columns.append(lines[2:])
    blank = jnp.zeros((width - 2 * levels, width), F32)
    e_later, w_later = [jnp.concatenate([columns[0][i], columns[1][i], blank], axis=0).T for i in range(2)]

    def update(c, q, halo, under, over, forcing):
        e, w, n, s = shifts(q, *halo)
        mixed = KV * land[...].astype(F32) * ((under - q) - (q - over))
        return c[0] * q + c[1] * e + c[2] * w + c[3] * n + c[4] * s + mixed + forcing

    def forcing(tracer, l):
        top = jnp.where(l == 0, 1.0, 0.0)
        if tracer == 0:
            return forced[0] * depth[pl.ds(l, 1), :] + top * forced[1]
        return top * forced[2]

    def first_step(l, _):
        surface = l == 0
        u = jnp.where(surface, flux[3], currents[0, l])
        v = jnp.where(surface, flux[4], currents[1, l])
        row = 5 * levels + l
        c = coefficients(
            u, v, column(e_turned, 4 * levels + l, last), column(w_turned, 4 * levels + l, 0),
            out_n[pl.ds(row, 1), :], out_s[pl.ds(row, 1), :], [passing[i] for i in range(4)],
        )
        for i, x in enumerate(c):
            weights[i, l] = x
        for tracer in range(2):
            row = tracer * levels + l
            halo = out_n[pl.ds(row, 1), :], out_s[pl.ds(row, 1), :], column(e_turned, row, last), column(w_turned, row, 0)
            under, over = tracers[tracer, jnp.minimum(l + 1, levels - 1)], tracers[tracer, jnp.maximum(l - 1, 0)]
            held[tracer, l] = update(c, tracers[tracer, l], halo, under, over, forcing(tracer, l))
        return 0

    lax.fori_loop(0, levels, first_step, 0)

    def second_step(l, _):
        c = [weights[i, l] for i in range(5)]
        for tracer in range(2):
            row = tracer * levels + l
            halo = line_n[pl.ds(row, 1), :], line_s[pl.ds(row, 1), :], column(e_later, row, last), column(w_later, row, 0)
            under, over = held[tracer, jnp.minimum(l + 1, levels - 1)], held[tracer, jnp.maximum(l - 1, 0)]
            out[tracer, l] = update(c, held[tracer, l], halo, under, over, forcing(tracer, l))
        return 0

    lax.fori_loop(0, levels, second_step, 0)


def backward_kernel(batch, slots, src, back, w, out, wide, picked, terms):
    step = pl.program_id(0)
    total, width = terms.shape
    blocks = out.shape[0]

    @pl.when(step == 0)
    def _():
        wide[...] = back[...].astype(F32).reshape(wide.shape)

        def pick(i, _):
            for j in range(8):
                picked[pl.ds(i * 8 + j, 1), :] = wide[pl.ds(slots[i * 8 + j], 1), :]
            return 0

        lax.fori_loop(0, total // 8, pick, 0, unroll=2)

    row = iota((16, width), 0)
    for g in range(batch // 16):
        at = pl.multiple_of(step * batch + g * 16, 16)
        rows = picked[pl.ds(at, 16), :]
        left = [jnp.where((row == r) | (row == 8 + r), rows, 0.0).astype(BF16) for r in range(8)]
        block = w[g * 16 : (g + 1) * 16].reshape(2, 8 * width, width)
        both = dot(jnp.concatenate(left, axis=1), jnp.concatenate([block[0], block[1]], axis=1), NN)
        terms[pl.ds(at, 8), :] = both[:8, :width]
        terms[pl.ds(at + 8, 8), :] = both[8:, width:]

    @pl.when(step == pl.num_programs(0) - 1)
    def _():
        hot = (iota((blocks, total), 0) == src[...]).astype(F32).astype(BF16)
        value = terms[...]
        high = value.astype(BF16)
        low = (value - high.astype(F32)).astype(BF16)
        both = dot(hot, jnp.concatenate([high, low], axis=1), NN)
        out[...] = both[:, :width] + both[:, width:]


def backward(back, w, src, slots, blocks, batch=64):
    total, width, _ = w.shape
    devices, cap, _ = back.shape
    return pl.pallas_call(
        functools.partial(backward_kernel, batch),
        grid_spec=pltpu.PrefetchScalarGridSpec(
            num_scalar_prefetch=1,
            grid=(total // batch,),
            in_specs=[
                pl.BlockSpec((1, total), lambda i, *_: (0, 0)),
                pl.BlockSpec(back.shape, lambda i, *_: (0, 0, 0)),
                pl.BlockSpec((batch, width, width), lambda i, *_: (i, 0, 0)),
            ],
            out_specs=pl.BlockSpec((blocks, width), lambda i, *_: (0, 0)),
            scratch_shapes=[
                pltpu.VMEM((devices * cap, width), F32),
                pltpu.VMEM((total, width), F32),
                pltpu.VMEM((total, width), F32),
            ],
        ),
        out_shape=jax.ShapeDtypeStruct((blocks, width), F32),
        compiler_params=kernel_params(24),
        cost_estimate=pl.CostEstimate(flops=2 * total * 8 * width * width, bytes_accessed=total * width * width * 2, transcendentals=0),
        name="backward_remap",
    )(slots, src.reshape(1, total), back, w)


def kernel(body, outs, name, mebibytes, bytes_accessed, scratch=()):
    return pl.pallas_call(
        body,
        out_shape=[jax.ShapeDtypeStruct(shape, dtype) for shape, dtype in outs],
        scratch_shapes=list(scratch),
        compiler_params=kernel_params(mebibytes),
        cost_estimate=pl.CostEstimate(flops=bytes_accessed, bytes_accessed=bytes_accessed, transcendentals=0),
        name=name,
    )


def neighbours(axis):
    count = lax.axis_size(axis)
    forward_pairs = [(i, i + 1) for i in range(count - 1)]
    return forward_pairs, [(b, a) for a, b in forward_pairs]


def on_device(atm_flux, remap_weights, remap_src, remap_dst, remap_owner, tracers, currents, land_sea):
    devices = lax.axis_size(EVERY)
    gy = lax.axis_size("gy")
    total, width, _ = remap_weights.shape
    _, levels, height, _ = tracers.shape
    cap = up(2 * total // devices, 8)

    send, slots = forward(atm_flux, remap_weights, remap_src, remap_owner[:, 0], remap_dst, devices, cap, gy)
    got = lax.all_to_all(send, EVERY, split_axis=0, concat_axis=0, tiled=True)

    side = (width, width)
    end = (7 * levels + 80, width)
    own_w, own_e = kernel(columns_kernel, [(side, F32)] * 2, "edge_columns", 16, 1 << 22)(tracers, currents, land_sea)
    to_north, to_south = neighbours(NORTH)
    to_east, to_west = neighbours("gy")
    from_e = lax.ppermute(own_w, "gy", to_west)
    from_w = lax.ppermute(own_e, "gy", to_east)
    own_s, own_n = kernel(rows_kernel, [(end, F32)] * 2, "edge_rows", 16, 1 << 20)(
        tracers.reshape(-1, width), currents.reshape(-1, width), land_sea, from_w, from_e
    )
    from_n = lax.ppermute(own_s, NORTH, to_south)
    from_s = lax.ppermute(own_n, NORTH, to_north)

    back, flux, rim, *edges = kernel(
        functools.partial(surface_kernel, cap, levels),
        [((devices, cap, width), BF16), ((5, height, width), F32), ((8, SENT * width), F32)] + ([(end, F32)] * 2 + [(side, F32)] * 2) * 2,
        "surface",
        32,
        1 << 22,
    )(got, tracers[0:1, 0:3], currents[:, 0:2], land_sea, own_n, own_s, own_e, own_w, from_n, from_s, from_e, from_w)
    returned = lax.all_to_all(back, EVERY, split_axis=0, concat_axis=0, tiled=True)

    plane = (height, width)
    (tracers_out,) = kernel(
        stencil_kernel,
        [(tracers.shape, F32)],
        "substeps",
        32,
        1 << 24,
        [
            pltpu.VMEM(tracers.shape, F32),
            pltpu.VMEM((5, levels) + plane, F32),
            pltpu.VMEM((2 * levels, width), F32),
            pltpu.VMEM((2 * levels, width), F32),
            pltpu.VMEM((levels, width), F32),
            pltpu.VMEM((3,) + plane, F32),
            pltpu.VMEM((4,) + plane, F32),
        ],
    )(tracers, currents, land_sea, flux, rim, *edges)
    return tracers_out, backward(returned, remap_weights, remap_src, slots, atm_flux.shape[0])


def solution(mesh):
    return jax.shard_map(
        on_device,
        mesh=mesh,
        in_specs=(
            P(EVERY, None, None),
            P(EVERY, None, None),
            P(EVERY),
            P(EVERY),
            P(EVERY, None),
            P(None, None, NORTH, "gy"),
            P(None, None, NORTH, "gy"),
            P(NORTH, "gy"),
        ),
        out_specs=(P(None, None, NORTH, "gy"), P(EVERY, None)),
        check_vma=False,
    )
```

time: 234 us -> 120 us (0.51)
  Pallas kernels: 0 us -> 42.2 us
  starting transfers between devices: 59.4 us -> 21.5 us
  matrix products: 32.1 us -> 0 us
  local copies, waits for them, and re-layouts: 54.1 us -> 22.5 us
  other arithmetic: 29 us -> 1.29 us
  waiting for transfers between devices: 57.3 us -> 31 us
    pallas_call x0 -> x6, Pallas kernels: none -> 42.2 us  [the longest x1 17.3 us: forward(): pl.pallas_call(functools.partial(forward_kernel, parts, cap, gy), in_spec...]
    dot_general x5 -> x0, matrix products: 32.1 us -> none  [the longest x1 15.1 us: on_device(): jnp.einsum('kij,kfj->kfi', remap_weights, gathered, preferred_element_typ...]
    ppermute x12 -> x4, starting transfers between devices: 37.8 us -> 9.23 us  [the longest x1 4.55 us: on_device(): from_s = lax.ppermute(own_n, NORTH, to_north)]
    slice x12 -> x2, local copies, waits for them, and re-layouts: 24.7 us -> 0.03 us  [the longest x1 0.02 us: on_device(): currents[:, 0:2]]
    ppermute x12 -> x4, waiting for transfers between devices: 38.7 us -> 17.7 us  [the longest x1 7.95 us: on_device(): from_s = lax.ppermute(own_n, NORTH, to_north)]
    unnamed x62 -> x54, local copies, waits for them, and re-layouts: 6.42 us -> 22.4 us
    add x6 -> x0, other arithmetic: 14.9 us -> none  [the longest x2 12.2 us: substep(): return centre + wet_centre * (advect + spread + vertical + forcing)]
    ppermute x6 -> x0, local copies, waits for them, and re-layouts: 14.4 us -> none  [the longest x3 7.25 us: extended_2(): lax.ppermute(lax.slice_in_dim(block, 0, width, axis=dim), axis, backward)]
  transfers between devices with their start and end apart: 15 -> 6, of which waited for: 5 -> 4; matrix products, arithmetic and copies ran while one was open for 24% -> 0% of each run, Pallas kernels for 0% -> 13%
where the time goes in v1:
time: 120 us; the launch traced here: 119 us
  Pallas kernels  42.2 us (35%)
  waiting for transfers between devices  31 us (26%)
  local copies, waits for them, and re-layouts  22.5 us (19%)
  starting transfers between devices  21.5 us (18%)
  other arithmetic  1.29 us (1%)
    unnamed x54, local copies, waits for them, and re-layouts  22.4 us
    pallas_call x1, Pallas kernels, forward(): pl.pallas_call(functools.partial(forward_kernel, parts, cap, gy), in_spec...  17.3 us
    all_to_all x1, waiting for transfers between devices, on_device(): got = lax.all_to_all(send, EVERY, split_axis=0, concat_axis=0, tiled=True)  13.3 us
    pallas_call x1, Pallas kernels, on_device(): kernel(stencil_kernel, [(tracers.shape, F32)], 'substeps', 32, 1 << 24, [...  10.2 us
    ppermute x1, waiting for transfers between devices, on_device(): from_s = lax.ppermute(own_n, NORTH, to_north)  7.95 us
    all_to_all x1, starting transfers between devices, on_device(): got = lax.all_to_all(send, EVERY, split_axis=0, concat_axis=0, tiled=True)  7.43 us
    ppermute x1, waiting for transfers between devices, on_device(): from_n = lax.ppermute(own_s, NORTH, to_south)  6.78 us
    pallas_call x1, Pallas kernels, backward(): pl.pallas_call(functools.partial(backward_kernel, batch), grid_spec=pltpu...  6.06 us
  transfers between devices with their start and end apart: 6, of which 4 were waited for; matrix products, arithmetic and copies ran while one was open for 0% of the time, Pallas kernels for 13%

profile of v1, /device:TPU:0, one launch (start us, length us, event | category | flops | bytes accessed | tf_op | source)
XLA Modules:
  0.0 119.4 jit_solution(11713832428480061772)
XLA Ops:
  0.6 1.3 %reduce.own = s32[640]{0:T(1024)} reduce(s32[640,1]{0,1:T(1,128)} %param.12, s32[]{:T(128)} %constant), dimensions={1}, to_apply=%param.12.reduce_sub_computation | reduce | bytes 5124 | tf_op args[4]
  1.9 17.3 %forward_remap.1 = (bf16[32,48,640]{2,1,0:T(8,128)(2,1)}, s32[640]{0:T(1024)}) custom-call(s32[640]{0:T(1024)} %src.1, s32[640]{0:T(1024)} %reduce.own, s32[640]{0:T(1024)} %dst.1, bf16[160,8,128]{2,1,0:T(8,128)(2,1)} %flux.1, bf16[640,128,128]{2,1,0:T(8,128)(2,1)} %w.3), custom_call_target="tpu_custom_call" | custom-call | flops 167772160 | bytes 20971520 | tf_op jit(solution)/shard_map/forward_remap/pallas_call | solution.py:167
  19.2 7.4 %all-to-all-start = ((bf16[32,48,640]{2,1,0:T(8,128)(2,1)}), bf16[32,48,640]{2,1,0:T(8,128)(2,1)}, u32[]{:S(2)}, u32[]{:S(2)}) async-start(bf16[32,48,640]{2,1,0:T(8,128)(2,1)} %get-tuple-element.19), calls=%async_computation | async-start | bytes 3932160 | tf_op jit(solution)/shard_map/all_to_all | solution.py:612
  26.7 1.6 %copy-done.2 = f32[2,16,128,128]{3,2,1,0:T(8,128)S(1)} copy-done((f32[2,16,128,128]{3,2,1,0:T(8,128)S(1)}, f32[2,16,128,128]{3,2,1,0:T(8,128)}, u32[]{:S(2)}) %copy-start.2) | copy-done | bytes 2097176
  28.3 5.1 %edge_columns.1 = (f32[128,128]{1,0:T(8,128)S(1)}, f32[128,128]{1,0:T(8,128)S(1)}) custom-call(f32[2,16,128,128]{3,2,1,0:T(8,128)S(1)} %copy-done.2, f32[2,16,128,128]{3,2,1,0:T(8,128)S(1)} %copy-done.1, s32[128,128]{1,0:T(8,128)S(1)} %copy-done.4), custom_call_target="tpu_custom_call" | custom-call | flops 4194304 | bytes 4194304 | tf_op jit(solution)/shard_map/edge_columns/pallas_call | solution.py:616
  33.4 2.1 %collective-permute-start = (f32[128,128]{1,0:T(8,128)S(1)}, f32[128,128]{1,0:T(8,128)S(1)}, u32[]{:S(2)}, u32[]{:S(2)}) collective-permute-start(f32[128,128]{1,0:T(8,128)S(1)} %get-tuple-element.20.own_e), channel_id=1, source_target_pairs={{0,1},{1,2},{2,3},{4,5},{5,6},{6,7},{8,9},{9,10},{10,11},{12,13},{... | collective-permute-start | bytes 196616 | tf_op jit(solution)/shard_map/ppermute | solution.py:620
  35.5 1.3 %collective-permute-start.1 = (f32[128,128]{1,0:T(8,128)S(1)}, f32[128,128]{1,0:T(8,128)S(1)}, u32[]{:S(2)}, u32[]{:S(2)}) collective-permute-start(f32[128,128]{1,0:T(8,128)S(1)} %get-tuple-element.21.own_w), channel_id=1, source_target_pairs={{1,0},{2,1},{3,2},{5,4},{6,5},{7,6},{9,8},{10,9},{11,10},{13,12},{... | collective-permute-start | bytes 196616 | tf_op jit(solution)/shard_map/ppermute | solution.py:619
  36.8 3.0 %collective-permute-done.1.from_east.from_e = f32[128,128]{1,0:T(8,128)S(1)} collective-permute-done((f32[128,128]{1,0:T(8,128)S(1)}, f32[128,128]{1,0:T(8,128)S(1)}, u32[]{:S(2)}, u32[]{:S(2)}) %collective-permute-start.1) | collective-permute-done | bytes 65568 | tf_op jit(solution)/shard_map/ppermute | solution.py:619
  39.9 1.3 %collective-permute-start.2 = (f32[192,128]{1,0:T(8,128)S(1)}, f32[192,128]{1,0:T(8,128)S(1)}, u32[]{:S(2)}, u32[]{:S(2)}) collective-permute-start(f32[192,128]{1,0:T(8,128)S(1)} %get-tuple-element.23.own_s), channel_id=1, source_target_pairs={{4,0},{8,4},{12,8},{16,12},{20,16},{24,20},{28,24},{5,1},{9,5},{13... | collective-permute-start | bytes 294920 | tf_op jit(solution)/shard_map/ppermute | solution.py:624
  41.2 4.6 %collective-permute-start.3 = (f32[192,128]{1,0:T(8,128)S(1)}, f32[192,128]{1,0:T(8,128)S(1)}, u32[]{:S(2)}, u32[]{:S(2)}) collective-permute-start(f32[192,128]{1,0:T(8,128)S(1)} %get-tuple-element.22.own_n), channel_id=1, source_target_pairs={{0,4},{4,8},{8,12},{12,16},{16,20},{20,24},{24,28},{1,5},{5,9},{9,... | collective-permute-start | bytes 294920 | tf_op jit(solution)/shard_map/ppermute | solution.py:625
  45.8 6.8 %collective-permute-done.2.from_n = f32[192,128]{1,0:T(8,128)S(1)} collective-permute-done((f32[192,128]{1,0:T(8,128)S(1)}, f32[192,128]{1,0:T(8,128)S(1)}, u32[]{:S(2)}, u32[]{:S(2)}) %collective-permute-start.2) | collective-permute-done | bytes 98336 | tf_op jit(solution)/shard_map/ppermute | solution.py:624
  52.6 0.6 copy-done.9
  53.3 8.0 %collective-permute-done.3.from_s = f32[192,128]{1,0:T(8,128)S(1)} collective-permute-done((f32[192,128]{1,0:T(8,128)S(1)}, f32[192,128]{1,0:T(8,128)S(1)}, u32[]{:S(2)}, u32[]{:S(2)}) %collective-permute-start.3) | collective-permute-done | bytes 98336 | tf_op jit(solution)/shard_map/ppermute | solution.py:625
  61.2 0.6 copy-done.11
  61.8 13.3 %all-to-all-done.got = bf16[32,48,640]{2,1,0:T(8,128)(2,1)} async-done(((bf16[32,48,640]{2,1,0:T(8,128)(2,1)}), bf16[32,48,640]{2,1,0:T(8,128)(2,1)}, u32[]{:S(2)}, u32[]{:S(2)}) %all-to-all-start) | async-done | bytes 1966112 | tf_op jit(solution)/shard_map/all_to_all | solution.py:612
  75.2 0.9 copy-done.6
  76.1 0.9 copy-done.8
  76.9 0.9 copy-done.10
  77.8 0.9 copy-done.12
  78.7 0.8 copy-done.20
  79.6 0.8 copy-done.22
  80.4 3.5 %surface.1 = (bf16[32,40,128]{2,1,0:T(8,128)(2,1)}, f32[5,128,128]{2,1,0:T(8,128)S(1)}, f32[8,640]{1,0:T(8,128)S(1)}, f32[192,128]{1,0:T(8,128)S(1)}, f32[192,12...) custom-call(bf16[32,48,640]{2,1,0:T(8,128)(2,1)} %all-to-all-done.go, ...), custom_call_target="tpu_custom_call" | custom-call | flops 4194304 | bytes 4194304 | tf_op jit(solution)/shard_map/surface/pallas_call | solution.py:627
  85.2 0.6 copy-done.17
  86.4 4.9 %all-to-all-start.1 = ((bf16[32,40,128]{2,1,0:T(8,128)(2,1)}), bf16[32,40,128]{2,1,0:T(8,128)(2,1)S(1)}, u32[]{:S(2)}, u32[]{:S(2)}) async-start(bf16[32,40,128]{2,1,0:T(8,128)(2,1)} %get-tuple-element.35), calls=%async_computation.1 | async-start | bytes 655360 | tf_op jit(solution)/shard_map/all_to_all | solution.py:634
  91.4 1.6 %copy-done.3 = f32[2,16,128,128]{3,2,1,0:T(8,128)S(1)} copy-done((f32[2,16,128,128]{3,2,1,0:T(8,128)S(1)}, f32[2,16,128,128]{3,2,1,0:T(8,128)}, u32[]{:S(2)}) %copy-start.3) | copy-done | bytes 2097176
  92.9 0.8 copy-done.14
  93.8 0.8 copy-done.16
  94.6 0.8 copy-done.18
  95.5 0.7 copy-done.24
  96.2 10.2 %substeps.1 = f32[2,16,128,128]{3,2,1,0:T(8,128)} custom-call(f32[2,16,128,128]{3,2,1,0:T(8,128)S(1)} %copy-done.3, f32[2,16,128,128]{3,2,1,0:T(8,128)S(1)} %copy-done.1, s32[128,128]{1,0:T(8,128)S(1)} %copy-done.4, f32[5,128,128]{2,1,0:T(8,128)S(1)} %get-tuple-element.24.flux, f32[8,640]{1,0:T(8,128)S(1)} %copy-done.24, ...), custom_call_target="tpu_custom_call" | custom-call | flops 16777216 | bytes 16777216 | tf_op jit(solution)/shard_map/substeps/pallas_call | solution.py:637
  106.4 7.0 %copy-done = bf16[640,128,128]{2,1,0:T(8,128)(2,1)S(1)} copy-done((bf16[640,128,128]{2,1,0:T(8,128)(2,1)S(1)}, bf16[640,128,128]{2,1,0:T(8,128)(2,1)}, u32[]{:S(2)}) %copy-start) | copy-done | bytes 20971544
  113.3 6.1 %backward_remap.1 = f32[160,128]{1,0:T(8,128)} custom-call(s32[640]{0:T(1024)S(1)} %copy-done.25, s32[1,640]{1,0:T(1,128)S(1)} %reshape.15.src, bf16[32,40,128]{2,1,0:T(8,128)(2,1)S(1)} %all-to-all-done.1.back, bf16[640,128,128]{2,1,0:T(8,128)(2,1)S(1)} %copy-done), custom_call_target="tpu_custom_call" | custom-call | flops 167772160 | bytes 20971520 | tf_op jit(solution)/shard_map/backward_remap/pallas_call | solution.py:563
  (44 shorter events, 2.1 us)
Async XLA Ops:
  19.2 7.5 %copy-start.1 = (f32[2,16,128,128]{3,2,1,0:T(8,128)S(1)}, f32[2,16,128,128]{3,2,1,0:T(8,128)}, u32[]{:S(2)}) copy-start(f32[2,16,128,128]{3,2,1,0:T(8,128)} %currents.3) | copy-start | bytes 6291460
  19.2 7.5 %copy-start.4 = (s32[128,128]{1,0:T(8,128)S(1)}, s32[128,128]{1,0:T(8,128)}, u32[]{:S(2)}) copy-start(s32[128,128]{1,0:T(8,128)} %land.7) | copy-start | bytes 196612
  19.2 55.9 %all-to-all-start = ((bf16[32,48,640]{2,1,0:T(8,128)(2,1)}), bf16[32,48,640]{2,1,0:T(8,128)(2,1)}, u32[]{:S(2)}, u32[]{:S(2)}) async-start(bf16[32,48,640]{2,1,0:T(8,128)(2,1)} %get-tuple-element.19), calls=%async_computation | async-start | bytes 3932160 | tf_op jit(solution)/shard_map/all_to_all | solution.py:612
  26.7 1.6 %copy-start.2 = (f32[2,16,128,128]{3,2,1,0:T(8,128)S(1)}, f32[2,16,128,128]{3,2,1,0:T(8,128)}, u32[]{:S(2)}) copy-start(f32[2,16,128,128]{3,2,1,0:T(8,128)} %tracers.3) | copy-start | bytes 6291460
  33.4 6.5 %copy-start.19 = (f32[128,128]{1,0:T(8,128)}, f32[128,128]{1,0:T(8,128)S(1)}, u32[]{:S(2)}) copy-start(f32[128,128]{1,0:T(8,128)S(1)} %get-tuple-element.21.own_w) | copy-start | bytes 196612
  33.4 6.5 %copy-start.21 = (f32[128,128]{1,0:T(8,128)}, f32[128,128]{1,0:T(8,128)S(1)}, u32[]{:S(2)}) copy-start(f32[128,128]{1,0:T(8,128)S(1)} %get-tuple-element.20.own_e) | copy-start | bytes 196612
  33.4 3.4 %collective-permute-start = (f32[128,128]{1,0:T(8,128)S(1)}, f32[128,128]{1,0:T(8,128)S(1)}, u32[]{:S(2)}, u32[]{:S(2)}) collective-permute-start(f32[128,128]{1,0:T(8,128)S(1)} %get-tuple-element.20.own_e), channel_id=1, source_target_pairs={{0,1},{1,2},{2,3},{4,5},{5,6},{6,7},{8,9},{9,10},{10,11},{12,13},{... | collective-permute-start | bytes 196616 | tf_op jit(solution)/shard_map/ppermute | solution.py:620
  35.5 4.3 %collective-permute-start.1 = (f32[128,128]{1,0:T(8,128)S(1)}, f32[128,128]{1,0:T(8,128)S(1)}, u32[]{:S(2)}, u32[]{:S(2)}) collective-permute-start(f32[128,128]{1,0:T(8,128)S(1)} %get-tuple-element.21.own_w), channel_id=1, source_target_pairs={{1,0},{2,1},{3,2},{5,4},{6,5},{7,6},{9,8},{10,9},{11,10},{13,12},{... | collective-permute-start | bytes 196616 | tf_op jit(solution)/shard_map/ppermute | solution.py:619
  39.9 21.3 %copy-start.5 = (f32[192,128]{1,0:T(8,128)}, f32[192,128]{1,0:T(8,128)S(1)}, u32[]{:S(2)}) copy-start(f32[192,128]{1,0:T(8,128)S(1)} %get-tuple-element.23.own_s) | copy-start | bytes 294916
  39.9 21.3 %copy-start.7 = (f32[192,128]{1,0:T(8,128)}, f32[192,128]{1,0:T(8,128)S(1)}, u32[]{:S(2)}) copy-start(f32[192,128]{1,0:T(8,128)S(1)} %get-tuple-element.22.own_n) | copy-start | bytes 294916
  39.9 12.7 %collective-permute-start.2 = (f32[192,128]{1,0:T(8,128)S(1)}, f32[192,128]{1,0:T(8,128)S(1)}, u32[]{:S(2)}, u32[]{:S(2)}) collective-permute-start(f32[192,128]{1,0:T(8,128)S(1)} %get-tuple-element.23.own_s), channel_id=1, source_target_pairs={{4,0},{8,4},{12,8},{16,12},{20,16},{24,20},{28,24},{5,1},{9,5},{13... | collective-permute-start | bytes 294920 | tf_op jit(solution)/shard_map/ppermute | solution.py:624
  41.2 20.0 %collective-permute-start.3 = (f32[192,128]{1,0:T(8,128)S(1)}, f32[192,128]{1,0:T(8,128)S(1)}, u32[]{:S(2)}, u32[]{:S(2)}) collective-permute-start(f32[192,128]{1,0:T(8,128)S(1)} %get-tuple-element.22.own_n), channel_id=1, source_target_pairs={{0,4},{4,8},{8,12},{12,16},{16,20},{20,24},{24,28},{1,5},{5,9},{9,... | collective-permute-start | bytes 294920 | tf_op jit(solution)/shard_map/ppermute | solution.py:625
  45.8 45.5 %copy-start.26 = (s32[640]{0:T(1024)S(1)}, s32[640]{0:T(1024)}, u32[]{:S(2)}) copy-start(s32[640]{0:T(1024)} %src.1) | copy-start | bytes 7684
  52.6 0.6 copy-start.9
  61.2 0.6 copy-start.11
  75.2 0.9 copy-start.6
  76.1 0.9 copy-start.8
  76.9 0.9 copy-start.10
  77.8 0.9 copy-start.12
  78.7 0.8 copy-start.20
  79.6 0.8 copy-start.22
  83.9 0.6 copy-start.13
  84.6 0.6 copy-start.15
  85.2 0.6 copy-start.17
  86.4 19.9 %all-to-all-start.1 = ((bf16[32,40,128]{2,1,0:T(8,128)(2,1)}), bf16[32,40,128]{2,1,0:T(8,128)(2,1)S(1)}, u32[]{:S(2)}, u32[]{:S(2)}) async-start(bf16[32,40,128]{2,1,0:T(8,128)(2,1)} %get-tuple-element.35), calls=%async_computation.1 | async-start | bytes 655360 | tf_op jit(solution)/shard_map/all_to_all | solution.py:634
  91.3 1.6 %copy-start.3 = (f32[2,16,128,128]{3,2,1,0:T(8,128)S(1)}, f32[2,16,128,128]{3,2,1,0:T(8,128)}, u32[]{:S(2)}) copy-start(f32[2,16,128,128]{3,2,1,0:T(8,128)} %tracers.3) | copy-start | bytes 6291460
  92.9 0.8 copy-start.14
  93.8 0.8 copy-start.16
  94.6 0.8 copy-start.18
  95.5 0.7 copy-start.24
  96.2 10.2 %copy-start.25 = (s32[640]{0:T(1024)S(1)}, s32[640]{0:T(1024)}, u32[]{:S(2)}) copy-start(s32[640]{0:T(1024)} %get-tuple-element.34.slots) | copy-start | bytes 7684
  106.4 7.0 %copy-start = (bf16[640,128,128]{2,1,0:T(8,128)(2,1)S(1)}, bf16[640,128,128]{2,1,0:T(8,128)(2,1)}, u32[]{:S(2)}) copy-start(bf16[640,128,128]{2,1,0:T(8,128)(2,1)} %w.3) | copy-start | bytes 62914564
  (1 other events, 0.6 us)

commit v2 on v1

--- a/solution.py
+++ b/solution.py
@@ -40,8 +40,10 @@
 ANY = pl.BlockSpec(memory_space=pl.ANY)
 
 
-def forward_kernel(parts, cap, gy, src, own, dst, flux, w, send, slots, held, mixed, acc, rows, xs, counts, sems):
-    devices, chunk, wide = send.shape
+def forward_kernel(parts, cap, grid, src, own, dst, flux, w, *refs):
+    sends, (slots, held, mixed, acc, rows, xs, counts, sems) = refs[:-8], refs[-8:]
+    n_sec, n_gx, n_gy = grid
+    devices, chunk, wide = xs.shape
     total, width, _ = held.shape
     batch = total // parts
     fields = flux.shape[1]
@@ -114,6 +116,8 @@
     for at, x in enumerate((0, 1, last, last - 1, 0, 0, last, last)):
         wanted = jnp.where(row == at, float(x), wanted)
     group = 8
+    plane = lax.axis_index("sec") * n_gy + lax.axis_index("gy")
+    line = lax.axis_index("gx")
 
     def owners(g, _):
         ds = [g * group + j for j in range(group)]
@@ -131,43 +135,49 @@
         sides = [dot(e, h, NN) for e, h in zip(edge, hot)]
         ends = [dot((f[:, :cap] == wanted).astype(F32).astype(BF16), x, NN) for f, x in zip(flat, five)]
         for d, f, side, end in zip(ds, flat, sides, ends):
+            here = lax.div(d, n_gx) ^ plane
+            here = (lax.div(here, n_gy) * n_gx + (lax.rem(d, n_gx) ^ line)) * n_gy + lax.rem(here, n_gy)
 
             def at(offset):
-                return lax.rem(d + offset + 2 * devices, devices)
-
-            xs[at(-gy), first : first + 1, :] = end[0:1]
-            xs[at(-gy), first + 1 : first + 2, 4 * width :] = end[1:2, 4 * width :]
-            xs[at(gy), first + 2 : first + 3, :] = end[2:3]
-            xs[at(gy), first + 3 : first + 4, 4 * width :] = end[3:4, 4 * width :]
-            xs[at(-gy - 1), first + 4 : first + 5, 3 * width :] = end[4:5, 3 * width :]
-            xs[at(-gy + 1), first + 5 : first + 6, 3 * width :] = end[5:6, 3 * width :]
-            xs[at(gy - 1), first + 6 : first + 7, 3 * width :] = end[6:7, 3 * width :]
-            xs[at(gy + 1), first + 7 : first + 8, 3 * width :] = end[7:8, 3 * width :]
-            xs[at(-1), first + 4 : first + 8, 0:width] = side[4:8]
-            xs[at(1), first + 4 : first + 8, width : 2 * width] = side[12:16]
-            xs[at(-1), first + 4 : first + 6, 2 * width : 3 * width] = side[20:22]
-            xs[at(1), first + 6 : first + 8, 2 * width : 3 * width] = side[22:24]
+                there = lax.rem(here + offset + 2 * devices, devices)
+                x = lax.div(there, n_gy)
+                there = lax.div(x, n_gx) * n_gy + lax.rem(there, n_gy)
+                return (there ^ plane) * n_gx + (lax.rem(x, n_gx) ^ line)
+
+            south_of, north_of, west_of, east_of = at(-n_gy), at(n_gy), at(-1), at(1)
+
+            xs[south_of, first : first + 1, :] = end[0:1]
+            xs[south_of, first + 1 : first + 2, 4 * width :] = end[1:2, 4 * width :]
+            xs[north_of, first + 2 : first + 3, :] = end[2:3]
+            xs[north_of, first + 3 : first + 4, 4 * width :] = end[3:4, 4 * width :]
+            xs[at(-n_gy - 1), first + 4 : first + 5, 3 * width :] = end[4:5, 3 * width :]
+            xs[at(-n_gy + 1), first + 5 : first + 6, 3 * width :] = end[5:6, 3 * width :]
+            xs[at(n_gy - 1), first + 6 : first + 7, 3 * width :] = end[6:7, 3 * width :]
+            xs[at(n_gy + 1), first + 7 : first + 8, 3 * width :] = end[7:8, 3 * width :]
+            xs[west_of, first + 4 : first + 8, 0:width] = side[4:8]
+            xs[east_of, first + 4 : first + 8, width : 2 * width] = side[12:16]
+            xs[west_of, first + 4 : first + 6, 2 * width : 3 * width] = side[20:22]
+            xs[east_of, first + 6 : first + 8, 2 * width : 3 * width] = side[22:24]
             xs[d, first + 1 : first + 2, 0:width] = f
         return 0
 
     lax.fori_loop(0, devices // group, owners, 0)
 
-    def out(d, _):
-        send[d] = xs[d].astype(BF16)
-        return 0
-
-    lax.fori_loop(0, devices, out, 0, unroll=8)
-
-
-def forward(flux, w, src, own, dst, devices, cap, gy, parts=20):
+    for m, send in enumerate(sends):
+        send[...] = xs[m * n_gx : (m + 1) * n_gx].astype(BF16)
+
+
+def forward(flux, w, src, own, dst, grid, cap, parts=20):
+    n_sec, n_gx, n_gy = grid
+    devices = n_sec * n_gx * n_gy
     total, width, _ = w.shape
     chunk = up(cap + 8, 16)
     fields = flux.shape[1]
     wide = SENT * width
     return pl.pallas_call(
-        functools.partial(forward_kernel, parts, cap, gy),
+        functools.partial(forward_kernel, parts, cap, grid),
         in_specs=[SMEM, SMEM, SMEM, VMEM, ANY],
-        out_specs=[VMEM, SMEM],
+        out_specs=[VMEM] * (n_sec * n_gy) + [SMEM],
         scratch_shapes=[
             pltpu.VMEM(w.shape, BF16),
             pltpu.VMEM(flux.shape, BF16),
@@ -177,11 +187,43 @@
             pltpu.SMEM((devices,), jnp.int32),
             pltpu.SemaphoreType.DMA((parts,)),
         ],
-        out_shape=[jax.ShapeDtypeStruct((devices, chunk, wide), BF16), jax.ShapeDtypeStruct((total,), jnp.int32)],
+        out_shape=[jax.ShapeDtypeStruct((n_gx, chunk, wide), BF16)] * (n_sec * n_gy) + [jax.ShapeDtypeStruct((total,), jnp.int32)],
         compiler_params=kernel_params(58),
         cost_estimate=pl.CostEstimate(flops=2 * total * 8 * width * width, bytes_accessed=total * width * width * 2, transcendentals=0),
         name="forward_remap",
     )(src, own, dst, flux, w)
+
+
+def merge_kernel(n_sources, *refs):
+    sources, lines_out, outs = refs[:n_sources], refs[n_sources], refs[n_sources + 1 :]
+    n_gx, chunk, wide = sources[0].shape
+    height = outs[0].shape[0] - 8
+    first = chunk - 8
+    count = len(sources) * chunk
+    for z in range(n_gx):
+        ext = None
+        where = []
+        for source in sources:
+            piece = source[z, first:chunk, :].astype(F32)
+            where.append(piece[1:2, :chunk])
+            ext = piece if ext is None else ext + piece
+        where = jnp.concatenate(where, axis=1)
+        lines_out[z] = where
+        hot = (iota((height, count), 0).astype(F32) == where).astype(F32).astype(BF16)
+        sums = dot(hot, jnp.concatenate([source[z] for source in sources], axis=0), NN)
+        outs[z][...] = jnp.concatenate([sums, ext], axis=0).astype(outs[z].dtype)
+
+
+def spread_kernel(cap, *refs):
+    n_gx, _, count = refs[0].shape
+    lines, tiles, backs = refs[0], refs[1 : 1 + n_gx], refs[1 + n_gx :]
+    chunk = count // len(backs)
+    height, width = tiles[0].shape
+    for z in range(n_gx):
+        hot = (iota((height, count), 0).astype(F32) == lines[z]).astype(F32)
+        picked = dot(hot.T.astype(BF16), tiles[z][...], NN).reshape(len(backs), chunk, width)
+        for m, back in enumerate(backs):
+            back[z] = picked[m, :cap].astype(BF16)
 
 
 def columns_kernel(tracers, currents, land, west, east):
@@ -349,24 +391,17 @@
     return edge
 
 
-def surface_kernel(
-    cap, levels, got, tracers, currents, land, own_n, own_s, own_e, own_w, from_n, from_s, from_e, from_w,
-    back, flux, rim, in_n, in_s, in_e, in_w, out_n, out_s, out_e, out_w,
-):
-    devices, chunk, wide = got.shape
+def surface_kernel(n_gx, levels, *refs):
+    parts, refs = refs[:n_gx], refs[n_gx:]
+    tracers, currents, land, own_n, own_s, own_e, own_w, from_n, from_s, from_e, from_w, *refs = refs
+    surface, flux, rim, in_n, in_s, in_e, in_w, out_n, out_s, out_e, out_w = refs
     height, width = land.shape
-    first = chunk - 8
     last = width - 1
     lane = iota((1, width), 1)
-    ext = got[0, first:chunk, :].astype(F32)
-    lines = [ext[1:2, :chunk]]
-    for d in range(1, devices):
-        piece = got[d, first:chunk, :].astype(F32)
-        lines.append(piece[1:2, :chunk])
-        ext = ext + piece
-    where = jnp.concatenate(lines, axis=1)
-    hot = (iota((height, devices * chunk), 0).astype(F32) == where).astype(F32)
-    sums = dot(hot.astype(BF16), got[...].reshape(devices * chunk, wide), NN)
+    sums = parts[0][...]
+    for part in parts[1:]:
+        sums = sums + part[...].astype(F32)
+    sums, ext = sums[:height], sums[height:]
     shortwave, heat, salt, stress_u, stress_v = [sums[:, f * width : (f + 1) * width] for f in range(SENT)]
     wet = land[...].astype(F32)
     u0 = currents[0, 0] + 0.1 * stress_u
@@ -433,9 +468,7 @@
     sides = jnp.concatenate([lines[2][0:8], lines[3][0:8], jnp.zeros((width - 16, width), F32)], axis=0).T
     halo = lines[0][0:1], lines[1][0:1], column(sides, 0, last), column(sides, 8, 0)
     t0 = horizontal(c0, t0, halo) + mix * (t1 - t0) + warm * profile[0:1] + wet * heat
-    sst = t0.astype(BF16)
-    picked = dot(hot.T.astype(BF16), sst, NN).reshape(devices, chunk, width)
-    back[...] = picked[:, :cap].astype(BF16)
+    surface[...] = t0.astype(BF16)
 
 
 def rim_flux(ext, width):
@@ -521,14 +554,17 @@
     lax.fori_loop(0, levels, second_step, 0)
 
 
-def backward_kernel(batch, slots, src, back, w, out, wide, picked, terms):
+def backward_kernel(batch, n_backs, slots, src, *refs):
+    backs, (w, out, wide, picked, terms) = refs[:n_backs], refs[n_backs:]
     step = pl.program_id(0)
     total, width = terms.shape
     blocks = out.shape[0]
 
     @pl.when(step == 0)
     def _():
-        wide[...] = back[...].astype(F32).reshape(wide.shape)
+        rows = wide.shape[0] // n_backs
+        for m, back in enumerate(backs):
+            wide[m * rows : (m + 1) * rows] = back[...].astype(F32).reshape(rows, width)
 
         def pick(i, _):
             for j in range(8):
@@ -557,22 +593,22 @@
         out[...] = both[:, :width] + both[:, width:]
 
 
-def backward(back, w, src, slots, blocks, batch=64):
+def backward(backs, w, src, slots, blocks, batch=64):
     total, width, _ = w.shape
-    devices, cap, _ = back.shape
+    n_gx, cap, _ = backs[0].shape
     return pl.pallas_call(
-        functools.partial(backward_kernel, batch),
+        functools.partial(backward_kernel, batch, len(backs)),
         grid_spec=pltpu.PrefetchScalarGridSpec(
             num_scalar_prefetch=1,
             grid=(total // batch,),
             in_specs=[
                 pl.BlockSpec((1, total), lambda i, *_: (0, 0)),
-                pl.BlockSpec(back.shape, lambda i, *_: (0, 0, 0)),
+                *[pl.BlockSpec((n_gx, cap, width), lambda i, *_: (0, 0, 0))] * len(backs),
                 pl.BlockSpec((batch, width, width), lambda i, *_: (i, 0, 0)),
             ],
             out_specs=pl.BlockSpec((blocks, width), lambda i, *_: (0, 0)),
             scratch_shapes=[
-                pltpu.VMEM((devices * cap, width), F32),
+                pltpu.VMEM((len(backs) * n_gx * cap, width), F32),
                 pltpu.VMEM((total, width), F32),
                 pltpu.VMEM((total, width), F32),
             ],
@@ -581,7 +617,7 @@
         compiler_params=kernel_params(24),
         cost_estimate=pl.CostEstimate(flops=2 * total * 8 * width * width, bytes_accessed=total * width * width * 2, transcendentals=0),
         name="backward_remap",
-    )(slots, src.reshape(1, total), back, w)
+    )(slots, src.reshape(1, total), *backs, w)
 
 
 def kernel(body, outs, name, mebibytes, bytes_accessed, scratch=()):
@@ -601,15 +637,33 @@
     return forward_pairs, [(b, a) for a, b in forward_pairs]
 
 
+def swapped(array, axes, count, step):
+    return lax.ppermute(array, axes, [(i, i ^ step) for i in range(count)])
+
+
 def on_device(atm_flux, remap_weights, remap_src, remap_dst, remap_owner, tracers, currents, land_sea):
-    devices = lax.axis_size(EVERY)
-    gy = lax.axis_size("gy")
+    grid = n_sec, n_gx, n_gy = [lax.axis_size(axis) for axis in EVERY]
+    planes = n_sec * n_gy
     total, width, _ = remap_weights.shape
     _, levels, height, _ = tracers.shape
-    cap = up(2 * total // devices, 8)
-
-    send, slots = forward(atm_flux, remap_weights, remap_src, remap_owner[:, 0], remap_dst, devices, cap, gy)
-    got = lax.all_to_all(send, EVERY, split_axis=0, concat_axis=0, tiled=True)
+    cap = up(2 * total // (planes * n_gx), 8)
+    wide = SENT * width
+
+    plane = lax.axis_index("sec") * n_gy + lax.axis_index("gy")
+    owner = remap_owner[:, 0]
+    x, y = owner // n_gy, owner % n_gy
+    owner = (((x // n_gx) * n_gy + y) ^ plane) * n_gx + ((x % n_gx) ^ lax.axis_index("gx"))
+    *sends, slots = forward(atm_flux, remap_weights, remap_src, owner, remap_dst, grid, cap)
+    got = [sends[0]] + [swapped(sends[m], ("sec", "gy"), planes, m) for m in range(1, planes)]
+    chunk = sends[0].shape[1]
+    lines, *merged = kernel(
+        functools.partial(merge_kernel, planes),
+        [((n_gx, 1, planes * chunk), F32), ((height + 8, wide), F32)] + [((height + 8, wide), BF16)] * (n_gx - 1),
+        "merge",
+        32,
+        1 << 22,
+    )(*got)
+    parts = [merged[0]] + [swapped(merged[m], "gx", n_gx, m) for m in range(1, n_gx)]
 
     side = (width, width)
     end = (7 * levels + 80, width)
@@ -624,14 +678,18 @@
     from_n = lax.ppermute(own_s, NORTH, to_south)
     from_s = lax.ppermute(own_n, NORTH, to_north)
 
-    back, flux, rim, *edges = kernel(
-        functools.partial(surface_kernel, cap, levels),
-        [((devices, cap, width), BF16), ((5, height, width), F32), ((8, SENT * width), F32)] + ([(end, F32)] * 2 + [(side, F32)] * 2) * 2,
+    surface, flux, rim, *edges = kernel(
+        functools.partial(surface_kernel, n_gx, levels),
+        [((height, width), BF16), ((5, height, width), F32), ((8, wide), F32)] + ([(end, F32)] * 2 + [(side, F32)] * 2) * 2,
         "surface",
         32,
         1 << 22,
-    )(got, tracers[0:1, 0:3], currents[:, 0:2], land_sea, own_n, own_s, own_e, own_w, from_n, from_s, from_e, from_w)
-    returned = lax.all_to_all(back, EVERY, split_axis=0, concat_axis=0, tiled=True)
+    )(*parts, tracers[0:1, 0:3], currents[:, 0:2], land_sea, own_n, own_s, own_e, own_w, from_n, from_s, from_e, from_w)
+    tiles = [surface] + [swapped(surface, "gx", n_gx, m) for m in range(1, n_gx)]
+    backs = kernel(
+        functools.partial(spread_kernel, cap), [((n_gx, cap, width), BF16)] * planes, "spread", 32, 1 << 22
+    )(lines, *tiles)
+    returned = [backs[0]] + [swapped(backs[m], ("sec", "gy"), planes, m) for m in range(1, planes)]
 
     plane = (height, width)
     (tracers_out,) = kernel(

time: 120 us -> 119 us (level)
  starting transfers between devices: 21.5 us -> 37.7 us
  local copies, waits for them, and re-layouts: 22.5 us -> 7.96 us
  waiting for transfers between devices: 31 us -> 28.7 us
    ppermute x0 -> x20, starting transfers between devices: none -> 28.8 us  [swapped(): return lax.ppermute(array, axes, [(i, i ^ step) for i in range(count)])]
    ppermute x0 -> x20, waiting for transfers between devices: none -> 23.3 us  [swapped(): return lax.ppermute(array, axes, [(i, i ^ step) for i in range(count)])]
    unnamed x54 -> x14, local copies, waits for them, and re-layouts: 22.4 us -> 7.93 us
    all_to_all x2 -> x0, waiting for transfers between devices: 13.3 us -> none  [the longest x1 13.3 us: on_device(): got = lax.all_to_all(send, EVERY, split_axis=0, concat_axis=0, tiled=True)]
    all_to_all x2 -> x0, starting transfers between devices: 12.3 us -> none  [the longest x1 7.43 us: on_device(): got = lax.all_to_all(send, EVERY, split_axis=0, concat_axis=0, tiled=True)]
    ppermute x1, waiting for transfers between devices: 7.95 us -> 1.54 us  [on_device(): from_s = lax.ppermute(own_n, NORTH, to_north)]
    ppermute x1, waiting for transfers between devices: 6.78 us -> 0.6 us  [on_device(): from_n = lax.ppermute(own_s, NORTH, to_south)]
    pallas_call x3 -> x5, Pallas kernels: 26.8 us -> 26 us  [the longest x1 18.1 us: forward(): pl.pallas_call(functools.partial(forward_kernel, parts, cap, grid), in_sp...]
  transfers between devices with their start and end apart: 6 -> 24, of which waited for: 4 -> 8; matrix products, arithmetic and copies ran while one was open for 0% -> 0% of each run, Pallas kernels for 13% -> 13%
where the time goes in v2:
time: 119 us; the launch traced here: 118 us
  Pallas kernels  41.4 us (35%)
  starting transfers between devices  37.7 us (32%)
  waiting for transfers between devices  28.7 us (24%)
  local copies, waits for them, and re-layouts  7.96 us (7%)
  other arithmetic  1.32 us (1%)
    ppermute x20, starting transfers between devices, swapped(): return lax.ppermute(array, axes, [(i, i ^ step) for i in range(count)])  28.8 us
    ppermute x20, waiting for transfers between devices, swapped(): return lax.ppermute(array, axes, [(i, i ^ step) for i in range(count)])  23.3 us
    pallas_call x1, Pallas kernels, forward(): pl.pallas_call(functools.partial(forward_kernel, parts, cap, grid), in_sp...  18.1 us
    pallas_call x1, Pallas kernels, on_device(): kernel(stencil_kernel, [(tracers.shape, F32)], 'substeps', 32, 1 << 24, [...  10.2 us
    unnamed x14, local copies, waits for them, and re-layouts  7.93 us
    pallas_call x1, Pallas kernels, backward(): pl.pallas_call(functools.partial(backward_kernel, batch, len(backs)), gri...  6.07 us
    pallas_call x1, Pallas kernels, on_device(): kernel(columns_kernel, [(side, F32)] * 2, 'edge_columns', 16, 1 << 22)  5.11 us
    ppermute x1, starting transfers between devices, on_device(): from_s = lax.ppermute(own_n, NORTH, to_north)  4.55 us
  transfers between devices with their start and end apart: 24, of which 8 were waited for; matrix products, arithmetic and copies ran while one was open for 0% of the time, Pallas kernels for 13%

profile of v2, /device:TPU:0, one launch (start us, length us, event | category | flops | bytes accessed | tf_op | source)
XLA Modules:
  0.0 118.0 jit_solution(2798929006492602866)
XLA Ops:
  0.6 0.7 reduce
  1.3 0.6 fusion.4.own
  2.0 18.1 %forward_remap.1 = (bf16[4,48,640]{2,1,0:T(8,128)(2,1)}, bf16[4,48,640]{2,1,0:T(8,128)(2,1)}, bf16[4,48,640]{2,1,0:T(8,128)(2,1)}, bf16[4,48,640]{2,1,0:T(8,128)...) custom-call(s32[640]{0:T(1024)} %src.1, ...), custom_call_target="tpu_custom_call" | custom-call | flops 167772160 | bytes 20971520 | tf_op jit(solution)/shard_map/forward_remap/pallas_call | solution.py:177
  20.6 2.6 %collective-permute-start.1 = (bf16[4,48,640]{2,1,0:T(8,128)(2,1)}, bf16[4,48,640]{2,1,0:T(8,128)(2,1)S(1)}, u32[]{:S(2)}, u32[]{:S(2)}) collective-permute-start(bf16[4,48,640]{2,1,0:T(8,128)(2,1)} %get-tuple-element.41), channel_id=1, source_target_pairs={{0,2},{1,3},{2,0},{3,1},{16,18},{17,19},{18,16},{19,17},{4,6},{5,7... | collective-permute-start | bytes 737288 | tf_op jit(solution)/shard_map/ppermute | solution.py:641
  23.2 1.8 %collective-permute-start.3 = (bf16[4,48,640]{2,1,0:T(8,128)(2,1)}, bf16[4,48,640]{2,1,0:T(8,128)(2,1)S(1)}, u32[]{:S(2)}, u32[]{:S(2)}) collective-permute-start(bf16[4,48,640]{2,1,0:T(8,128)(2,1)} %get-tuple-element.43), channel_id=1, source_target_pairs={{0,16},{1,17},{2,18},{3,19},{16,0},{17,1},{18,2},{19,3},{4,20},{5,... | collective-permute-start | bytes 737288 | tf_op jit(solution)/shard_map/ppermute | solution.py:641
  25.0 2.6 %collective-permute-start.5 = (bf16[4,48,640]{2,1,0:T(8,128)(2,1)}, bf16[4,48,640]{2,1,0:T(8,128)(2,1)S(1)}, u32[]{:S(2)}, u32[]{:S(2)}) collective-permute-start(bf16[4,48,640]{2,1,0:T(8,128)(2,1)} %get-tuple-element.45), channel_id=1, source_target_pairs={{0,18},{1,19},{2,16},{3,17},{16,2},{17,3},{18,0},{19,1},{4,22},{5,... | collective-permute-start | bytes 737288 | tf_op jit(solution)/shard_map/ppermute | solution.py:641
  27.6 2.6 %collective-permute-done.1.refs_2_ = bf16[4,48,640]{2,1,0:T(8,128)(2,1)S(1)} collective-permute-done((bf16[4,48,640]{2,1,0:T(8,128)(2,1)}, bf16[4,48,640]{2,1,0:T(8,128)(2,1)S(1)}, u32[]{:S(2)}, u32[]{:S(2)}) %collective-permute-start.1) | collective-permute-done | bytes 245792 | tf_op jit(solution)/shard_map/ppermute | solution.py:641
  30.1 1.7 %collective-permute-start.6 = (bf16[4,48,640]{2,1,0:T(8,128)(2,1)}, bf16[4,48,640]{2,1,0:T(8,128)(2,1)S(1)}, u32[]{:S(2)}, u32[]{:S(2)}) collective-permute-start(bf16[4,48,640]{2,1,0:T(8,128)(2,1)} %get-tuple-element.46), channel_id=1, source_target_pairs={{0,19},{1,18},{2,17},{3,16},{16,3},{17,2},{18,1},{19,0},{4,23},{5,... | collective-permute-start | bytes 737288 | tf_op jit(solution)/shard_map/ppermute | solution.py:641
  31.9 3.1 %collective-permute-done.2.refs_3_ = bf16[4,48,640]{2,1,0:T(8,128)(2,1)S(1)} collective-permute-done((bf16[4,48,640]{2,1,0:T(8,128)(2,1)}, bf16[4,48,640]{2,1,0:T(8,128)(2,1)S(1)}, u32[]{:S(2)}, u32[]{:S(2)}) %collective-permute-start.2) | collective-permute-done | bytes 245792 | tf_op jit(solution)/shard_map/ppermute | solution.py:641
  35.0 11.8 %collective-permute-done.4.refs_5_ = bf16[4,48,640]{2,1,0:T(8,128)(2,1)S(1)} collective-permute-done((bf16[4,48,640]{2,1,0:T(8,128)(2,1)}, bf16[4,48,640]{2,1,0:T(8,128)(2,1)S(1)}, u32[]{:S(2)}, u32[]{:S(2)}) %collective-permute-start.4) | collective-permute-done | bytes 245792 | tf_op jit(solution)/shard_map/ppermute | solution.py:641
  46.8 0.9 copy-done.4
  47.7 0.6 merge.1
  48.4 2.0 %collective-permute-start.7 = (bf16[136,640]{1,0:T(8,128)(2,1)S(1)}, bf16[136,640]{1,0:T(8,128)(2,1)S(1)}, u32[]{:S(2)}, u32[]{:S(2)}) collective-permute-start(bf16[136,640]{1,0:T(8,128)(2,1)S(1)} %get-tuple-element.48), channel_id=1, source_target_pairs={{0,4},{4,0},{8,12},{12,8},{1,5},{5,1},{9,13},{13,9},{2,6},{6,2},{1... | collective-permute-start | bytes 522248 | tf_op jit(solution)/shard_map/ppermute | solution.py:641
  50.3 2.6 %collective-permute-start.8 = (bf16[136,640]{1,0:T(8,128)(2,1)S(1)}, bf16[136,640]{1,0:T(8,128)(2,1)S(1)}, u32[]{:S(2)}, u32[]{:S(2)}) collective-permute-start(bf16[136,640]{1,0:T(8,128)(2,1)S(1)} %get-tuple-element.49), channel_id=1, source_target_pairs={{0,8},{4,12},{8,0},{12,4},{1,9},{5,13},{9,1},{13,5},{2,10},{6,14},... | collective-permute-start | bytes 522248 | tf_op jit(solution)/shard_map/ppermute | solution.py:641
  52.9 5.1 %edge_columns.1 = (f32[128,128]{1,0:T(8,128)S(1)}, f32[128,128]{1,0:T(8,128)S(1)}) custom-call(f32[2,16,128,128]{3,2,1,0:T(8,128)S(1)} %copy-done.2, f32[2,16,128,128]{3,2,1,0:T(8,128)S(1)} %copy-done.1, s32[128,128]{1,0:T(8,128)S(1)} %copy-done.3), custom_call_target="tpu_custom_call" | custom-call | flops 4194304 | bytes 4194304 | tf_op jit(solution)/shard_map/edge_columns/pallas_call | solution.py:670
  58.0 1.8 %collective-permute-start.10 = (f32[128,128]{1,0:T(8,128)S(1)}, f32[128,128]{1,0:T(8,128)S(1)}, u32[]{:S(2)}, u32[]{:S(2)}) collective-permute-start(f32[128,128]{1,0:T(8,128)S(1)} %get-tuple-element.51.refs_9_), channel_id=1, source_target_pairs={{0,1},{1,2},{2,3},{4,5},{5,6},{6,7},{8,9},{9,10},{10,11},{12,13},{... | collective-permute-start | bytes 196616 | tf_op jit(solution)/shard_map/ppermute | solution.py:674
  59.8 1.3 %collective-permute-start.11 = (f32[128,128]{1,0:T(8,128)S(1)}, f32[128,128]{1,0:T(8,128)S(1)}, u32[]{:S(2)}, u32[]{:S(2)}) collective-permute-start(f32[128,128]{1,0:T(8,128)S(1)} %get-tuple-element.52.refs_10_), channel_id=1, source_target_pairs={{1,0},{2,1},{3,2},{5,4},{6,5},{7,6},{9,8},{10,9},{11,10},{13,12},{... | collective-permute-start | bytes 196616 | tf_op jit(solution)/shard_map/ppermute | solution.py:673
  61.1 3.3 %collective-permute-done.11.from_east.refs_13_ = f32[128,128]{1,0:T(8,128)S(1)} collective-permute-done((f32[128,128]{1,0:T(8,128)S(1)}, f32[128,128]{1,0:T(8,128)S(1)}, u32[]{:S(2)}, u32[]{:S(2)}) %collective-permute-start.11) | collective-permute-done | bytes 65568 | tf_op jit(solution)/shard_map/ppermute | solution.py:673
  64.5 1.3 %collective-permute-start.12 = (f32[192,128]{1,0:T(8,128)S(1)}, f32[192,128]{1,0:T(8,128)S(1)}, u32[]{:S(2)}, u32[]{:S(2)}) collective-permute-start(f32[192,128]{1,0:T(8,128)S(1)} %get-tuple-element.54.refs_8_), channel_id=1, source_target_pairs={{4,0},{8,4},{12,8},{16,12},{20,16},{24,20},{28,24},{5,1},{9,5},{13... | collective-permute-start | bytes 294920 | tf_op jit(solution)/shard_map/ppermute | solution.py:678
  65.8 4.6 %collective-permute-start.13 = (f32[192,128]{1,0:T(8,128)S(1)}, f32[192,128]{1,0:T(8,128)S(1)}, u32[]{:S(2)}, u32[]{:S(2)}) collective-permute-start(f32[192,128]{1,0:T(8,128)S(1)} %get-tuple-element.53.refs_7_), channel_id=1, source_target_pairs={{0,4},{4,8},{8,12},{12,16},{16,20},{20,24},{24,28},{1,5},{5,9},{9,... | collective-permute-start | bytes 294920 | tf_op jit(solution)/shard_map/ppermute | solution.py:679
  71.0 1.5 %collective-permute-done.13.refs_12_ = f32[192,128]{1,0:T(8,128)S(1)} collective-permute-done((f32[192,128]{1,0:T(8,128)S(1)}, f32[192,128]{1,0:T(8,128)S(1)}, u32[]{:S(2)}, u32[]{:S(2)}) %collective-permute-start.13) | collective-permute-done | bytes 98336 | tf_op jit(solution)/shard_map/ppermute | solution.py:679
  72.6 0.9 surface.1
  73.5 2.5 %collective-permute-start.14 = (bf16[128,128]{1,0:T(8,128)(2,1)S(1)}, bf16[128,128]{1,0:T(8,128)(2,1)S(1)}, u32[]{:S(2)}, u32[]{:S(2)}) collective-permute-start(bf16[128,128]{1,0:T(8,128)(2,1)S(1)} %get-tuple-element.67.refs_1_), channel_id=1, source_target_pairs={{0,4},{4,0},{8,12},{12,8},{1,5},{5,1},{9,13},{13,9},{2,6},{6,2},{1... | collective-permute-start | bytes 98312 | tf_op jit(solution)/shard_map/ppermute | solution.py:641
  75.9 4.5 %collective-permute-start.15 = (bf16[128,128]{1,0:T(8,128)(2,1)S(1)}, bf16[128,128]{1,0:T(8,128)(2,1)S(1)}, u32[]{:S(2)}, u32[]{:S(2)}) collective-permute-start(bf16[128,128]{1,0:T(8,128)(2,1)S(1)} %get-tuple-element.67.refs_1_), channel_id=1, source_target_pairs={{0,8},{4,12},{8,0},{12,4},{1,9},{5,13},{9,1},{13,5},{2,10},{6,14},... | collective-permute-start | bytes 98312 | tf_op jit(solution)/shard_map/ppermute | solution.py:641
  80.4 2.0 %collective-permute-done.15.refs_3_ = bf16[128,128]{1,0:T(8,128)(2,1)S(1)} collective-permute-done((bf16[128,128]{1,0:T(8,128)(2,1)S(1)}, bf16[128,128]{1,0:T(8,128)(2,1)S(1)}, u32[]{:S(2)}, u32[]{:S(2)}) %collective-permute-start.15) | collective-permute-done | bytes 32800 | tf_op jit(solution)/shard_map/ppermute | solution.py:641
  82.4 3.8 %collective-permute-done.16.refs_4_ = bf16[128,128]{1,0:T(8,128)(2,1)S(1)} collective-permute-done((bf16[128,128]{1,0:T(8,128)(2,1)S(1)}, bf16[128,128]{1,0:T(8,128)(2,1)S(1)}, u32[]{:S(2)}, u32[]{:S(2)}) %collective-permute-start.16) | collective-permute-done | bytes 32800 | tf_op jit(solution)/shard_map/ppermute | solution.py:641
  86.7 2.7 %collective-permute-start.18 = (bf16[4,40,128]{2,1,0:T(8,128)(2,1)S(1)}, bf16[4,40,128]{2,1,0:T(8,128)(2,1)S(1)}, u32[]{:S(2)}, u32[]{:S(2)}) collective-permute-start(bf16[4,40,128]{2,1,0:T(8,128)(2,1)S(1)} %get-tuple-element.70), channel_id=1, source_target_pairs={{0,2},{1,3},{2,0},{3,1},{16,18},{17,19},{18,16},{19,17},{4,6},{5,7... | collective-permute-start | bytes 122888 | tf_op jit(solution)/shard_map/ppermute | solution.py:641
  89.5 2.2 %collective-permute-start.20 = (bf16[4,40,128]{2,1,0:T(8,128)(2,1)S(1)}, bf16[4,40,128]{2,1,0:T(8,128)(2,1)S(1)}, u32[]{:S(2)}, u32[]{:S(2)}) collective-permute-start(bf16[4,40,128]{2,1,0:T(8,128)(2,1)S(1)} %get-tuple-element.72), channel_id=1, source_target_pairs={{0,16},{1,17},{2,18},{3,19},{16,0},{17,1},{18,2},{19,3},{4,20},{5,... | collective-permute-start | bytes 122888 | tf_op jit(solution)/shard_map/ppermute | solution.py:641
  91.7 2.9 %collective-permute-start.22 = (bf16[4,40,128]{2,1,0:T(8,128)(2,1)S(1)}, bf16[4,40,128]{2,1,0:T(8,128)(2,1)S(1)}, u32[]{:S(2)}, u32[]{:S(2)}) collective-permute-start(bf16[4,40,128]{2,1,0:T(8,128)(2,1)S(1)} %get-tuple-element.74), channel_id=1, source_target_pairs={{0,18},{1,19},{2,16},{3,17},{16,2},{17,3},{18,0},{19,1},{4,22},{5,... | collective-permute-start | bytes 122888 | tf_op jit(solution)/shard_map/ppermute | solution.py:641
  94.7 10.2 %substeps.1 = f32[2,16,128,128]{3,2,1,0:T(8,128)} custom-call(f32[2,16,128,128]{3,2,1,0:T(8,128)S(1)} %copy-done.2, f32[2,16,128,128]{3,2,1,0:T(8,128)S(1)} %copy-done.1, s32[128,128]{1,0:T(8,128)S(1)} %copy-done.3, f32[5,128,128]{2,1,0:T(8,128)S(1)} %get-tuple-element.55.flux, f32[8,640]{1,0:T(8,128)S(1)} %get-tuple-element.56.rim, ...), custom_call_target="tpu_custom_call" | custom-call | flops 16777216 | bytes 16777216 | tf_op jit(solution)/shard_map/substeps/pallas_call | solution.py:695
  105.0 7.0 %copy-done = bf16[640,128,128]{2,1,0:T(8,128)(2,1)S(1)} copy-done((bf16[640,128,128]{2,1,0:T(8,128)(2,1)S(1)}, bf16[640,128,128]{2,1,0:T(8,128)(2,1)}, u32[]{:S(2)}) %copy-start) | copy-done | bytes 20971544
  111.9 6.1 %backward_remap.1 = f32[160,128]{1,0:T(8,128)} custom-call(s32[640]{0:T(1024)S(1)} %copy-done.5, s32[1,640]{1,0:T(1,128)S(1)} %reshape.15.src, bf16[4,40,128]{2,1,0:T(8,128)(2,1)S(1)} %get-tuple-element.68.refs_0_, bf16[4,40,128]{2,1,0:T(8,128)(2,1)S(1)} %collective-permute-done.17.refs_1_, bf16[4,40,128]{2,1,0:T(8,128)(2,1)S(1)} %collective-permute-done.18.refs_2_, ...), custom_call_target="tpu_custom_call" | custom-call | flops 167772160 | bytes 20971520 | tf_op jit(solution)/shard_map/backward_remap/pallas_call | solution.py:599
  (43 shorter events, 2.1 us)
Async XLA Ops:
  2.0 51.0 %copy-start.1 = (f32[2,16,128,128]{3,2,1,0:T(8,128)S(1)}, f32[2,16,128,128]{3,2,1,0:T(8,128)}, u32[]{:S(2)}) copy-start(f32[2,16,128,128]{3,2,1,0:T(8,128)} %currents.3) | copy-start | bytes 6291460
  2.0 51.0 %copy-start.2 = (f32[2,16,128,128]{3,2,1,0:T(8,128)S(1)}, f32[2,16,128,128]{3,2,1,0:T(8,128)}, u32[]{:S(2)}) copy-start(f32[2,16,128,128]{3,2,1,0:T(8,128)} %tracers.3) | copy-start | bytes 6291460
  2.0 51.0 %copy-start.3 = (s32[128,128]{1,0:T(8,128)S(1)}, s32[128,128]{1,0:T(8,128)}, u32[]{:S(2)}) copy-start(s32[128,128]{1,0:T(8,128)} %land.5) | copy-start | bytes 196612
  20.0 4.9 %collective-permute-start = (bf16[4,48,640]{2,1,0:T(8,128)(2,1)}, bf16[4,48,640]{2,1,0:T(8,128)(2,1)S(1)}, u32[]{:S(2)}, u32[]{:S(2)}) collective-permute-start(bf16[4,48,640]{2,1,0:T(8,128)(2,1)} %get-tuple-element.40), channel_id=1, source_target_pairs={{0,1},{1,0},{2,3},{3,2},{16,17},{17,16},{18,19},{19,18},{4,5},{5,4... | collective-permute-start | bytes 737288 | tf_op jit(solution)/shard_map/ppermute | solution.py:641
  20.6 9.6 %collective-permute-start.1 = (bf16[4,48,640]{2,1,0:T(8,128)(2,1)}, bf16[4,48,640]{2,1,0:T(8,128)(2,1)S(1)}, u32[]{:S(2)}, u32[]{:S(2)}) collective-permute-start(bf16[4,48,640]{2,1,0:T(8,128)(2,1)} %get-tuple-element.41), channel_id=1, source_target_pairs={{0,2},{1,3},{2,0},{3,1},{16,18},{17,19},{18,16},{19,17},{4,6},{5,7... | collective-permute-start | bytes 737288 | tf_op jit(solution)/shard_map/ppermute | solution.py:641
  23.1 11.9 %collective-permute-start.2 = (bf16[4,48,640]{2,1,0:T(8,128)(2,1)}, bf16[4,48,640]{2,1,0:T(8,128)(2,1)S(1)}, u32[]{:S(2)}, u32[]{:S(2)}) collective-permute-start(bf16[4,48,640]{2,1,0:T(8,128)(2,1)} %get-tuple-element.42), channel_id=1, source_target_pairs={{0,3},{1,2},{2,1},{3,0},{16,19},{17,18},{18,17},{19,16},{4,7},{5,6... | collective-permute-start | bytes 737288 | tf_op jit(solution)/shard_map/ppermute | solution.py:641
  23.2 11.8 %collective-permute-start.3 = (bf16[4,48,640]{2,1,0:T(8,128)(2,1)}, bf16[4,48,640]{2,1,0:T(8,128)(2,1)S(1)}, u32[]{:S(2)}, u32[]{:S(2)}) collective-permute-start(bf16[4,48,640]{2,1,0:T(8,128)(2,1)} %get-tuple-element.43), channel_id=1, source_target_pairs={{0,16},{1,17},{2,18},{3,19},{16,0},{17,1},{18,2},{19,3},{4,20},{5,... | collective-permute-start | bytes 737288 | tf_op jit(solution)/shard_map/ppermute | solution.py:641
  25.0 21.8 %collective-permute-start.4 = (bf16[4,48,640]{2,1,0:T(8,128)(2,1)}, bf16[4,48,640]{2,1,0:T(8,128)(2,1)S(1)}, u32[]{:S(2)}, u32[]{:S(2)}) collective-permute-start(bf16[4,48,640]{2,1,0:T(8,128)(2,1)} %get-tuple-element.44), channel_id=1, source_target_pairs={{0,17},{1,16},{2,19},{3,18},{16,1},{17,0},{18,3},{19,2},{4,21},{5,... | collective-permute-start | bytes 737288 | tf_op jit(solution)/shard_map/ppermute | solution.py:641
  25.0 21.8 %collective-permute-start.5 = (bf16[4,48,640]{2,1,0:T(8,128)(2,1)}, bf16[4,48,640]{2,1,0:T(8,128)(2,1)S(1)}, u32[]{:S(2)}, u32[]{:S(2)}) collective-permute-start(bf16[4,48,640]{2,1,0:T(8,128)(2,1)} %get-tuple-element.45), channel_id=1, source_target_pairs={{0,18},{1,19},{2,16},{3,17},{16,2},{17,3},{18,0},{19,1},{4,22},{5,... | collective-permute-start | bytes 737288 | tf_op jit(solution)/shard_map/ppermute | solution.py:641
  30.1 16.7 %collective-permute-start.6 = (bf16[4,48,640]{2,1,0:T(8,128)(2,1)}, bf16[4,48,640]{2,1,0:T(8,128)(2,1)S(1)}, u32[]{:S(2)}, u32[]{:S(2)}) collective-permute-start(bf16[4,48,640]{2,1,0:T(8,128)(2,1)} %get-tuple-element.46), channel_id=1, source_target_pairs={{0,19},{1,18},{2,17},{3,16},{16,3},{17,2},{18,1},{19,0},{4,23},{5,... | collective-permute-start | bytes 737288 | tf_op jit(solution)/shard_map/ppermute | solution.py:641
  46.8 0.9 copy-start.4
  48.4 24.2 %collective-permute-start.7 = (bf16[136,640]{1,0:T(8,128)(2,1)S(1)}, bf16[136,640]{1,0:T(8,128)(2,1)S(1)}, u32[]{:S(2)}, u32[]{:S(2)}) collective-permute-start(bf16[136,640]{1,0:T(8,128)(2,1)S(1)} %get-tuple-element.48), channel_id=1, source_target_pairs={{0,4},{4,0},{8,12},{12,8},{1,5},{5,1},{9,13},{13,9},{2,6},{6,2},{1... | collective-permute-start | bytes 522248 | tf_op jit(solution)/shard_map/ppermute | solution.py:641
  50.3 22.2 %collective-permute-start.8 = (bf16[136,640]{1,0:T(8,128)(2,1)S(1)}, bf16[136,640]{1,0:T(8,128)(2,1)S(1)}, u32[]{:S(2)}, u32[]{:S(2)}) collective-permute-start(bf16[136,640]{1,0:T(8,128)(2,1)S(1)} %get-tuple-element.49), channel_id=1, source_target_pairs={{0,8},{4,12},{8,0},{12,4},{1,9},{5,13},{9,1},{13,5},{2,10},{6,14},... | collective-permute-start | bytes 522248 | tf_op jit(solution)/shard_map/ppermute | solution.py:641
  52.9 19.7 %collective-permute-start.9 = (bf16[136,640]{1,0:T(8,128)(2,1)S(1)}, bf16[136,640]{1,0:T(8,128)(2,1)S(1)}, u32[]{:S(2)}, u32[]{:S(2)}) collective-permute-start(bf16[136,640]{1,0:T(8,128)(2,1)S(1)} %get-tuple-element.50), channel_id=1, source_target_pairs={{0,12},{4,8},{8,4},{12,0},{1,13},{5,9},{9,5},{13,1},{2,14},{6,10},... | collective-permute-start | bytes 522248 | tf_op jit(solution)/shard_map/ppermute | solution.py:641
  58.0 3.1 %collective-permute-start.10 = (f32[128,128]{1,0:T(8,128)S(1)}, f32[128,128]{1,0:T(8,128)S(1)}, u32[]{:S(2)}, u32[]{:S(2)}) collective-permute-start(f32[128,128]{1,0:T(8,128)S(1)} %get-tuple-element.51.refs_9_), channel_id=1, source_target_pairs={{0,1},{1,2},{2,3},{4,5},{5,6},{6,7},{8,9},{9,10},{10,11},{12,13},{... | collective-permute-start | bytes 196616 | tf_op jit(solution)/shard_map/ppermute | solution.py:674
  59.8 4.6 %collective-permute-start.11 = (f32[128,128]{1,0:T(8,128)S(1)}, f32[128,128]{1,0:T(8,128)S(1)}, u32[]{:S(2)}, u32[]{:S(2)}) collective-permute-start(f32[128,128]{1,0:T(8,128)S(1)} %get-tuple-element.52.refs_10_), channel_id=1, source_target_pairs={{1,0},{2,1},{3,2},{5,4},{6,5},{7,6},{9,8},{10,9},{11,10},{13,12},{... | collective-permute-start | bytes 196616 | tf_op jit(solution)/shard_map/ppermute | solution.py:673
  64.5 30.1 %copy-start.6 = (s32[640]{0:T(1024)S(1)}, s32[640]{0:T(1024)}, u32[]{:S(2)}) copy-start(s32[640]{0:T(1024)} %src.1) | copy-start | bytes 7684
  64.5 6.5 %collective-permute-start.12 = (f32[192,128]{1,0:T(8,128)S(1)}, f32[192,128]{1,0:T(8,128)S(1)}, u32[]{:S(2)}, u32[]{:S(2)}) collective-permute-start(f32[192,128]{1,0:T(8,128)S(1)} %get-tuple-element.54.refs_8_), channel_id=1, source_target_pairs={{4,0},{8,4},{12,8},{16,12},{20,16},{24,20},{28,24},{5,1},{9,5},{13... | collective-permute-start | bytes 294920 | tf_op jit(solution)/shard_map/ppermute | solution.py:678
  65.8 6.8 %collective-permute-start.13 = (f32[192,128]{1,0:T(8,128)S(1)}, f32[192,128]{1,0:T(8,128)S(1)}, u32[]{:S(2)}, u32[]{:S(2)}) collective-permute-start(f32[192,128]{1,0:T(8,128)S(1)} %get-tuple-element.53.refs_7_), channel_id=1, source_target_pairs={{0,4},{4,8},{8,12},{12,16},{16,20},{20,24},{24,28},{1,5},{5,9},{9,... | collective-permute-start | bytes 294920 | tf_op jit(solution)/shard_map/ppermute | solution.py:679
  73.5 6.9 %collective-permute-start.14 = (bf16[128,128]{1,0:T(8,128)(2,1)S(1)}, bf16[128,128]{1,0:T(8,128)(2,1)S(1)}, u32[]{:S(2)}, u32[]{:S(2)}) collective-permute-start(bf16[128,128]{1,0:T(8,128)(2,1)S(1)} %get-tuple-element.67.refs_1_), channel_id=1, source_target_pairs={{0,4},{4,0},{8,12},{12,8},{1,5},{5,1},{9,13},{13,9},{2,6},{6,2},{1... | collective-permute-start | bytes 98312 | tf_op jit(solution)/shard_map/ppermute | solution.py:641
  75.9 6.5 %collective-permute-start.15 = (bf16[128,128]{1,0:T(8,128)(2,1)S(1)}, bf16[128,128]{1,0:T(8,128)(2,1)S(1)}, u32[]{:S(2)}, u32[]{:S(2)}) collective-permute-start(bf16[128,128]{1,0:T(8,128)(2,1)S(1)} %get-tuple-element.67.refs_1_), channel_id=1, source_target_pairs={{0,8},{4,12},{8,0},{12,4},{1,9},{5,13},{9,1},{13,5},{2,10},{6,14},... | collective-permute-start | bytes 98312 | tf_op jit(solution)/shard_map/ppermute | solution.py:641
  80.4 5.8 %collective-permute-start.16 = (bf16[128,128]{1,0:T(8,128)(2,1)S(1)}, bf16[128,128]{1,0:T(8,128)(2,1)S(1)}, u32[]{:S(2)}, u32[]{:S(2)}) collective-permute-start(bf16[128,128]{1,0:T(8,128)(2,1)S(1)} %get-tuple-element.67.refs_1_), channel_id=1, source_target_pairs={{0,12},{4,8},{8,4},{12,0},{1,13},{5,9},{9,5},{13,1},{2,14},{6,10},... | collective-permute-start | bytes 98312 | tf_op jit(solution)/shard_map/ppermute | solution.py:641
  86.5 5.1 %collective-permute-start.17 = (bf16[4,40,128]{2,1,0:T(8,128)(2,1)S(1)}, bf16[4,40,128]{2,1,0:T(8,128)(2,1)S(1)}, u32[]{:S(2)}, u32[]{:S(2)}) collective-permute-start(bf16[4,40,128]{2,1,0:T(8,128)(2,1)S(1)} %get-tuple-element.69), channel_id=1, source_target_pairs={{0,1},{1,0},{2,3},{3,2},{16,17},{17,16},{18,19},{19,18},{4,5},{5,4... | collective-permute-start | bytes 122888 | tf_op jit(solution)/shard_map/ppermute | solution.py:641
  86.7 7.8 %collective-permute-start.18 = (bf16[4,40,128]{2,1,0:T(8,128)(2,1)S(1)}, bf16[4,40,128]{2,1,0:T(8,128)(2,1)S(1)}, u32[]{:S(2)}, u32[]{:S(2)}) collective-permute-start(bf16[4,40,128]{2,1,0:T(8,128)(2,1)S(1)} %get-tuple-element.70), channel_id=1, source_target_pairs={{0,2},{1,3},{2,0},{3,1},{16,18},{17,19},{18,16},{19,17},{4,6},{5,7... | collective-permute-start | bytes 122888 | tf_op jit(solution)/shard_map/ppermute | solution.py:641
  89.4 15.5 %collective-permute-start.19 = (bf16[4,40,128]{2,1,0:T(8,128)(2,1)S(1)}, bf16[4,40,128]{2,1,0:T(8,128)(2,1)S(1)}, u32[]{:S(2)}, u32[]{:S(2)}) collective-permute-start(bf16[4,40,128]{2,1,0:T(8,128)(2,1)S(1)} %get-tuple-element.71), channel_id=1, source_target_pairs={{0,3},{1,2},{2,1},{3,0},{16,19},{17,18},{18,17},{19,16},{4,7},{5,6... | collective-permute-start | bytes 122888 | tf_op jit(solution)/shard_map/ppermute | solution.py:641
  89.5 15.4 %collective-permute-start.20 = (bf16[4,40,128]{2,1,0:T(8,128)(2,1)S(1)}, bf16[4,40,128]{2,1,0:T(8,128)(2,1)S(1)}, u32[]{:S(2)}, u32[]{:S(2)}) collective-permute-start(bf16[4,40,128]{2,1,0:T(8,128)(2,1)S(1)} %get-tuple-element.72), channel_id=1, source_target_pairs={{0,16},{1,17},{2,18},{3,19},{16,0},{17,1},{18,2},{19,3},{4,20},{5,... | collective-permute-start | bytes 122888 | tf_op jit(solution)/shard_map/ppermute | solution.py:641
  91.7 13.3 %collective-permute-start.21 = (bf16[4,40,128]{2,1,0:T(8,128)(2,1)S(1)}, bf16[4,40,128]{2,1,0:T(8,128)(2,1)S(1)}, u32[]{:S(2)}, u32[]{:S(2)}) collective-permute-start(bf16[4,40,128]{2,1,0:T(8,128)(2,1)S(1)} %get-tuple-element.73), channel_id=1, source_target_pairs={{0,17},{1,16},{2,19},{3,18},{16,1},{17,0},{18,3},{19,2},{4,21},{5,... | collective-permute-start | bytes 122888 | tf_op jit(solution)/shard_map/ppermute | solution.py:641
  91.7 13.3 %collective-permute-start.22 = (bf16[4,40,128]{2,1,0:T(8,128)(2,1)S(1)}, bf16[4,40,128]{2,1,0:T(8,128)(2,1)S(1)}, u32[]{:S(2)}, u32[]{:S(2)}) collective-permute-start(bf16[4,40,128]{2,1,0:T(8,128)(2,1)S(1)} %get-tuple-element.74), channel_id=1, source_target_pairs={{0,18},{1,19},{2,16},{3,17},{16,2},{17,3},{18,0},{19,1},{4,22},{5,... | collective-permute-start | bytes 122888 | tf_op jit(solution)/shard_map/ppermute | solution.py:641
  94.5 10.4 %collective-permute-start.23 = (bf16[4,40,128]{2,1,0:T(8,128)(2,1)S(1)}, bf16[4,40,128]{2,1,0:T(8,128)(2,1)S(1)}, u32[]{:S(2)}, u32[]{:S(2)}) collective-permute-start(bf16[4,40,128]{2,1,0:T(8,128)(2,1)S(1)} %get-tuple-element.75), channel_id=1, source_target_pairs={{0,19},{1,18},{2,17},{3,16},{16,3},{17,2},{18,1},{19,0},{4,23},{5,... | collective-permute-start | bytes 122888 | tf_op jit(solution)/shard_map/ppermute | solution.py:641
  94.7 10.3 %copy-start.5 = (s32[640]{0:T(1024)S(1)}, s32[640]{0:T(1024)}, u32[]{:S(2)}) copy-start(s32[640]{0:T(1024)} %get-tuple-element.65.slots) | copy-start | bytes 7684
  104.9 7.0 %copy-start = (bf16[640,128,128]{2,1,0:T(8,128)(2,1)S(1)}, bf16[640,128,128]{2,1,0:T(8,128)(2,1)}, u32[]{:S(2)}) copy-start(bf16[640,128,128]{2,1,0:T(8,128)(2,1)} %refs_8_.1) | copy-start | bytes 62914564

commit v3 on v2

--- a/solution.py
+++ b/solution.py
@@ -41,7 +41,7 @@
 
 
 def forward_kernel(parts, cap, grid, src, own, dst, flux, w, *refs):
-    sends, (slots, held, mixed, acc, rows, xs, counts, sems) = refs[:-8], refs[-8:]
+    sends, (slots, held, mixed, acc, rows, xs, counts, renumbered, sems) = refs[:-9], refs[-9:]
     n_sec, n_gx, n_gy = grid
     devices, chunk, wide = xs.shape
     total, width, _ = held.shape
@@ -56,8 +56,17 @@
     for c in range(parts):
         copy(c).start()
 
+    plane = lax.axis_index("sec") * n_gy + lax.axis_index("gy")
+    line = lax.axis_index("gx")
+
+    def renumber(owner):
+        x = lax.div(owner, n_gy)
+        there = lax.div(x, n_gx) * n_gy + lax.rem(owner, n_gy)
+        return (there ^ plane) * n_gx + (lax.rem(x, n_gx) ^ line)
+
     def clear(o, _):
         counts[o] = 0
+        renumbered[o] = renumber(o)
         return 0
 
     lax.fori_loop(0, devices, clear, 0)
@@ -74,16 +83,6 @@
         [one[0], heat_high, salt_high, one[6], one[7], heat - heat_high, salt - salt_high, jnp.zeros_like(heat)], axis=1
     ).astype(BF16)
 
-    def place(k, _):
-        owner = own[k]
-        at = counts[owner]
-        counts[owner] = at + 1
-        slot = owner * cap + jnp.minimum(at, cap - 1)
-        slots[k] = slot
-        rows[pl.ds(slot, 1), :] = jnp.full((1, width), dst[k].astype(F32), F32)
-        return 0
-
-    lax.fori_loop(0, total, place, 0, unroll=8)
     low_rows = iota((fields, width), 0)
     low_rows = (low_rows == 1) | (low_rows == 2)
 
@@ -95,7 +94,14 @@
             both = dot(left, held[pl.ds(k, 2)].reshape(2 * width, width), NT)
             for z, part in enumerate((both[:fields, :width], both[fields:, width:])):
                 part = part + jnp.where(low_rows, pltpu.roll(part, fields - 4, 0), 0.0)
-                acc[pl.ds(pl.multiple_of(slots[k + z] * fields, fields), fields), :] = part
+                owner = own[k + z]
+                at = counts[owner]
+                counts[owner] = at + 1
+                at = jnp.minimum(at, cap - 1)
+                slots[k + z] = owner * cap + at
+                slot = renumbered[owner] * cap + at
+                acc[pl.ds(pl.multiple_of(slot * fields, fields), fields), :] = part
+                rows[pl.ds(slot, 1), :] = jnp.full((1, width), dst[k + z].astype(F32), F32)
         return 0
 
     lax.fori_loop(0, parts, work, 0)
@@ -116,8 +122,6 @@
     for at, x in enumerate((0, 1, last, last - 1, 0, 0, last, last)):
         wanted = jnp.where(row == at, float(x), wanted)
     group = 8
-    plane = lax.axis_index("sec") * n_gy + lax.axis_index("gy")
-    line = lax.axis_index("gx")
 
     def owners(g, _):
         ds = [g * group + j for j in range(group)]
@@ -139,10 +143,7 @@
             here = (lax.div(here, n_gy) * n_gx + (lax.rem(d, n_gx) ^ line)) * n_gy + lax.rem(here, n_gy)
 
             def at(offset):
-                there = lax.rem(here + offset + 2 * devices, devices)
-                x = lax.div(there, n_gy)
-                there = lax.div(x, n_gx) * n_gy + lax.rem(there, n_gy)
-                return (there ^ plane) * n_gx + (lax.rem(x, n_gx) ^ line)
+                return renumbered[lax.rem(here + offset + 2 * devices, devices)]
 
             south_of, north_of, west_of, east_of = at(-n_gy), at(n_gy), at(-1), at(1)
 
@@ -163,8 +164,11 @@
 
     lax.fori_loop(0, devices // group, owners, 0)
 
-    for m, send in enumerate(sends):
-        send[...] = xs[m * n_gx : (m + 1) * n_gx].astype(BF16)
+    half = n_gx // 2
+    planes = n_sec * n_gy
+    for m in range(planes):
+        sends[m][...] = xs[m * n_gx + half : (m + 1) * n_gx].astype(BF16)
+        sends[planes + m][...] = xs[m * n_gx : m * n_gx + half].astype(BF16)
 
 
 def forward(flux, w, src, own, dst, grid, cap, parts=20):
@@ -177,7 +181,7 @@
     return pl.pallas_call(
         functools.partial(forward_kernel, parts, cap, grid),
         in_specs=[SMEM, SMEM, SMEM, VMEM, ANY],
-        out_specs=[VMEM] * (n_sec * n_gy) + [SMEM],
+        out_specs=[VMEM] * (2 * n_sec * n_gy) + [SMEM],
         scratch_shapes=[
             pltpu.VMEM(w.shape, BF16),
             pltpu.VMEM(flux.shape, BF16),
@@ -185,22 +189,23 @@
             pltpu.VMEM((devices * cap, width), F32),
             pltpu.VMEM((devices, chunk, wide), F32),
             pltpu.SMEM((devices,), jnp.int32),
+            pltpu.SMEM((devices,), jnp.int32),
             pltpu.SemaphoreType.DMA((parts,)),
         ],
-        out_shape=[jax.ShapeDtypeStruct((n_gx, chunk, wide), BF16)] * (n_sec * n_gy) + [jax.ShapeDtypeStruct((total,), jnp.int32)],
-        compiler_params=kernel_params(58),
+        out_shape=[jax.ShapeDtypeStruct((n_gx // 2, chunk, wide), BF16)] * (2 * n_sec * n_gy) + [jax.ShapeDtypeStruct((total,), jnp.int32)],
+        compiler_params=kernel_params(42),
         cost_estimate=pl.CostEstimate(flops=2 * total * 8 * width * width, bytes_accessed=total * width * width * 2, transcendentals=0),
         name="forward_remap",
     )(src, own, dst, flux, w)
 
 
 def merge_kernel(n_sources, *refs):
-    sources, lines_out, outs = refs[:n_sources], refs[n_sources], refs[n_sources + 1 :]
-    n_gx, chunk, wide = sources[0].shape
+    sources, outs = refs[:n_sources], refs[n_sources:]
+    chunk = sources[0].shape[1]
     height = outs[0].shape[0] - 8
     first = chunk - 8
-    count = len(sources) * chunk
-    for z in range(n_gx):
+    count = n_sources * chunk
+    for z, out in enumerate(outs):
         ext = None
         where = []
         for source in sources:
@@ -208,52 +213,36 @@
             where.append(piece[1:2, :chunk])
             ext = piece if ext is None else ext + piece
         where = jnp.concatenate(where, axis=1)
-        lines_out[z] = where
         hot = (iota((height, count), 0).astype(F32) == where).astype(F32).astype(BF16)
         sums = dot(hot, jnp.concatenate([source[z] for source in sources], axis=0), NN)
-        outs[z][...] = jnp.concatenate([sums, ext], axis=0).astype(outs[z].dtype)
-
-
-def spread_kernel(cap, *refs):
-    n_gx, _, count = refs[0].shape
-    lines, tiles, backs = refs[0], refs[1 : 1 + n_gx], refs[1 + n_gx :]
-    chunk = count // len(backs)
-    height, width = tiles[0].shape
-    for z in range(n_gx):
-        hot = (iota((height, count), 0).astype(F32) == lines[z]).astype(F32)
-        picked = dot(hot.T.astype(BF16), tiles[z][...], NN).reshape(len(backs), chunk, width)
-        for m, back in enumerate(backs):
-            back[z] = picked[m, :cap].astype(BF16)
+        row3 = jnp.concatenate([where, ext[3:4, count:]], axis=1)
+        ext = jnp.where(iota((8, 1), 0) == 3, row3, ext)
+        out[...] = jnp.concatenate([sums, ext], axis=0).astype(out.dtype)
 
 
 def columns_kernel(tracers, currents, land, west, east):
     levels = tracers.shape[1]
     width = tracers.shape[3]
     last = width - 1
-    lane = iota((width, width), 1)
-
-    def put(held, plane, row, column):
-        return jnp.where(lane == row, pltpu.roll(plane, lax.rem(row - column + width, width), 1), held)
-
-    def level(l, held):
-        w, e = held
+    west[...] = jnp.zeros_like(west)
+    east[...] = jnp.zeros_like(east)
+
+    def put(plane, near, far):
+        turned = plane.T
+        for out, edge, second in ((west, 0, 1), (east, last, last - 1)):
+            out[pl.ds(near, 1), :] = turned[edge : edge + 1]
+            if far is not None:
+                out[pl.ds(far, 1), :] = turned[second : second + 1]
+
+    def level(l, _):
         for t in range(2):
-            q = tracers[t, l]
-            w = put(put(w, q, t * levels + l, 0), q, (2 + t) * levels + l, 1)
-            e = put(put(e, q, t * levels + l, last), q, (2 + t) * levels + l, last - 1)
-        u = currents[0, l]
-        w = put(put(w, u, 4 * levels + l, 0), u, 6 * levels + l, 1)
-        e = put(put(e, u, 4 * levels + l, last), u, 6 * levels + l, last - 1)
-        v = currents[1, l]
-        return put(w, v, 5 * levels + l, 0), put(e, v, 5 * levels + l, last)
-
-    zero = jnp.zeros((width, width), F32)
-    w, e = lax.fori_loop(0, levels, level, (zero, zero))
-    wet = land[...].astype(F32)
-    w = put(put(w, wet, 7 * levels, 0), wet, 7 * levels + 1, 1)
-    e = put(put(e, wet, 7 * levels, last), wet, 7 * levels + 1, last - 1)
-    west[...] = w.T
-    east[...] = e.T
+            put(tracers[t, l], t * levels + l, (2 + t) * levels + l)
+        put(currents[0, l], 4 * levels + l, 6 * levels + l)
+        put(currents[1, l], 5 * levels + l, None)
+        return 0
+
+    lax.fori_loop(0, levels, level, 0, unroll=2)
+    put(land[...].astype(F32), 7 * levels, 7 * levels + 1)
 
 
 def rows_kernel(tracers, currents, land, from_west, from_east, south, north):
@@ -391,17 +380,19 @@
     return edge
 
 
-def surface_kernel(n_gx, levels, *refs):
+def surface_kernel(grid, chunk, levels, *refs):
+    n_sec, n_gx, n_gy = grid
+    planes = n_sec * n_gy
     parts, refs = refs[:n_gx], refs[n_gx:]
     tracers, currents, land, own_n, own_s, own_e, own_w, from_n, from_s, from_e, from_w, *refs = refs
-    surface, flux, rim, in_n, in_s, in_e, in_w, out_n, out_s, out_e, out_w = refs
+    back, flux, rim, in_n, in_s, in_e, in_w, out_n, out_s, out_e, out_w = refs
     height, width = land.shape
     last = width - 1
     lane = iota((1, width), 1)
     sums = parts[0][...]
     for part in parts[1:]:
         sums = sums + part[...].astype(F32)
-    sums, ext = sums[:height], sums[height:]
+    sums, ext = sums[:height], sums[height : height + 8]
     shortwave, heat, salt, stress_u, stress_v = [sums[:, f * width : (f + 1) * width] for f in range(SENT)]
     wet = land[...].astype(F32)
     u0 = currents[0, 0] + 0.1 * stress_u
@@ -468,7 +459,17 @@
     sides = jnp.concatenate([lines[2][0:8], lines[3][0:8], jnp.zeros((width - 16, width), F32)], axis=0).T
     halo = lines[0][0:1], lines[1][0:1], column(sides, 0, last), column(sides, 8, 0)
     t0 = horizontal(c0, t0, halo) + mix * (t1 - t0) + warm * profile[0:1] + wet * heat
-    surface[...] = t0.astype(BF16)
+    sst = t0.astype(BF16)
+    plane = lax.axis_index("sec") * n_gy + lax.axis_index("gy")
+    line = lax.axis_index("gx")
+    for z, part in enumerate(parts):
+        where = part[height + 3 : height + 4, : planes * chunk].astype(F32)
+        hot = (iota((height, planes * chunk), 0).astype(F32) == where).astype(F32)
+        picked = dot(hot.T.astype(BF16), sst, NN).reshape(planes, chunk, width)
+        for m in range(planes):
+            there = plane ^ m
+            device = (lax.div(there, n_gy) * n_gx + (line ^ z)) * n_gy + lax.rem(there, n_gy)
+            back[device] = picked[m, : back.shape[1]].astype(BF16)
 
 
 def rim_flux(ext, width):
@@ -554,70 +555,66 @@
     lax.fori_loop(0, levels, second_step, 0)
 
 
-def backward_kernel(batch, n_backs, slots, src, *refs):
-    backs, (w, out, wide, picked, terms) = refs[:n_backs], refs[n_backs:]
-    step = pl.program_id(0)
+def backward_kernel(parts, slots, src, back, w, out, held, wide, picked, terms, sems):
     total, width = terms.shape
     blocks = out.shape[0]
-
-    @pl.when(step == 0)
-    def _():
-        rows = wide.shape[0] // n_backs
-        for m, back in enumerate(backs):
-            wide[m * rows : (m + 1) * rows] = back[...].astype(F32).reshape(rows, width)
-
-        def pick(i, _):
-            for j in range(8):
-                picked[pl.ds(i * 8 + j, 1), :] = wide[pl.ds(slots[i * 8 + j], 1), :]
-            return 0
-
-        lax.fori_loop(0, total // 8, pick, 0, unroll=2)
-
+    batch = total // parts
+
+    def copy(c):
+        return pltpu.make_async_copy(w.at[pl.ds(c * batch, batch)], held.at[pl.ds(c * batch, batch)], sems.at[c])
+
+    for c in range(parts):
+        copy(c).start()
+    wide[...] = back[...].astype(F32).reshape(wide.shape)
+
+    def pick(i, _):
+        for j in range(16):
+            picked[pl.ds(i * 16 + j, 1), :] = wide[pl.ds(slots[i * 16 + j], 1), :]
+        return 0
+
+    lax.fori_loop(0, total // 16, pick, 0, unroll=2)
     row = iota((16, width), 0)
-    for g in range(batch // 16):
-        at = pl.multiple_of(step * batch + g * 16, 16)
-        rows = picked[pl.ds(at, 16), :]
-        left = [jnp.where((row == r) | (row == 8 + r), rows, 0.0).astype(BF16) for r in range(8)]
-        block = w[g * 16 : (g + 1) * 16].reshape(2, 8 * width, width)
-        both = dot(jnp.concatenate(left, axis=1), jnp.concatenate([block[0], block[1]], axis=1), NN)
-        terms[pl.ds(at, 8), :] = both[:8, :width]
-        terms[pl.ds(at + 8, 8), :] = both[8:, width:]
-
-    @pl.when(step == pl.num_programs(0) - 1)
-    def _():
-        hot = (iota((blocks, total), 0) == src[...]).astype(F32).astype(BF16)
-        value = terms[...]
-        high = value.astype(BF16)
-        low = (value - high.astype(F32)).astype(BF16)
-        both = dot(hot, jnp.concatenate([high, low], axis=1), NN)
-        out[...] = both[:, :width] + both[:, width:]
-
-
-def backward(backs, w, src, slots, blocks, batch=64):
+
+    def work(c, _):
+        copy(c).wait()
+        for g in range(batch // 16):
+            at = pl.multiple_of(c * batch + g * 16, 16)
+            rows = picked[pl.ds(at, 16), :]
+            left = [jnp.where((row == r) | (row == 8 + r), rows, 0.0).astype(BF16) for r in range(8)]
+            block = held[pl.ds(at, 16)].reshape(2, 8 * width, width)
+            both = dot(jnp.concatenate(left, axis=1), jnp.concatenate([block[0], block[1]], axis=1), NN)
+            terms[pl.ds(at, 8), :] = both[:8, :width]
+            terms[pl.ds(at + 8, 8), :] = both[8:, width:]
+        return 0
+
+    lax.fori_loop(0, parts, work, 0)
+    hot = (iota((blocks, total), 0) == src[...]).astype(F32).astype(BF16)
+    value = terms[...]
+    high = value.astype(BF16)
+    low = (value - high.astype(F32)).astype(BF16)
+    both = dot(hot, jnp.concatenate([high, low], axis=1), NN)
+    out[...] = both[:, :width] + both[:, width:]
+
+
+def backward(back, w, src, slots, blocks, parts=20):
     total, width, _ = w.shape
-    n_gx, cap, _ = backs[0].shape
+    devices, cap, _ = back.shape
     return pl.pallas_call(
-        functools.partial(backward_kernel, batch, len(backs)),
-        grid_spec=pltpu.PrefetchScalarGridSpec(
-            num_scalar_prefetch=1,
-            grid=(total // batch,),
-            in_specs=[
-                pl.BlockSpec((1, total), lambda i, *_: (0, 0)),
-                *[pl.BlockSpec((n_gx, cap, width), lambda i, *_: (0, 0, 0))] * len(backs),
-                pl.BlockSpec((batch, width, width), lambda i, *_: (i, 0, 0)),
-            ],
-            out_specs=pl.BlockSpec((blocks, width), lambda i, *_: (0, 0)),
-            scratch_shapes=[
-                pltpu.VMEM((len(backs) * n_gx * cap, width), F32),
-                pltpu.VMEM((total, width), F32),
-                pltpu.VMEM((total, width), F32),
-            ],
-        ),
+        functools.partial(backward_kernel, parts),
+        in_specs=[SMEM, VMEM, VMEM, ANY],
+        out_specs=VMEM,
+        scratch_shapes=[
+            pltpu.VMEM(w.shape, BF16),
+            pltpu.VMEM((devices * cap, width), F32),
+            pltpu.VMEM((total, width), F32),
+            pltpu.VMEM((total, width), F32),
+            pltpu.SemaphoreType.DMA((parts,)),
+        ],
         out_shape=jax.ShapeDtypeStruct((blocks, width), F32),
-        compiler_params=kernel_params(24),
+        compiler_params=kernel_params(58),
         cost_estimate=pl.CostEstimate(flops=2 * total * 8 * width * width, bytes_accessed=total * width * width * 2, transcendentals=0),
         name="backward_remap",
-    )(slots, src.reshape(1, total), *backs, w)
+    )(slots, src.reshape(1, total), back, w)
 
 
 def kernel(body, outs, name, mebibytes, bytes_accessed, scratch=()):
@@ -649,21 +646,10 @@
     cap = up(2 * total // (planes * n_gx), 8)
     wide = SENT * width
 
-    plane = lax.axis_index("sec") * n_gy + lax.axis_index("gy")
-    owner = remap_owner[:, 0]
-    x, y = owner // n_gy, owner % n_gy
-    owner = (((x // n_gx) * n_gy + y) ^ plane) * n_gx + ((x % n_gx) ^ lax.axis_index("gx"))
-    *sends, slots = forward(atm_flux, remap_weights, remap_src, owner, remap_dst, grid, cap)
-    got = [sends[0]] + [swapped(sends[m], ("sec", "gy"), planes, m) for m in range(1, planes)]
+    *sends, slots = forward(atm_flux, remap_weights, remap_src, remap_owner.reshape(total), remap_dst, grid, cap)
     chunk = sends[0].shape[1]
-    lines, *merged = kernel(
-        functools.partial(merge_kernel, planes),
-        [((n_gx, 1, planes * chunk), F32), ((height + 8, wide), F32)] + [((height + 8, wide), BF16)] * (n_gx - 1),
-        "merge",
-        32,
-        1 << 22,
-    )(*got)
-    parts = [merged[0]] + [swapped(merged[m], "gx", n_gx, m) for m in range(1, n_gx)]
+    sends = sends[:planes], sends[planes:]
+    got = [[send[0]] + [swapped(send[m], ("sec", "gy"), planes, m) for m in range(1, planes)] for send in sends]
 
     side = (width, width)
     end = (7 * levels + 80, width)
@@ -678,18 +664,25 @@
     from_n = lax.ppermute(own_s, NORTH, to_south)
     from_s = lax.ppermute(own_n, NORTH, to_north)
 
-    surface, flux, rim, *edges = kernel(
-        functools.partial(surface_kernel, n_gx, levels),
-        [((height, width), BF16), ((5, height, width), F32), ((8, wide), F32)] + ([(end, F32)] * 2 + [(side, F32)] * 2) * 2,
+    merged = []
+    for far, chunks in zip((1, 0), got):
+        if far:
+            chunks, from_n, from_s = lax.optimization_barrier((chunks, from_n, from_s))
+        here = [((height + 8, wide), BF16)] * (n_gx // 2)
+        if not far:
+            here = [((height + 8, wide), F32)] + here[1:]
+        merged.append(kernel(functools.partial(merge_kernel, planes), here, "merge", 24, 1 << 22)(*chunks))
+    merged = list(merged[1]) + list(merged[0])
+    parts = [merged[0]] + [swapped(merged[m], "gx", n_gx, m) for m in range(1, n_gx)]
+
+    back, flux, rim, *edges = kernel(
+        functools.partial(surface_kernel, grid, chunk, levels),
+        [((planes * n_gx, cap, width), BF16), ((5, height, width), F32), ((8, wide), F32)] + ([(end, F32)] * 2 + [(side, F32)] * 2) * 2,
         "surface",
-        32,
+        58,
         1 << 22,
     )(*parts, tracers[0:1, 0:3], currents[:, 0:2], land_sea, own_n, own_s, own_e, own_w, from_n, from_s, from_e, from_w)
-    tiles = [surface] + [swapped(surface, "gx", n_gx, m) for m in range(1, n_gx)]
-    backs = kernel(
-        functools.partial(spread_kernel, cap), [((n_gx, cap, width), BF16)] * planes, "spread", 32, 1 << 22
-    )(lines, *tiles)
-    returned = [backs[0]] + [swapped(backs[m], ("sec", "gy"), planes, m) for m in range(1, planes)]
+    returned = lax.all_to_all(back, EVERY, split_axis=0, concat_axis=0, tiled=True)
 
     plane = (height, width)
     (tracers_out,) = kernel(

time: 119 us -> 123 us (1.034)
  local copies, waits for them, and re-layouts: 7.96 us -> 16.8 us
  waiting for transfers between devices: 28.7 us -> 24.5 us
  starting transfers between devices: 37.7 us -> 40.3 us
  Pallas kernels: 41.4 us -> 39.2 us
    unnamed x14 -> x66, local copies, waits for them, and re-layouts: 7.93 us -> 14.8 us
    all_to_all x0 -> x1, starting transfers between devices: none -> 6.33 us  [on_device(): lax.all_to_all(back, EVERY, split_axis=0, concat_axis=0, tiled=True)]
    pallas_call x4, Pallas kernels: 7.9 us -> 13.8 us  [the longest x1 9.27 us: backward(): pl.pallas_call(functools.partial(backward_kernel, parts), in_specs=[SMEM,...]
    ppermute x20 -> x17, starting transfers between devices: 28.8 us -> 24.2 us  [swapped(): return lax.ppermute(array, axes, [(i, i ^ step) for i in range(count)])]
    pallas_call x1, Pallas kernels: 18.1 us -> 13.5 us  [forward(): pl.pallas_call(functools.partial(forward_kernel, parts, cap, grid), in_sp...]
    pallas_call x1, Pallas kernels: 5.11 us -> 1.63 us  [on_device(): kernel(columns_kernel, [(side, F32)] * 2, 'edge_columns', 16, 1 << 22)]
    ppermute x1, waiting for transfers between devices: 3.29 us -> 0.01 us  [on_device(): from_e = lax.ppermute(own_w, 'gy', to_west)]
    ppermute x1, waiting for transfers between devices: 1.54 us -> 0.01 us  [on_device(): from_s = lax.ppermute(own_n, NORTH, to_north)]
  transfers between devices with their start and end apart: 24 -> 22, of which waited for: 8 -> 5; matrix products, arithmetic and copies ran while one was open for 0% -> 2% of each run, Pallas kernels for 13% -> 10%
where the time goes in v3:
time: 123 us; the launch traced here: 122 us
  starting transfers between devices  40.3 us (33%)
  Pallas kernels  39.2 us (32%)
  waiting for transfers between devices  24.5 us (20%)
  local copies, waits for them, and re-layouts  16.8 us (14%)
    ppermute x17, waiting for transfers between devices, swapped(): return lax.ppermute(array, axes, [(i, i ^ step) for i in range(count)])  24.5 us
    ppermute x17, starting transfers between devices, swapped(): return lax.ppermute(array, axes, [(i, i ^ step) for i in range(count)])  24.2 us
    unnamed x66, local copies, waits for them, and re-layouts  14.8 us
    pallas_call x1, Pallas kernels, forward(): pl.pallas_call(functools.partial(forward_kernel, parts, cap, grid), in_sp...  13.5 us
    pallas_call x1, Pallas kernels, on_device(): kernel(stencil_kernel, [(tracers.shape, F32)], 'substeps', 32, 1 << 24, [...  10.2 us
    pallas_call x1, Pallas kernels, backward(): pl.pallas_call(functools.partial(backward_kernel, parts), in_specs=[SMEM,...  9.27 us
    all_to_all x1, starting transfers between devices, on_device(): lax.all_to_all(back, EVERY, split_axis=0, concat_axis=0, tiled=True)  6.33 us
    ppermute x1, starting transfers between devices, on_device(): from_s = lax.ppermute(own_n, NORTH, to_north)  4.55 us
  transfers between devices with their start and end apart: 22, of which 5 were waited for; matrix products, arithmetic and copies ran while one was open for 2% of the time, Pallas kernels for 10%

profile of v3, /device:TPU:0, one launch (start us, length us, event | category | flops | bytes accessed | tf_op | source)
XLA Modules:
  0.0 122.4 jit_solution(13588915454904443933)
XLA Ops:
  1.3 1.0 copy-done.7
  3.7 13.5 %forward_remap.1 = (bf16[2,48,640]{2,1,0:T(8,128)(2,1)S(1)}, bf16[2,48,640]{2,1,0:T(8,128)(2,1)S(1)}, bf16[2,48,640]{2,1,0:T(8,128)(2,1)S(1)}, bf16[2,48,640]{2,...) custom-call(s32[640]{0:T(1024)S(1)} %copy-done.23, ...), custom_call_target="tpu_custom_call" | custom-call | flops 167772160 | bytes 20971520 | tf_op jit(solution)/shard_map/forward_remap/pallas_call | solution.py:181
  17.2 2.4 %collective-permute-start.10 = (bf16[2,48,640]{2,1,0:T(8,128)(2,1)S(1)}, bf16[2,48,640]{2,1,0:T(8,128)(2,1)S(1)}, u32[]{:S(2)}, u32[]{:S(2)}) collective-permute-start(bf16[2,48,640]{2,1,0:T(8,128)(2,1)S(1)} %get-tuple-element.61), channel_id=1, source_target_pairs={{0,3},{1,2},{2,1},{3,0},{16,19},{17,18},{18,17},{19,16},{4,7},{5,6... | collective-permute-start | bytes 368648 | tf_op jit(solution)/shard_map/ppermute | solution.py:638
  19.7 1.6 %edge_columns.1 = (f32[128,128]{1,0:T(8,128)S(1)}, f32[128,128]{1,0:T(8,128)S(1)}) custom-call(f32[2,16,128,128]{3,2,1,0:T(8,128)S(1)} %copy-done.1, f32[2,16,128,128]{3,2,1,0:T(8,128)S(1)} %copy-done, s32[128,128]{1,0:T(8,128)S(1)} %copy-done.3), custom_call_target="tpu_custom_call" | custom-call | flops 4194304 | bytes 4194304 | tf_op jit(solution)/shard_map/edge_columns/pallas_call | solution.py:656
  21.3 2.6 %collective-permute-start.15 = (f32[128,128]{1,0:T(8,128)S(1)}, f32[128,128]{1,0:T(8,128)S(1)}, u32[]{:S(2)}, u32[]{:S(2)}) collective-permute-start(f32[128,128]{1,0:T(8,128)S(1)} %get-tuple-element.66.refs_9_), channel_id=1, source_target_pairs={{0,1},{1,2},{2,3},{4,5},{5,6},{6,7},{8,9},{9,10},{10,11},{12,13},{... | collective-permute-start | bytes 196616 | tf_op jit(solution)/shard_map/ppermute | solution.py:660
  23.9 1.3 %collective-permute-start.16 = (f32[128,128]{1,0:T(8,128)S(1)}, f32[128,128]{1,0:T(8,128)S(1)}, u32[]{:S(2)}, u32[]{:S(2)}) collective-permute-start(f32[128,128]{1,0:T(8,128)S(1)} %get-tuple-element.67.refs_10_), channel_id=1, source_target_pairs={{1,0},{2,1},{3,2},{5,4},{6,5},{7,6},{9,8},{10,9},{11,10},{13,12},{... | collective-permute-start | bytes 196616 | tf_op jit(solution)/shard_map/ppermute | solution.py:659
  25.2 1.6 %collective-permute-start.11 = (bf16[2,48,640]{2,1,0:T(8,128)(2,1)S(1)}, bf16[2,48,640]{2,1,0:T(8,128)(2,1)S(1)}, u32[]{:S(2)}, u32[]{:S(2)}) collective-permute-start(bf16[2,48,640]{2,1,0:T(8,128)(2,1)S(1)} %get-tuple-element.62), channel_id=1, source_target_pairs={{0,16},{1,17},{2,18},{3,19},{16,0},{17,1},{18,2},{19,3},{4,20},{5,... | collective-permute-start | bytes 368648 | tf_op jit(solution)/shard_map/ppermute | solution.py:638
  26.8 1.0 collective-permute-start.12
  27.8 1.5 %collective-permute-start.13 = (bf16[2,48,640]{2,1,0:T(8,128)(2,1)S(1)}, bf16[2,48,640]{2,1,0:T(8,128)(2,1)S(1)}, u32[]{:S(2)}, u32[]{:S(2)}) collective-permute-start(bf16[2,48,640]{2,1,0:T(8,128)(2,1)S(1)} %get-tuple-element.64), channel_id=1, source_target_pairs={{0,18},{1,19},{2,16},{3,17},{16,2},{17,3},{18,0},{19,1},{4,22},{5,... | collective-permute-start | bytes 368648 | tf_op jit(solution)/shard_map/ppermute | solution.py:638
  29.3 1.1 collective-permute-start
  31.8 4.9 %collective-permute-done.12.refs_5_ = bf16[2,48,640]{2,1,0:T(8,128)(2,1)S(1)} collective-permute-done((bf16[2,48,640]{2,1,0:T(8,128)(2,1)S(1)}, bf16[2,48,640]{2,1,0:T(8,128)(2,1)S(1)}, u32[]{:S(2)}, u32[]{:S(2)}) %collective-permute-start.12) | collective-permute-done | bytes 122912 | tf_op jit(solution)/shard_map/ppermute | solution.py:638
  36.7 1.5 %collective-permute-start.3 = (bf16[2,48,640]{2,1,0:T(8,128)(2,1)S(1)}, bf16[2,48,640]{2,1,0:T(8,128)(2,1)S(1)}, u32[]{:S(2)}, u32[]{:S(2)}) collective-permute-start(bf16[2,48,640]{2,1,0:T(8,128)(2,1)S(1)} %get-tuple-element.52), channel_id=1, source_target_pairs={{0,16},{1,17},{2,18},{3,19},{16,0},{17,1},{18,2},{19,3},{4,20},{5,... | collective-permute-start | bytes 368648 | tf_op jit(solution)/shard_map/ppermute | solution.py:638
  38.3 1.7 %collective-permute-start.5 = (bf16[2,48,640]{2,1,0:T(8,128)(2,1)S(1)}, bf16[2,48,640]{2,1,0:T(8,128)(2,1)S(1)}, u32[]{:S(2)}, u32[]{:S(2)}) collective-permute-start(bf16[2,48,640]{2,1,0:T(8,128)(2,1)S(1)} %get-tuple-element.54), channel_id=1, source_target_pairs={{0,18},{1,19},{2,16},{3,17},{16,2},{17,3},{18,0},{19,1},{4,22},{5,... | collective-permute-start | bytes 368648 | tf_op jit(solution)/shard_map/ppermute | solution.py:638
  40.0 1.2 collective-permute-start.6
  41.2 1.5 %collective-permute-start.14 = (bf16[2,48,640]{2,1,0:T(8,128)(2,1)S(1)}, bf16[2,48,640]{2,1,0:T(8,128)(2,1)S(1)}, u32[]{:S(2)}, u32[]{:S(2)}) collective-permute-start(bf16[2,48,640]{2,1,0:T(8,128)(2,1)S(1)} %get-tuple-element.65), channel_id=1, source_target_pairs={{0,19},{1,18},{2,17},{3,16},{16,3},{17,2},{18,1},{19,0},{4,23},{5,... | collective-permute-start | bytes 368648 | tf_op jit(solution)/shard_map/ppermute | solution.py:638
  42.6 7.9 %collective-permute-done.3.refs_4_ = bf16[2,48,640]{2,1,0:T(8,128)(2,1)S(1)} collective-permute-done((bf16[2,48,640]{2,1,0:T(8,128)(2,1)S(1)}, bf16[2,48,640]{2,1,0:T(8,128)(2,1)S(1)}, u32[]{:S(2)}, u32[]{:S(2)}) %collective-permute-start.3) | collective-permute-done | bytes 122912 | tf_op jit(solution)/shard_map/ppermute | solution.py:638
  50.5 1.3 %collective-permute-done.4.refs_5_ = bf16[2,48,640]{2,1,0:T(8,128)(2,1)S(1)} collective-permute-done((bf16[2,48,640]{2,1,0:T(8,128)(2,1)S(1)}, bf16[2,48,640]{2,1,0:T(8,128)(2,1)S(1)}, u32[]{:S(2)}, u32[]{:S(2)}) %collective-permute-start.4) | collective-permute-done | bytes 122912 | tf_op jit(solution)/shard_map/ppermute | solution.py:638
  51.8 1.4 %collective-permute-start.9 = (bf16[2,48,640]{2,1,0:T(8,128)(2,1)S(1)}, bf16[2,48,640]{2,1,0:T(8,128)(2,1)S(1)}, u32[]{:S(2)}, u32[]{:S(2)}) collective-permute-start(bf16[2,48,640]{2,1,0:T(8,128)(2,1)S(1)} %get-tuple-element.60), channel_id=1, source_target_pairs={{0,2},{1,3},{2,0},{3,1},{16,18},{17,19},{18,16},{19,17},{4,6},{5,7... | collective-permute-start | bytes 368648 | tf_op jit(solution)/shard_map/ppermute | solution.py:638
  53.4 1.3 %collective-permute-start.17 = (f32[192,128]{1,0:T(8,128)S(1)}, f32[192,128]{1,0:T(8,128)S(1)}, u32[]{:S(2)}, u32[]{:S(2)}) collective-permute-start(f32[192,128]{1,0:T(8,128)S(1)} %get-tuple-element.68.refs_8_), channel_id=1, source_target_pairs={{4,0},{8,4},{12,8},{16,12},{20,16},{24,20},{28,24},{5,1},{9,5},{13... | collective-permute-start | bytes 294920 | tf_op jit(solution)/shard_map/ppermute | solution.py:664
  54.7 4.6 %collective-permute-start.18 = (f32[192,128]{1,0:T(8,128)S(1)}, f32[192,128]{1,0:T(8,128)S(1)}, u32[]{:S(2)}, u32[]{:S(2)}) collective-permute-start(f32[192,128]{1,0:T(8,128)S(1)} %get-tuple-element.69.refs_7_), channel_id=1, source_target_pairs={{0,4},{4,8},{8,12},{12,16},{16,20},{20,24},{24,28},{1,5},{5,9},{9,... | collective-permute-start | bytes 294920 | tf_op jit(solution)/shard_map/ppermute | solution.py:665
  60.4 1.6 %collective-permute-start.7 = (bf16[136,640]{1,0:T(8,128)(2,1)S(1)}, bf16[136,640]{1,0:T(8,128)(2,1)S(1)}, u32[]{:S(2)}, u32[]{:S(2)}) collective-permute-start(bf16[136,640]{1,0:T(8,128)(2,1)S(1)} %get-tuple-element.57), channel_id=1, source_target_pairs={{0,4},{4,0},{8,12},{12,8},{1,5},{5,1},{9,13},{13,9},{2,6},{6,2},{1... | collective-permute-start | bytes 522248 | tf_op jit(solution)/shard_map/ppermute | solution.py:638
  62.5 5.4 %collective-permute-start.19 = (bf16[136,640]{1,0:T(8,128)(2,1)S(1)}, bf16[136,640]{1,0:T(8,128)(2,1)S(1)}, u32[]{:S(2)}, u32[]{:S(2)}) collective-permute-start(bf16[136,640]{1,0:T(8,128)(2,1)S(1)} %get-tuple-element.78), channel_id=1, source_target_pairs={{0,8},{4,12},{8,0},{12,4},{1,9},{5,13},{9,1},{13,5},{2,10},{6,14},... | collective-permute-start | bytes 522248 | tf_op jit(solution)/shard_map/ppermute | solution.py:638
  67.8 1.4 %collective-permute-start.20 = (bf16[136,640]{1,0:T(8,128)(2,1)S(1)}, bf16[136,640]{1,0:T(8,128)(2,1)S(1)}, u32[]{:S(2)}, u32[]{:S(2)}) collective-permute-start(bf16[136,640]{1,0:T(8,128)(2,1)S(1)} %get-tuple-element.79), channel_id=1, source_target_pairs={{0,12},{4,8},{8,4},{12,0},{1,13},{5,9},{9,5},{13,1},{2,14},{6,10},... | collective-permute-start | bytes 522248 | tf_op jit(solution)/shard_map/ppermute | solution.py:638
  70.7 9.9 %collective-permute-done.19.refs_2_ = bf16[136,640]{1,0:T(8,128)(2,1)S(1)} collective-permute-done((bf16[136,640]{1,0:T(8,128)(2,1)S(1)}, bf16[136,640]{1,0:T(8,128)(2,1)S(1)}, u32[]{:S(2)}, u32[]{:S(2)}) %collective-permute-start.19) | collective-permute-done | bytes 174112 | tf_op jit(solution)/shard_map/ppermute | solution.py:638
  81.4 3.7 %surface.1 = (bf16[32,40,128]{2,1,0:T(8,128)(2,1)}, f32[5,128,128]{2,1,0:T(8,128)}, f32[8,640]{1,0:T(8,128)}, f32[192,128]{1,0:T(8,128)}, f32[192,128]{1,0:T(8,1...) custom-call(f32[136,640]{1,0:T(8,128)} %copy-done.5, ...), custom_call_target="tpu_custom_call" | custom-call | flops 4194304 | bytes 4194304 | tf_op jit(solution)/shard_map/surface/pallas_call | solution.py:678
  85.0 6.3 %all-to-all-start = ((bf16[32,40,128]{2,1,0:T(8,128)(2,1)}), bf16[32,40,128]{2,1,0:T(8,128)(2,1)S(1)}, u32[]{:S(2)}, u32[]{:S(2)}) async-start(bf16[32,40,128]{2,1,0:T(8,128)(2,1)} %get-tuple-element.93), calls=%async_computation | async-start | bytes 655360 | tf_op jit(solution)/shard_map/all_to_all | solution.py:685
  92.0 1.6 %copy-done.2 = f32[2,16,128,128]{3,2,1,0:T(8,128)S(1)} copy-done((f32[2,16,128,128]{3,2,1,0:T(8,128)S(1)}, f32[2,16,128,128]{3,2,1,0:T(8,128)}, u32[]{:S(2)}) %copy-start.2) | copy-done | bytes 2097176
  93.6 1.0 copy-done.6
  95.4 0.9 copy-done.11
  96.3 0.9 copy-done.12
  102.2 10.2 %substeps.1 = f32[2,16,128,128]{3,2,1,0:T(8,128)} custom-call(f32[2,16,128,128]{3,2,1,0:T(8,128)S(1)} %copy-done.2, f32[2,16,128,128]{3,2,1,0:T(8,128)S(1)} %copy-done, s32[128,128]{1,0:T(8,128)S(1)} %copy-done.4, f32[5,128,128]{2,1,0:T(8,128)S(1)} %copy-done.6, f32[8,640]{1,0:T(8,128)S(1)} %copy-done.22, f32[192,128]{1,0:T(8,128)S(1)} %copy-done.10, ...), custom_call_target="tpu_custom_call" | custom-call | flops 16777216 | bytes 16777216 | tf_op jit(solution)/shard_map/substeps/pallas_call | solution.py:688
  113.1 9.3 %backward_remap.1 = f32[160,128]{1,0:T(8,128)} custom-call(s32[640]{0:T(1024)} %copy-done.25, s32[1,640]{1,0:T(1,128)} %reshape.19.src, bf16[32,40,128]{2,1,0:T(8,128)(2,1)} %copy-done.27, bf16[640,128,128]{2,1,0:T(8,128)(2,1)} %w.3), custom_call_target="tpu_custom_call" | custom-call | flops 167772160 | bytes 20971520 | tf_op jit(solution)/shard_map/backward_remap/pallas_call | solution.py:602
  (90 shorter events, 14.6 us)
Async XLA Ops:
  17.2 13.2 %collective-permute-start.10 = (bf16[2,48,640]{2,1,0:T(8,128)(2,1)S(1)}, bf16[2,48,640]{2,1,0:T(8,128)(2,1)S(1)}, u32[]{:S(2)}, u32[]{:S(2)}) collective-permute-start(bf16[2,48,640]{2,1,0:T(8,128)(2,1)S(1)} %get-tuple-element.61), channel_id=1, source_target_pairs={{0,3},{1,2},{2,1},{3,0},{16,19},{17,18},{18,17},{19,16},{4,7},{5,6... | collective-permute-start | bytes 368648 | tf_op jit(solution)/shard_map/ppermute | solution.py:638
  21.3 32.0 %copy-start.20 = (f32[128,128]{1,0:T(8,128)}, f32[128,128]{1,0:T(8,128)S(1)}, u32[]{:S(2)}) copy-start(f32[128,128]{1,0:T(8,128)S(1)} %get-tuple-element.67.refs_10_) | copy-start | bytes 196612
  21.3 32.0 %copy-start.21 = (f32[128,128]{1,0:T(8,128)}, f32[128,128]{1,0:T(8,128)S(1)}, u32[]{:S(2)}) copy-start(f32[128,128]{1,0:T(8,128)S(1)} %get-tuple-element.66.refs_9_) | copy-start | bytes 196612
  21.3 6.4 %collective-permute-start.15 = (f32[128,128]{1,0:T(8,128)S(1)}, f32[128,128]{1,0:T(8,128)S(1)}, u32[]{:S(2)}, u32[]{:S(2)}) collective-permute-start(f32[128,128]{1,0:T(8,128)S(1)} %get-tuple-element.66.refs_9_), channel_id=1, source_target_pairs={{0,1},{1,2},{2,3},{4,5},{5,6},{6,7},{8,9},{9,10},{10,11},{12,13},{... | collective-permute-start | bytes 196616 | tf_op jit(solution)/shard_map/ppermute | solution.py:660
  23.9 5.3 %collective-permute-start.16 = (f32[128,128]{1,0:T(8,128)S(1)}, f32[128,128]{1,0:T(8,128)S(1)}, u32[]{:S(2)}, u32[]{:S(2)}) collective-permute-start(f32[128,128]{1,0:T(8,128)S(1)} %get-tuple-element.67.refs_10_), channel_id=1, source_target_pairs={{1,0},{2,1},{3,2},{5,4},{6,5},{7,6},{9,8},{10,9},{11,10},{13,12},{... | collective-permute-start | bytes 196616 | tf_op jit(solution)/shard_map/ppermute | solution.py:659
  25.2 6.1 %collective-permute-start.11 = (bf16[2,48,640]{2,1,0:T(8,128)(2,1)S(1)}, bf16[2,48,640]{2,1,0:T(8,128)(2,1)S(1)}, u32[]{:S(2)}, u32[]{:S(2)}) collective-permute-start(bf16[2,48,640]{2,1,0:T(8,128)(2,1)S(1)} %get-tuple-element.62), channel_id=1, source_target_pairs={{0,16},{1,17},{2,18},{3,19},{16,0},{17,1},{18,2},{19,3},{4,20},{5,... | collective-permute-start | bytes 368648 | tf_op jit(solution)/shard_map/ppermute | solution.py:638
  26.8 9.9 %collective-permute-start.12 = (bf16[2,48,640]{2,1,0:T(8,128)(2,1)S(1)}, bf16[2,48,640]{2,1,0:T(8,128)(2,1)S(1)}, u32[]{:S(2)}, u32[]{:S(2)}) collective-permute-start(bf16[2,48,640]{2,1,0:T(8,128)(2,1)S(1)} %get-tuple-element.63), channel_id=1, source_target_pairs={{0,17},{1,16},{2,19},{3,18},{16,1},{17,0},{18,3},{19,2},{4,21},{5,... | collective-permute-start | bytes 368648 | tf_op jit(solution)/shard_map/ppermute | solution.py:638
  27.8 25.6 %copy-start.8 = (f32[128,128]{1,0:T(8,128)}, f32[128,128]{1,0:T(8,128)S(1)}, u32[]{:S(2)}) copy-start(f32[128,128]{1,0:T(8,128)S(1)} %collective-permute-done.15.from_west.refs_14_) | copy-start | bytes 196612
  27.8 10.5 %collective-permute-start.13 = (bf16[2,48,640]{2,1,0:T(8,128)(2,1)S(1)}, bf16[2,48,640]{2,1,0:T(8,128)(2,1)S(1)}, u32[]{:S(2)}, u32[]{:S(2)}) collective-permute-start(bf16[2,48,640]{2,1,0:T(8,128)(2,1)S(1)} %get-tuple-element.64), channel_id=1, source_target_pairs={{0,18},{1,19},{2,16},{3,17},{16,2},{17,3},{18,0},{19,1},{4,22},{5,... | collective-permute-start | bytes 368648 | tf_op jit(solution)/shard_map/ppermute | solution.py:638
  29.3 24.1 %copy-start.9 = (f32[128,128]{1,0:T(8,128)}, f32[128,128]{1,0:T(8,128)S(1)}, u32[]{:S(2)}) copy-start(f32[128,128]{1,0:T(8,128)S(1)} %collective-permute-done.16.from_east.refs_13_) | copy-start | bytes 196612
  29.3 9.0 %collective-permute-start = (bf16[2,48,640]{2,1,0:T(8,128)(2,1)S(1)}, bf16[2,48,640]{2,1,0:T(8,128)(2,1)S(1)}, u32[]{:S(2)}, u32[]{:S(2)}) collective-permute-start(bf16[2,48,640]{2,1,0:T(8,128)(2,1)S(1)} %get-tuple-element.49), channel_id=1, source_target_pairs={{0,1},{1,0},{2,3},{3,2},{16,17},{17,16},{18,19},{19,18},{4,5},{5,4... | collective-permute-start | bytes 368648 | tf_op jit(solution)/shard_map/ppermute | solution.py:638
  30.4 9.6 %collective-permute-start.1 = (bf16[2,48,640]{2,1,0:T(8,128)(2,1)S(1)}, bf16[2,48,640]{2,1,0:T(8,128)(2,1)S(1)}, u32[]{:S(2)}, u32[]{:S(2)}) collective-permute-start(bf16[2,48,640]{2,1,0:T(8,128)(2,1)S(1)} %get-tuple-element.50), channel_id=1, source_target_pairs={{0,2},{1,3},{2,0},{3,1},{16,18},{17,19},{18,16},{19,17},{4,6},{5,7... | collective-permute-start | bytes 368648 | tf_op jit(solution)/shard_map/ppermute | solution.py:638
  31.3 9.8 %collective-permute-start.2 = (bf16[2,48,640]{2,1,0:T(8,128)(2,1)S(1)}, bf16[2,48,640]{2,1,0:T(8,128)(2,1)S(1)}, u32[]{:S(2)}, u32[]{:S(2)}) collective-permute-start(bf16[2,48,640]{2,1,0:T(8,128)(2,1)S(1)} %get-tuple-element.51), channel_id=1, source_target_pairs={{0,3},{1,2},{2,1},{3,0},{16,19},{17,18},{18,17},{19,16},{4,7},{5,6... | collective-permute-start | bytes 368648 | tf_op jit(solution)/shard_map/ppermute | solution.py:638
  36.7 13.8 %collective-permute-start.3 = (bf16[2,48,640]{2,1,0:T(8,128)(2,1)S(1)}, bf16[2,48,640]{2,1,0:T(8,128)(2,1)S(1)}, u32[]{:S(2)}, u32[]{:S(2)}) collective-permute-start(bf16[2,48,640]{2,1,0:T(8,128)(2,1)S(1)} %get-tuple-element.52), channel_id=1, source_target_pairs={{0,16},{1,17},{2,18},{3,19},{16,0},{17,1},{18,2},{19,3},{4,20},{5,... | collective-permute-start | bytes 368648 | tf_op jit(solution)/shard_map/ppermute | solution.py:638
  38.3 13.5 %collective-permute-start.4 = (bf16[2,48,640]{2,1,0:T(8,128)(2,1)S(1)}, bf16[2,48,640]{2,1,0:T(8,128)(2,1)S(1)}, u32[]{:S(2)}, u32[]{:S(2)}) collective-permute-start(bf16[2,48,640]{2,1,0:T(8,128)(2,1)S(1)} %get-tuple-element.53), channel_id=1, source_target_pairs={{0,17},{1,16},{2,19},{3,18},{16,1},{17,0},{18,3},{19,2},{4,21},{5,... | collective-permute-start | bytes 368648 | tf_op jit(solution)/shard_map/ppermute | solution.py:638
  38.3 15.1 %collective-permute-start.5 = (bf16[2,48,640]{2,1,0:T(8,128)(2,1)S(1)}, bf16[2,48,640]{2,1,0:T(8,128)(2,1)S(1)}, u32[]{:S(2)}, u32[]{:S(2)}) collective-permute-start(bf16[2,48,640]{2,1,0:T(8,128)(2,1)S(1)} %get-tuple-element.54), channel_id=1, source_target_pairs={{0,18},{1,19},{2,16},{3,17},{16,2},{17,3},{18,0},{19,1},{4,22},{5,... | collective-permute-start | bytes 368648 | tf_op jit(solution)/shard_map/ppermute | solution.py:638
  40.0 14.7 %collective-permute-start.6 = (bf16[2,48,640]{2,1,0:T(8,128)(2,1)S(1)}, bf16[2,48,640]{2,1,0:T(8,128)(2,1)S(1)}, u32[]{:S(2)}, u32[]{:S(2)}) collective-permute-start(bf16[2,48,640]{2,1,0:T(8,128)(2,1)S(1)} %get-tuple-element.55), channel_id=1, source_target_pairs={{0,19},{1,18},{2,17},{3,16},{16,3},{17,2},{18,1},{19,0},{4,23},{5,... | collective-permute-start | bytes 368648 | tf_op jit(solution)/shard_map/ppermute | solution.py:638
  41.2 19.2 %collective-permute-start.14 = (bf16[2,48,640]{2,1,0:T(8,128)(2,1)S(1)}, bf16[2,48,640]{2,1,0:T(8,128)(2,1)S(1)}, u32[]{:S(2)}, u32[]{:S(2)}) collective-permute-start(bf16[2,48,640]{2,1,0:T(8,128)(2,1)S(1)} %get-tuple-element.65), channel_id=1, source_target_pairs={{0,19},{1,18},{2,17},{3,16},{16,3},{17,2},{18,1},{19,0},{4,23},{5,... | collective-permute-start | bytes 368648 | tf_op jit(solution)/shard_map/ppermute | solution.py:638
  50.5 11.4 %collective-permute-start.8 = (bf16[2,48,640]{2,1,0:T(8,128)(2,1)S(1)}, bf16[2,48,640]{2,1,0:T(8,128)(2,1)S(1)}, u32[]{:S(2)}, u32[]{:S(2)}) collective-permute-start(bf16[2,48,640]{2,1,0:T(8,128)(2,1)S(1)} %get-tuple-element.59), channel_id=1, source_target_pairs={{0,1},{1,0},{2,3},{3,2},{16,17},{17,16},{18,19},{19,18},{4,5},{5,4... | collective-permute-start | bytes 368648 | tf_op jit(solution)/shard_map/ppermute | solution.py:638
  51.8 10.2 %collective-permute-start.9 = (bf16[2,48,640]{2,1,0:T(8,128)(2,1)S(1)}, bf16[2,48,640]{2,1,0:T(8,128)(2,1)S(1)}, u32[]{:S(2)}, u32[]{:S(2)}) collective-permute-start(bf16[2,48,640]{2,1,0:T(8,128)(2,1)S(1)} %get-tuple-element.60), channel_id=1, source_target_pairs={{0,2},{1,3},{2,0},{3,1},{16,18},{17,19},{18,16},{19,17},{4,6},{5,7... | collective-permute-start | bytes 368648 | tf_op jit(solution)/shard_map/ppermute | solution.py:638
  53.3 27.3 %copy-start.14 = (f32[192,128]{1,0:T(8,128)}, f32[192,128]{1,0:T(8,128)S(1)}, u32[]{:S(2)}) copy-start(f32[192,128]{1,0:T(8,128)S(1)} %get-tuple-element.68.refs_8_) | copy-start | bytes 294916
  53.3 27.3 %copy-start.15 = (f32[192,128]{1,0:T(8,128)}, f32[192,128]{1,0:T(8,128)S(1)}, u32[]{:S(2)}) copy-start(f32[192,128]{1,0:T(8,128)S(1)} %get-tuple-element.69.refs_7_) | copy-start | bytes 294916
  53.4 8.6 %collective-permute-start.17 = (f32[192,128]{1,0:T(8,128)S(1)}, f32[192,128]{1,0:T(8,128)S(1)}, u32[]{:S(2)}, u32[]{:S(2)}) collective-permute-start(f32[192,128]{1,0:T(8,128)S(1)} %get-tuple-element.68.refs_8_), channel_id=1, source_target_pairs={{4,0},{8,4},{12,8},{16,12},{20,16},{24,20},{28,24},{5,1},{9,5},{13... | collective-permute-start | bytes 294920 | tf_op jit(solution)/shard_map/ppermute | solution.py:664
  54.7 7.3 %collective-permute-start.18 = (f32[192,128]{1,0:T(8,128)S(1)}, f32[192,128]{1,0:T(8,128)S(1)}, u32[]{:S(2)}, u32[]{:S(2)}) collective-permute-start(f32[192,128]{1,0:T(8,128)S(1)} %get-tuple-element.69.refs_7_), channel_id=1, source_target_pairs={{0,4},{4,8},{8,12},{12,16},{16,20},{20,24},{24,28},{1,5},{5,9},{9,... | collective-permute-start | bytes 294920 | tf_op jit(solution)/shard_map/ppermute | solution.py:665
  60.4 10.3 %collective-permute-start.7 = (bf16[136,640]{1,0:T(8,128)(2,1)S(1)}, bf16[136,640]{1,0:T(8,128)(2,1)S(1)}, u32[]{:S(2)}, u32[]{:S(2)}) collective-permute-start(bf16[136,640]{1,0:T(8,128)(2,1)S(1)} %get-tuple-element.57), channel_id=1, source_target_pairs={{0,4},{4,0},{8,12},{12,8},{1,5},{5,1},{9,13},{13,9},{2,6},{6,2},{1... | collective-permute-start | bytes 522248 | tf_op jit(solution)/shard_map/ppermute | solution.py:638
  62.0 18.7 %copy-start.31 = (f32[192,128]{1,0:T(8,128)}, f32[192,128]{1,0:T(8,128)S(1)}, u32[]{:S(2)}) copy-start(f32[192,128]{1,0:T(8,128)S(1)} %collective-permute-done.17.refs_11_) | copy-start | bytes 294916
  62.0 18.7 %copy-start.32 = (f32[192,128]{1,0:T(8,128)}, f32[192,128]{1,0:T(8,128)S(1)}, u32[]{:S(2)}) copy-start(f32[192,128]{1,0:T(8,128)S(1)} %collective-permute-done.18.refs_12_) | copy-start | bytes 294916
  62.0 29.4 %copy-start.24 = (s32[640]{0:T(1024)S(1)}, s32[640]{0:T(1024)}, u32[]{:S(2)}) copy-start(s32[640]{0:T(1024)} %src.1) | copy-start | bytes 7684
  62.0 30.0 %copy-start.4 = (s32[128,128]{1,0:T(8,128)S(1)}, s32[128,128]{1,0:T(8,128)}, u32[]{:S(2)}) copy-start(s32[128,128]{1,0:T(8,128)} %land.5) | copy-start | bytes 196612
  62.5 18.2 %collective-permute-start.19 = (bf16[136,640]{1,0:T(8,128)(2,1)S(1)}, bf16[136,640]{1,0:T(8,128)(2,1)S(1)}, u32[]{:S(2)}, u32[]{:S(2)}) collective-permute-start(bf16[136,640]{1,0:T(8,128)(2,1)S(1)} %get-tuple-element.78), channel_id=1, source_target_pairs={{0,8},{4,12},{8,0},{12,4},{1,9},{5,13},{9,1},{13,5},{2,10},{6,14},... | collective-permute-start | bytes 522248 | tf_op jit(solution)/shard_map/ppermute | solution.py:638
  67.8 12.8 %collective-permute-start.20 = (bf16[136,640]{1,0:T(8,128)(2,1)S(1)}, bf16[136,640]{1,0:T(8,128)(2,1)S(1)}, u32[]{:S(2)}, u32[]{:S(2)}) collective-permute-start(bf16[136,640]{1,0:T(8,128)(2,1)S(1)} %get-tuple-element.79), channel_id=1, source_target_pairs={{0,12},{4,8},{8,4},{12,0},{1,13},{5,9},{9,5},{13,1},{2,14},{6,10},... | collective-permute-start | bytes 522248 | tf_op jit(solution)/shard_map/ppermute | solution.py:638
  85.0 27.4 %all-to-all-start = ((bf16[32,40,128]{2,1,0:T(8,128)(2,1)}), bf16[32,40,128]{2,1,0:T(8,128)(2,1)S(1)}, u32[]{:S(2)}, u32[]{:S(2)}) async-start(bf16[32,40,128]{2,1,0:T(8,128)(2,1)} %get-tuple-element.93), calls=%async_computation | async-start | bytes 655360 | tf_op jit(solution)/shard_map/all_to_all | solution.py:685
  (23 other events, 77.4 us)

commit v4 on v3

--- a/solution.py
+++ b/solution.py
@@ -193,7 +193,7 @@
             pltpu.SemaphoreType.DMA((parts,)),
         ],
         out_shape=[jax.ShapeDtypeStruct((n_gx // 2, chunk, wide), BF16)] * (2 * n_sec * n_gy) + [jax.ShapeDtypeStruct((total,), jnp.int32)],
-        compiler_params=kernel_params(42),
+        compiler_params=kernel_params(58),
         cost_estimate=pl.CostEstimate(flops=2 * total * 8 * width * width, bytes_accessed=total * width * width * 2, transcendentals=0),
         name="forward_remap",
     )(src, own, dst, flux, w)
@@ -648,8 +648,14 @@
 
     *sends, slots = forward(atm_flux, remap_weights, remap_src, remap_owner.reshape(total), remap_dst, grid, cap)
     chunk = sends[0].shape[1]
-    sends = sends[:planes], sends[planes:]
-    got = [[send[0]] + [swapped(send[m], ("sec", "gy"), planes, m) for m in range(1, planes)] for send in sends]
+    far_sends, near_sends = sends[:planes], sends[planes:]
+
+    def in_plane(chunks):
+        return [chunks[0]] + [swapped(chunks[m], ("sec", "gy"), planes, m) for m in range(1, planes)]
+
+    def merge(chunks, dtypes):
+        outs = [((height + 8, wide), dtype) for dtype in dtypes]
+        return kernel(functools.partial(merge_kernel, planes), outs, "merge", 24, 1 << 22)(*chunks)
 
     side = (width, width)
     end = (7 * levels + 80, width)
@@ -658,22 +664,18 @@
     to_east, to_west = neighbours("gy")
     from_e = lax.ppermute(own_w, "gy", to_west)
     from_w = lax.ppermute(own_e, "gy", to_east)
+
+    far = merge(in_plane(far_sends), [BF16] * (n_gx // 2))
+    far, near_sends, from_e, from_w = lax.optimization_barrier((far, near_sends, from_e, from_w))
+    far = [swapped(part, "gx", n_gx, n_gx // 2 + m) for m, part in enumerate(far)]
     own_s, own_n = kernel(rows_kernel, [(end, F32)] * 2, "edge_rows", 16, 1 << 20)(
         tracers.reshape(-1, width), currents.reshape(-1, width), land_sea, from_w, from_e
     )
     from_n = lax.ppermute(own_s, NORTH, to_south)
     from_s = lax.ppermute(own_n, NORTH, to_north)
-
-    merged = []
-    for far, chunks in zip((1, 0), got):
-        if far:
-            chunks, from_n, from_s = lax.optimization_barrier((chunks, from_n, from_s))
-        here = [((height + 8, wide), BF16)] * (n_gx // 2)
-        if not far:
-            here = [((height + 8, wide), F32)] + here[1:]
-        merged.append(kernel(functools.partial(merge_kernel, planes), here, "merge", 24, 1 << 22)(*chunks))
-    merged = list(merged[1]) + list(merged[0])
-    parts = [merged[0]] + [swapped(merged[m], "gx", n_gx, m) for m in range(1, n_gx)]
+    near, from_n, from_s = lax.optimization_barrier((in_plane(near_sends), from_n, from_s))
+    near = merge(near, [F32] + [BF16] * (n_gx // 2 - 1))
+    parts = [near[0]] + [swapped(near[m], "gx", n_gx, m) for m in range(1, n_gx // 2)] + far
 
     back, flux, rim, *edges = kernel(
         functools.partial(surface_kernel, grid, chunk, levels),
@@ -689,7 +691,7 @@
         stencil_kernel,
         [(tracers.shape, F32)],
         "substeps",
-        32,
+        58,
         1 << 24,
         [
             pltpu.VMEM(tracers.shape, F32),

time: 123 us -> 104 us (0.85)
  waiting for transfers between devices: 24.5 us -> 8.99 us
  local copies, waits for them, and re-layouts: 16.8 us -> 3.42 us
  starting transfers between devices: 40.3 us -> 45.6 us
  Pallas kernels: 39.2 us -> 43.1 us
    ppermute x17, waiting for transfers between devices: 24.5 us -> 7.94 us  [swapped(): return lax.ppermute(array, axes, [(i, i ^ step) for i in range(count)])]
    unnamed x66 -> x52, local copies, waits for them, and re-layouts: 14.8 us -> 1.43 us
    ppermute x17, starting transfers between devices: 24.2 us -> 31.4 us  [swapped(): return lax.ppermute(array, axes, [(i, i ^ step) for i in range(count)])]
    all_to_all x1, starting transfers between devices: 6.33 us -> 3.11 us  [on_device(): lax.all_to_all(back, EVERY, split_axis=0, concat_axis=0, tiled=True)]
    pallas_call x3, Pallas kernels: 11 us -> 13.9 us  [the longest x1 13 us: on_device(): kernel(stencil_kernel, [(tracers.shape, F32)], 'substeps', 58, 1 << 24, [...]
    ppermute x1, starting transfers between devices: 2.58 us -> 3.84 us  [on_device(): from_w = lax.ppermute(own_e, 'gy', to_east)]
  transfers between devices with their start and end apart: 22 -> 22, of which waited for: 5 -> 5; matrix products, arithmetic and copies ran while one was open for 2% -> 2% of each run, Pallas kernels for 10% -> 15%
where the time goes in v4:
time: 104 us; the launch traced here: 103 us
  starting transfers between devices  45.6 us (44%)
  Pallas kernels  43.1 us (41%)
  waiting for transfers between devices  8.99 us (9%)
  local copies, waits for them, and re-layouts  3.42 us (3%)
  other arithmetic  1.29 us (1%)
    ppermute x17, starting transfers between devices, swapped(): return lax.ppermute(array, axes, [(i, i ^ step) for i in range(count)])  31.4 us
    pallas_call x1, Pallas kernels, forward(): pl.pallas_call(functools.partial(forward_kernel, parts, cap, grid), in_sp...  14.6 us
    pallas_call x1, Pallas kernels, on_device(): kernel(stencil_kernel, [(tracers.shape, F32)], 'substeps', 58, 1 << 24, [...  13 us
    pallas_call x1, Pallas kernels, backward(): pl.pallas_call(functools.partial(backward_kernel, parts), in_specs=[SMEM,...  9.27 us
    ppermute x17, waiting for transfers between devices, swapped(): return lax.ppermute(array, axes, [(i, i ^ step) for i in range(count)])  7.94 us
    ppermute x1, starting transfers between devices, on_device(): from_s = lax.ppermute(own_n, NORTH, to_north)  4.55 us
    ppermute x1, starting transfers between devices, on_device(): from_w = lax.ppermute(own_e, 'gy', to_east)  3.84 us
    pallas_call x1, Pallas kernels, on_device(): kernel(functools.partial(surface_kernel, grid, chunk, levels), [((planes...  3.62 us
  transfers between devices with their start and end apart: 22, of which 5 were waited for; matrix products, arithmetic and copies ran while one was open for 2% of the time, Pallas kernels for 15%

profile of v4, /device:TPU:0, one launch (start us, length us, event | category | flops | bytes accessed | tf_op | source)
XLA Modules:
  0.0 103.3 jit_solution(10534805576932783871)
XLA Ops:
  0.6 1.3 %reduce.own = s32[640]{0:T(1024)} reduce(s32[640,1]{0,1:T(1,128)} %param.12, s32[]{:T(128)} %constant), dimensions={1}, to_apply=%param.12.reduce_sub_computation | reduce | bytes 5124 | tf_op args[4]
  1.9 14.6 %forward_remap.1 = (bf16[2,48,640]{2,1,0:T(8,128)(2,1)}, bf16[2,48,640]{2,1,0:T(8,128)(2,1)}, bf16[2,48,640]{2,1,0:T(8,128)(2,1)}, bf16[2,48,640]{2,1,0:T(8,128)...) custom-call(s32[640]{0:T(1024)} %src.1, ...), custom_call_target="tpu_custom_call" | custom-call | flops 167772160 | bytes 20971520 | tf_op jit(solution)/shard_map/forward_remap/pallas_call | solution.py:181
  16.5 0.5 collective-permute-start
  17.1 2.6 %collective-permute-start.1 = (bf16[2,48,640]{2,1,0:T(8,128)(2,1)}, bf16[2,48,640]{2,1,0:T(8,128)(2,1)S(1)}, u32[]{:S(2)}, u32[]{:S(2)}) collective-permute-start(bf16[2,48,640]{2,1,0:T(8,128)(2,1)} %get-tuple-element.62), channel_id=1, source_target_pairs={{0,2},{1,3},{2,0},{3,1},{16,18},{17,19},{18,16},{19,17},{4,6},{5,7... | collective-permute-start | bytes 368648 | tf_op jit(solution)/shard_map/ppermute | solution.py:638
  19.7 1.8 %collective-permute-start.3 = (bf16[2,48,640]{2,1,0:T(8,128)(2,1)}, bf16[2,48,640]{2,1,0:T(8,128)(2,1)S(1)}, u32[]{:S(2)}, u32[]{:S(2)}) collective-permute-start(bf16[2,48,640]{2,1,0:T(8,128)(2,1)} %get-tuple-element.64), channel_id=1, source_target_pairs={{0,16},{1,17},{2,18},{3,19},{16,0},{17,1},{18,2},{19,3},{4,20},{5,... | collective-permute-start | bytes 368648 | tf_op jit(solution)/shard_map/ppermute | solution.py:638
  21.5 2.6 %collective-permute-start.5 = (bf16[2,48,640]{2,1,0:T(8,128)(2,1)}, bf16[2,48,640]{2,1,0:T(8,128)(2,1)S(1)}, u32[]{:S(2)}, u32[]{:S(2)}) collective-permute-start(bf16[2,48,640]{2,1,0:T(8,128)(2,1)} %get-tuple-element.66), channel_id=1, source_target_pairs={{0,18},{1,19},{2,16},{3,17},{16,2},{17,3},{18,0},{19,1},{4,22},{5,... | collective-permute-start | bytes 368648 | tf_op jit(solution)/shard_map/ppermute | solution.py:638
  24.1 1.6 %collective-permute-start.6 = (bf16[2,48,640]{2,1,0:T(8,128)(2,1)}, bf16[2,48,640]{2,1,0:T(8,128)(2,1)S(1)}, u32[]{:S(2)}, u32[]{:S(2)}) collective-permute-start(bf16[2,48,640]{2,1,0:T(8,128)(2,1)} %get-tuple-element.67), channel_id=1, source_target_pairs={{0,19},{1,18},{2,17},{3,16},{16,3},{17,2},{18,1},{19,0},{4,23},{5,... | collective-permute-start | bytes 368648 | tf_op jit(solution)/shard_map/ppermute | solution.py:638
  25.7 1.6 %edge_columns.1 = (f32[128,128]{1,0:T(8,128)S(1)}, f32[128,128]{1,0:T(8,128)S(1)}) custom-call(f32[2,16,128,128]{3,2,1,0:T(8,128)S(1)} %copy-done.1, f32[2,16,128,128]{3,2,1,0:T(8,128)S(1)} %copy-done, s32[128,128]{1,0:T(8,128)S(1)} %copy-done.2), custom_call_target="tpu_custom_call" | custom-call | flops 4194304 | bytes 4194304 | tf_op jit(solution)/shard_map/edge_columns/pallas_call | solution.py:662
  27.4 1.3 %collective-permute-start.7 = (f32[128,128]{1,0:T(8,128)S(1)}, f32[128,128]{1,0:T(8,128)S(1)}, u32[]{:S(2)}, u32[]{:S(2)}) collective-permute-start(f32[128,128]{1,0:T(8,128)S(1)} %get-tuple-element.78.refs_10_), channel_id=1, source_target_pairs={{1,0},{2,1},{3,2},{5,4},{6,5},{7,6},{9,8},{10,9},{11,10},{13,12},{... | collective-permute-start | bytes 196616 | tf_op jit(solution)/shard_map/ppermute | solution.py:665
  28.7 3.8 %collective-permute-start.8 = (f32[128,128]{1,0:T(8,128)S(1)}, f32[128,128]{1,0:T(8,128)S(1)}, u32[]{:S(2)}, u32[]{:S(2)}) collective-permute-start(f32[128,128]{1,0:T(8,128)S(1)} %get-tuple-element.79.refs_9_), channel_id=1, source_target_pairs={{0,1},{1,2},{2,3},{4,5},{5,6},{6,7},{8,9},{9,10},{10,11},{12,13},{... | collective-permute-start | bytes 196616 | tf_op jit(solution)/shard_map/ppermute | solution.py:666
  32.8 0.4 merge.2
  33.5 2.2 %collective-permute-start.9 = (bf16[2,48,640]{2,1,0:T(8,128)(2,1)S(1)}, bf16[2,48,640]{2,1,0:T(8,128)(2,1)S(1)}, u32[]{:S(2)}, u32[]{:S(2)}) collective-permute-start(bf16[2,48,640]{2,1,0:T(8,128)(2,1)S(1)} %copy-done.25), channel_id=1, source_target_pairs={{0,1},{1,0},{2,3},{3,2},{16,17},{17,16},{18,19},{19,18},{4,5},{5,4... | collective-permute-start | bytes 368648 | tf_op jit(solution)/shard_map/ppermute | solution.py:638
  35.6 2.3 %collective-permute-start.10 = (bf16[2,48,640]{2,1,0:T(8,128)(2,1)S(1)}, bf16[2,48,640]{2,1,0:T(8,128)(2,1)S(1)}, u32[]{:S(2)}, u32[]{:S(2)}) collective-permute-start(bf16[2,48,640]{2,1,0:T(8,128)(2,1)S(1)} %copy-done.24), channel_id=1, source_target_pairs={{0,2},{1,3},{2,0},{3,1},{16,18},{17,19},{18,16},{19,17},{4,6},{5,7... | collective-permute-start | bytes 368648 | tf_op jit(solution)/shard_map/ppermute | solution.py:638
  38.1 1.4 %collective-permute-start.16 = (f32[192,128]{1,0:T(8,128)S(1)}, f32[192,128]{1,0:T(8,128)S(1)}, u32[]{:S(2)}, u32[]{:S(2)}) collective-permute-start(f32[192,128]{1,0:T(8,128)S(1)} %get-tuple-element.90.refs_8_), channel_id=1, source_target_pairs={{4,0},{8,4},{12,8},{16,12},{20,16},{24,20},{28,24},{5,1},{9,5},{13... | collective-permute-start | bytes 294920 | tf_op jit(solution)/shard_map/ppermute | solution.py:674
  39.6 4.6 %collective-permute-start.17 = (f32[192,128]{1,0:T(8,128)S(1)}, f32[192,128]{1,0:T(8,128)S(1)}, u32[]{:S(2)}, u32[]{:S(2)}) collective-permute-start(f32[192,128]{1,0:T(8,128)S(1)} %get-tuple-element.91.refs_7_), channel_id=1, source_target_pairs={{0,4},{4,8},{8,12},{12,16},{16,20},{20,24},{24,28},{1,5},{5,9},{9,... | collective-permute-start | bytes 294920 | tf_op jit(solution)/shard_map/ppermute | solution.py:675
  44.2 0.8 collective-permute-done.16.refs_11_
  45.0 2.8 %collective-permute-start.12 = (bf16[2,48,640]{2,1,0:T(8,128)(2,1)S(1)}, bf16[2,48,640]{2,1,0:T(8,128)(2,1)S(1)}, u32[]{:S(2)}, u32[]{:S(2)}) collective-permute-start(bf16[2,48,640]{2,1,0:T(8,128)(2,1)S(1)} %copy-done.22), channel_id=1, source_target_pairs={{0,16},{1,17},{2,18},{3,19},{16,0},{17,1},{18,2},{19,3},{4,20},{5,... | collective-permute-start | bytes 368648 | tf_op jit(solution)/shard_map/ppermute | solution.py:638
  47.9 5.0 %collective-permute-start.13 = (bf16[2,48,640]{2,1,0:T(8,128)(2,1)S(1)}, bf16[2,48,640]{2,1,0:T(8,128)(2,1)S(1)}, u32[]{:S(2)}, u32[]{:S(2)}) collective-permute-start(bf16[2,48,640]{2,1,0:T(8,128)(2,1)S(1)} %copy-done.21), channel_id=1, source_target_pairs={{0,17},{1,16},{2,19},{3,18},{16,1},{17,0},{18,3},{19,2},{4,21},{5,... | collective-permute-start | bytes 368648 | tf_op jit(solution)/shard_map/ppermute | solution.py:638
  52.9 1.4 %collective-permute-start.14 = (bf16[2,48,640]{2,1,0:T(8,128)(2,1)S(1)}, bf16[2,48,640]{2,1,0:T(8,128)(2,1)S(1)}, u32[]{:S(2)}, u32[]{:S(2)}) collective-permute-start(bf16[2,48,640]{2,1,0:T(8,128)(2,1)S(1)} %copy-done.20), channel_id=1, source_target_pairs={{0,18},{1,19},{2,16},{3,17},{16,2},{17,3},{18,0},{19,1},{4,22},{5,... | collective-permute-start | bytes 368648 | tf_op jit(solution)/shard_map/ppermute | solution.py:638
  54.4 2.6 %collective-permute-start.15 = (bf16[2,48,640]{2,1,0:T(8,128)(2,1)S(1)}, bf16[2,48,640]{2,1,0:T(8,128)(2,1)S(1)}, u32[]{:S(2)}, u32[]{:S(2)}) collective-permute-start(bf16[2,48,640]{2,1,0:T(8,128)(2,1)S(1)} %copy-done.19), channel_id=1, source_target_pairs={{0,19},{1,18},{2,17},{3,16},{16,3},{17,2},{18,1},{19,0},{4,23},{5,... | collective-permute-start | bytes 368648 | tf_op jit(solution)/shard_map/ppermute | solution.py:638
  56.9 5.7 %collective-permute-start.20 = (bf16[136,640]{1,0:T(8,128)(2,1)S(1)}, bf16[136,640]{1,0:T(8,128)(2,1)S(1)}, u32[]{:S(2)}, u32[]{:S(2)}) collective-permute-start(bf16[136,640]{1,0:T(8,128)(2,1)S(1)} %get-tuple-element.103), channel_id=1, source_target_pairs={{0,12},{4,8},{8,4},{12,0},{1,13},{5,9},{9,5},{13,1},{2,14},{6,10},... | collective-permute-start | bytes 522248 | tf_op jit(solution)/shard_map/ppermute | solution.py:638
  63.2 0.7 slice.6.refs_4_
  63.9 0.7 slice.7.refs_5_
  64.6 4.1 %collective-permute-done.19.refs_2_ = bf16[136,640]{1,0:T(8,128)(2,1)S(1)} collective-permute-done((bf16[136,640]{1,0:T(8,128)(2,1)S(1)}, bf16[136,640]{1,0:T(8,128)(2,1)S(1)}, u32[]{:S(2)}, u32[]{:S(2)}) %collective-permute-start.19) | collective-permute-done | bytes 174112 | tf_op jit(solution)/shard_map/ppermute | solution.py:638
  68.7 3.6 %collective-permute-done.18.refs_1_ = bf16[136,640]{1,0:T(8,128)(2,1)S(1)} collective-permute-done((bf16[136,640]{1,0:T(8,128)(2,1)S(1)}, bf16[136,640]{1,0:T(8,128)(2,1)S(1)}, u32[]{:S(2)}, u32[]{:S(2)}) %collective-permute-start.18) | collective-permute-done | bytes 174112 | tf_op jit(solution)/shard_map/ppermute | solution.py:638
  72.4 0.6 copy-done.15
  73.0 3.6 %surface.1 = (bf16[32,40,128]{2,1,0:T(8,128)(2,1)}, f32[5,128,128]{2,1,0:T(8,128)}, f32[8,640]{1,0:T(8,128)}, f32[192,128]{1,0:T(8,128)}, f32[192,128]{1,0:T(8,1...) custom-call(f32[136,640]{1,0:T(8,128)} %copy-done.3, ...), custom_call_target="tpu_custom_call" | custom-call | flops 4194304 | bytes 4194304 | tf_op jit(solution)/shard_map/surface/pallas_call | solution.py:680
  76.6 3.1 %all-to-all-start = ((bf16[32,40,128]{2,1,0:T(8,128)(2,1)}), bf16[32,40,128]{2,1,0:T(8,128)(2,1)S(1)}, u32[]{:S(2)}, u32[]{:S(2)}) async-start(bf16[32,40,128]{2,1,0:T(8,128)(2,1)} %get-tuple-element.117), calls=%async_computation | async-start | bytes 655360 | tf_op jit(solution)/shard_map/all_to_all | solution.py:687
  79.7 0.6 reshape.19.src
  80.3 13.0 %substeps.1 = f32[2,16,128,128]{3,2,1,0:T(8,128)} custom-call(f32[2,16,128,128]{3,2,1,0:T(8,128)} %tracers.3, f32[2,16,128,128]{3,2,1,0:T(8,128)} %currents.3, s32[128,128]{1,0:T(8,128)} %land.5, f32[5,128,128]{2,1,0:T(8,128)} %get-tuple-element.106.flux, f32[8,640]{1,0:T(8,128)} %get-tuple-element.107.rim, f32[192,128]{1,0:T(8,128)} %get-tuple-element.108.in_n, ...), custom_call_target="tpu_custom_call" | custom-call | flops 16777216 | bytes 16777216 | tf_op jit(solution)/shard_map/substeps/pallas_call | solution.py:690
  93.3 0.7 copy-done.12
  94.1 9.3 %backward_remap.1 = f32[160,128]{1,0:T(8,128)} custom-call(s32[640]{0:T(1024)} %get-tuple-element.116.slots, s32[1,640]{1,0:T(1,128)} %reshape.19.src, bf16[32,40,128]{2,1,0:T(8,128)(2,1)} %copy-done.12, bf16[640,128,128]{2,1,0:T(8,128)(2,1)} %w.3), custom_call_target="tpu_custom_call" | custom-call | flops 167772160 | bytes 20971520 | tf_op jit(solution)/shard_map/backward_remap/pallas_call | solution.py:602
  (76 shorter events, 1.3 us)
Async XLA Ops:
  1.9 23.8 %copy-start = (f32[2,16,128,128]{3,2,1,0:T(8,128)S(1)}, f32[2,16,128,128]{3,2,1,0:T(8,128)}, u32[]{:S(2)}) copy-start(f32[2,16,128,128]{3,2,1,0:T(8,128)} %currents.3) | copy-start | bytes 6291460
  1.9 23.8 %copy-start.1 = (f32[2,16,128,128]{3,2,1,0:T(8,128)S(1)}, f32[2,16,128,128]{3,2,1,0:T(8,128)}, u32[]{:S(2)}) copy-start(f32[2,16,128,128]{3,2,1,0:T(8,128)} %tracers.3) | copy-start | bytes 6291460
  1.9 23.8 %copy-start.2 = (s32[128,128]{1,0:T(8,128)S(1)}, s32[128,128]{1,0:T(8,128)}, u32[]{:S(2)}) copy-start(s32[128,128]{1,0:T(8,128)} %land.5) | copy-start | bytes 196612
  16.5 4.9 %collective-permute-start = (bf16[2,48,640]{2,1,0:T(8,128)(2,1)}, bf16[2,48,640]{2,1,0:T(8,128)(2,1)S(1)}, u32[]{:S(2)}, u32[]{:S(2)}) collective-permute-start(bf16[2,48,640]{2,1,0:T(8,128)(2,1)} %get-tuple-element.61), channel_id=1, source_target_pairs={{0,1},{1,0},{2,3},{3,2},{16,17},{17,16},{18,19},{19,18},{4,5},{5,4... | collective-permute-start | bytes 368648 | tf_op jit(solution)/shard_map/ppermute | solution.py:638
  17.1 7.0 %collective-permute-start.1 = (bf16[2,48,640]{2,1,0:T(8,128)(2,1)}, bf16[2,48,640]{2,1,0:T(8,128)(2,1)S(1)}, u32[]{:S(2)}, u32[]{:S(2)}) collective-permute-start(bf16[2,48,640]{2,1,0:T(8,128)(2,1)} %get-tuple-element.62), channel_id=1, source_target_pairs={{0,2},{1,3},{2,0},{3,1},{16,18},{17,19},{18,16},{19,17},{4,6},{5,7... | collective-permute-start | bytes 368648 | tf_op jit(solution)/shard_map/ppermute | solution.py:638
  19.6 7.8 %collective-permute-start.2 = (bf16[2,48,640]{2,1,0:T(8,128)(2,1)}, bf16[2,48,640]{2,1,0:T(8,128)(2,1)S(1)}, u32[]{:S(2)}, u32[]{:S(2)}) collective-permute-start(bf16[2,48,640]{2,1,0:T(8,128)(2,1)} %get-tuple-element.63), channel_id=1, source_target_pairs={{0,3},{1,2},{2,1},{3,0},{16,19},{17,18},{18,17},{19,16},{4,7},{5,6... | collective-permute-start | bytes 368648 | tf_op jit(solution)/shard_map/ppermute | solution.py:638
  19.7 9.0 %collective-permute-start.3 = (bf16[2,48,640]{2,1,0:T(8,128)(2,1)}, bf16[2,48,640]{2,1,0:T(8,128)(2,1)S(1)}, u32[]{:S(2)}, u32[]{:S(2)}) collective-permute-start(bf16[2,48,640]{2,1,0:T(8,128)(2,1)} %get-tuple-element.64), channel_id=1, source_target_pairs={{0,16},{1,17},{2,18},{3,19},{16,0},{17,1},{18,2},{19,3},{4,20},{5,... | collective-permute-start | bytes 368648 | tf_op jit(solution)/shard_map/ppermute | solution.py:638
  21.5 11.3 %collective-permute-start.4 = (bf16[2,48,640]{2,1,0:T(8,128)(2,1)}, bf16[2,48,640]{2,1,0:T(8,128)(2,1)S(1)}, u32[]{:S(2)}, u32[]{:S(2)}) collective-permute-start(bf16[2,48,640]{2,1,0:T(8,128)(2,1)} %get-tuple-element.65), channel_id=1, source_target_pairs={{0,17},{1,16},{2,19},{3,18},{16,1},{17,0},{18,3},{19,2},{4,21},{5,... | collective-permute-start | bytes 368648 | tf_op jit(solution)/shard_map/ppermute | solution.py:638
  21.5 11.3 %collective-permute-start.5 = (bf16[2,48,640]{2,1,0:T(8,128)(2,1)}, bf16[2,48,640]{2,1,0:T(8,128)(2,1)S(1)}, u32[]{:S(2)}, u32[]{:S(2)}) collective-permute-start(bf16[2,48,640]{2,1,0:T(8,128)(2,1)} %get-tuple-element.66), channel_id=1, source_target_pairs={{0,18},{1,19},{2,16},{3,17},{16,2},{17,3},{18,0},{19,1},{4,22},{5,... | collective-permute-start | bytes 368648 | tf_op jit(solution)/shard_map/ppermute | solution.py:638
  24.1 8.7 %collective-permute-start.6 = (bf16[2,48,640]{2,1,0:T(8,128)(2,1)}, bf16[2,48,640]{2,1,0:T(8,128)(2,1)S(1)}, u32[]{:S(2)}, u32[]{:S(2)}) collective-permute-start(bf16[2,48,640]{2,1,0:T(8,128)(2,1)} %get-tuple-element.67), channel_id=1, source_target_pairs={{0,19},{1,18},{2,17},{3,16},{16,3},{17,2},{18,1},{19,0},{4,23},{5,... | collective-permute-start | bytes 368648 | tf_op jit(solution)/shard_map/ppermute | solution.py:638
  27.4 5.8 %collective-permute-start.7 = (f32[128,128]{1,0:T(8,128)S(1)}, f32[128,128]{1,0:T(8,128)S(1)}, u32[]{:S(2)}, u32[]{:S(2)}) collective-permute-start(f32[128,128]{1,0:T(8,128)S(1)} %get-tuple-element.78.refs_10_), channel_id=1, source_target_pairs={{1,0},{2,1},{3,2},{5,4},{6,5},{7,6},{9,8},{10,9},{11,10},{13,12},{... | collective-permute-start | bytes 196616 | tf_op jit(solution)/shard_map/ppermute | solution.py:665
  28.7 4.7 %collective-permute-start.8 = (f32[128,128]{1,0:T(8,128)S(1)}, f32[128,128]{1,0:T(8,128)S(1)}, u32[]{:S(2)}, u32[]{:S(2)}) collective-permute-start(f32[128,128]{1,0:T(8,128)S(1)} %get-tuple-element.79.refs_9_), channel_id=1, source_target_pairs={{0,1},{1,2},{2,3},{4,5},{5,6},{6,7},{8,9},{9,10},{10,11},{12,13},{... | collective-permute-start | bytes 196616 | tf_op jit(solution)/shard_map/ppermute | solution.py:666
  33.5 19.5 %collective-permute-start.9 = (bf16[2,48,640]{2,1,0:T(8,128)(2,1)S(1)}, bf16[2,48,640]{2,1,0:T(8,128)(2,1)S(1)}, u32[]{:S(2)}, u32[]{:S(2)}) collective-permute-start(bf16[2,48,640]{2,1,0:T(8,128)(2,1)S(1)} %copy-done.25), channel_id=1, source_target_pairs={{0,1},{1,0},{2,3},{3,2},{16,17},{17,16},{18,19},{19,18},{4,5},{5,4... | collective-permute-start | bytes 368648 | tf_op jit(solution)/shard_map/ppermute | solution.py:638
  35.6 18.7 %collective-permute-start.10 = (bf16[2,48,640]{2,1,0:T(8,128)(2,1)S(1)}, bf16[2,48,640]{2,1,0:T(8,128)(2,1)S(1)}, u32[]{:S(2)}, u32[]{:S(2)}) collective-permute-start(bf16[2,48,640]{2,1,0:T(8,128)(2,1)S(1)} %copy-done.24), channel_id=1, source_target_pairs={{0,2},{1,3},{2,0},{3,1},{16,18},{17,19},{18,16},{19,17},{4,6},{5,7... | collective-permute-start | bytes 368648 | tf_op jit(solution)/shard_map/ppermute | solution.py:638
  38.0 16.4 %copy-start.19 = (bf16[2,48,640]{2,1,0:T(8,128)(2,1)S(1)}, bf16[2,48,640]{2,1,0:T(8,128)(2,1)}, u32[]{:S(2)}) copy-start(bf16[2,48,640]{2,1,0:T(8,128)(2,1)} %get-tuple-element.87) | copy-start | bytes 368644
  38.0 24.7 %copy-start.6 = (bf16[2,48,640]{2,1,0:T(8,128)(2,1)S(1)}, bf16[2,48,640]{2,1,0:T(8,128)(2,1)}, u32[]{:S(2)}) copy-start(bf16[2,48,640]{2,1,0:T(8,128)(2,1)} %get-tuple-element.92.refs_0_) | copy-start | bytes 368644
  38.1 34.2 %copy-start.8 = (f32[192,128]{1,0:T(8,128)}, f32[192,128]{1,0:T(8,128)S(1)}, u32[]{:S(2)}) copy-start(f32[192,128]{1,0:T(8,128)S(1)} %get-tuple-element.90.refs_8_) | copy-start | bytes 294916
  38.1 34.2 %copy-start.9 = (f32[192,128]{1,0:T(8,128)}, f32[192,128]{1,0:T(8,128)S(1)}, u32[]{:S(2)}) copy-start(f32[192,128]{1,0:T(8,128)S(1)} %get-tuple-element.91.refs_7_) | copy-start | bytes 294916
  38.1 6.9 %collective-permute-start.16 = (f32[192,128]{1,0:T(8,128)S(1)}, f32[192,128]{1,0:T(8,128)S(1)}, u32[]{:S(2)}, u32[]{:S(2)}) collective-permute-start(f32[192,128]{1,0:T(8,128)S(1)} %get-tuple-element.90.refs_8_), channel_id=1, source_target_pairs={{4,0},{8,4},{12,8},{16,12},{20,16},{24,20},{28,24},{5,1},{9,5},{13... | collective-permute-start | bytes 294920 | tf_op jit(solution)/shard_map/ppermute | solution.py:674
  39.6 40.1 %copy-start.18 = (s32[640]{0:T(1024)S(1)}, s32[640]{0:T(1024)}, u32[]{:S(2)}) copy-start(s32[640]{0:T(1024)} %src.1) | copy-start | bytes 7684
  39.6 8.3 %collective-permute-start.17 = (f32[192,128]{1,0:T(8,128)S(1)}, f32[192,128]{1,0:T(8,128)S(1)}, u32[]{:S(2)}, u32[]{:S(2)}) collective-permute-start(f32[192,128]{1,0:T(8,128)S(1)} %get-tuple-element.91.refs_7_), channel_id=1, source_target_pairs={{0,4},{4,8},{8,12},{12,16},{16,20},{20,24},{24,28},{1,5},{5,9},{9,... | collective-permute-start | bytes 294920 | tf_op jit(solution)/shard_map/ppermute | solution.py:675
  44.1 12.8 %collective-permute-start.11 = (bf16[2,48,640]{2,1,0:T(8,128)(2,1)S(1)}, bf16[2,48,640]{2,1,0:T(8,128)(2,1)S(1)}, u32[]{:S(2)}, u32[]{:S(2)}) collective-permute-start(bf16[2,48,640]{2,1,0:T(8,128)(2,1)S(1)} %copy-done.23), channel_id=1, source_target_pairs={{0,3},{1,2},{2,1},{3,0},{16,19},{17,18},{18,17},{19,16},{4,7},{5,6... | collective-permute-start | bytes 368648 | tf_op jit(solution)/shard_map/ppermute | solution.py:638
  45.0 27.3 %copy-start.16 = (f32[192,128]{1,0:T(8,128)}, f32[192,128]{1,0:T(8,128)S(1)}, u32[]{:S(2)}) copy-start(f32[192,128]{1,0:T(8,128)S(1)} %collective-permute-done.16.refs_11_) | copy-start | bytes 294916
  45.0 11.9 %collective-permute-start.12 = (bf16[2,48,640]{2,1,0:T(8,128)(2,1)S(1)}, bf16[2,48,640]{2,1,0:T(8,128)(2,1)S(1)}, u32[]{:S(2)}, u32[]{:S(2)}) collective-permute-start(bf16[2,48,640]{2,1,0:T(8,128)(2,1)S(1)} %copy-done.22), channel_id=1, source_target_pairs={{0,16},{1,17},{2,18},{3,19},{16,0},{17,1},{18,2},{19,3},{4,20},{5,... | collective-permute-start | bytes 368648 | tf_op jit(solution)/shard_map/ppermute | solution.py:638
  47.9 24.5 %copy-start.17 = (f32[192,128]{1,0:T(8,128)}, f32[192,128]{1,0:T(8,128)S(1)}, u32[]{:S(2)}) copy-start(f32[192,128]{1,0:T(8,128)S(1)} %collective-permute-done.17.refs_12_) | copy-start | bytes 294916
  47.9 14.8 %collective-permute-start.13 = (bf16[2,48,640]{2,1,0:T(8,128)(2,1)S(1)}, bf16[2,48,640]{2,1,0:T(8,128)(2,1)S(1)}, u32[]{:S(2)}, u32[]{:S(2)}) collective-permute-start(bf16[2,48,640]{2,1,0:T(8,128)(2,1)S(1)} %copy-done.21), channel_id=1, source_target_pairs={{0,17},{1,16},{2,19},{3,18},{16,1},{17,0},{18,3},{19,2},{4,21},{5,... | collective-permute-start | bytes 368648 | tf_op jit(solution)/shard_map/ppermute | solution.py:638
  52.9 9.7 %collective-permute-start.14 = (bf16[2,48,640]{2,1,0:T(8,128)(2,1)S(1)}, bf16[2,48,640]{2,1,0:T(8,128)(2,1)S(1)}, u32[]{:S(2)}, u32[]{:S(2)}) collective-permute-start(bf16[2,48,640]{2,1,0:T(8,128)(2,1)S(1)} %copy-done.20), channel_id=1, source_target_pairs={{0,18},{1,19},{2,16},{3,17},{16,2},{17,3},{18,0},{19,1},{4,22},{5,... | collective-permute-start | bytes 368648 | tf_op jit(solution)/shard_map/ppermute | solution.py:638
  54.4 8.3 %collective-permute-start.15 = (bf16[2,48,640]{2,1,0:T(8,128)(2,1)S(1)}, bf16[2,48,640]{2,1,0:T(8,128)(2,1)S(1)}, u32[]{:S(2)}, u32[]{:S(2)}) collective-permute-start(bf16[2,48,640]{2,1,0:T(8,128)(2,1)S(1)} %copy-done.19), channel_id=1, source_target_pairs={{0,19},{1,18},{2,17},{3,16},{16,3},{17,2},{18,1},{19,0},{4,23},{5,... | collective-permute-start | bytes 368648 | tf_op jit(solution)/shard_map/ppermute | solution.py:638
  56.9 11.8 %collective-permute-start.19 = (bf16[136,640]{1,0:T(8,128)(2,1)S(1)}, bf16[136,640]{1,0:T(8,128)(2,1)S(1)}, u32[]{:S(2)}, u32[]{:S(2)}) collective-permute-start(bf16[136,640]{1,0:T(8,128)(2,1)S(1)} %get-tuple-element.102), channel_id=1, source_target_pairs={{0,8},{4,12},{8,0},{12,4},{1,9},{5,13},{9,1},{13,5},{2,10},{6,14},... | collective-permute-start | bytes 522248 | tf_op jit(solution)/shard_map/ppermute | solution.py:638
  56.9 11.8 %collective-permute-start.20 = (bf16[136,640]{1,0:T(8,128)(2,1)S(1)}, bf16[136,640]{1,0:T(8,128)(2,1)S(1)}, u32[]{:S(2)}, u32[]{:S(2)}) collective-permute-start(bf16[136,640]{1,0:T(8,128)(2,1)S(1)} %get-tuple-element.103), channel_id=1, source_target_pairs={{0,12},{4,8},{8,4},{12,0},{1,13},{5,9},{9,5},{13,1},{2,14},{6,10},... | collective-permute-start | bytes 522248 | tf_op jit(solution)/shard_map/ppermute | solution.py:638
  63.1 9.2 %collective-permute-start.18 = (bf16[136,640]{1,0:T(8,128)(2,1)S(1)}, bf16[136,640]{1,0:T(8,128)(2,1)S(1)}, u32[]{:S(2)}, u32[]{:S(2)}) collective-permute-start(bf16[136,640]{1,0:T(8,128)(2,1)S(1)} %get-tuple-element.101), channel_id=1, source_target_pairs={{0,4},{4,0},{8,12},{12,8},{1,5},{5,1},{9,13},{13,9},{2,6},{6,2},{1... | collective-permute-start | bytes 522248 | tf_op jit(solution)/shard_map/ppermute | solution.py:638
  76.6 16.7 %all-to-all-start = ((bf16[32,40,128]{2,1,0:T(8,128)(2,1)}), bf16[32,40,128]{2,1,0:T(8,128)(2,1)S(1)}, u32[]{:S(2)}, u32[]{:S(2)}) async-start(bf16[32,40,128]{2,1,0:T(8,128)(2,1)} %get-tuple-element.117), calls=%async_computation | async-start | bytes 655360 | tf_op jit(solution)/shard_map/all_to_all | solution.py:687
  (16 other events, 108.8 us)

commit v5 on v4

--- a/solution.py
+++ b/solution.py
@@ -164,11 +164,8 @@
 
     lax.fori_loop(0, devices // group, owners, 0)
 
-    half = n_gx // 2
-    planes = n_sec * n_gy
-    for m in range(planes):
-        sends[m][...] = xs[m * n_gx + half : (m + 1) * n_gx].astype(BF16)
-        sends[planes + m][...] = xs[m * n_gx : m * n_gx + half].astype(BF16)
+    for m, send in enumerate(sends):
+        send[...] = xs[m * n_gx : (m + 1) * n_gx].astype(BF16)
 
 
 def forward(flux, w, src, own, dst, grid, cap, parts=20):
@@ -181,7 +178,7 @@
     return pl.pallas_call(
         functools.partial(forward_kernel, parts, cap, grid),
         in_specs=[SMEM, SMEM, SMEM, VMEM, ANY],
-        out_specs=[VMEM] * (2 * n_sec * n_gy) + [SMEM],
+        out_specs=[VMEM] * (n_sec * n_gy) + [SMEM],
         scratch_shapes=[
             pltpu.VMEM(w.shape, BF16),
             pltpu.VMEM(flux.shape, BF16),
@@ -192,7 +189,7 @@
             pltpu.SMEM((devices,), jnp.int32),
             pltpu.SemaphoreType.DMA((parts,)),
         ],
-        out_shape=[jax.ShapeDtypeStruct((n_gx // 2, chunk, wide), BF16)] * (2 * n_sec * n_gy) + [jax.ShapeDtypeStruct((total,), jnp.int32)],
+        out_shape=[jax.ShapeDtypeStruct((n_gx, chunk, wide), BF16)] * (n_sec * n_gy) + [jax.ShapeDtypeStruct((total,), jnp.int32)],
         compiler_params=kernel_params(58),
         cost_estimate=pl.CostEstimate(flops=2 * total * 8 * width * width, bytes_accessed=total * width * width * 2, transcendentals=0),
         name="forward_remap",
@@ -648,14 +645,7 @@
 
     *sends, slots = forward(atm_flux, remap_weights, remap_src, remap_owner.reshape(total), remap_dst, grid, cap)
     chunk = sends[0].shape[1]
-    far_sends, near_sends = sends[:planes], sends[planes:]
-
-    def in_plane(chunks):
-        return [chunks[0]] + [swapped(chunks[m], ("sec", "gy"), planes, m) for m in range(1, planes)]
-
-    def merge(chunks, dtypes):
-        outs = [((height + 8, wide), dtype) for dtype in dtypes]
-        return kernel(functools.partial(merge_kernel, planes), outs, "merge", 24, 1 << 22)(*chunks)
+    got = [sends[0]] + [swapped(sends[m], ("sec", "gy"), planes, m) for m in range(1, planes)]
 
     side = (width, width)
     end = (7 * levels + 80, width)
@@ -665,17 +655,15 @@
     from_e = lax.ppermute(own_w, "gy", to_west)
     from_w = lax.ppermute(own_e, "gy", to_east)
 
-    far = merge(in_plane(far_sends), [BF16] * (n_gx // 2))
-    far, near_sends, from_e, from_w = lax.optimization_barrier((far, near_sends, from_e, from_w))
-    far = [swapped(part, "gx", n_gx, n_gx // 2 + m) for m, part in enumerate(far)]
     own_s, own_n = kernel(rows_kernel, [(end, F32)] * 2, "edge_rows", 16, 1 << 20)(
         tracers.reshape(-1, width), currents.reshape(-1, width), land_sea, from_w, from_e
     )
     from_n = lax.ppermute(own_s, NORTH, to_south)
     from_s = lax.ppermute(own_n, NORTH, to_north)
-    near, from_n, from_s = lax.optimization_barrier((in_plane(near_sends), from_n, from_s))
-    near = merge(near, [F32] + [BF16] * (n_gx // 2 - 1))
-    parts = [near[0]] + [swapped(near[m], "gx", n_gx, m) for m in range(1, n_gx // 2)] + far
+    got, from_n, from_s = lax.optimization_barrier((got, from_n, from_s))
+    part = (height + 8, wide)
+    merged = kernel(functools.partial(merge_kernel, planes), [(part, F32)] + [(part, BF16)] * (n_gx - 1), "merge", 24, 1 << 22)(*got)
+    parts = [merged[0]] + [swapped(merged[m], "gx", n_gx, m) for m in range(1, n_gx)]
 
     back, flux, rim, *edges = kernel(
         functools.partial(surface_kernel, grid, chunk, levels),

time: 104 us -> 111 us (1.067)
  waiting for transfers between devices: 8.99 us -> 31.4 us
  starting transfers between devices: 45.6 us -> 30.1 us
    ppermute x17 -> x10, waiting for transfers between devices: 7.94 us -> 28.8 us  [swapped(): return lax.ppermute(array, axes, [(i, i ^ step) for i in range(count)])]
    ppermute x17 -> x10, starting transfers between devices: 31.4 us -> 17.5 us  [swapped(): return lax.ppermute(array, axes, [(i, i ^ step) for i in range(count)])]
    ppermute x1, waiting for transfers between devices: 0.01 us -> 1.83 us  [on_device(): from_e = lax.ppermute(own_w, 'gy', to_west)]
    ppermute x1, starting transfers between devices: 3.84 us -> 2.07 us  [on_device(): from_w = lax.ppermute(own_e, 'gy', to_east)]
    all_to_all x1, starting transfers between devices: 3.11 us -> 4.52 us  [on_device(): lax.all_to_all(back, EVERY, split_axis=0, concat_axis=0, tiled=True)]
  transfers between devices with their start and end apart: 22 -> 15, of which waited for: 5 -> 6; matrix products, arithmetic and copies ran while one was open for 2% -> 2% of each run, Pallas kernels for 15% -> 13%
where the time goes in v5:
time: 111 us
  Pallas kernels  43 us (39%)
  waiting for transfers between devices  31.4 us (28%)
  starting transfers between devices  30.1 us (27%)
  local copies, waits for them, and re-layouts  3.95 us (4%)
  other arithmetic  1.29 us (1%)
    ppermute x10, waiting for transfers between devices, swapped(): return lax.ppermute(array, axes, [(i, i ^ step) for i in range(count)])  28.8 us
    ppermute x10, starting transfers between devices, swapped(): return lax.ppermute(array, axes, [(i, i ^ step) for i in range(count)])  17.5 us
    pallas_call x1, Pallas kernels, forward(): pl.pallas_call(functools.partial(forward_kernel, parts, cap, grid), in_sp...  14.6 us
    pallas_call x1, Pallas kernels, on_device(): kernel(stencil_kernel, [(tracers.shape, F32)], 'substeps', 58, 1 << 24, [...  13.1 us
    pallas_call x1, Pallas kernels, backward(): pl.pallas_call(functools.partial(backward_kernel, parts), in_specs=[SMEM,...  9.27 us
    all_to_all x1, starting transfers between devices, on_device(): lax.all_to_all(back, EVERY, split_axis=0, concat_axis=0, tiled=True)  4.52 us
    pallas_call x1, Pallas kernels, on_device(): kernel(functools.partial(surface_kernel, grid, chunk, levels), [((planes...  3.64 us
    ppermute x1, starting transfers between devices, on_device(): from_s = lax.ppermute(own_n, NORTH, to_north)  3.48 us
  transfers between devices with their start and end apart: 15, of which 6 were waited for; matrix products, arithmetic and copies ran while one was open for 2% of the time, Pallas kernels for 13%

profile of v5, /device:TPU:0, one launch (start us, length us, event | category | flops | bytes accessed | tf_op | source)
XLA Modules:
  0.0 110.7 jit_solution(459187496923623233)
XLA Ops:
  0.6 1.3 %reduce.own = s32[640]{0:T(1024)} reduce(s32[640,1]{0,1:T(1,128)} %param.12, s32[]{:T(128)} %constant), dimensions={1}, to_apply=%param.12.reduce_sub_computation | reduce | bytes 5124 | tf_op args[4]
  1.9 14.6 %forward_remap.1 = (bf16[4,48,640]{2,1,0:T(8,128)(2,1)}, bf16[4,48,640]{2,1,0:T(8,128)(2,1)}, bf16[4,48,640]{2,1,0:T(8,128)(2,1)}, bf16[4,48,640]{2,1,0:T(8,128)...) custom-call(s32[640]{0:T(1024)} %src.1, ...), custom_call_target="tpu_custom_call" | custom-call | flops 167772160 | bytes 20971520 | tf_op jit(solution)/shard_map/forward_remap/pallas_call | solution.py:178
  16.6 0.5 collective-permute-start
  17.1 2.6 %collective-permute-start.1 = (bf16[4,48,640]{2,1,0:T(8,128)(2,1)}, bf16[4,48,640]{2,1,0:T(8,128)(2,1)S(1)}, u32[]{:S(2)}, u32[]{:S(2)}) collective-permute-start(bf16[4,48,640]{2,1,0:T(8,128)(2,1)} %get-tuple-element.42), channel_id=1, source_target_pairs={{0,2},{1,3},{2,0},{3,1},{16,18},{17,19},{18,16},{19,17},{4,6},{5,7... | collective-permute-start | bytes 737288 | tf_op jit(solution)/shard_map/ppermute | solution.py:635
  19.7 1.6 %edge_columns.1 = (f32[128,128]{1,0:T(8,128)S(1)}, f32[128,128]{1,0:T(8,128)S(1)}) custom-call(f32[2,16,128,128]{3,2,1,0:T(8,128)S(1)} %copy-done.1, f32[2,16,128,128]{3,2,1,0:T(8,128)S(1)} %copy-done, s32[128,128]{1,0:T(8,128)S(1)} %copy-done.2), custom_call_target="tpu_custom_call" | custom-call | flops 4194304 | bytes 4194304 | tf_op jit(solution)/shard_map/edge_columns/pallas_call | solution.py:652
  21.3 2.1 %collective-permute-start.7 = (f32[128,128]{1,0:T(8,128)S(1)}, f32[128,128]{1,0:T(8,128)S(1)}, u32[]{:S(2)}, u32[]{:S(2)}) collective-permute-start(f32[128,128]{1,0:T(8,128)S(1)} %get-tuple-element.48.refs_9_), channel_id=1, source_target_pairs={{0,1},{1,2},{2,3},{4,5},{5,6},{6,7},{8,9},{9,10},{10,11},{12,13},{... | collective-permute-start | bytes 196616 | tf_op jit(solution)/shard_map/ppermute | solution.py:656
  23.4 1.3 %collective-permute-start.8 = (f32[128,128]{1,0:T(8,128)S(1)}, f32[128,128]{1,0:T(8,128)S(1)}, u32[]{:S(2)}, u32[]{:S(2)}) collective-permute-start(f32[128,128]{1,0:T(8,128)S(1)} %get-tuple-element.49.refs_10_), channel_id=1, source_target_pairs={{1,0},{2,1},{3,2},{5,4},{6,5},{7,6},{9,8},{10,9},{11,10},{13,12},{... | collective-permute-start | bytes 196616 | tf_op jit(solution)/shard_map/ppermute | solution.py:655
  24.7 1.8 %collective-permute-done.8.from_east.refs_13_ = f32[128,128]{1,0:T(8,128)S(1)} collective-permute-done((f32[128,128]{1,0:T(8,128)S(1)}, f32[128,128]{1,0:T(8,128)S(1)}, u32[]{:S(2)}, u32[]{:S(2)}) %collective-permute-start.8) | collective-permute-done | bytes 65568 | tf_op jit(solution)/shard_map/ppermute | solution.py:655
  26.7 0.5 copy-done.5
  27.2 3.5 %collective-permute-start.10 = (f32[192,128]{1,0:T(8,128)S(1)}, f32[192,128]{1,0:T(8,128)S(1)}, u32[]{:S(2)}, u32[]{:S(2)}) collective-permute-start(f32[192,128]{1,0:T(8,128)S(1)} %get-tuple-element.51.refs_7_), channel_id=1, source_target_pairs={{0,4},{4,8},{8,12},{12,16},{16,20},{20,24},{24,28},{1,5},{5,9},{9,... | collective-permute-start | bytes 294920 | tf_op jit(solution)/shard_map/ppermute | solution.py:662
  30.7 1.3 %collective-permute-start.9 = (f32[192,128]{1,0:T(8,128)S(1)}, f32[192,128]{1,0:T(8,128)S(1)}, u32[]{:S(2)}, u32[]{:S(2)}) collective-permute-start(f32[192,128]{1,0:T(8,128)S(1)} %get-tuple-element.50.refs_8_), channel_id=1, source_target_pairs={{4,0},{8,4},{12,8},{16,12},{20,16},{24,20},{28,24},{5,1},{9,5},{13... | collective-permute-start | bytes 294920 | tf_op jit(solution)/shard_map/ppermute | solution.py:661
  32.1 0.8 collective-permute-done.10.refs_12_
  32.9 5.1 %collective-permute-start.3 = (bf16[4,48,640]{2,1,0:T(8,128)(2,1)S(1)}, bf16[4,48,640]{2,1,0:T(8,128)(2,1)S(1)}, u32[]{:S(2)}, u32[]{:S(2)}) collective-permute-start(bf16[4,48,640]{2,1,0:T(8,128)(2,1)S(1)} %copy-done.21), channel_id=1, source_target_pairs={{0,16},{1,17},{2,18},{3,19},{16,0},{17,1},{18,2},{19,3},{4,20},{5,... | collective-permute-start | bytes 737288 | tf_op jit(solution)/shard_map/ppermute | solution.py:635
  37.9 2.9 %collective-permute-start.4 = (bf16[4,48,640]{2,1,0:T(8,128)(2,1)S(1)}, bf16[4,48,640]{2,1,0:T(8,128)(2,1)S(1)}, u32[]{:S(2)}, u32[]{:S(2)}) collective-permute-start(bf16[4,48,640]{2,1,0:T(8,128)(2,1)S(1)} %copy-done.20), channel_id=1, source_target_pairs={{0,17},{1,16},{2,19},{3,18},{16,1},{17,0},{18,3},{19,2},{4,21},{5,... | collective-permute-start | bytes 737288 | tf_op jit(solution)/shard_map/ppermute | solution.py:635
  40.8 0.9 collective-permute-start.5
  41.7 1.0 collective-permute-start.6
  42.7 10.5 %collective-permute-done.3.refs_4_ = bf16[4,48,640]{2,1,0:T(8,128)(2,1)S(1)} collective-permute-done((bf16[4,48,640]{2,1,0:T(8,128)(2,1)S(1)}, bf16[4,48,640]{2,1,0:T(8,128)(2,1)S(1)}, u32[]{:S(2)}, u32[]{:S(2)}) %collective-permute-start.3) | collective-permute-done | bytes 245792 | tf_op jit(solution)/shard_map/ppermute | solution.py:635
  53.3 7.3 %collective-permute-done.4.refs_5_ = bf16[4,48,640]{2,1,0:T(8,128)(2,1)S(1)} collective-permute-done((bf16[4,48,640]{2,1,0:T(8,128)(2,1)S(1)}, bf16[4,48,640]{2,1,0:T(8,128)(2,1)S(1)}, u32[]{:S(2)}, u32[]{:S(2)}) %collective-permute-start.4) | collective-permute-done | bytes 245792 | tf_op jit(solution)/shard_map/ppermute | solution.py:635
  60.6 0.6 merge.1
  61.3 4.0 %collective-permute-start.12 = (bf16[136,640]{1,0:T(8,128)(2,1)S(1)}, bf16[136,640]{1,0:T(8,128)(2,1)S(1)}, u32[]{:S(2)}, u32[]{:S(2)}) collective-permute-start(bf16[136,640]{1,0:T(8,128)(2,1)S(1)} %get-tuple-element.62), channel_id=1, source_target_pairs={{0,8},{4,12},{8,0},{12,4},{1,9},{5,13},{9,1},{13,5},{2,10},{6,14},... | collective-permute-start | bytes 522248 | tf_op jit(solution)/shard_map/ppermute | solution.py:635
  65.3 0.3 collective-permute-start.13
  65.7 0.7 slice.7.refs_5_
  66.4 0.7 slice.6.refs_4_
  67.1 3.3 %collective-permute-done.11.refs_1_ = bf16[136,640]{1,0:T(8,128)(2,1)S(1)} collective-permute-done((bf16[136,640]{1,0:T(8,128)(2,1)S(1)}, bf16[136,640]{1,0:T(8,128)(2,1)S(1)}, u32[]{:S(2)}, u32[]{:S(2)}) %collective-permute-start.11) | collective-permute-done | bytes 174112 | tf_op jit(solution)/shard_map/ppermute | solution.py:635
  70.4 7.7 %collective-permute-done.12.refs_2_ = bf16[136,640]{1,0:T(8,128)(2,1)S(1)} collective-permute-done((bf16[136,640]{1,0:T(8,128)(2,1)S(1)}, bf16[136,640]{1,0:T(8,128)(2,1)S(1)}, u32[]{:S(2)}, u32[]{:S(2)}) %collective-permute-start.12) | collective-permute-done | bytes 174112 | tf_op jit(solution)/shard_map/ppermute | solution.py:635
  78.1 0.6 copy-done.13
  78.8 3.6 %surface.1 = (bf16[32,40,128]{2,1,0:T(8,128)(2,1)}, f32[5,128,128]{2,1,0:T(8,128)}, f32[8,640]{1,0:T(8,128)}, f32[192,128]{1,0:T(8,128)}, f32[192,128]{1,0:T(8,1...) custom-call(f32[136,640]{1,0:T(8,128)} %copy-done.3, ...), custom_call_target="tpu_custom_call" | custom-call | flops 4194304 | bytes 4194304 | tf_op jit(solution)/shard_map/surface/pallas_call | solution.py:668
  82.4 4.5 %all-to-all-start = ((bf16[32,40,128]{2,1,0:T(8,128)(2,1)}), bf16[32,40,128]{2,1,0:T(8,128)(2,1)S(1)}, u32[]{:S(2)}, u32[]{:S(2)}) async-start(bf16[32,40,128]{2,1,0:T(8,128)(2,1)} %get-tuple-element.77), calls=%async_computation | async-start | bytes 655360 | tf_op jit(solution)/shard_map/all_to_all | solution.py:675
  87.0 0.6 reshape.19.src
  87.6 13.1 %substeps.1 = f32[2,16,128,128]{3,2,1,0:T(8,128)} custom-call(f32[2,16,128,128]{3,2,1,0:T(8,128)} %tracers.3, f32[2,16,128,128]{3,2,1,0:T(8,128)} %currents.3, s32[128,128]{1,0:T(8,128)} %land.5, f32[5,128,128]{2,1,0:T(8,128)} %get-tuple-element.66.flux, f32[8,640]{1,0:T(8,128)} %get-tuple-element.67.rim, f32[192,128]{1,0:T(8,128)} %get-tuple-element.68.in_n, ...), custom_call_target="tpu_custom_call" | custom-call | flops 16777216 | bytes 16777216 | tf_op jit(solution)/shard_map/substeps/pallas_call | solution.py:678
  100.7 0.7 copy-done.11
  101.4 9.3 %backward_remap.1 = f32[160,128]{1,0:T(8,128)} custom-call(s32[640]{0:T(1024)} %get-tuple-element.76.slots, s32[1,640]{1,0:T(1,128)} %reshape.19.src, bf16[32,40,128]{2,1,0:T(8,128)(2,1)} %copy-done.11, bf16[640,128,128]{2,1,0:T(8,128)(2,1)} %w.3), custom_call_target="tpu_custom_call" | custom-call | flops 167772160 | bytes 20971520 | tf_op jit(solution)/shard_map/backward_remap/pallas_call | solution.py:599
  (55 shorter events, 0.4 us)
Async XLA Ops:
  1.9 17.7 %copy-start = (f32[2,16,128,128]{3,2,1,0:T(8,128)S(1)}, f32[2,16,128,128]{3,2,1,0:T(8,128)}, u32[]{:S(2)}) copy-start(f32[2,16,128,128]{3,2,1,0:T(8,128)} %currents.3) | copy-start | bytes 6291460
  1.9 17.7 %copy-start.1 = (f32[2,16,128,128]{3,2,1,0:T(8,128)S(1)}, f32[2,16,128,128]{3,2,1,0:T(8,128)}, u32[]{:S(2)}) copy-start(f32[2,16,128,128]{3,2,1,0:T(8,128)} %tracers.3) | copy-start | bytes 6291460
  1.9 17.7 %copy-start.2 = (s32[128,128]{1,0:T(8,128)S(1)}, s32[128,128]{1,0:T(8,128)}, u32[]{:S(2)}) copy-start(s32[128,128]{1,0:T(8,128)} %land.5) | copy-start | bytes 196612
  16.6 24.3 %collective-permute-start = (bf16[4,48,640]{2,1,0:T(8,128)(2,1)}, bf16[4,48,640]{2,1,0:T(8,128)(2,1)S(1)}, u32[]{:S(2)}, u32[]{:S(2)}) collective-permute-start(bf16[4,48,640]{2,1,0:T(8,128)(2,1)} %get-tuple-element.41), channel_id=1, source_target_pairs={{0,1},{1,0},{2,3},{3,2},{16,17},{17,16},{18,19},{19,18},{4,5},{5,4... | collective-permute-start | bytes 737288 | tf_op jit(solution)/shard_map/ppermute | solution.py:635
  17.1 24.6 %collective-permute-start.1 = (bf16[4,48,640]{2,1,0:T(8,128)(2,1)}, bf16[4,48,640]{2,1,0:T(8,128)(2,1)S(1)}, u32[]{:S(2)}, u32[]{:S(2)}) collective-permute-start(bf16[4,48,640]{2,1,0:T(8,128)(2,1)} %get-tuple-element.42), channel_id=1, source_target_pairs={{0,2},{1,3},{2,0},{3,1},{16,18},{17,19},{18,16},{19,17},{4,6},{5,7... | collective-permute-start | bytes 737288 | tf_op jit(solution)/shard_map/ppermute | solution.py:635
  21.3 5.4 %copy-start.9 = (f32[128,128]{1,0:T(8,128)}, f32[128,128]{1,0:T(8,128)S(1)}, u32[]{:S(2)}) copy-start(f32[128,128]{1,0:T(8,128)S(1)} %get-tuple-element.49.refs_10_) | copy-start | bytes 196612
  21.3 3.4 %collective-permute-start.7 = (f32[128,128]{1,0:T(8,128)S(1)}, f32[128,128]{1,0:T(8,128)S(1)}, u32[]{:S(2)}, u32[]{:S(2)}) collective-permute-start(f32[128,128]{1,0:T(8,128)S(1)} %get-tuple-element.48.refs_9_), channel_id=1, source_target_pairs={{0,1},{1,2},{2,3},{4,5},{5,6},{6,7},{8,9},{9,10},{10,11},{12,13},{... | collective-permute-start | bytes 196616 | tf_op jit(solution)/shard_map/ppermute | solution.py:656
  23.4 3.1 %collective-permute-start.8 = (f32[128,128]{1,0:T(8,128)S(1)}, f32[128,128]{1,0:T(8,128)S(1)}, u32[]{:S(2)}, u32[]{:S(2)}) collective-permute-start(f32[128,128]{1,0:T(8,128)S(1)} %get-tuple-element.49.refs_10_), channel_id=1, source_target_pairs={{1,0},{2,1},{3,2},{5,4},{6,5},{7,6},{9,8},{10,9},{11,10},{13,12},{... | collective-permute-start | bytes 196616 | tf_op jit(solution)/shard_map/ppermute | solution.py:655
  26.6 5.4 %copy-start.22 = (bf16[4,48,640]{2,1,0:T(8,128)(2,1)S(1)}, bf16[4,48,640]{2,1,0:T(8,128)(2,1)}, u32[]{:S(2)}) copy-start(bf16[4,48,640]{2,1,0:T(8,128)(2,1)} %get-tuple-element.43) | copy-start | bytes 737284
  26.6 6.3 %copy-start.21 = (bf16[4,48,640]{2,1,0:T(8,128)(2,1)S(1)}, bf16[4,48,640]{2,1,0:T(8,128)(2,1)}, u32[]{:S(2)}) copy-start(bf16[4,48,640]{2,1,0:T(8,128)(2,1)} %get-tuple-element.44) | copy-start | bytes 737284
  26.6 11.4 %copy-start.20 = (bf16[4,48,640]{2,1,0:T(8,128)(2,1)S(1)}, bf16[4,48,640]{2,1,0:T(8,128)(2,1)}, u32[]{:S(2)}) copy-start(bf16[4,48,640]{2,1,0:T(8,128)(2,1)} %get-tuple-element.45) | copy-start | bytes 737284
  26.6 14.3 %copy-start.19 = (bf16[4,48,640]{2,1,0:T(8,128)(2,1)S(1)}, bf16[4,48,640]{2,1,0:T(8,128)(2,1)}, u32[]{:S(2)}) copy-start(bf16[4,48,640]{2,1,0:T(8,128)(2,1)} %get-tuple-element.46) | copy-start | bytes 737284
  26.6 15.2 %copy-start.18 = (bf16[4,48,640]{2,1,0:T(8,128)(2,1)S(1)}, bf16[4,48,640]{2,1,0:T(8,128)(2,1)}, u32[]{:S(2)}) copy-start(bf16[4,48,640]{2,1,0:T(8,128)(2,1)} %get-tuple-element.47) | copy-start | bytes 737284
  26.6 34.0 %copy-start.6 = (bf16[4,48,640]{2,1,0:T(8,128)(2,1)S(1)}, bf16[4,48,640]{2,1,0:T(8,128)(2,1)}, u32[]{:S(2)}) copy-start(bf16[4,48,640]{2,1,0:T(8,128)(2,1)} %get-tuple-element.52.refs_0_) | copy-start | bytes 737284
  27.2 50.9 %copy-start.7 = (f32[192,128]{1,0:T(8,128)}, f32[192,128]{1,0:T(8,128)S(1)}, u32[]{:S(2)}) copy-start(f32[192,128]{1,0:T(8,128)S(1)} %get-tuple-element.50.refs_8_) | copy-start | bytes 294916
  27.2 50.9 %copy-start.8 = (f32[192,128]{1,0:T(8,128)}, f32[192,128]{1,0:T(8,128)S(1)}, u32[]{:S(2)}) copy-start(f32[192,128]{1,0:T(8,128)S(1)} %get-tuple-element.51.refs_7_) | copy-start | bytes 294916
  27.2 5.7 %collective-permute-start.10 = (f32[192,128]{1,0:T(8,128)S(1)}, f32[192,128]{1,0:T(8,128)S(1)}, u32[]{:S(2)}, u32[]{:S(2)}) collective-permute-start(f32[192,128]{1,0:T(8,128)S(1)} %get-tuple-element.51.refs_7_), channel_id=1, source_target_pairs={{0,4},{4,8},{8,12},{12,16},{16,20},{20,24},{24,28},{1,5},{5,9},{9,... | collective-permute-start | bytes 294920 | tf_op jit(solution)/shard_map/ppermute | solution.py:662
  30.7 7.3 %collective-permute-start.9 = (f32[192,128]{1,0:T(8,128)S(1)}, f32[192,128]{1,0:T(8,128)S(1)}, u32[]{:S(2)}, u32[]{:S(2)}) collective-permute-start(f32[192,128]{1,0:T(8,128)S(1)} %get-tuple-element.50.refs_8_), channel_id=1, source_target_pairs={{4,0},{8,4},{12,8},{16,12},{20,16},{24,20},{28,24},{5,1},{9,5},{13... | collective-permute-start | bytes 294920 | tf_op jit(solution)/shard_map/ppermute | solution.py:661
  32.0 10.8 %collective-permute-start.2 = (bf16[4,48,640]{2,1,0:T(8,128)(2,1)S(1)}, bf16[4,48,640]{2,1,0:T(8,128)(2,1)S(1)}, u32[]{:S(2)}, u32[]{:S(2)}) collective-permute-start(bf16[4,48,640]{2,1,0:T(8,128)(2,1)S(1)} %copy-done.22), channel_id=1, source_target_pairs={{0,3},{1,2},{2,1},{3,0},{16,19},{17,18},{18,17},{19,16},{4,7},{5,6... | collective-permute-start | bytes 737288 | tf_op jit(solution)/shard_map/ppermute | solution.py:635
  32.9 45.2 %copy-start.15 = (f32[192,128]{1,0:T(8,128)}, f32[192,128]{1,0:T(8,128)S(1)}, u32[]{:S(2)}) copy-start(f32[192,128]{1,0:T(8,128)S(1)} %collective-permute-done.10.refs_12_) | copy-start | bytes 294916
  32.9 20.4 %collective-permute-start.3 = (bf16[4,48,640]{2,1,0:T(8,128)(2,1)S(1)}, bf16[4,48,640]{2,1,0:T(8,128)(2,1)S(1)}, u32[]{:S(2)}, u32[]{:S(2)}) collective-permute-start(bf16[4,48,640]{2,1,0:T(8,128)(2,1)S(1)} %copy-done.21), channel_id=1, source_target_pairs={{0,16},{1,17},{2,18},{3,19},{16,0},{17,1},{18,2},{19,3},{4,20},{5,... | collective-permute-start | bytes 737288 | tf_op jit(solution)/shard_map/ppermute | solution.py:635
  37.9 40.2 %copy-start.16 = (f32[192,128]{1,0:T(8,128)}, f32[192,128]{1,0:T(8,128)S(1)}, u32[]{:S(2)}) copy-start(f32[192,128]{1,0:T(8,128)S(1)} %collective-permute-done.9.refs_11_) | copy-start | bytes 294916
  37.9 22.6 %collective-permute-start.4 = (bf16[4,48,640]{2,1,0:T(8,128)(2,1)S(1)}, bf16[4,48,640]{2,1,0:T(8,128)(2,1)S(1)}, u32[]{:S(2)}, u32[]{:S(2)}) collective-permute-start(bf16[4,48,640]{2,1,0:T(8,128)(2,1)S(1)} %copy-done.20), channel_id=1, source_target_pairs={{0,17},{1,16},{2,19},{3,18},{16,1},{17,0},{18,3},{19,2},{4,21},{5,... | collective-permute-start | bytes 737288 | tf_op jit(solution)/shard_map/ppermute | solution.py:635
  40.8 19.7 %collective-permute-start.5 = (bf16[4,48,640]{2,1,0:T(8,128)(2,1)S(1)}, bf16[4,48,640]{2,1,0:T(8,128)(2,1)S(1)}, u32[]{:S(2)}, u32[]{:S(2)}) collective-permute-start(bf16[4,48,640]{2,1,0:T(8,128)(2,1)S(1)} %copy-done.19), channel_id=1, source_target_pairs={{0,18},{1,19},{2,16},{3,17},{16,2},{17,3},{18,0},{19,1},{4,22},{5,... | collective-permute-start | bytes 737288 | tf_op jit(solution)/shard_map/ppermute | solution.py:635
  41.7 18.8 %collective-permute-start.6 = (bf16[4,48,640]{2,1,0:T(8,128)(2,1)S(1)}, bf16[4,48,640]{2,1,0:T(8,128)(2,1)S(1)}, u32[]{:S(2)}, u32[]{:S(2)}) collective-permute-start(bf16[4,48,640]{2,1,0:T(8,128)(2,1)S(1)} %copy-done.18), channel_id=1, source_target_pairs={{0,19},{1,18},{2,17},{3,16},{16,3},{17,2},{18,1},{19,0},{4,23},{5,... | collective-permute-start | bytes 737288 | tf_op jit(solution)/shard_map/ppermute | solution.py:635
  61.2 5.9 %copy-start.3 = (f32[136,640]{1,0:T(8,128)}, f32[136,640]{1,0:T(8,128)S(1)}, u32[]{:S(2)}) copy-start(f32[136,640]{1,0:T(8,128)S(1)} %get-tuple-element.60.refs_0_) | copy-start | bytes 1044484
  61.2 25.8 %copy-start.17 = (s32[640]{0:T(1024)S(1)}, s32[640]{0:T(1024)}, u32[]{:S(2)}) copy-start(s32[640]{0:T(1024)} %src.1) | copy-start | bytes 7684
  61.2 9.1 %collective-permute-start.11 = (bf16[136,640]{1,0:T(8,128)(2,1)S(1)}, bf16[136,640]{1,0:T(8,128)(2,1)S(1)}, u32[]{:S(2)}, u32[]{:S(2)}) collective-permute-start(bf16[136,640]{1,0:T(8,128)(2,1)S(1)} %get-tuple-element.61), channel_id=1, source_target_pairs={{0,4},{4,0},{8,12},{12,8},{1,5},{5,1},{9,13},{13,9},{2,6},{6,2},{1... | collective-permute-start | bytes 522248 | tf_op jit(solution)/shard_map/ppermute | solution.py:635
  61.3 16.8 %collective-permute-start.12 = (bf16[136,640]{1,0:T(8,128)(2,1)S(1)}, bf16[136,640]{1,0:T(8,128)(2,1)S(1)}, u32[]{:S(2)}, u32[]{:S(2)}) collective-permute-start(bf16[136,640]{1,0:T(8,128)(2,1)S(1)} %get-tuple-element.62), channel_id=1, source_target_pairs={{0,8},{4,12},{8,0},{12,4},{1,9},{5,13},{9,1},{13,5},{2,10},{6,14},... | collective-permute-start | bytes 522248 | tf_op jit(solution)/shard_map/ppermute | solution.py:635
  65.3 12.8 %collective-permute-start.13 = (bf16[136,640]{1,0:T(8,128)(2,1)S(1)}, bf16[136,640]{1,0:T(8,128)(2,1)S(1)}, u32[]{:S(2)}, u32[]{:S(2)}) collective-permute-start(bf16[136,640]{1,0:T(8,128)(2,1)S(1)} %get-tuple-element.63), channel_id=1, source_target_pairs={{0,12},{4,8},{8,4},{12,0},{1,13},{5,9},{9,5},{13,1},{2,14},{6,10},... | collective-permute-start | bytes 522248 | tf_op jit(solution)/shard_map/ppermute | solution.py:635
  70.4 7.8 %copy-start.12 = (bf16[136,640]{1,0:T(8,128)(2,1)}, bf16[136,640]{1,0:T(8,128)(2,1)S(1)}, u32[]{:S(2)}) copy-start(bf16[136,640]{1,0:T(8,128)(2,1)S(1)} %collective-permute-done.11.refs_1_) | copy-start | bytes 522244
  82.4 18.2 %all-to-all-start = ((bf16[32,40,128]{2,1,0:T(8,128)(2,1)}), bf16[32,40,128]{2,1,0:T(8,128)(2,1)S(1)}, u32[]{:S(2)}, u32[]{:S(2)}) async-start(bf16[32,40,128]{2,1,0:T(8,128)(2,1)} %get-tuple-element.77), calls=%async_computation | async-start | bytes 655360 | tf_op jit(solution)/shard_map/all_to_all | solution.py:675
  (6 other events, 10.1 us)

commit v6 on v5

--- a/solution.py
+++ b/solution.py
@@ -649,18 +649,19 @@
 
     side = (width, width)
     end = (7 * levels + 80, width)
-    own_w, own_e = kernel(columns_kernel, [(side, F32)] * 2, "edge_columns", 16, 1 << 22)(tracers, currents, land_sea)
+    got[1], planes_in, currents_in = lax.optimization_barrier((got[1], tracers, currents))
+    own_w, own_e = kernel(columns_kernel, [(side, F32)] * 2, "edge_columns", 16, 1 << 22)(planes_in, currents_in, land_sea)
     to_north, to_south = neighbours(NORTH)
     to_east, to_west = neighbours("gy")
     from_e = lax.ppermute(own_w, "gy", to_west)
     from_w = lax.ppermute(own_e, "gy", to_east)
 
+    got, from_e, from_w = lax.optimization_barrier((got, from_e, from_w))
     own_s, own_n = kernel(rows_kernel, [(end, F32)] * 2, "edge_rows", 16, 1 << 20)(
         tracers.reshape(-1, width), currents.reshape(-1, width), land_sea, from_w, from_e
     )
     from_n = lax.ppermute(own_s, NORTH, to_south)
     from_s = lax.ppermute(own_n, NORTH, to_north)
-    got, from_n, from_s = lax.optimization_barrier((got, from_n, from_s))
     part = (height + 8, wide)
     merged = kernel(functools.partial(merge_kernel, planes), [(part, F32)] + [(part, BF16)] * (n_gx - 1), "merge", 24, 1 << 22)(*got)
     parts = [merged[0]] + [swapped(merged[m], "gx", n_gx, m) for m in range(1, n_gx)]

time: 111 us -> 101 us (0.910)
  waiting for transfers between devices: 31.4 us -> 16.9 us
  starting transfers between devices: 30.1 us -> 35.3 us
    ppermute x10, waiting for transfers between devices: 28.8 us -> 13.2 us  [swapped(): return lax.ppermute(array, axes, [(i, i ^ step) for i in range(count)])]
    all_to_all x1, starting transfers between devices: 4.52 us -> 11.1 us  [on_device(): lax.all_to_all(back, EVERY, split_axis=0, concat_axis=0, tiled=True)]
    ppermute x10, starting transfers between devices: 17.5 us -> 13.8 us  [swapped(): return lax.ppermute(array, axes, [(i, i ^ step) for i in range(count)])]
    ppermute x1, waiting for transfers between devices: 0.8 us -> 3.56 us  [on_device(): from_s = lax.ppermute(own_n, NORTH, to_north)]
    ppermute x1, waiting for transfers between devices: 1.83 us -> 0.01 us  [on_device(): from_e = lax.ppermute(own_w, 'gy', to_west)]
  transfers between devices with their start and end apart: 15 -> 15, of which waited for: 6 -> 6; matrix products, arithmetic and copies ran while one was open for 2% -> 2% of each run, Pallas kernels for 13% -> 15%
where the time goes in v6:
time: 101 us
  Pallas kernels  43 us (43%)
  starting transfers between devices  35.3 us (35%)
  waiting for transfers between devices  16.9 us (17%)
  local copies, waits for them, and re-layouts  3.47 us (3%)
  other arithmetic  1.29 us (1%)
    pallas_call x1, Pallas kernels, forward(): pl.pallas_call(functools.partial(forward_kernel, parts, cap, grid), in_sp...  14.6 us
    ppermute x10, starting transfers between devices, swapped(): return lax.ppermute(array, axes, [(i, i ^ step) for i in range(count)])  13.8 us
    ppermute x10, waiting for transfers between devices, swapped(): return lax.ppermute(array, axes, [(i, i ^ step) for i in range(count)])  13.2 us
    pallas_call x1, Pallas kernels, on_device(): kernel(stencil_kernel, [(tracers.shape, F32)], 'substeps', 58, 1 << 24, [...  13 us
    all_to_all x1, starting transfers between devices, on_device(): lax.all_to_all(back, EVERY, split_axis=0, concat_axis=0, tiled=True)  11.1 us
    pallas_call x1, Pallas kernels, backward(): pl.pallas_call(functools.partial(backward_kernel, parts), in_specs=[SMEM,...  9.27 us
    ppermute x1, starting transfers between devices, on_device(): from_s = lax.ppermute(own_n, NORTH, to_north)  4.55 us
    pallas_call x1, Pallas kernels, on_device(): kernel(functools.partial(surface_kernel, grid, chunk, levels), [((planes...  3.68 us
  transfers between devices with their start and end apart: 15, of which 6 were waited for; matrix products, arithmetic and copies ran while one was open for 2% of the time, Pallas kernels for 15%

profile of v6, /device:TPU:0, one launch (start us, length us, event | category | flops | bytes accessed | tf_op | source)
XLA Modules:
  0.0 100.8 jit_solution(9658187127049857138)
XLA Ops:
  0.6 1.3 %reduce.own = s32[640]{0:T(1024)} reduce(s32[640,1]{0,1:T(1,128)} %param.12, s32[]{:T(128)} %constant), dimensions={1}, to_apply=%param.12.reduce_sub_computation | reduce | bytes 5124 | tf_op args[4]
  1.9 14.6 %forward_remap.1 = (bf16[4,48,640]{2,1,0:T(8,128)(2,1)}, bf16[4,48,640]{2,1,0:T(8,128)(2,1)}, bf16[4,48,640]{2,1,0:T(8,128)(2,1)}, bf16[4,48,640]{2,1,0:T(8,128)...) custom-call(s32[640]{0:T(1024)} %src.1, ...), custom_call_target="tpu_custom_call" | custom-call | flops 167772160 | bytes 20971520 | tf_op jit(solution)/shard_map/forward_remap/pallas_call | solution.py:178
  16.6 0.5 collective-permute-start
  17.1 2.6 %collective-permute-start.1 = (bf16[4,48,640]{2,1,0:T(8,128)(2,1)}, bf16[4,48,640]{2,1,0:T(8,128)(2,1)S(1)}, u32[]{:S(2)}, u32[]{:S(2)}) collective-permute-start(bf16[4,48,640]{2,1,0:T(8,128)(2,1)} %get-tuple-element.46), channel_id=1, source_target_pairs={{0,2},{1,3},{2,0},{3,1},{16,18},{17,19},{18,16},{19,17},{4,6},{5,7... | collective-permute-start | bytes 737288 | tf_op jit(solution)/shard_map/ppermute | solution.py:635
  19.6 0.1 collective-permute-start.2
  19.7 1.8 %collective-permute-start.3 = (bf16[4,48,640]{2,1,0:T(8,128)(2,1)}, bf16[4,48,640]{2,1,0:T(8,128)(2,1)S(1)}, u32[]{:S(2)}, u32[]{:S(2)}) collective-permute-start(bf16[4,48,640]{2,1,0:T(8,128)(2,1)} %get-tuple-element.48), channel_id=1, source_target_pairs={{0,16},{1,17},{2,18},{3,19},{16,0},{17,1},{18,2},{19,3},{4,20},{5,... | collective-permute-start | bytes 737288 | tf_op jit(solution)/shard_map/ppermute | solution.py:635
  21.5 2.6 %collective-permute-start.5 = (bf16[4,48,640]{2,1,0:T(8,128)(2,1)}, bf16[4,48,640]{2,1,0:T(8,128)(2,1)S(1)}, u32[]{:S(2)}, u32[]{:S(2)}) collective-permute-start(bf16[4,48,640]{2,1,0:T(8,128)(2,1)} %get-tuple-element.50), channel_id=1, source_target_pairs={{0,18},{1,19},{2,16},{3,17},{16,2},{17,3},{18,0},{19,1},{4,22},{5,... | collective-permute-start | bytes 737288 | tf_op jit(solution)/shard_map/ppermute | solution.py:635
  24.1 2.6 %collective-permute-done.1.refs_2_ = bf16[4,48,640]{2,1,0:T(8,128)(2,1)S(1)} collective-permute-done((bf16[4,48,640]{2,1,0:T(8,128)(2,1)}, bf16[4,48,640]{2,1,0:T(8,128)(2,1)S(1)}, u32[]{:S(2)}, u32[]{:S(2)}) %collective-permute-start.1) | collective-permute-done | bytes 245792 | tf_op jit(solution)/shard_map/ppermute | solution.py:635
  26.7 1.7 %collective-permute-start.6 = (bf16[4,48,640]{2,1,0:T(8,128)(2,1)}, bf16[4,48,640]{2,1,0:T(8,128)(2,1)S(1)}, u32[]{:S(2)}, u32[]{:S(2)}) collective-permute-start(bf16[4,48,640]{2,1,0:T(8,128)(2,1)} %get-tuple-element.51), channel_id=1, source_target_pairs={{0,19},{1,18},{2,17},{3,16},{16,3},{17,2},{18,1},{19,0},{4,23},{5,... | collective-permute-start | bytes 737288 | tf_op jit(solution)/shard_map/ppermute | solution.py:635
  28.4 1.6 %edge_columns.1 = (f32[128,128]{1,0:T(8,128)S(1)}, f32[128,128]{1,0:T(8,128)S(1)}) custom-call(f32[2,16,128,128]{3,2,1,0:T(8,128)S(1)} %copy-done.1, f32[2,16,128,128]{3,2,1,0:T(8,128)S(1)} %copy-done, s32[128,128]{1,0:T(8,128)S(1)} %copy-done.2), custom_call_target="tpu_custom_call" | custom-call | flops 4194304 | bytes 4194304 | tf_op jit(solution)/shard_map/edge_columns/pallas_call | solution.py:653
  30.1 1.4 %collective-permute-done.2.refs_3_ = bf16[4,48,640]{2,1,0:T(8,128)(2,1)S(1)} collective-permute-done((bf16[4,48,640]{2,1,0:T(8,128)(2,1)}, bf16[4,48,640]{2,1,0:T(8,128)(2,1)S(1)}, u32[]{:S(2)}, u32[]{:S(2)}) %collective-permute-start.2) | collective-permute-done | bytes 245792 | tf_op jit(solution)/shard_map/ppermute | solution.py:635
  31.5 1.3 %collective-permute-start.7 = (f32[128,128]{1,0:T(8,128)S(1)}, f32[128,128]{1,0:T(8,128)S(1)}, u32[]{:S(2)}, u32[]{:S(2)}) collective-permute-start(f32[128,128]{1,0:T(8,128)S(1)} %get-tuple-element.54.refs_10_), channel_id=1, source_target_pairs={{1,0},{2,1},{3,2},{5,4},{6,5},{7,6},{9,8},{10,9},{11,10},{13,12},{... | collective-permute-start | bytes 196616 | tf_op jit(solution)/shard_map/ppermute | solution.py:656
  32.8 3.1 %collective-permute-start.8 = (f32[128,128]{1,0:T(8,128)S(1)}, f32[128,128]{1,0:T(8,128)S(1)}, u32[]{:S(2)}, u32[]{:S(2)}) collective-permute-start(f32[128,128]{1,0:T(8,128)S(1)} %get-tuple-element.55.refs_9_), channel_id=1, source_target_pairs={{0,1},{1,2},{2,3},{4,5},{5,6},{6,7},{8,9},{9,10},{10,11},{12,13},{... | collective-permute-start | bytes 196616 | tf_op jit(solution)/shard_map/ppermute | solution.py:657
  35.9 7.4 %collective-permute-done.4.refs_5_ = bf16[4,48,640]{2,1,0:T(8,128)(2,1)S(1)} collective-permute-done((bf16[4,48,640]{2,1,0:T(8,128)(2,1)}, bf16[4,48,640]{2,1,0:T(8,128)(2,1)S(1)}, u32[]{:S(2)}, u32[]{:S(2)}) %collective-permute-start.4) | collective-permute-done | bytes 245792 | tf_op jit(solution)/shard_map/ppermute | solution.py:635
  43.4 0.6 merge.1
  44.0 1.9 %collective-permute-start.9 = (bf16[136,640]{1,0:T(8,128)(2,1)S(1)}, bf16[136,640]{1,0:T(8,128)(2,1)S(1)}, u32[]{:S(2)}, u32[]{:S(2)}) collective-permute-start(bf16[136,640]{1,0:T(8,128)(2,1)S(1)} %get-tuple-element.65), channel_id=1, source_target_pairs={{0,4},{4,0},{8,12},{12,8},{1,5},{5,1},{9,13},{13,9},{2,6},{6,2},{1... | collective-permute-start | bytes 522248 | tf_op jit(solution)/shard_map/ppermute | solution.py:635
  45.9 2.6 %collective-permute-start.10 = (bf16[136,640]{1,0:T(8,128)(2,1)S(1)}, bf16[136,640]{1,0:T(8,128)(2,1)S(1)}, u32[]{:S(2)}, u32[]{:S(2)}) collective-permute-start(bf16[136,640]{1,0:T(8,128)(2,1)S(1)} %get-tuple-element.66), channel_id=1, source_target_pairs={{0,8},{4,12},{8,0},{12,4},{1,9},{5,13},{9,1},{13,5},{2,10},{6,14},... | collective-permute-start | bytes 522248 | tf_op jit(solution)/shard_map/ppermute | solution.py:635
  48.6 0.1 edge_rows.1
  48.8 1.4 %collective-permute-start.12 = (f32[192,128]{1,0:T(8,128)S(1)}, f32[192,128]{1,0:T(8,128)S(1)}, u32[]{:S(2)}, u32[]{:S(2)}) collective-permute-start(f32[192,128]{1,0:T(8,128)S(1)} %get-tuple-element.71.refs_8_), channel_id=1, source_target_pairs={{4,0},{8,4},{12,8},{16,12},{20,16},{24,20},{28,24},{5,1},{9,5},{13... | collective-permute-start | bytes 294920 | tf_op jit(solution)/shard_map/ppermute | solution.py:663
  50.2 4.6 %collective-permute-start.13 = (f32[192,128]{1,0:T(8,128)S(1)}, f32[192,128]{1,0:T(8,128)S(1)}, u32[]{:S(2)}, u32[]{:S(2)}) collective-permute-start(f32[192,128]{1,0:T(8,128)S(1)} %get-tuple-element.70.refs_7_), channel_id=1, source_target_pairs={{0,4},{4,8},{8,12},{12,16},{16,20},{20,24},{24,28},{1,5},{5,9},{9,... | collective-permute-start | bytes 294920 | tf_op jit(solution)/shard_map/ppermute | solution.py:664
  54.7 0.7 slice.6.refs_4_
  55.4 0.7 slice.7.refs_5_
  56.2 0.2 collective-permute-done.12.refs_11_
  56.3 3.6 %collective-permute-done.13.refs_12_ = f32[192,128]{1,0:T(8,128)S(1)} collective-permute-done((f32[192,128]{1,0:T(8,128)S(1)}, f32[192,128]{1,0:T(8,128)S(1)}, u32[]{:S(2)}, u32[]{:S(2)}) %collective-permute-start.13) | collective-permute-done | bytes 98336 | tf_op jit(solution)/shard_map/ppermute | solution.py:664
  59.9 1.7 %collective-permute-done.10.refs_2_ = bf16[136,640]{1,0:T(8,128)(2,1)S(1)} collective-permute-done((bf16[136,640]{1,0:T(8,128)(2,1)S(1)}, bf16[136,640]{1,0:T(8,128)(2,1)S(1)}, u32[]{:S(2)}, u32[]{:S(2)}) %collective-permute-start.10) | collective-permute-done | bytes 174112 | tf_op jit(solution)/shard_map/ppermute | solution.py:635
  61.7 0.6 copy-done.13
  62.4 3.7 %surface.1 = (bf16[32,40,128]{2,1,0:T(8,128)(2,1)}, f32[5,128,128]{2,1,0:T(8,128)}, f32[8,640]{1,0:T(8,128)}, f32[192,128]{1,0:T(8,128)}, f32[192,128]{1,0:T(8,1...) custom-call(f32[136,640]{1,0:T(8,128)} %copy-done.3, ...), custom_call_target="tpu_custom_call" | custom-call | flops 4194304 | bytes 4194304 | tf_op jit(solution)/shard_map/surface/pallas_call | solution.py:669
  66.0 11.1 %all-to-all-start = ((bf16[32,40,128]{2,1,0:T(8,128)(2,1)}), bf16[32,40,128]{2,1,0:T(8,128)(2,1)S(1)}, u32[]{:S(2)}, u32[]{:S(2)}) async-start(bf16[32,40,128]{2,1,0:T(8,128)(2,1)} %get-tuple-element.83), calls=%async_computation | async-start | bytes 655360 | tf_op jit(solution)/shard_map/all_to_all | solution.py:676
  77.2 0.6 reshape.19.src
  77.7 13.0 %substeps.1 = f32[2,16,128,128]{3,2,1,0:T(8,128)} custom-call(f32[2,16,128,128]{3,2,1,0:T(8,128)} %tracers.2, f32[2,16,128,128]{3,2,1,0:T(8,128)} %currents.2, s32[128,128]{1,0:T(8,128)} %land.5, f32[5,128,128]{2,1,0:T(8,128)} %get-tuple-element.72.flux, f32[8,640]{1,0:T(8,128)} %get-tuple-element.73.rim, f32[192,128]{1,0:T(8,128)} %get-tuple-element.74.in_n, ...), custom_call_target="tpu_custom_call" | custom-call | flops 16777216 | bytes 16777216 | tf_op jit(solution)/shard_map/substeps/pallas_call | solution.py:679
  90.8 0.7 copy-done.11
  91.5 9.3 %backward_remap.1 = f32[160,128]{1,0:T(8,128)} custom-call(s32[640]{0:T(1024)} %get-tuple-element.82.slots, s32[1,640]{1,0:T(1,128)} %reshape.19.src, bf16[32,40,128]{2,1,0:T(8,128)(2,1)} %copy-done.11, bf16[640,128,128]{2,1,0:T(8,128)(2,1)} %w.3), custom_call_target="tpu_custom_call" | custom-call | flops 167772160 | bytes 20971520 | tf_op jit(solution)/shard_map/backward_remap/pallas_call | solution.py:599
  (45 shorter events, 0.2 us)
Async XLA Ops:
  1.9 26.5 %copy-start = (f32[2,16,128,128]{3,2,1,0:T(8,128)S(1)}, f32[2,16,128,128]{3,2,1,0:T(8,128)}, u32[]{:S(2)}) copy-start(f32[2,16,128,128]{3,2,1,0:T(8,128)} %currents.2) | copy-start | bytes 6291460
  1.9 26.5 %copy-start.1 = (f32[2,16,128,128]{3,2,1,0:T(8,128)S(1)}, f32[2,16,128,128]{3,2,1,0:T(8,128)}, u32[]{:S(2)}) copy-start(f32[2,16,128,128]{3,2,1,0:T(8,128)} %tracers.2) | copy-start | bytes 6291460
  1.9 26.5 %copy-start.2 = (s32[128,128]{1,0:T(8,128)S(1)}, s32[128,128]{1,0:T(8,128)}, u32[]{:S(2)}) copy-start(s32[128,128]{1,0:T(8,128)} %land.5) | copy-start | bytes 196612
  16.6 4.9 %collective-permute-start = (bf16[4,48,640]{2,1,0:T(8,128)(2,1)}, bf16[4,48,640]{2,1,0:T(8,128)(2,1)S(1)}, u32[]{:S(2)}, u32[]{:S(2)}) collective-permute-start(bf16[4,48,640]{2,1,0:T(8,128)(2,1)} %get-tuple-element.44), channel_id=1, source_target_pairs={{0,1},{1,0},{2,3},{3,2},{16,17},{17,16},{18,19},{19,18},{4,5},{5,4... | collective-permute-start | bytes 737288 | tf_op jit(solution)/shard_map/ppermute | solution.py:635
  17.1 9.6 %collective-permute-start.1 = (bf16[4,48,640]{2,1,0:T(8,128)(2,1)}, bf16[4,48,640]{2,1,0:T(8,128)(2,1)S(1)}, u32[]{:S(2)}, u32[]{:S(2)}) collective-permute-start(bf16[4,48,640]{2,1,0:T(8,128)(2,1)} %get-tuple-element.46), channel_id=1, source_target_pairs={{0,2},{1,3},{2,0},{3,1},{16,18},{17,19},{18,16},{19,17},{4,6},{5,7... | collective-permute-start | bytes 737288 | tf_op jit(solution)/shard_map/ppermute | solution.py:635
  19.6 11.9 %collective-permute-start.2 = (bf16[4,48,640]{2,1,0:T(8,128)(2,1)}, bf16[4,48,640]{2,1,0:T(8,128)(2,1)S(1)}, u32[]{:S(2)}, u32[]{:S(2)}) collective-permute-start(bf16[4,48,640]{2,1,0:T(8,128)(2,1)} %get-tuple-element.47), channel_id=1, source_target_pairs={{0,3},{1,2},{2,1},{3,0},{16,19},{17,18},{18,17},{19,16},{4,7},{5,6... | collective-permute-start | bytes 737288 | tf_op jit(solution)/shard_map/ppermute | solution.py:635
  19.7 13.1 %collective-permute-start.3 = (bf16[4,48,640]{2,1,0:T(8,128)(2,1)}, bf16[4,48,640]{2,1,0:T(8,128)(2,1)S(1)}, u32[]{:S(2)}, u32[]{:S(2)}) collective-permute-start(bf16[4,48,640]{2,1,0:T(8,128)(2,1)} %get-tuple-element.48), channel_id=1, source_target_pairs={{0,16},{1,17},{2,18},{3,19},{16,0},{17,1},{18,2},{19,3},{4,20},{5,... | collective-permute-start | bytes 737288 | tf_op jit(solution)/shard_map/ppermute | solution.py:635
  21.5 21.8 %collective-permute-start.4 = (bf16[4,48,640]{2,1,0:T(8,128)(2,1)}, bf16[4,48,640]{2,1,0:T(8,128)(2,1)S(1)}, u32[]{:S(2)}, u32[]{:S(2)}) collective-permute-start(bf16[4,48,640]{2,1,0:T(8,128)(2,1)} %get-tuple-element.49), channel_id=1, source_target_pairs={{0,17},{1,16},{2,19},{3,18},{16,1},{17,0},{18,3},{19,2},{4,21},{5,... | collective-permute-start | bytes 737288 | tf_op jit(solution)/shard_map/ppermute | solution.py:635
  21.5 21.8 %collective-permute-start.5 = (bf16[4,48,640]{2,1,0:T(8,128)(2,1)}, bf16[4,48,640]{2,1,0:T(8,128)(2,1)S(1)}, u32[]{:S(2)}, u32[]{:S(2)}) collective-permute-start(bf16[4,48,640]{2,1,0:T(8,128)(2,1)} %get-tuple-element.50), channel_id=1, source_target_pairs={{0,18},{1,19},{2,16},{3,17},{16,2},{17,3},{18,0},{19,1},{4,22},{5,... | collective-permute-start | bytes 737288 | tf_op jit(solution)/shard_map/ppermute | solution.py:635
  26.7 16.7 %copy-start.6 = (bf16[4,48,640]{2,1,0:T(8,128)(2,1)S(1)}, bf16[4,48,640]{2,1,0:T(8,128)(2,1)}, u32[]{:S(2)}) copy-start(bf16[4,48,640]{2,1,0:T(8,128)(2,1)} %get-tuple-element.56.refs_0_) | copy-start | bytes 737284
  26.7 16.7 %collective-permute-start.6 = (bf16[4,48,640]{2,1,0:T(8,128)(2,1)}, bf16[4,48,640]{2,1,0:T(8,128)(2,1)S(1)}, u32[]{:S(2)}, u32[]{:S(2)}) collective-permute-start(bf16[4,48,640]{2,1,0:T(8,128)(2,1)} %get-tuple-element.51), channel_id=1, source_target_pairs={{0,19},{1,18},{2,17},{3,16},{16,3},{17,2},{18,1},{19,0},{4,23},{5,... | collective-permute-start | bytes 737288 | tf_op jit(solution)/shard_map/ppermute | solution.py:635
  30.0 18.6 %copy-start.9 = (f32[128,128]{1,0:T(8,128)}, f32[128,128]{1,0:T(8,128)S(1)}, u32[]{:S(2)}) copy-start(f32[128,128]{1,0:T(8,128)S(1)} %get-tuple-element.54.refs_10_) | copy-start | bytes 196612
  30.1 18.6 %copy-start.10 = (f32[128,128]{1,0:T(8,128)}, f32[128,128]{1,0:T(8,128)S(1)}, u32[]{:S(2)}) copy-start(f32[128,128]{1,0:T(8,128)S(1)} %get-tuple-element.55.refs_9_) | copy-start | bytes 196612
  31.5 11.8 %collective-permute-start.7 = (f32[128,128]{1,0:T(8,128)S(1)}, f32[128,128]{1,0:T(8,128)S(1)}, u32[]{:S(2)}, u32[]{:S(2)}) collective-permute-start(f32[128,128]{1,0:T(8,128)S(1)} %get-tuple-element.54.refs_10_), channel_id=1, source_target_pairs={{1,0},{2,1},{3,2},{5,4},{6,5},{7,6},{9,8},{10,9},{11,10},{13,12},{... | collective-permute-start | bytes 196616 | tf_op jit(solution)/shard_map/ppermute | solution.py:656
  32.8 10.5 %collective-permute-start.8 = (f32[128,128]{1,0:T(8,128)S(1)}, f32[128,128]{1,0:T(8,128)S(1)}, u32[]{:S(2)}, u32[]{:S(2)}) collective-permute-start(f32[128,128]{1,0:T(8,128)S(1)} %get-tuple-element.55.refs_9_), channel_id=1, source_target_pairs={{0,1},{1,2},{2,3},{4,5},{5,6},{6,7},{8,9},{9,10},{10,11},{12,13},{... | collective-permute-start | bytes 196616 | tf_op jit(solution)/shard_map/ppermute | solution.py:657
  43.3 5.4 %copy-start.4 = (f32[128,128]{1,0:T(8,128)}, f32[128,128]{1,0:T(8,128)S(1)}, u32[]{:S(2)}) copy-start(f32[128,128]{1,0:T(8,128)S(1)} %collective-permute-done.7.from_east.refs_13_) | copy-start | bytes 196612
  43.3 5.4 %copy-start.5 = (f32[128,128]{1,0:T(8,128)}, f32[128,128]{1,0:T(8,128)S(1)}, u32[]{:S(2)}) copy-start(f32[128,128]{1,0:T(8,128)S(1)} %collective-permute-done.8.from_west.refs_14_) | copy-start | bytes 196612
  44.0 4.7 %copy-start.3 = (f32[136,640]{1,0:T(8,128)}, f32[136,640]{1,0:T(8,128)S(1)}, u32[]{:S(2)}) copy-start(f32[136,640]{1,0:T(8,128)S(1)} %get-tuple-element.64.refs_0_) | copy-start | bytes 1044484
  44.0 15.9 %collective-permute-start.9 = (bf16[136,640]{1,0:T(8,128)(2,1)S(1)}, bf16[136,640]{1,0:T(8,128)(2,1)S(1)}, u32[]{:S(2)}, u32[]{:S(2)}) collective-permute-start(bf16[136,640]{1,0:T(8,128)(2,1)S(1)} %get-tuple-element.65), channel_id=1, source_target_pairs={{0,4},{4,0},{8,12},{12,8},{1,5},{5,1},{9,13},{13,9},{2,6},{6,2},{1... | collective-permute-start | bytes 522248 | tf_op jit(solution)/shard_map/ppermute | solution.py:635
  45.9 15.7 %collective-permute-start.10 = (bf16[136,640]{1,0:T(8,128)(2,1)S(1)}, bf16[136,640]{1,0:T(8,128)(2,1)S(1)}, u32[]{:S(2)}, u32[]{:S(2)}) collective-permute-start(bf16[136,640]{1,0:T(8,128)(2,1)S(1)} %get-tuple-element.66), channel_id=1, source_target_pairs={{0,8},{4,12},{8,0},{12,4},{1,9},{5,13},{9,1},{13,5},{2,10},{6,14},... | collective-permute-start | bytes 522248 | tf_op jit(solution)/shard_map/ppermute | solution.py:635
  48.6 13.0 %collective-permute-start.11 = (bf16[136,640]{1,0:T(8,128)(2,1)S(1)}, bf16[136,640]{1,0:T(8,128)(2,1)S(1)}, u32[]{:S(2)}, u32[]{:S(2)}) collective-permute-start(bf16[136,640]{1,0:T(8,128)(2,1)S(1)} %get-tuple-element.67), channel_id=1, source_target_pairs={{0,12},{4,8},{8,4},{12,0},{1,13},{5,9},{9,5},{13,1},{2,14},{6,10},... | collective-permute-start | bytes 522248 | tf_op jit(solution)/shard_map/ppermute | solution.py:635
  48.7 12.9 %copy-start.7 = (f32[192,128]{1,0:T(8,128)}, f32[192,128]{1,0:T(8,128)S(1)}, u32[]{:S(2)}) copy-start(f32[192,128]{1,0:T(8,128)S(1)} %get-tuple-element.71.refs_8_) | copy-start | bytes 294916
  48.7 12.9 %copy-start.8 = (f32[192,128]{1,0:T(8,128)}, f32[192,128]{1,0:T(8,128)S(1)}, u32[]{:S(2)}) copy-start(f32[192,128]{1,0:T(8,128)S(1)} %get-tuple-element.70.refs_7_) | copy-start | bytes 294916
  48.7 28.4 %copy-start.17 = (s32[640]{0:T(1024)S(1)}, s32[640]{0:T(1024)}, u32[]{:S(2)}) copy-start(s32[640]{0:T(1024)} %src.1) | copy-start | bytes 7684
  48.8 7.6 %collective-permute-start.12 = (f32[192,128]{1,0:T(8,128)S(1)}, f32[192,128]{1,0:T(8,128)S(1)}, u32[]{:S(2)}, u32[]{:S(2)}) collective-permute-start(f32[192,128]{1,0:T(8,128)S(1)} %get-tuple-element.71.refs_8_), channel_id=1, source_target_pairs={{4,0},{8,4},{12,8},{16,12},{20,16},{24,20},{28,24},{5,1},{9,5},{13... | collective-permute-start | bytes 294920 | tf_op jit(solution)/shard_map/ppermute | solution.py:663
  50.2 9.7 %collective-permute-start.13 = (f32[192,128]{1,0:T(8,128)S(1)}, f32[192,128]{1,0:T(8,128)S(1)}, u32[]{:S(2)}, u32[]{:S(2)}) collective-permute-start(f32[192,128]{1,0:T(8,128)S(1)} %get-tuple-element.70.refs_7_), channel_id=1, source_target_pairs={{0,4},{4,8},{8,12},{12,16},{16,20},{20,24},{24,28},{1,5},{5,9},{9,... | collective-permute-start | bytes 294920 | tf_op jit(solution)/shard_map/ppermute | solution.py:664
  56.3 5.3 %copy-start.15 = (f32[192,128]{1,0:T(8,128)}, f32[192,128]{1,0:T(8,128)S(1)}, u32[]{:S(2)}) copy-start(f32[192,128]{1,0:T(8,128)S(1)} %collective-permute-done.12.refs_11_) | copy-start | bytes 294916
  59.9 1.8 %copy-start.16 = (f32[192,128]{1,0:T(8,128)}, f32[192,128]{1,0:T(8,128)S(1)}, u32[]{:S(2)}) copy-start(f32[192,128]{1,0:T(8,128)S(1)} %collective-permute-done.13.refs_12_) | copy-start | bytes 294916
  59.9 1.8 %copy-start.12 = (bf16[136,640]{1,0:T(8,128)(2,1)}, bf16[136,640]{1,0:T(8,128)(2,1)S(1)}, u32[]{:S(2)}) copy-start(bf16[136,640]{1,0:T(8,128)(2,1)S(1)} %collective-permute-done.9.refs_1_) | copy-start | bytes 522244
  61.6 0.7 copy-start.14
  66.0 24.8 %all-to-all-start = ((bf16[32,40,128]{2,1,0:T(8,128)(2,1)}), bf16[32,40,128]{2,1,0:T(8,128)(2,1)S(1)}, u32[]{:S(2)}, u32[]{:S(2)}) async-start(bf16[32,40,128]{2,1,0:T(8,128)(2,1)} %get-tuple-element.83), calls=%async_computation | async-start | bytes 655360 | tf_op jit(solution)/shard_map/all_to_all | solution.py:676
  90.8 0.7 copy-start.11
  (1 other events, 0.7 us)

commit v7 on v5

--- a/solution.py
+++ b/solution.py
@@ -94,7 +94,7 @@
             both = dot(left, held[pl.ds(k, 2)].reshape(2 * width, width), NT)
             for z, part in enumerate((both[:fields, :width], both[fields:, width:])):
                 part = part + jnp.where(low_rows, pltpu.roll(part, fields - 4, 0), 0.0)
-                owner = own[k + z]
+                owner = own[0, k + z]
                 at = counts[owner]
                 counts[owner] = at + 1
                 at = jnp.minimum(at, cap - 1)
@@ -217,16 +217,34 @@
         out[...] = jnp.concatenate([sums, ext], axis=0).astype(out.dtype)
 
 
-def columns_kernel(tracers, currents, land, west, east):
+def rows_kernel(tracers, currents, land, south, north):
+    height, width = land.shape
+    levels = tracers.shape[0] // 2 // height
+    for out, edge, second in ((south, 0, 1), (north, height - 1, height - 2)):
+        out[...] = jnp.concatenate(
+            [
+                tracers[pl.ds(edge, 2 * levels, stride=height), :],
+                tracers[pl.ds(second, 2 * levels, stride=height), :],
+                currents[pl.ds(edge, 2 * levels, stride=height), :],
+                currents[pl.ds(levels * height + second, levels, stride=height), :],
+                *[land[x : x + 1, :].astype(F32) for x in (edge, second)],
+                jnp.zeros((out.shape[0] - 7 * levels - 2, width), F32),
+            ],
+            axis=0,
+        ).astype(BF16)
+
+
+def columns_kernel(tracers, currents, land, from_n, from_s, west, east, west_wide, east_wide):
     levels = tracers.shape[1]
     width = tracers.shape[3]
     last = width - 1
-    west[...] = jnp.zeros_like(west)
-    east[...] = jnp.zeros_like(east)
+    lane = iota((1, width), 1)
+    west_wide[...] = jnp.zeros_like(west_wide)
+    east_wide[...] = jnp.zeros_like(east_wide)
 
     def put(plane, near, far):
         turned = plane.T
-        for out, edge, second in ((west, 0, 1), (east, last, last - 1)):
+        for out, edge, second in ((west_wide, 0, 1), (east_wide, last, last - 1)):
             out[pl.ds(near, 1), :] = turned[edge : edge + 1]
             if far is not None:
                 out[pl.ds(far, 1), :] = turned[second : second + 1]
@@ -240,25 +258,14 @@
 
     lax.fori_loop(0, levels, level, 0, unroll=2)
     put(land[...].astype(F32), 7 * levels, 7 * levels + 1)
-
-
-def rows_kernel(tracers, currents, land, from_west, from_east, south, north):
-    levels = tracers.shape[0] // 2 // land.shape[0]
-    height, width = land.shape
-    lane = iota((1, width), 1)
-    for out, edge, second in ((south, 0, 1), (north, height - 1, height - 2)):
-        out[0 : 2 * levels] = tracers[pl.ds(edge, 2 * levels, stride=height), :]
-        out[2 * levels : 4 * levels] = tracers[pl.ds(second, 2 * levels, stride=height), :]
-        out[4 * levels : 6 * levels] = currents[pl.ds(edge, 2 * levels, stride=height), :]
-        out[6 * levels : 7 * levels] = currents[pl.ds(levels * height + second, levels, stride=height), :]
-        wet = [land[x : x + 1, :].astype(F32) for x in (edge, second)]
-        out[7 * levels : 7 * levels + 8] = jnp.concatenate(wet + [jnp.zeros((6, width), F32)], axis=0)
     base = 7 * levels + 8
+    n_all, s_all = from_n[...].astype(F32), from_s[...].astype(F32)
     for start, stop, at in ((0, 2 * levels, 0), (4 * levels, 6 * levels, 2 * levels), (7 * levels, 7 * levels + 8, 4 * levels)):
-        w, e = from_west[start:stop], from_east[start:stop]
-        there = slice(base + at, base + at + stop - start)
-        south[there] = jnp.where(lane == 0, w, pltpu.roll(e, width - 1, 1))
-        north[there] = jnp.where(lane == width - 1, e, pltpu.roll(w, 1, 1))
+        n, s = n_all[start:stop], s_all[start:stop]
+        west_wide[base + at : base + at + stop - start] = jnp.where(lane == last, pltpu.roll(n, last, 1), s)
+        east_wide[base + at : base + at + stop - start] = jnp.where(lane == last, n, pltpu.roll(s, 1, 1))
+    west[...] = west_wide[...].astype(BF16)
+    east[...] = east_wide[...].astype(BF16)
 
 
 def plus_side(q, other, speed, speed_other, passable):
@@ -304,9 +311,9 @@
         return x[at : at + count]
 
     def corners(at, count):
-        n, s = part(north, base + at, count), part(south, base + at, count)
-        e = jnp.where(lane == width - 1, n, pltpu.roll(s, 1, 1))
-        w = jnp.where(lane == width - 1, pltpu.roll(n, width - 1, 1), s)
+        e, w = part(east, base + at, count), part(west, base + at, count)
+        n = jnp.where(lane == width - 1, e, pltpu.roll(w, 1, 1))
+        s = jnp.where(lane == width - 1, pltpu.roll(e, width - 1, 1), w)
         return n, s, e, w
 
     corner_q = corners(tracer * levels, levels)
@@ -377,12 +384,38 @@
     return edge
 
 
+def corrected_edges(levels, ext, stress_u, stress_v, near, far):
+    height, width = stress_u.shape
+    last = width - 1
+    lane = iota((1, width), 1)
+
+    def block(r, b):
+        return ext[r : r + 1, b * width : (b + 1) * width]
+
+    u, v, second = 4 * levels, 5 * levels, 6 * levels
+    base = 7 * levels + 8
+    corners = []
+    for b in (3, 4):
+        ne, nw, se, sw = [block(r, b) for r in (4, 5, 6, 7)]
+        corners.append((jnp.where(lane == last, pltpu.roll(ne, last, 1), se), jnp.where(lane == last, nw, pltpu.roll(sw, 1, 1))))
+    turned = stress_u.T
+    own = [[(v, stress_v[last:])], [(v, stress_v[0:1])], [(u, turned[last:])], [(u, turned[0:1])]]
+    beside = [
+        [(u, block(0, 3)), (v, block(0, 4)), (second, block(1, 4))],
+        [(u, block(2, 3)), (v, block(2, 4)), (second, block(3, 4))],
+        [(u, block(6, 0)), (v, block(7, 0)), (second, block(5, 2)), (base + 2 * levels, corners[0][0]), (base + 3 * levels, corners[1][0])],
+        [(u, block(6, 1)), (v, block(7, 1)), (second, block(7, 2)), (base + 2 * levels, corners[0][1]), (base + 3 * levels, corners[1][1])],
+    ]
+    near = [corrected(edge[...].astype(F32), x) for edge, x in zip(near, own)]
+    return near, [corrected(edge[...].astype(F32), x) for edge, x in zip(far, beside)]
+
+
 def surface_kernel(grid, chunk, levels, *refs):
     n_sec, n_gx, n_gy = grid
     planes = n_sec * n_gy
     parts, refs = refs[:n_gx], refs[n_gx:]
     tracers, currents, land, own_n, own_s, own_e, own_w, from_n, from_s, from_e, from_w, *refs = refs
-    back, flux, rim, in_n, in_s, in_e, in_w, out_n, out_s, out_e, out_w = refs
+    back, flux, rim = refs
     height, width = land.shape
     last = width - 1
     lane = iota((1, width), 1)
@@ -394,45 +427,18 @@
     wet = land[...].astype(F32)
     u0 = currents[0, 0] + 0.1 * stress_u
     v0 = currents[1, 0] + 0.1 * stress_v
-    flux[0], flux[1], flux[2], flux[3], flux[4] = shortwave, heat, salt, u0, v0
+    flux[0], flux[1], flux[2], flux[3], flux[4] = shortwave, heat, salt, stress_u, stress_v
     rim[...] = ext
 
-    def block(r, b):
-        return ext[r : r + 1, b * width : (b + 1) * width]
-
-    n_flux, s_flux = [[block(r, b) for b in range(SENT)] for r in (0, 2)]
-    ne, nw, se, sw = [[block(r, b) for b in (3, 4)] for r in (4, 5, 6, 7)]
-    level0_u, level0_v, second = 4 * levels, 5 * levels, 6 * levels
-    base = 7 * levels + 8
-    corner_n = jnp.where(lane == last, pltpu.roll(ne[0], last, 1), pltpu.roll(nw[0], 1, 1))
-    corner_s = jnp.where(lane == last, pltpu.roll(se[0], last, 1), pltpu.roll(sw[0], 1, 1))
-    corner_n_v = jnp.where(lane == last, pltpu.roll(ne[1], last, 1), pltpu.roll(nw[1], 1, 1))
-    corner_s_v = jnp.where(lane == last, pltpu.roll(se[1], last, 1), pltpu.roll(sw[1], 1, 1))
-    far_n = corrected(
-        from_n[...],
-        [(level0_u, n_flux[3]), (level0_v, n_flux[4]), (second, block(1, 4)), (base + 2 * levels, corner_n), (base + 3 * levels, corner_n_v)],
-    )
-    far_s = corrected(
-        from_s[...],
-        [(level0_u, s_flux[3]), (level0_v, s_flux[4]), (second, block(3, 4)), (base + 2 * levels, corner_s), (base + 3 * levels, corner_s_v)],
-    )
-    far_e = corrected(from_e[...], [(level0_u, block(6, 0)), (level0_v, block(7, 0)), (second, block(5, 2))])
-    far_w = corrected(from_w[...], [(level0_u, block(6, 1)), (level0_v, block(7, 1)), (second, block(7, 2))])
-    turned = stress_u.T
-    near_n = corrected(own_n[...], [(level0_v, stress_v[height - 1 : height])])
-    near_s = corrected(own_s[...], [(level0_v, stress_v[0:1])])
-    near_e = corrected(own_e[...], [(level0_u, turned[last : last + 1])])
-    near_w = corrected(own_w[...], [(level0_u, turned[0:1])])
-    in_n[...], in_s[...], in_e[...], in_w[...] = near_n, near_s, near_e, near_w
-    out_n[...], out_s[...], out_e[...], out_w[...] = far_n, far_s, far_e, far_w
-
-    e_turned, w_turned = far_e.T, far_w.T
+    near, far = corrected_edges(levels, ext, stress_u, stress_v, (own_n, own_s, own_e, own_w), (from_n, from_s, from_e, from_w))
+    far_n, far_s, far_e, far_w = far
+    e_turned, w_turned = far_e[:width].T, far_w[:width].T
     east = lambda index: column(e_turned, index, last)
     west = lambda index: column(w_turned, index, 0)
     passable = wet_products(
         wet, far_n[7 * levels : 7 * levels + 1], far_s[7 * levels : 7 * levels + 1], east(7 * levels), west(7 * levels)
     )
-    lines = strips(0, levels, (near_n, near_s, near_e, near_w), (far_n, far_s, far_e, far_w), rim_flux(ext, width))
+    lines = strips(0, levels, near, far, rim_flux(ext, width))
     profile = level_profile(levels, width)
     mix = KV * wet
     warm = 0.3 * wet * shortwave
@@ -482,15 +488,29 @@
 
 
 def stencil_kernel(
-    tracers, currents, land, flux, rim, in_n, in_s, in_e, in_w, out_n, out_s, out_e, out_w,
-    out, held, weights, line_n, line_s, depth, forced, passing,
+    tracers_in, currents_in, land, flux, rim, own_n, own_s, own_e, own_w, from_n, from_s, from_e, from_w,
+    result, tracers, currents, out, held, weights, edge_n, edge_s, line_n, line_s, depth, forced, passing, sems,
 ):
+    copies = [
+        pltpu.make_async_copy(tracers_in, tracers, sems.at[0]),
+        pltpu.make_async_copy(currents_in, currents, sems.at[1]),
+    ]
+    for copy in copies:
+        copy.start()
     levels = tracers.shape[1]
+
+    def send(l):
+        return pltpu.make_async_copy(out.at[:, l], result.at[:, l], sems.at[2 + l])
+
     height, width = land.shape
     last = width - 1
     wet = land[...].astype(F32)
-    far_n, far_s, far_e, far_w = out_n[...], out_s[...], out_e[...], out_w[...]
-    e_turned, w_turned = far_e.T, far_w.T
+    near, far = corrected_edges(
+        levels, rim[...], flux[3], flux[4], (own_n, own_s, own_e, own_w), (from_n, from_s, from_e, from_w)
+    )
+    far_n, far_s, far_e, far_w = far
+    edge_n[...], edge_s[...] = far_n, far_s
+    e_turned, w_turned = far_e[:width].T, far_w[:width].T
     at = 7 * levels
     for i, x in enumerate(
         wet_products(wet, far_n[at : at + 1], far_s[at : at + 1], column(e_turned, at, last), column(w_turned, at, 0))
@@ -501,7 +521,7 @@
     columns = []
     for tracer in range(2):
         lines = strips(
-            tracer, levels, (in_n[...], in_s[...], in_e[...], in_w[...]), (far_n, far_s, far_e, far_w), rim_flux(rim[...], width)
+            tracer, levels, near, far, rim_flux(rim[...], width)
         )
         line_n[tracer * levels : (tracer + 1) * levels] = lines[0]
         line_s[tracer * levels : (tracer + 1) * levels] = lines[1]
@@ -520,20 +540,23 @@
             return forced[0] * depth[pl.ds(l, 1), :] + top * forced[1]
         return top * forced[2]
 
+    for copy in copies:
+        copy.wait()
+    currents[0, 0] = currents[0, 0] + 0.1 * flux[3]
+    currents[1, 0] = currents[1, 0] + 0.1 * flux[4]
+
     def first_step(l, _):
-        surface = l == 0
-        u = jnp.where(surface, flux[3], currents[0, l])
-        v = jnp.where(surface, flux[4], currents[1, l])
+        u, v = currents[0, l], currents[1, l]
         row = 5 * levels + l
         c = coefficients(
             u, v, column(e_turned, 4 * levels + l, last), column(w_turned, 4 * levels + l, 0),
-            out_n[pl.ds(row, 1), :], out_s[pl.ds(row, 1), :], [passing[i] for i in range(4)],
+            edge_n[pl.ds(row, 1), :], edge_s[pl.ds(row, 1), :], [passing[i] for i in range(4)],
         )
         for i, x in enumerate(c):
             weights[i, l] = x
         for tracer in range(2):
             row = tracer * levels + l
-            halo = out_n[pl.ds(row, 1), :], out_s[pl.ds(row, 1), :], column(e_turned, row, last), column(w_turned, row, 0)
+            halo = edge_n[pl.ds(row, 1), :], edge_s[pl.ds(row, 1), :], column(e_turned, row, last), column(w_turned, row, 0)
             under, over = tracers[tracer, jnp.minimum(l + 1, levels - 1)], tracers[tracer, jnp.maximum(l - 1, 0)]
             held[tracer, l] = update(c, tracers[tracer, l], halo, under, over, forcing(tracer, l))
         return 0
@@ -547,12 +570,15 @@
             halo = line_n[pl.ds(row, 1), :], line_s[pl.ds(row, 1), :], column(e_later, row, last), column(w_later, row, 0)
             under, over = held[tracer, jnp.minimum(l + 1, levels - 1)], held[tracer, jnp.maximum(l - 1, 0)]
             out[tracer, l] = update(c, held[tracer, l], halo, under, over, forcing(tracer, l))
+        send(l).start()
         return 0
 
     lax.fori_loop(0, levels, second_step, 0)
-
-
-def backward_kernel(parts, slots, src, back, w, out, held, wide, picked, terms, sems):
+    for l in range(levels):
+        send(l).wait()
+
+
+def backward_kernel(parts, slots_in, src, back, w, out, held, wide, picked, terms, slots, sems):
     total, width = terms.shape
     blocks = out.shape[0]
     batch = total // parts
@@ -560,8 +586,11 @@
     def copy(c):
         return pltpu.make_async_copy(w.at[pl.ds(c * batch, batch)], held.at[pl.ds(c * batch, batch)], sems.at[c])
 
+    slots_copy = pltpu.make_async_copy(slots_in, slots, sems.at[parts])
+    slots_copy.start()
     for c in range(parts):
         copy(c).start()
+    slots_copy.wait()
     wide[...] = back[...].astype(F32).reshape(wide.shape)
 
     def pick(i, _):
@@ -598,14 +627,15 @@
     devices, cap, _ = back.shape
     return pl.pallas_call(
         functools.partial(backward_kernel, parts),
-        in_specs=[SMEM, VMEM, VMEM, ANY],
+        in_specs=[ANY, VMEM, VMEM, ANY],
         out_specs=VMEM,
         scratch_shapes=[
             pltpu.VMEM(w.shape, BF16),
             pltpu.VMEM((devices * cap, width), F32),
             pltpu.VMEM((total, width), F32),
             pltpu.VMEM((total, width), F32),
-            pltpu.SemaphoreType.DMA((parts,)),
+            pltpu.SMEM((total,), jnp.int32),
+            pltpu.SemaphoreType.DMA((parts + 1,)),
         ],
         out_shape=jax.ShapeDtypeStruct((blocks, width), F32),
         compiler_params=kernel_params(58),
@@ -614,7 +644,7 @@
     )(slots, src.reshape(1, total), back, w)
 
 
-def kernel(body, outs, name, mebibytes, bytes_accessed, scratch=()):
+def kernel(body, outs, name, mebibytes, bytes_accessed, scratch=(), **specs):
     return pl.pallas_call(
         body,
         out_shape=[jax.ShapeDtypeStruct(shape, dtype) for shape, dtype in outs],
@@ -622,6 +652,7 @@
         compiler_params=kernel_params(mebibytes),
         cost_estimate=pl.CostEstimate(flops=bytes_accessed, bytes_accessed=bytes_accessed, transcendentals=0),
         name=name,
+        **specs,
     )
 
 
@@ -643,35 +674,38 @@
     cap = up(2 * total // (planes * n_gx), 8)
     wide = SENT * width
 
-    *sends, slots = forward(atm_flux, remap_weights, remap_src, remap_owner.reshape(total), remap_dst, grid, cap)
+    *sends, slots = forward(atm_flux, remap_weights, remap_src, remap_owner.reshape(1, total), remap_dst, grid, cap)
     chunk = sends[0].shape[1]
     got = [sends[0]] + [swapped(sends[m], ("sec", "gy"), planes, m) for m in range(1, planes)]
 
     side = (width, width)
     end = (7 * levels + 80, width)
-    own_w, own_e = kernel(columns_kernel, [(side, F32)] * 2, "edge_columns", 16, 1 << 22)(tracers, currents, land_sea)
     to_north, to_south = neighbours(NORTH)
     to_east, to_west = neighbours("gy")
-    from_e = lax.ppermute(own_w, "gy", to_west)
-    from_w = lax.ppermute(own_e, "gy", to_east)
-
-    own_s, own_n = kernel(rows_kernel, [(end, F32)] * 2, "edge_rows", 16, 1 << 20)(
-        tracers.reshape(-1, width), currents.reshape(-1, width), land_sea, from_w, from_e
+    got[1], tracers_there, currents_there = lax.optimization_barrier((got[1], tracers, currents))
+    own_s, own_n = kernel(rows_kernel, [(side, BF16)] * 2, "edge_rows", 16, 1 << 20)(
+        tracers_there.reshape(-1, width), currents_there.reshape(-1, width), land_sea
     )
     from_n = lax.ppermute(own_s, NORTH, to_south)
     from_s = lax.ppermute(own_n, NORTH, to_north)
     got, from_n, from_s = lax.optimization_barrier((got, from_n, from_s))
+    own_w, own_e = kernel(columns_kernel, [(end, BF16)] * 2, "edge_columns", 16, 1 << 22, [pltpu.VMEM(end, F32)] * 2)(
+        tracers, currents, land_sea, from_n, from_s
+    )
+    from_e = lax.ppermute(own_w, "gy", to_west)
+    from_w = lax.ppermute(own_e, "gy", to_east)
     part = (height + 8, wide)
     merged = kernel(functools.partial(merge_kernel, planes), [(part, F32)] + [(part, BF16)] * (n_gx - 1), "merge", 24, 1 << 22)(*got)
     parts = [merged[0]] + [swapped(merged[m], "gx", n_gx, m) for m in range(1, n_gx)]
 
-    back, flux, rim, *edges = kernel(
+    edges = own_n, own_s, own_e, own_w, from_n, from_s, from_e, from_w
+    back, flux, rim = kernel(
         functools.partial(surface_kernel, grid, chunk, levels),
-        [((planes * n_gx, cap, width), BF16), ((5, height, width), F32), ((8, wide), F32)] + ([(end, F32)] * 2 + [(side, F32)] * 2) * 2,
+        [((planes * n_gx, cap, width), BF16), ((5, height, width), F32), ((8, wide), F32)],
         "surface",
         58,
         1 << 22,
-    )(*parts, tracers[0:1, 0:3], currents[:, 0:2], land_sea, own_n, own_s, own_e, own_w, from_n, from_s, from_e, from_w)
+    )(*parts, tracers[0:1, 0:3], currents[:, 0:2], land_sea, *edges)
     returned = lax.all_to_all(back, EVERY, split_axis=0, concat_axis=0, tiled=True)
 
     plane = (height, width)
@@ -683,13 +717,21 @@
         1 << 24,
         [
             pltpu.VMEM(tracers.shape, F32),
+            pltpu.VMEM(currents.shape, F32),
+            pltpu.VMEM(tracers.shape, F32),
+            pltpu.VMEM(tracers.shape, F32),
             pltpu.VMEM((5, levels) + plane, F32),
+            pltpu.VMEM(side, F32),
+            pltpu.VMEM(side, F32),
             pltpu.VMEM((2 * levels, width), F32),
             pltpu.VMEM((2 * levels, width), F32),
             pltpu.VMEM((levels, width), F32),
             pltpu.VMEM((3,) + plane, F32),
             pltpu.VMEM((4,) + plane, F32),
+            pltpu.SemaphoreType.DMA((2 + levels,)),
         ],
+        in_specs=[ANY, ANY] + [VMEM] * 11,
+        out_specs=[ANY],
     )(tracers, currents, land_sea, flux, rim, *edges)
     return tracers_out, backward(returned, remap_weights, remap_src, slots, atm_flux.shape[0])
 

time: 111 us -> 94.7 us (0.85)
  waiting for transfers between devices: 31.4 us -> 16.6 us
  other arithmetic: 1.29 us -> 0 us
    ppermute x10, waiting for transfers between devices: 28.8 us -> 16.5 us  [swapped(): return lax.ppermute(array, axes, [(i, i ^ step) for i in range(count)])]
    ppermute x10, starting transfers between devices: 17.5 us -> 14.5 us  [swapped(): return lax.ppermute(array, axes, [(i, i ^ step) for i in range(count)])]
    ppermute x1, waiting for transfers between devices: 1.83 us -> 0.01 us  [on_device(): from_e = lax.ppermute(own_w, 'gy', to_west)]
    all_to_all x1, starting transfers between devices: 4.52 us -> 6.33 us  [on_device(): lax.all_to_all(back, EVERY, split_axis=0, concat_axis=0, tiled=True)]
    unnamed x1 -> x0, other arithmetic: 1.29 us -> none
  transfers between devices with their start and end apart: 15 -> 15, of which waited for: 6 -> 4; matrix products, arithmetic and copies ran while one was open for 2% -> 2% of each run, Pallas kernels for 13% -> 15%
where the time goes in v7:
time: 94.7 us; the launch traced here: 94.3 us
  Pallas kernels  42.2 us (45%)
  starting transfers between devices  31.1 us (33%)
  waiting for transfers between devices  16.6 us (18%)
  local copies, waits for them, and re-layouts  3.51 us (4%)
  between operations  0.96 us (1%)
    ppermute x10, waiting for transfers between devices, swapped(): return lax.ppermute(array, axes, [(i, i ^ step) for i in range(count)])  16.5 us
    pallas_call x1, Pallas kernels, forward(): pl.pallas_call(functools.partial(forward_kernel, parts, cap, grid), in_sp...  14.7 us
    ppermute x10, starting transfers between devices, swapped(): return lax.ppermute(array, axes, [(i, i ^ step) for i in range(count)])  14.5 us
    pallas_call x1, Pallas kernels, on_device(): kernel(stencil_kernel, [(tracers.shape, F32)], 'substeps', 58, 1 << 24, [...  12.6 us
    pallas_call x1, Pallas kernels, backward(): pl.pallas_call(functools.partial(backward_kernel, parts), in_specs=[ANY,...  9.27 us
    all_to_all x1, starting transfers between devices, on_device(): lax.all_to_all(back, EVERY, split_axis=0, concat_axis=0, tiled=True)  6.33 us
    ppermute x1, starting transfers between devices, on_device(): from_s = lax.ppermute(own_n, NORTH, to_north)  4.55 us
    pallas_call x1, Pallas kernels, on_device(): kernel(functools.partial(surface_kernel, grid, chunk, levels), [((planes...  3.29 us
  transfers between devices with their start and end apart: 15, of which 4 were waited for; matrix products, arithmetic and copies ran while one was open for 2% of the time, Pallas kernels for 15%

profile of v7, /device:TPU:0, one launch (start us, length us, event | category | flops | bytes accessed | tf_op | source)
XLA Modules:
  0.0 94.3 jit_solution(17153880506366572304)
XLA Ops:
  0.7 0.0 copy-start.2
  0.7 14.7 %forward_remap.1 = (bf16[4,48,640]{2,1,0:T(8,128)(2,1)}, bf16[4,48,640]{2,1,0:T(8,128)(2,1)}, bf16[4,48,640]{2,1,0:T(8,128)(2,1)}, bf16[4,48,640]{2,1,0:T(8,128)...) custom-call(s32[640]{0:T(1024)} %src.1, ...), custom_call_target="tpu_custom_call" | custom-call | flops 167772160 | bytes 20971520 | tf_op jit(solution)/shard_map/forward_remap/pallas_call | solution.py:178
  15.3 0.5 collective-permute-start
  15.8 2.6 %collective-permute-start.1 = (bf16[4,48,640]{2,1,0:T(8,128)(2,1)}, bf16[4,48,640]{2,1,0:T(8,128)(2,1)S(1)}, u32[]{:S(2)}, u32[]{:S(2)}) collective-permute-start(bf16[4,48,640]{2,1,0:T(8,128)(2,1)} %get-tuple-element.38), channel_id=1, source_target_pairs={{0,2},{1,3},{2,0},{3,1},{16,18},{17,19},{18,16},{19,17},{4,6},{5,7... | collective-permute-start | bytes 737288 | tf_op jit(solution)/shard_map/ppermute | solution.py:666
  18.4 0.1 collective-permute-start.2
  18.5 1.8 %collective-permute-start.3 = (bf16[4,48,640]{2,1,0:T(8,128)(2,1)}, bf16[4,48,640]{2,1,0:T(8,128)(2,1)S(1)}, u32[]{:S(2)}, u32[]{:S(2)}) collective-permute-start(bf16[4,48,640]{2,1,0:T(8,128)(2,1)} %get-tuple-element.40), channel_id=1, source_target_pairs={{0,16},{1,17},{2,18},{3,19},{16,0},{17,1},{18,2},{19,3},{4,20},{5,... | collective-permute-start | bytes 737288 | tf_op jit(solution)/shard_map/ppermute | solution.py:666
  20.3 2.6 %collective-permute-start.5 = (bf16[4,48,640]{2,1,0:T(8,128)(2,1)}, bf16[4,48,640]{2,1,0:T(8,128)(2,1)S(1)}, u32[]{:S(2)}, u32[]{:S(2)}) collective-permute-start(bf16[4,48,640]{2,1,0:T(8,128)(2,1)} %get-tuple-element.42), channel_id=1, source_target_pairs={{0,18},{1,19},{2,16},{3,17},{16,2},{17,3},{18,0},{19,1},{4,22},{5,... | collective-permute-start | bytes 737288 | tf_op jit(solution)/shard_map/ppermute | solution.py:666
  22.9 2.6 %collective-permute-done.1.refs_2_ = bf16[4,48,640]{2,1,0:T(8,128)(2,1)S(1)} collective-permute-done((bf16[4,48,640]{2,1,0:T(8,128)(2,1)}, bf16[4,48,640]{2,1,0:T(8,128)(2,1)S(1)}, u32[]{:S(2)}, u32[]{:S(2)}) %collective-permute-start.1) | collective-permute-done | bytes 245792 | tf_op jit(solution)/shard_map/ppermute | solution.py:666
  25.4 1.7 %collective-permute-start.6 = (bf16[4,48,640]{2,1,0:T(8,128)(2,1)}, bf16[4,48,640]{2,1,0:T(8,128)(2,1)S(1)}, u32[]{:S(2)}, u32[]{:S(2)}) collective-permute-start(bf16[4,48,640]{2,1,0:T(8,128)(2,1)} %get-tuple-element.43), channel_id=1, source_target_pairs={{0,19},{1,18},{2,17},{3,16},{16,3},{17,2},{18,1},{19,0},{4,23},{5,... | collective-permute-start | bytes 737288 | tf_op jit(solution)/shard_map/ppermute | solution.py:666
  27.2 0.1 edge_rows.1
  27.3 3.0 %collective-permute-done.2.refs_3_ = bf16[4,48,640]{2,1,0:T(8,128)(2,1)S(1)} collective-permute-done((bf16[4,48,640]{2,1,0:T(8,128)(2,1)}, bf16[4,48,640]{2,1,0:T(8,128)(2,1)S(1)}, u32[]{:S(2)}, u32[]{:S(2)}) %collective-permute-start.2) | collective-permute-done | bytes 245792 | tf_op jit(solution)/shard_map/ppermute | solution.py:666
  30.3 1.3 %collective-permute-start.7 = (bf16[128,128]{1,0:T(8,128)(2,1)S(1)}, bf16[128,128]{1,0:T(8,128)(2,1)S(1)}, u32[]{:S(2)}, u32[]{:S(2)}) collective-permute-start(bf16[128,128]{1,0:T(8,128)(2,1)S(1)} %get-tuple-element.46.refs_8_.own_s), channel_id=1, source_target_pairs={{4,0},{8,4},{12,8},{16,12},{20,16},{24,20},{28,24},{5,1},{9,5},{13... | collective-permute-start | bytes 98312 | tf_op jit(solution)/shard_map/ppermute | solution.py:689
  31.6 4.5 %collective-permute-start.8 = (bf16[128,128]{1,0:T(8,128)(2,1)S(1)}, bf16[128,128]{1,0:T(8,128)(2,1)S(1)}, u32[]{:S(2)}, u32[]{:S(2)}) collective-permute-start(bf16[128,128]{1,0:T(8,128)(2,1)S(1)} %get-tuple-element.47.refs_7_.own_n), channel_id=1, source_target_pairs={{0,4},{4,8},{8,12},{12,16},{16,20},{20,24},{24,28},{1,5},{5,9},{9,... | collective-permute-start | bytes 98312 | tf_op jit(solution)/shard_map/ppermute | solution.py:690
  36.1 6.0 %collective-permute-done.4.refs_5_ = bf16[4,48,640]{2,1,0:T(8,128)(2,1)S(1)} collective-permute-done((bf16[4,48,640]{2,1,0:T(8,128)(2,1)}, bf16[4,48,640]{2,1,0:T(8,128)(2,1)S(1)}, u32[]{:S(2)}, u32[]{:S(2)}) %collective-permute-start.4) | collective-permute-done | bytes 245792 | tf_op jit(solution)/shard_map/ppermute | solution.py:666
  42.1 0.6 merge.1
  42.8 0.0 copy-start.3
  42.8 1.9 %collective-permute-start.9 = (bf16[136,640]{1,0:T(8,128)(2,1)S(1)}, bf16[136,640]{1,0:T(8,128)(2,1)S(1)}, u32[]{:S(2)}, u32[]{:S(2)}) collective-permute-start(bf16[136,640]{1,0:T(8,128)(2,1)S(1)} %get-tuple-element.57), channel_id=1, source_target_pairs={{0,4},{4,0},{8,12},{12,8},{1,5},{5,1},{9,13},{13,9},{2,6},{6,2},{1... | collective-permute-start | bytes 522248 | tf_op jit(solution)/shard_map/ppermute | solution.py:666
  44.7 3.3 %collective-permute-start.10 = (bf16[136,640]{1,0:T(8,128)(2,1)S(1)}, bf16[136,640]{1,0:T(8,128)(2,1)S(1)}, u32[]{:S(2)}, u32[]{:S(2)}) collective-permute-start(bf16[136,640]{1,0:T(8,128)(2,1)S(1)} %get-tuple-element.58), channel_id=1, source_target_pairs={{0,8},{4,12},{8,0},{12,4},{1,9},{5,13},{9,1},{13,5},{2,10},{6,14},... | collective-permute-start | bytes 522248 | tf_op jit(solution)/shard_map/ppermute | solution.py:666
  48.0 1.7 %edge_columns.1 = (bf16[192,128]{1,0:T(8,128)(2,1)S(1)}, bf16[192,128]{1,0:T(8,128)(2,1)S(1)}) custom-call(f32[2,16,128,128]{3,2,1,0:T(8,128)S(1)} %copy-done.1, f32[2,16,128,128]{3,2,1,0:T(8,128)S(1)} %copy-done, s32[128,128]{1,0:T(8,128)S(1)} %copy-done.2, bf16[128,128]{1,0:T(8,128)(2,1)S(1)} %collective-permute-done.7.from_n.refs_11_, ...), custom_call_target="tpu_custom_call" | custom-call | flops 4194304 | bytes 4194304 | tf_op jit(solution)/shard_map/edge_columns/pallas_call | solution.py:692
  49.8 1.4 %collective-permute-start.12 = (bf16[192,128]{1,0:T(8,128)(2,1)S(1)}, bf16[192,128]{1,0:T(8,128)(2,1)S(1)}, u32[]{:S(2)}, u32[]{:S(2)}) collective-permute-start(bf16[192,128]{1,0:T(8,128)(2,1)S(1)} %get-tuple-element.63.refs_10_.own_w), channel_id=1, source_target_pairs={{1,0},{2,1},{3,2},{5,4},{6,5},{7,6},{9,8},{10,9},{11,10},{13,12},{... | collective-permute-start | bytes 147464 | tf_op jit(solution)/shard_map/ppermute | solution.py:695
  51.2 3.0 %collective-permute-start.13 = (bf16[192,128]{1,0:T(8,128)(2,1)S(1)}, bf16[192,128]{1,0:T(8,128)(2,1)S(1)}, u32[]{:S(2)}, u32[]{:S(2)}) collective-permute-start(bf16[192,128]{1,0:T(8,128)(2,1)S(1)} %get-tuple-element.62.refs_9_.own_e), channel_id=1, source_target_pairs={{0,1},{1,2},{2,3},{4,5},{5,6},{6,7},{8,9},{9,10},{10,11},{12,13},{... | collective-permute-start | bytes 147464 | tf_op jit(solution)/shard_map/ppermute | solution.py:696
  54.3 0.7 slice.6.refs_4_
  55.0 0.7 slice.7.refs_5_
  55.8 5.0 %collective-permute-done.10.refs_2_ = bf16[136,640]{1,0:T(8,128)(2,1)S(1)} collective-permute-done((bf16[136,640]{1,0:T(8,128)(2,1)S(1)}, bf16[136,640]{1,0:T(8,128)(2,1)S(1)}, u32[]{:S(2)}, u32[]{:S(2)}) %collective-permute-start.10) | collective-permute-done | bytes 174112 | tf_op jit(solution)/shard_map/ppermute | solution.py:666
  60.8 0.6 copy-done.15
  61.4 0.1 copy-done.16
  61.5 3.3 %surface.1 = (bf16[32,40,128]{2,1,0:T(8,128)(2,1)}, f32[5,128,128]{2,1,0:T(8,128)}, f32[8,640]{1,0:T(8,128)}) custom-call(f32[136,640]{1,0:T(8,128)} %copy-done.3, bf16[136,640]{1,0:T(8,128)(2,1)} %copy-done.14, bf16[136,640]{1,0:T(8,128)(2,1)} %copy-done.15, bf16[136,640]{1,0:T(8,128)(2,1)} %copy-done.16, f32[1,3,128,128]{3,2,1,0:T(8,128)} %slice.6.refs_4_, ...), custom_call_target="tpu_custom_call" | custom-call | flops 4194304 | bytes 4194304 | tf_op jit(solution)/shard_map/surface/pallas_call | solution.py:702
  64.8 6.3 %all-to-all-start = ((bf16[32,40,128]{2,1,0:T(8,128)(2,1)}), bf16[32,40,128]{2,1,0:T(8,128)(2,1)S(1)}, u32[]{:S(2)}, u32[]{:S(2)}) async-start(bf16[32,40,128]{2,1,0:T(8,128)(2,1)} %get-tuple-element.67), calls=%async_computation | async-start | bytes 655360 | tf_op jit(solution)/shard_map/all_to_all | solution.py:709
  71.1 0.6 reshape.19.src
  71.7 12.6 %substeps.1 = f32[2,16,128,128]{3,2,1,0:T(8,128)} custom-call(f32[2,16,128,128]{3,2,1,0:T(8,128)} %tracers_in.1, f32[2,16,128,128]{3,2,1,0:T(8,128)} %currents_in.1, s32[128,128]{1,0:T(8,128)} %land.5, f32[5,128,128]{2,1,0:T(8,128)} %get-tuple-element.64.flux, f32[8,640]{1,0:T(8,128)} %get-tuple-element.65.rim, bf16[128,128]{1,0:T(8,128)(2,1)} %copy-done.10, ...), custom_call_target="tpu_custom_call" | custom-call | flops 16777216 | bytes 16777216 | tf_op jit(solution)/shard_map/substeps/pallas_call | solution.py:712
  84.4 0.7 copy-done.11
  85.1 9.3 %backward_remap.1 = f32[160,128]{1,0:T(8,128)} custom-call(s32[640]{0:T(1024)} %get-tuple-element.66.slots_in, s32[1,640]{1,0:T(1,128)} %reshape.19.src, bf16[32,40,128]{2,1,0:T(8,128)(2,1)} %copy-done.11, bf16[640,128,128]{2,1,0:T(8,128)(2,1)} %w.3), custom_call_target="tpu_custom_call" | custom-call | flops 167772160 | bytes 20971520 | tf_op jit(solution)/shard_map/backward_remap/pallas_call | solution.py:628
  (44 shorter events, 0.1 us)
Async XLA Ops:
  0.6 26.5 %copy-start = (f32[2,16,128,128]{3,2,1,0:T(8,128)S(1)}, f32[2,16,128,128]{3,2,1,0:T(8,128)}, u32[]{:S(2)}) copy-start(f32[2,16,128,128]{3,2,1,0:T(8,128)} %currents_in.1) | copy-start | bytes 6291460
  0.6 26.5 %copy-start.1 = (f32[2,16,128,128]{3,2,1,0:T(8,128)S(1)}, f32[2,16,128,128]{3,2,1,0:T(8,128)}, u32[]{:S(2)}) copy-start(f32[2,16,128,128]{3,2,1,0:T(8,128)} %tracers_in.1) | copy-start | bytes 6291460
  0.7 26.5 %copy-start.2 = (s32[128,128]{1,0:T(8,128)S(1)}, s32[128,128]{1,0:T(8,128)}, u32[]{:S(2)}) copy-start(s32[128,128]{1,0:T(8,128)} %land.5) | copy-start | bytes 196612
  15.3 4.9 %collective-permute-start = (bf16[4,48,640]{2,1,0:T(8,128)(2,1)}, bf16[4,48,640]{2,1,0:T(8,128)(2,1)S(1)}, u32[]{:S(2)}, u32[]{:S(2)}) collective-permute-start(bf16[4,48,640]{2,1,0:T(8,128)(2,1)} %get-tuple-element.36), channel_id=1, source_target_pairs={{0,1},{1,0},{2,3},{3,2},{16,17},{17,16},{18,19},{19,18},{4,5},{5,4... | collective-permute-start | bytes 737288 | tf_op jit(solution)/shard_map/ppermute | solution.py:666
  15.8 9.6 %collective-permute-start.1 = (bf16[4,48,640]{2,1,0:T(8,128)(2,1)}, bf16[4,48,640]{2,1,0:T(8,128)(2,1)S(1)}, u32[]{:S(2)}, u32[]{:S(2)}) collective-permute-start(bf16[4,48,640]{2,1,0:T(8,128)(2,1)} %get-tuple-element.38), channel_id=1, source_target_pairs={{0,2},{1,3},{2,0},{3,1},{16,18},{17,19},{18,16},{19,17},{4,6},{5,7... | collective-permute-start | bytes 737288 | tf_op jit(solution)/shard_map/ppermute | solution.py:666
  18.4 11.9 %collective-permute-start.2 = (bf16[4,48,640]{2,1,0:T(8,128)(2,1)}, bf16[4,48,640]{2,1,0:T(8,128)(2,1)S(1)}, u32[]{:S(2)}, u32[]{:S(2)}) collective-permute-start(bf16[4,48,640]{2,1,0:T(8,128)(2,1)} %get-tuple-element.39), channel_id=1, source_target_pairs={{0,3},{1,2},{2,1},{3,0},{16,19},{17,18},{18,17},{19,16},{4,7},{5,6... | collective-permute-start | bytes 737288 | tf_op jit(solution)/shard_map/ppermute | solution.py:666
  18.5 13.1 %collective-permute-start.3 = (bf16[4,48,640]{2,1,0:T(8,128)(2,1)}, bf16[4,48,640]{2,1,0:T(8,128)(2,1)S(1)}, u32[]{:S(2)}, u32[]{:S(2)}) collective-permute-start(bf16[4,48,640]{2,1,0:T(8,128)(2,1)} %get-tuple-element.40), channel_id=1, source_target_pairs={{0,16},{1,17},{2,18},{3,19},{16,0},{17,1},{18,2},{19,3},{4,20},{5,... | collective-permute-start | bytes 737288 | tf_op jit(solution)/shard_map/ppermute | solution.py:666
  20.2 21.8 %collective-permute-start.4 = (bf16[4,48,640]{2,1,0:T(8,128)(2,1)}, bf16[4,48,640]{2,1,0:T(8,128)(2,1)S(1)}, u32[]{:S(2)}, u32[]{:S(2)}) collective-permute-start(bf16[4,48,640]{2,1,0:T(8,128)(2,1)} %get-tuple-element.41), channel_id=1, source_target_pairs={{0,17},{1,16},{2,19},{3,18},{16,1},{17,0},{18,3},{19,2},{4,21},{5,... | collective-permute-start | bytes 737288 | tf_op jit(solution)/shard_map/ppermute | solution.py:666
  20.3 21.8 %collective-permute-start.5 = (bf16[4,48,640]{2,1,0:T(8,128)(2,1)}, bf16[4,48,640]{2,1,0:T(8,128)(2,1)S(1)}, u32[]{:S(2)}, u32[]{:S(2)}) collective-permute-start(bf16[4,48,640]{2,1,0:T(8,128)(2,1)} %get-tuple-element.42), channel_id=1, source_target_pairs={{0,18},{1,19},{2,16},{3,17},{16,2},{17,3},{18,0},{19,1},{4,22},{5,... | collective-permute-start | bytes 737288 | tf_op jit(solution)/shard_map/ppermute | solution.py:666
  25.4 16.7 %collective-permute-start.6 = (bf16[4,48,640]{2,1,0:T(8,128)(2,1)}, bf16[4,48,640]{2,1,0:T(8,128)(2,1)S(1)}, u32[]{:S(2)}, u32[]{:S(2)}) collective-permute-start(bf16[4,48,640]{2,1,0:T(8,128)(2,1)} %get-tuple-element.43), channel_id=1, source_target_pairs={{0,19},{1,18},{2,17},{3,16},{16,3},{17,2},{18,1},{19,0},{4,23},{5,... | collective-permute-start | bytes 737288 | tf_op jit(solution)/shard_map/ppermute | solution.py:666
  27.1 15.0 %copy-start.6 = (bf16[4,48,640]{2,1,0:T(8,128)(2,1)S(1)}, bf16[4,48,640]{2,1,0:T(8,128)(2,1)}, u32[]{:S(2)}) copy-start(bf16[4,48,640]{2,1,0:T(8,128)(2,1)} %get-tuple-element.48.refs_0_) | copy-start | bytes 737284
  27.2 22.5 %copy-start.9 = (bf16[128,128]{1,0:T(8,128)(2,1)}, bf16[128,128]{1,0:T(8,128)(2,1)S(1)}, u32[]{:S(2)}) copy-start(bf16[128,128]{1,0:T(8,128)(2,1)S(1)} %get-tuple-element.46.refs_8_.own_s) | copy-start | bytes 98308
  27.2 22.5 %copy-start.10 = (bf16[128,128]{1,0:T(8,128)(2,1)}, bf16[128,128]{1,0:T(8,128)(2,1)S(1)}, u32[]{:S(2)}) copy-start(bf16[128,128]{1,0:T(8,128)(2,1)S(1)} %get-tuple-element.47.refs_7_.own_n) | copy-start | bytes 98308
  30.3 11.8 %collective-permute-start.7 = (bf16[128,128]{1,0:T(8,128)(2,1)S(1)}, bf16[128,128]{1,0:T(8,128)(2,1)S(1)}, u32[]{:S(2)}, u32[]{:S(2)}) collective-permute-start(bf16[128,128]{1,0:T(8,128)(2,1)S(1)} %get-tuple-element.46.refs_8_.own_s), channel_id=1, source_target_pairs={{4,0},{8,4},{12,8},{16,12},{20,16},{24,20},{28,24},{5,1},{9,5},{13... | collective-permute-start | bytes 98312 | tf_op jit(solution)/shard_map/ppermute | solution.py:689
  31.6 10.5 %collective-permute-start.8 = (bf16[128,128]{1,0:T(8,128)(2,1)S(1)}, bf16[128,128]{1,0:T(8,128)(2,1)S(1)}, u32[]{:S(2)}, u32[]{:S(2)}) collective-permute-start(bf16[128,128]{1,0:T(8,128)(2,1)S(1)} %get-tuple-element.47.refs_7_.own_n), channel_id=1, source_target_pairs={{0,4},{4,8},{8,12},{12,16},{16,20},{20,24},{24,28},{1,5},{5,9},{9,... | collective-permute-start | bytes 98312 | tf_op jit(solution)/shard_map/ppermute | solution.py:690
  42.1 7.7 %copy-start.4 = (bf16[128,128]{1,0:T(8,128)(2,1)}, bf16[128,128]{1,0:T(8,128)(2,1)S(1)}, u32[]{:S(2)}) copy-start(bf16[128,128]{1,0:T(8,128)(2,1)S(1)} %collective-permute-done.7.from_n.refs_11_) | copy-start | bytes 98308
  42.1 7.7 %copy-start.5 = (bf16[128,128]{1,0:T(8,128)(2,1)}, bf16[128,128]{1,0:T(8,128)(2,1)S(1)}, u32[]{:S(2)}) copy-start(bf16[128,128]{1,0:T(8,128)(2,1)S(1)} %collective-permute-done.8.from_s.refs_12_) | copy-start | bytes 98308
  42.8 7.0 %copy-start.3 = (f32[136,640]{1,0:T(8,128)}, f32[136,640]{1,0:T(8,128)S(1)}, u32[]{:S(2)}) copy-start(f32[136,640]{1,0:T(8,128)S(1)} %get-tuple-element.56.refs_0_) | copy-start | bytes 1044484
  42.8 13.0 %collective-permute-start.9 = (bf16[136,640]{1,0:T(8,128)(2,1)S(1)}, bf16[136,640]{1,0:T(8,128)(2,1)S(1)}, u32[]{:S(2)}, u32[]{:S(2)}) collective-permute-start(bf16[136,640]{1,0:T(8,128)(2,1)S(1)} %get-tuple-element.57), channel_id=1, source_target_pairs={{0,4},{4,0},{8,12},{12,8},{1,5},{5,1},{9,13},{13,9},{2,6},{6,2},{1... | collective-permute-start | bytes 522248 | tf_op jit(solution)/shard_map/ppermute | solution.py:666
  44.7 16.1 %collective-permute-start.10 = (bf16[136,640]{1,0:T(8,128)(2,1)S(1)}, bf16[136,640]{1,0:T(8,128)(2,1)S(1)}, u32[]{:S(2)}, u32[]{:S(2)}) collective-permute-start(bf16[136,640]{1,0:T(8,128)(2,1)S(1)} %get-tuple-element.58), channel_id=1, source_target_pairs={{0,8},{4,12},{8,0},{12,4},{1,9},{5,13},{9,1},{13,5},{2,10},{6,14},... | collective-permute-start | bytes 522248 | tf_op jit(solution)/shard_map/ppermute | solution.py:666
  48.0 12.7 %collective-permute-start.11 = (bf16[136,640]{1,0:T(8,128)(2,1)S(1)}, bf16[136,640]{1,0:T(8,128)(2,1)S(1)}, u32[]{:S(2)}, u32[]{:S(2)}) collective-permute-start(bf16[136,640]{1,0:T(8,128)(2,1)S(1)} %get-tuple-element.59), channel_id=1, source_target_pairs={{0,12},{4,8},{8,4},{12,0},{1,13},{5,9},{9,5},{13,1},{2,14},{6,10},... | collective-permute-start | bytes 522248 | tf_op jit(solution)/shard_map/ppermute | solution.py:666
  49.8 11.0 %copy-start.7 = (bf16[192,128]{1,0:T(8,128)(2,1)}, bf16[192,128]{1,0:T(8,128)(2,1)S(1)}, u32[]{:S(2)}) copy-start(bf16[192,128]{1,0:T(8,128)(2,1)S(1)} %get-tuple-element.63.refs_10_.own_w) | copy-start | bytes 147460
  49.8 11.0 %copy-start.8 = (bf16[192,128]{1,0:T(8,128)(2,1)}, bf16[192,128]{1,0:T(8,128)(2,1)S(1)}, u32[]{:S(2)}) copy-start(bf16[192,128]{1,0:T(8,128)(2,1)S(1)} %get-tuple-element.62.refs_9_.own_e) | copy-start | bytes 147460
  49.8 21.3 %copy-start.17 = (s32[640]{0:T(1024)S(1)}, s32[640]{0:T(1024)}, u32[]{:S(2)}) copy-start(s32[640]{0:T(1024)} %src.1) | copy-start | bytes 7684
  49.8 5.9 %collective-permute-start.12 = (bf16[192,128]{1,0:T(8,128)(2,1)S(1)}, bf16[192,128]{1,0:T(8,128)(2,1)S(1)}, u32[]{:S(2)}, u32[]{:S(2)}) collective-permute-start(bf16[192,128]{1,0:T(8,128)(2,1)S(1)} %get-tuple-element.63.refs_10_.own_w), channel_id=1, source_target_pairs={{1,0},{2,1},{3,2},{5,4},{6,5},{7,6},{9,8},{10,9},{11,10},{13,12},{... | collective-permute-start | bytes 147464 | tf_op jit(solution)/shard_map/ppermute | solution.py:695
  51.2 4.5 %collective-permute-start.13 = (bf16[192,128]{1,0:T(8,128)(2,1)S(1)}, bf16[192,128]{1,0:T(8,128)(2,1)S(1)}, u32[]{:S(2)}, u32[]{:S(2)}) collective-permute-start(bf16[192,128]{1,0:T(8,128)(2,1)S(1)} %get-tuple-element.62.refs_9_.own_e), channel_id=1, source_target_pairs={{0,1},{1,2},{2,3},{4,5},{5,6},{6,7},{8,9},{9,10},{10,11},{12,13},{... | collective-permute-start | bytes 147464 | tf_op jit(solution)/shard_map/ppermute | solution.py:696
  55.7 5.1 %copy-start.12 = (bf16[192,128]{1,0:T(8,128)(2,1)}, bf16[192,128]{1,0:T(8,128)(2,1)S(1)}, u32[]{:S(2)}) copy-start(bf16[192,128]{1,0:T(8,128)(2,1)S(1)} %collective-permute-done.12.refs_13_.from_e) | copy-start | bytes 147460
  55.7 5.1 %copy-start.13 = (bf16[192,128]{1,0:T(8,128)(2,1)}, bf16[192,128]{1,0:T(8,128)(2,1)S(1)}, u32[]{:S(2)}) copy-start(bf16[192,128]{1,0:T(8,128)(2,1)S(1)} %collective-permute-done.13.refs_14_.from_w) | copy-start | bytes 147460
  55.7 5.1 %copy-start.14 = (bf16[136,640]{1,0:T(8,128)(2,1)}, bf16[136,640]{1,0:T(8,128)(2,1)S(1)}, u32[]{:S(2)}) copy-start(bf16[136,640]{1,0:T(8,128)(2,1)S(1)} %collective-permute-done.9.refs_1_) | copy-start | bytes 522244
  60.8 0.7 copy-start.16
  64.8 19.6 %all-to-all-start = ((bf16[32,40,128]{2,1,0:T(8,128)(2,1)}), bf16[32,40,128]{2,1,0:T(8,128)(2,1)S(1)}, u32[]{:S(2)}, u32[]{:S(2)}) async-start(bf16[32,40,128]{2,1,0:T(8,128)(2,1)} %get-tuple-element.67), calls=%async_computation | async-start | bytes 655360 | tf_op jit(solution)/shard_map/all_to_all | solution.py:709
  84.3 0.7 copy-start.11
  (1 other events, 0.7 us)

commit v8 on v7

--- a/solution.py
+++ b/solution.py
@@ -164,8 +164,11 @@
 
     lax.fori_loop(0, devices // group, owners, 0)
 
-    for m, send in enumerate(sends):
-        send[...] = xs[m * n_gx : (m + 1) * n_gx].astype(BF16)
+    half = n_gx // 2
+    planes = n_sec * n_gy
+    for m in range(planes):
+        sends[m][...] = xs[m * n_gx + half : (m + 1) * n_gx].astype(BF16)
+        sends[planes + m][...] = xs[m * n_gx : m * n_gx + half].astype(BF16)
 
 
 def forward(flux, w, src, own, dst, grid, cap, parts=20):
@@ -178,7 +181,7 @@
     return pl.pallas_call(
         functools.partial(forward_kernel, parts, cap, grid),
         in_specs=[SMEM, SMEM, SMEM, VMEM, ANY],
-        out_specs=[VMEM] * (n_sec * n_gy) + [SMEM],
+        out_specs=[VMEM] * (2 * n_sec * n_gy) + [SMEM],
         scratch_shapes=[
             pltpu.VMEM(w.shape, BF16),
             pltpu.VMEM(flux.shape, BF16),
@@ -189,7 +192,7 @@
             pltpu.SMEM((devices,), jnp.int32),
             pltpu.SemaphoreType.DMA((parts,)),
         ],
-        out_shape=[jax.ShapeDtypeStruct((n_gx, chunk, wide), BF16)] * (n_sec * n_gy) + [jax.ShapeDtypeStruct((total,), jnp.int32)],
+        out_shape=[jax.ShapeDtypeStruct((n_gx // 2, chunk, wide), BF16)] * (2 * n_sec * n_gy) + [jax.ShapeDtypeStruct((total,), jnp.int32)],
         compiler_params=kernel_params(58),
         cost_estimate=pl.CostEstimate(flops=2 * total * 8 * width * width, bytes_accessed=total * width * width * 2, transcendentals=0),
         name="forward_remap",
@@ -638,7 +641,7 @@
             pltpu.SemaphoreType.DMA((parts + 1,)),
         ],
         out_shape=jax.ShapeDtypeStruct((blocks, width), F32),
-        compiler_params=kernel_params(58),
+        compiler_params=kernel_params(46),
         cost_estimate=pl.CostEstimate(flops=2 * total * 8 * width * width, bytes_accessed=total * width * width * 2, transcendentals=0),
         name="backward_remap",
     )(slots, src.reshape(1, total), back, w)
@@ -676,27 +679,38 @@
 
     *sends, slots = forward(atm_flux, remap_weights, remap_src, remap_owner.reshape(1, total), remap_dst, grid, cap)
     chunk = sends[0].shape[1]
-    got = [sends[0]] + [swapped(sends[m], ("sec", "gy"), planes, m) for m in range(1, planes)]
+    far_sends, near_sends = sends[:planes], sends[planes:]
+
+    def in_plane(chunks):
+        return [chunks[0]] + [swapped(chunks[m], ("sec", "gy"), planes, m) for m in range(1, planes)]
+
+    def merge(chunks, dtypes):
+        outs = [((height + 8, wide), dtype) for dtype in dtypes]
+        return kernel(functools.partial(merge_kernel, planes), outs, "merge", 24, 1 << 22)(*chunks)
+
+    far = in_plane(far_sends)
+    far[1], near_sends, tracers_there, currents_there = lax.optimization_barrier((far[1], near_sends, tracers, currents))
+    near = in_plane(near_sends)
 
     side = (width, width)
     end = (7 * levels + 80, width)
     to_north, to_south = neighbours(NORTH)
     to_east, to_west = neighbours("gy")
-    got[1], tracers_there, currents_there = lax.optimization_barrier((got[1], tracers, currents))
     own_s, own_n = kernel(rows_kernel, [(side, BF16)] * 2, "edge_rows", 16, 1 << 20)(
         tracers_there.reshape(-1, width), currents_there.reshape(-1, width), land_sea
     )
     from_n = lax.ppermute(own_s, NORTH, to_south)
     from_s = lax.ppermute(own_n, NORTH, to_north)
-    got, from_n, from_s = lax.optimization_barrier((got, from_n, from_s))
+    far = merge(far, [BF16] * (n_gx // 2))
+    far, from_n, from_s = lax.optimization_barrier((far, from_n, from_s))
+    far = [swapped(part, "gx", n_gx, n_gx // 2 + m) for m, part in enumerate(far)]
     own_w, own_e = kernel(columns_kernel, [(end, BF16)] * 2, "edge_columns", 16, 1 << 22, [pltpu.VMEM(end, F32)] * 2)(
         tracers, currents, land_sea, from_n, from_s
     )
     from_e = lax.ppermute(own_w, "gy", to_west)
     from_w = lax.ppermute(own_e, "gy", to_east)
-    part = (height + 8, wide)
-    merged = kernel(functools.partial(merge_kernel, planes), [(part, F32)] + [(part, BF16)] * (n_gx - 1), "merge", 24, 1 << 22)(*got)
-    parts = [merged[0]] + [swapped(merged[m], "gx", n_gx, m) for m in range(1, n_gx)]
+    near = merge(near, [F32] + [BF16] * (n_gx // 2 - 1))
+    parts = [near[0]] + [swapped(near[m], "gx", n_gx, m) for m in range(1, n_gx // 2)] + far
 
     edges = own_n, own_s, own_e, own_w, from_n, from_s, from_e, from_w
     back, flux, rim = kernel(

time: 94.7 us -> 96.2 us (1.016)
  starting transfers between devices: 31.1 us -> 43.9 us
  waiting for transfers between devices: 16.6 us -> 7.29 us
  local copies, waits for them, and re-layouts: 3.51 us -> 2.13 us
    ppermute x10 -> x17, starting transfers between devices: 14.5 us -> 30.7 us  [swapped(): return lax.ppermute(array, axes, [(i, i ^ step) for i in range(count)])]
    ppermute x10 -> x17, waiting for transfers between devices: 16.5 us -> 6.1 us  [swapped(): return lax.ppermute(array, axes, [(i, i ^ step) for i in range(count)])]
    ppermute x1, starting transfers between devices: 3.03 us -> 1.42 us  [on_device(): from_w = lax.ppermute(own_e, 'gy', to_east)]
    all_to_all x1, starting transfers between devices: 6.33 us -> 4.74 us  [on_device(): lax.all_to_all(back, EVERY, split_axis=0, concat_axis=0, tiled=True)]
    ppermute x1, waiting for transfers between devices: 0.01 us -> 1.18 us  [on_device(): from_e = lax.ppermute(own_w, 'gy', to_west)]
    pallas_call x1, Pallas kernels: 9.27 us -> 8.3 us  [backward(): pl.pallas_call(functools.partial(backward_kernel, parts), in_specs=[ANY,...]
  transfers between devices with their start and end apart: 15 -> 22, of which waited for: 4 -> 4; matrix products, arithmetic and copies ran while one was open for 2% -> 1% of each run, Pallas kernels for 15% -> 16%
where the time goes in v8:
time: 96.2 us; the launch traced here: 95.8 us
  starting transfers between devices  43.9 us (46%)
  Pallas kernels  41.4 us (43%)
  waiting for transfers between devices  7.29 us (8%)
  local copies, waits for them, and re-layouts  2.13 us (2%)
  between operations  1.04 us (1%)
    ppermute x17, starting transfers between devices, swapped(): return lax.ppermute(array, axes, [(i, i ^ step) for i in range(count)])  30.7 us
    pallas_call x1, Pallas kernels, forward(): pl.pallas_call(functools.partial(forward_kernel, parts, cap, grid), in_sp...  14.6 us
    pallas_call x1, Pallas kernels, on_device(): kernel(stencil_kernel, [(tracers.shape, F32)], 'substeps', 58, 1 << 24, [...  12.6 us
    pallas_call x1, Pallas kernels, backward(): pl.pallas_call(functools.partial(backward_kernel, parts), in_specs=[ANY,...  8.3 us
    ppermute x17, waiting for transfers between devices, swapped(): return lax.ppermute(array, axes, [(i, i ^ step) for i in range(count)])  6.1 us
    all_to_all x1, starting transfers between devices, on_device(): lax.all_to_all(back, EVERY, split_axis=0, concat_axis=0, tiled=True)  4.74 us
    ppermute x1, starting transfers between devices, on_device(): from_s = lax.ppermute(own_n, NORTH, to_north)  4.55 us
    pallas_call x1, Pallas kernels, on_device(): kernel(functools.partial(surface_kernel, grid, chunk, levels), [((planes...  3.27 us
  transfers between devices with their start and end apart: 22, of which 4 were waited for; matrix products, arithmetic and copies ran while one was open for 1% of the time, Pallas kernels for 16%

profile of v8, /device:TPU:0, one launch (start us, length us, event | category | flops | bytes accessed | tf_op | source)
XLA Modules:
  0.0 95.8 jit_solution(10784408500745474083)
XLA Ops:
  0.7 14.6 %forward_remap.1 = (bf16[2,48,640]{2,1,0:T(8,128)(2,1)}, bf16[2,48,640]{2,1,0:T(8,128)(2,1)}, bf16[2,48,640]{2,1,0:T(8,128)(2,1)}, bf16[2,48,640]{2,1,0:T(8,128)...) custom-call(s32[640]{0:T(1024)} %src.1, ...), custom_call_target="tpu_custom_call" | custom-call | flops 167772160 | bytes 20971520 | tf_op jit(solution)/shard_map/forward_remap/pallas_call | solution.py:181
  15.3 0.5 collective-permute-start
  15.8 2.6 %collective-permute-start.9 = (bf16[2,48,640]{2,1,0:T(8,128)(2,1)}, bf16[2,48,640]{2,1,0:T(8,128)(2,1)S(1)}, u32[]{:S(2)}, u32[]{:S(2)}) collective-permute-start(bf16[2,48,640]{2,1,0:T(8,128)(2,1)} %get-tuple-element.66), channel_id=1, source_target_pairs={{0,2},{1,3},{2,0},{3,1},{16,18},{17,19},{18,16},{19,17},{4,6},{5,7... | collective-permute-start | bytes 368648 | tf_op jit(solution)/shard_map/ppermute | solution.py:669
  18.5 1.8 %collective-permute-start.11 = (bf16[2,48,640]{2,1,0:T(8,128)(2,1)}, bf16[2,48,640]{2,1,0:T(8,128)(2,1)S(1)}, u32[]{:S(2)}, u32[]{:S(2)}) collective-permute-start(bf16[2,48,640]{2,1,0:T(8,128)(2,1)} %get-tuple-element.68), channel_id=1, source_target_pairs={{0,16},{1,17},{2,18},{3,19},{16,0},{17,1},{18,2},{19,3},{4,20},{5,... | collective-permute-start | bytes 368648 | tf_op jit(solution)/shard_map/ppermute | solution.py:669
  20.2 2.6 %collective-permute-start.13 = (bf16[2,48,640]{2,1,0:T(8,128)(2,1)}, bf16[2,48,640]{2,1,0:T(8,128)(2,1)S(1)}, u32[]{:S(2)}, u32[]{:S(2)}) collective-permute-start(bf16[2,48,640]{2,1,0:T(8,128)(2,1)} %get-tuple-element.70), channel_id=1, source_target_pairs={{0,18},{1,19},{2,16},{3,17},{16,2},{17,3},{18,0},{19,1},{4,22},{5,... | collective-permute-start | bytes 368648 | tf_op jit(solution)/shard_map/ppermute | solution.py:669
  22.9 1.6 %collective-permute-start.14 = (bf16[2,48,640]{2,1,0:T(8,128)(2,1)}, bf16[2,48,640]{2,1,0:T(8,128)(2,1)S(1)}, u32[]{:S(2)}, u32[]{:S(2)}) collective-permute-start(bf16[2,48,640]{2,1,0:T(8,128)(2,1)} %get-tuple-element.71), channel_id=1, source_target_pairs={{0,19},{1,18},{2,17},{3,16},{16,3},{17,2},{18,1},{19,0},{4,23},{5,... | collective-permute-start | bytes 368648 | tf_op jit(solution)/shard_map/ppermute | solution.py:669
  24.5 0.5 collective-permute-done.10.refs_3_
  25.0 0.8 collective-permute-start.1
  25.8 1.7 %collective-permute-start.2 = (bf16[2,48,640]{2,1,0:T(8,128)(2,1)}, bf16[2,48,640]{2,1,0:T(8,128)(2,1)S(1)}, u32[]{:S(2)}, u32[]{:S(2)}) collective-permute-start(bf16[2,48,640]{2,1,0:T(8,128)(2,1)} %get-tuple-element.56), channel_id=1, source_target_pairs={{0,2},{1,3},{2,0},{3,1},{16,18},{17,19},{18,16},{19,17},{4,6},{5,7... | collective-permute-start | bytes 368648 | tf_op jit(solution)/shard_map/ppermute | solution.py:669
  27.7 3.9 %collective-permute-done.12.refs_5_ = bf16[2,48,640]{2,1,0:T(8,128)(2,1)S(1)} collective-permute-done((bf16[2,48,640]{2,1,0:T(8,128)(2,1)}, bf16[2,48,640]{2,1,0:T(8,128)(2,1)S(1)}, u32[]{:S(2)}, u32[]{:S(2)}) %collective-permute-start.12) | collective-permute-done | bytes 122912 | tf_op jit(solution)/shard_map/ppermute | solution.py:669
  31.5 1.3 %collective-permute-start.15 = (bf16[128,128]{1,0:T(8,128)(2,1)S(1)}, bf16[128,128]{1,0:T(8,128)(2,1)S(1)}, u32[]{:S(2)}, u32[]{:S(2)}) collective-permute-start(bf16[128,128]{1,0:T(8,128)(2,1)S(1)} %get-tuple-element.76.refs_8_.own_s), channel_id=1, source_target_pairs={{4,0},{8,4},{12,8},{16,12},{20,16},{24,20},{28,24},{5,1},{9,5},{13... | collective-permute-start | bytes 98312 | tf_op jit(solution)/shard_map/ppermute | solution.py:702
  32.8 4.5 %collective-permute-start.16 = (bf16[128,128]{1,0:T(8,128)(2,1)S(1)}, bf16[128,128]{1,0:T(8,128)(2,1)S(1)}, u32[]{:S(2)}, u32[]{:S(2)}) collective-permute-start(bf16[128,128]{1,0:T(8,128)(2,1)S(1)} %get-tuple-element.77.refs_7_.own_n), channel_id=1, source_target_pairs={{0,4},{4,8},{8,12},{12,16},{16,20},{20,24},{24,28},{1,5},{5,9},{9,... | collective-permute-start | bytes 98312 | tf_op jit(solution)/shard_map/ppermute | solution.py:703
  37.4 1.6 %collective-permute-start.3 = (bf16[2,48,640]{2,1,0:T(8,128)(2,1)S(1)}, bf16[2,48,640]{2,1,0:T(8,128)(2,1)S(1)}, u32[]{:S(2)}, u32[]{:S(2)}) collective-permute-start(bf16[2,48,640]{2,1,0:T(8,128)(2,1)S(1)} %copy-done.23), channel_id=1, source_target_pairs={{0,3},{1,2},{2,1},{3,0},{16,19},{17,18},{18,17},{19,16},{4,7},{5,6... | collective-permute-start | bytes 368648 | tf_op jit(solution)/shard_map/ppermute | solution.py:669
  39.0 3.4 %collective-permute-start.4 = (bf16[2,48,640]{2,1,0:T(8,128)(2,1)S(1)}, bf16[2,48,640]{2,1,0:T(8,128)(2,1)S(1)}, u32[]{:S(2)}, u32[]{:S(2)}) collective-permute-start(bf16[2,48,640]{2,1,0:T(8,128)(2,1)S(1)} %copy-done.22), channel_id=1, source_target_pairs={{0,16},{1,17},{2,18},{3,19},{16,0},{17,1},{18,2},{19,3},{4,20},{5,... | collective-permute-start | bytes 368648 | tf_op jit(solution)/shard_map/ppermute | solution.py:669
  42.4 4.1 %collective-permute-start.5 = (bf16[2,48,640]{2,1,0:T(8,128)(2,1)S(1)}, bf16[2,48,640]{2,1,0:T(8,128)(2,1)S(1)}, u32[]{:S(2)}, u32[]{:S(2)}) collective-permute-start(bf16[2,48,640]{2,1,0:T(8,128)(2,1)S(1)} %copy-done.21), channel_id=1, source_target_pairs={{0,17},{1,16},{2,19},{3,18},{16,1},{17,0},{18,3},{19,2},{4,21},{5,... | collective-permute-start | bytes 368648 | tf_op jit(solution)/shard_map/ppermute | solution.py:669
  46.5 1.7 %collective-permute-start.6 = (bf16[2,48,640]{2,1,0:T(8,128)(2,1)S(1)}, bf16[2,48,640]{2,1,0:T(8,128)(2,1)S(1)}, u32[]{:S(2)}, u32[]{:S(2)}) collective-permute-start(bf16[2,48,640]{2,1,0:T(8,128)(2,1)S(1)} %copy-done.20), channel_id=1, source_target_pairs={{0,18},{1,19},{2,16},{3,17},{16,2},{17,3},{18,0},{19,1},{4,22},{5,... | collective-permute-start | bytes 368648 | tf_op jit(solution)/shard_map/ppermute | solution.py:669
  48.2 1.4 %collective-permute-start.7 = (bf16[2,48,640]{2,1,0:T(8,128)(2,1)S(1)}, bf16[2,48,640]{2,1,0:T(8,128)(2,1)S(1)}, u32[]{:S(2)}, u32[]{:S(2)}) collective-permute-start(bf16[2,48,640]{2,1,0:T(8,128)(2,1)S(1)} %copy-done.19), channel_id=1, source_target_pairs={{0,19},{1,18},{2,17},{3,16},{16,3},{17,2},{18,1},{19,0},{4,23},{5,... | collective-permute-start | bytes 368648 | tf_op jit(solution)/shard_map/ppermute | solution.py:669
  49.6 0.4 merge.3
  50.1 6.7 %collective-permute-start.18 = (bf16[136,640]{1,0:T(8,128)(2,1)S(1)}, bf16[136,640]{1,0:T(8,128)(2,1)S(1)}, u32[]{:S(2)}, u32[]{:S(2)}) collective-permute-start(bf16[136,640]{1,0:T(8,128)(2,1)S(1)} %get-tuple-element.79), channel_id=1, source_target_pairs={{0,12},{4,8},{8,4},{12,0},{1,13},{5,9},{9,5},{13,1},{2,14},{6,10},... | collective-permute-start | bytes 522248 | tf_op jit(solution)/shard_map/ppermute | solution.py:669
  56.8 0.4 merge.2
  57.4 1.7 %edge_columns.1 = (bf16[192,128]{1,0:T(8,128)(2,1)S(1)}, bf16[192,128]{1,0:T(8,128)(2,1)S(1)}) custom-call(f32[2,16,128,128]{3,2,1,0:T(8,128)S(1)} %copy-done.1, f32[2,16,128,128]{3,2,1,0:T(8,128)S(1)} %copy-done, s32[128,128]{1,0:T(8,128)S(1)} %copy-done.2, bf16[128,128]{1,0:T(8,128)(2,1)S(1)} %collective-permute-done.15.from_n.refs_11_, ...), custom_call_target="tpu_custom_call" | custom-call | flops 4194304 | bytes 4194304 | tf_op jit(solution)/shard_map/edge_columns/pallas_call | solution.py:707
  59.1 1.4 %collective-permute-start.20 = (bf16[192,128]{1,0:T(8,128)(2,1)S(1)}, bf16[192,128]{1,0:T(8,128)(2,1)S(1)}, u32[]{:S(2)}, u32[]{:S(2)}) collective-permute-start(bf16[192,128]{1,0:T(8,128)(2,1)S(1)} %get-tuple-element.82.refs_9_.own_e), channel_id=1, source_target_pairs={{0,1},{1,2},{2,3},{4,5},{5,6},{6,7},{8,9},{9,10},{10,11},{12,13},{... | collective-permute-start | bytes 147464 | tf_op jit(solution)/shard_map/ppermute | solution.py:711
  60.6 1.3 %collective-permute-start.19 = (bf16[192,128]{1,0:T(8,128)(2,1)S(1)}, bf16[192,128]{1,0:T(8,128)(2,1)S(1)}, u32[]{:S(2)}, u32[]{:S(2)}) collective-permute-start(bf16[192,128]{1,0:T(8,128)(2,1)S(1)} %get-tuple-element.83.refs_10_.own_w), channel_id=1, source_target_pairs={{1,0},{2,1},{3,2},{5,4},{6,5},{7,6},{9,8},{10,9},{11,10},{13,12},{... | collective-permute-start | bytes 147464 | tf_op jit(solution)/shard_map/ppermute | solution.py:710
  61.9 0.7 slice.6.refs_4_
  62.6 0.7 slice.7.refs_5_
  63.3 1.2 %collective-permute-done.19.refs_13_.from_e = bf16[192,128]{1,0:T(8,128)(2,1)S(1)} collective-permute-done((bf16[192,128]{1,0:T(8,128)(2,1)S(1)}, bf16[192,128]{1,0:T(8,128)(2,1)S(1)}, u32[]{:S(2)}, u32[]{:S(2)}) %collective-permute-start.19) | collective-permute-done | bytes 49184 | tf_op jit(solution)/shard_map/ppermute | solution.py:710
  64.5 1.7 %collective-permute-done.8.refs_1_ = bf16[136,640]{1,0:T(8,128)(2,1)S(1)} collective-permute-done((bf16[136,640]{1,0:T(8,128)(2,1)S(1)}, bf16[136,640]{1,0:T(8,128)(2,1)S(1)}, u32[]{:S(2)}, u32[]{:S(2)}) %collective-permute-start.8) | collective-permute-done | bytes 174112 | tf_op jit(solution)/shard_map/ppermute | solution.py:669
  66.2 0.6 copy-done.17
  66.9 3.3 %surface.1 = (bf16[32,40,128]{2,1,0:T(8,128)(2,1)}, f32[5,128,128]{2,1,0:T(8,128)}, f32[8,640]{1,0:T(8,128)}) custom-call(f32[136,640]{1,0:T(8,128)} %copy-done.3, bf16[136,640]{1,0:T(8,128)(2,1)} %copy-done.17, bf16[136,640]{1,0:T(8,128)(2,1)} %copy-done.15, bf16[136,640]{1,0:T(8,128)(2,1)} %copy-done.16, f32[1,3,128,128]{3,2,1,0:T(8,128)} %slice.6.refs_4_, ...), custom_call_target="tpu_custom_call" | custom-call | flops 4194304 | bytes 4194304 | tf_op jit(solution)/shard_map/surface/pallas_call | solution.py:716
  70.1 4.7 %all-to-all-start = ((bf16[32,40,128]{2,1,0:T(8,128)(2,1)}), bf16[32,40,128]{2,1,0:T(8,128)(2,1)S(1)}, u32[]{:S(2)}, u32[]{:S(2)}) async-start(bf16[32,40,128]{2,1,0:T(8,128)(2,1)} %get-tuple-element.87), calls=%async_computation | async-start | bytes 655360 | tf_op jit(solution)/shard_map/all_to_all | solution.py:723
  74.9 12.6 %substeps.1 = f32[2,16,128,128]{3,2,1,0:T(8,128)} custom-call(f32[2,16,128,128]{3,2,1,0:T(8,128)} %tracers_in.1, f32[2,16,128,128]{3,2,1,0:T(8,128)} %currents_in.1, s32[128,128]{1,0:T(8,128)} %land.5, f32[5,128,128]{2,1,0:T(8,128)} %get-tuple-element.84.flux, f32[8,640]{1,0:T(8,128)} %get-tuple-element.85.rim, bf16[128,128]{1,0:T(8,128)(2,1)} %copy-done.9, ...), custom_call_target="tpu_custom_call" | custom-call | flops 16777216 | bytes 16777216 | tf_op jit(solution)/shard_map/substeps/pallas_call | solution.py:726
  87.5 8.3 %backward_remap.1 = f32[160,128]{1,0:T(8,128)} custom-call(s32[640]{0:T(1024)S(1)} %copy-done.12, s32[1,640]{1,0:T(1,128)S(1)} %reshape.19.src, bf16[32,40,128]{2,1,0:T(8,128)(2,1)S(1)} %all-to-all-done.back, bf16[640,128,128]{2,1,0:T(8,128)(2,1)} %w.3), custom_call_target="tpu_custom_call" | custom-call | flops 167772160 | bytes 20971520 | tf_op jit(solution)/shard_map/backward_remap/pallas_call | solution.py:631
  (71 shorter events, 0.4 us)
Async XLA Ops:
  0.6 26.9 %copy-start = (f32[2,16,128,128]{3,2,1,0:T(8,128)S(1)}, f32[2,16,128,128]{3,2,1,0:T(8,128)}, u32[]{:S(2)}) copy-start(f32[2,16,128,128]{3,2,1,0:T(8,128)} %currents_in.1) | copy-start | bytes 6291460
  0.6 26.8 %copy-start.1 = (f32[2,16,128,128]{3,2,1,0:T(8,128)S(1)}, f32[2,16,128,128]{3,2,1,0:T(8,128)}, u32[]{:S(2)}) copy-start(f32[2,16,128,128]{3,2,1,0:T(8,128)} %tracers_in.1) | copy-start | bytes 6291460
  0.7 26.8 %copy-start.2 = (s32[128,128]{1,0:T(8,128)S(1)}, s32[128,128]{1,0:T(8,128)}, u32[]{:S(2)}) copy-start(s32[128,128]{1,0:T(8,128)} %land.5) | copy-start | bytes 196612
  15.3 4.9 %collective-permute-start = (bf16[2,48,640]{2,1,0:T(8,128)(2,1)}, bf16[2,48,640]{2,1,0:T(8,128)(2,1)S(1)}, u32[]{:S(2)}, u32[]{:S(2)}) collective-permute-start(bf16[2,48,640]{2,1,0:T(8,128)(2,1)} %get-tuple-element.45), channel_id=1, source_target_pairs={{0,1},{1,0},{2,3},{3,2},{16,17},{17,16},{18,19},{19,18},{4,5},{5,4... | collective-permute-start | bytes 368648 | tf_op jit(solution)/shard_map/ppermute | solution.py:669
  15.8 7.0 %collective-permute-start.9 = (bf16[2,48,640]{2,1,0:T(8,128)(2,1)}, bf16[2,48,640]{2,1,0:T(8,128)(2,1)S(1)}, u32[]{:S(2)}, u32[]{:S(2)}) collective-permute-start(bf16[2,48,640]{2,1,0:T(8,128)(2,1)} %get-tuple-element.66), channel_id=1, source_target_pairs={{0,2},{1,3},{2,0},{3,1},{16,18},{17,19},{18,16},{19,17},{4,6},{5,7... | collective-permute-start | bytes 368648 | tf_op jit(solution)/shard_map/ppermute | solution.py:669
  18.4 6.6 %collective-permute-start.10 = (bf16[2,48,640]{2,1,0:T(8,128)(2,1)}, bf16[2,48,640]{2,1,0:T(8,128)(2,1)S(1)}, u32[]{:S(2)}, u32[]{:S(2)}) collective-permute-start(bf16[2,48,640]{2,1,0:T(8,128)(2,1)} %get-tuple-element.67), channel_id=1, source_target_pairs={{0,3},{1,2},{2,1},{3,0},{16,19},{17,18},{18,17},{19,16},{4,7},{5,6... | collective-permute-start | bytes 368648 | tf_op jit(solution)/shard_map/ppermute | solution.py:669
  18.5 7.3 %collective-permute-start.11 = (bf16[2,48,640]{2,1,0:T(8,128)(2,1)}, bf16[2,48,640]{2,1,0:T(8,128)(2,1)S(1)}, u32[]{:S(2)}, u32[]{:S(2)}) collective-permute-start(bf16[2,48,640]{2,1,0:T(8,128)(2,1)} %get-tuple-element.68), channel_id=1, source_target_pairs={{0,16},{1,17},{2,18},{3,19},{16,0},{17,1},{18,2},{19,3},{4,20},{5,... | collective-permute-start | bytes 368648 | tf_op jit(solution)/shard_map/ppermute | solution.py:669
  20.2 11.3 %collective-permute-start.12 = (bf16[2,48,640]{2,1,0:T(8,128)(2,1)}, bf16[2,48,640]{2,1,0:T(8,128)(2,1)S(1)}, u32[]{:S(2)}, u32[]{:S(2)}) collective-permute-start(bf16[2,48,640]{2,1,0:T(8,128)(2,1)} %get-tuple-element.69), channel_id=1, source_target_pairs={{0,17},{1,16},{2,19},{3,18},{16,1},{17,0},{18,3},{19,2},{4,21},{5,... | collective-permute-start | bytes 368648 | tf_op jit(solution)/shard_map/ppermute | solution.py:669
  20.2 12.6 %collective-permute-start.13 = (bf16[2,48,640]{2,1,0:T(8,128)(2,1)}, bf16[2,48,640]{2,1,0:T(8,128)(2,1)S(1)}, u32[]{:S(2)}, u32[]{:S(2)}) collective-permute-start(bf16[2,48,640]{2,1,0:T(8,128)(2,1)} %get-tuple-element.70), channel_id=1, source_target_pairs={{0,18},{1,19},{2,16},{3,17},{16,2},{17,3},{18,0},{19,1},{4,22},{5,... | collective-permute-start | bytes 368648 | tf_op jit(solution)/shard_map/ppermute | solution.py:669
  22.9 14.5 %collective-permute-start.14 = (bf16[2,48,640]{2,1,0:T(8,128)(2,1)}, bf16[2,48,640]{2,1,0:T(8,128)(2,1)S(1)}, u32[]{:S(2)}, u32[]{:S(2)}) collective-permute-start(bf16[2,48,640]{2,1,0:T(8,128)(2,1)} %get-tuple-element.71), channel_id=1, source_target_pairs={{0,19},{1,18},{2,17},{3,16},{16,3},{17,2},{18,1},{19,0},{4,23},{5,... | collective-permute-start | bytes 368648 | tf_op jit(solution)/shard_map/ppermute | solution.py:669
  25.0 21.6 %collective-permute-start.1 = (bf16[2,48,640]{2,1,0:T(8,128)(2,1)}, bf16[2,48,640]{2,1,0:T(8,128)(2,1)S(1)}, u32[]{:S(2)}, u32[]{:S(2)}) collective-permute-start(bf16[2,48,640]{2,1,0:T(8,128)(2,1)} %get-tuple-element.55), channel_id=1, source_target_pairs={{0,1},{1,0},{2,3},{3,2},{16,17},{17,16},{18,19},{19,18},{4,5},{5,4... | collective-permute-start | bytes 368648 | tf_op jit(solution)/shard_map/ppermute | solution.py:669
  25.8 22.4 %collective-permute-start.2 = (bf16[2,48,640]{2,1,0:T(8,128)(2,1)}, bf16[2,48,640]{2,1,0:T(8,128)(2,1)S(1)}, u32[]{:S(2)}, u32[]{:S(2)}) collective-permute-start(bf16[2,48,640]{2,1,0:T(8,128)(2,1)} %get-tuple-element.56), channel_id=1, source_target_pairs={{0,2},{1,3},{2,0},{3,1},{16,18},{17,19},{18,16},{19,17},{4,6},{5,7... | collective-permute-start | bytes 368648 | tf_op jit(solution)/shard_map/ppermute | solution.py:669
  27.5 19.0 %copy-start.20 = (bf16[2,48,640]{2,1,0:T(8,128)(2,1)S(1)}, bf16[2,48,640]{2,1,0:T(8,128)(2,1)}, u32[]{:S(2)}) copy-start(bf16[2,48,640]{2,1,0:T(8,128)(2,1)} %get-tuple-element.60) | copy-start | bytes 368644
  27.5 20.7 %copy-start.19 = (bf16[2,48,640]{2,1,0:T(8,128)(2,1)S(1)}, bf16[2,48,640]{2,1,0:T(8,128)(2,1)}, u32[]{:S(2)}) copy-start(bf16[2,48,640]{2,1,0:T(8,128)(2,1)} %get-tuple-element.61) | copy-start | bytes 368644
  27.5 22.0 %copy-start.11 = (bf16[2,48,640]{2,1,0:T(8,128)(2,1)S(1)}, bf16[2,48,640]{2,1,0:T(8,128)(2,1)}, u32[]{:S(2)}) copy-start(bf16[2,48,640]{2,1,0:T(8,128)(2,1)} %get-tuple-element.64.refs_0_) | copy-start | bytes 368644
  27.6 29.3 %copy-start.10 = (bf16[2,48,640]{2,1,0:T(8,128)(2,1)S(1)}, bf16[2,48,640]{2,1,0:T(8,128)(2,1)}, u32[]{:S(2)}) copy-start(bf16[2,48,640]{2,1,0:T(8,128)(2,1)} %get-tuple-element.54.refs_0_) | copy-start | bytes 368644
  27.6 31.4 %copy-start.8 = (bf16[128,128]{1,0:T(8,128)(2,1)}, bf16[128,128]{1,0:T(8,128)(2,1)S(1)}, u32[]{:S(2)}) copy-start(bf16[128,128]{1,0:T(8,128)(2,1)S(1)} %get-tuple-element.76.refs_8_.own_s) | copy-start | bytes 98308
  27.6 31.4 %copy-start.9 = (bf16[128,128]{1,0:T(8,128)(2,1)}, bf16[128,128]{1,0:T(8,128)(2,1)S(1)}, u32[]{:S(2)}) copy-start(bf16[128,128]{1,0:T(8,128)(2,1)S(1)} %get-tuple-element.77.refs_7_.own_n) | copy-start | bytes 98308
  31.5 7.5 %collective-permute-start.15 = (bf16[128,128]{1,0:T(8,128)(2,1)S(1)}, bf16[128,128]{1,0:T(8,128)(2,1)S(1)}, u32[]{:S(2)}, u32[]{:S(2)}) collective-permute-start(bf16[128,128]{1,0:T(8,128)(2,1)S(1)} %get-tuple-element.76.refs_8_.own_s), channel_id=1, source_target_pairs={{4,0},{8,4},{12,8},{16,12},{20,16},{24,20},{28,24},{5,1},{9,5},{13... | collective-permute-start | bytes 98312 | tf_op jit(solution)/shard_map/ppermute | solution.py:702
  32.8 9.6 %collective-permute-start.16 = (bf16[128,128]{1,0:T(8,128)(2,1)S(1)}, bf16[128,128]{1,0:T(8,128)(2,1)S(1)}, u32[]{:S(2)}, u32[]{:S(2)}) collective-permute-start(bf16[128,128]{1,0:T(8,128)(2,1)S(1)} %get-tuple-element.77.refs_7_.own_n), channel_id=1, source_target_pairs={{0,4},{4,8},{8,12},{12,16},{16,20},{20,24},{24,28},{1,5},{5,9},{9,... | collective-permute-start | bytes 98312 | tf_op jit(solution)/shard_map/ppermute | solution.py:703
  37.4 12.6 %collective-permute-start.3 = (bf16[2,48,640]{2,1,0:T(8,128)(2,1)S(1)}, bf16[2,48,640]{2,1,0:T(8,128)(2,1)S(1)}, u32[]{:S(2)}, u32[]{:S(2)}) collective-permute-start(bf16[2,48,640]{2,1,0:T(8,128)(2,1)S(1)} %copy-done.23), channel_id=1, source_target_pairs={{0,3},{1,2},{2,1},{3,0},{16,19},{17,18},{18,17},{19,16},{4,7},{5,6... | collective-permute-start | bytes 368648 | tf_op jit(solution)/shard_map/ppermute | solution.py:669
  39.0 20.1 %copy-start.4 = (bf16[128,128]{1,0:T(8,128)(2,1)}, bf16[128,128]{1,0:T(8,128)(2,1)S(1)}, u32[]{:S(2)}) copy-start(bf16[128,128]{1,0:T(8,128)(2,1)S(1)} %collective-permute-done.15.from_n.refs_11_) | copy-start | bytes 98308
  39.0 11.1 %collective-permute-start.4 = (bf16[2,48,640]{2,1,0:T(8,128)(2,1)S(1)}, bf16[2,48,640]{2,1,0:T(8,128)(2,1)S(1)}, u32[]{:S(2)}, u32[]{:S(2)}) collective-permute-start(bf16[2,48,640]{2,1,0:T(8,128)(2,1)S(1)} %copy-done.22), channel_id=1, source_target_pairs={{0,16},{1,17},{2,18},{3,19},{16,0},{17,1},{18,2},{19,3},{4,20},{5,... | collective-permute-start | bytes 368648 | tf_op jit(solution)/shard_map/ppermute | solution.py:669
  42.4 14.4 %collective-permute-start.5 = (bf16[2,48,640]{2,1,0:T(8,128)(2,1)S(1)}, bf16[2,48,640]{2,1,0:T(8,128)(2,1)S(1)}, u32[]{:S(2)}, u32[]{:S(2)}) collective-permute-start(bf16[2,48,640]{2,1,0:T(8,128)(2,1)S(1)} %copy-done.21), channel_id=1, source_target_pairs={{0,17},{1,16},{2,19},{3,18},{16,1},{17,0},{18,3},{19,2},{4,21},{5,... | collective-permute-start | bytes 368648 | tf_op jit(solution)/shard_map/ppermute | solution.py:669
  46.5 10.3 %collective-permute-start.6 = (bf16[2,48,640]{2,1,0:T(8,128)(2,1)S(1)}, bf16[2,48,640]{2,1,0:T(8,128)(2,1)S(1)}, u32[]{:S(2)}, u32[]{:S(2)}) collective-permute-start(bf16[2,48,640]{2,1,0:T(8,128)(2,1)S(1)} %copy-done.20), channel_id=1, source_target_pairs={{0,18},{1,19},{2,16},{3,17},{16,2},{17,3},{18,0},{19,1},{4,22},{5,... | collective-permute-start | bytes 368648 | tf_op jit(solution)/shard_map/ppermute | solution.py:669
  48.2 8.6 %collective-permute-start.7 = (bf16[2,48,640]{2,1,0:T(8,128)(2,1)S(1)}, bf16[2,48,640]{2,1,0:T(8,128)(2,1)S(1)}, u32[]{:S(2)}, u32[]{:S(2)}) collective-permute-start(bf16[2,48,640]{2,1,0:T(8,128)(2,1)S(1)} %copy-done.19), channel_id=1, source_target_pairs={{0,19},{1,18},{2,17},{3,16},{16,3},{17,2},{18,1},{19,0},{4,23},{5,... | collective-permute-start | bytes 368648 | tf_op jit(solution)/shard_map/ppermute | solution.py:669
  50.0 14.5 %collective-permute-start.17 = (bf16[136,640]{1,0:T(8,128)(2,1)S(1)}, bf16[136,640]{1,0:T(8,128)(2,1)S(1)}, u32[]{:S(2)}, u32[]{:S(2)}) collective-permute-start(bf16[136,640]{1,0:T(8,128)(2,1)S(1)} %get-tuple-element.78), channel_id=1, source_target_pairs={{0,8},{4,12},{8,0},{12,4},{1,9},{5,13},{9,1},{13,5},{2,10},{6,14},... | collective-permute-start | bytes 522248 | tf_op jit(solution)/shard_map/ppermute | solution.py:669
  50.1 14.4 %collective-permute-start.18 = (bf16[136,640]{1,0:T(8,128)(2,1)S(1)}, bf16[136,640]{1,0:T(8,128)(2,1)S(1)}, u32[]{:S(2)}, u32[]{:S(2)}) collective-permute-start(bf16[136,640]{1,0:T(8,128)(2,1)S(1)} %get-tuple-element.79), channel_id=1, source_target_pairs={{0,12},{4,8},{8,4},{12,0},{1,13},{5,9},{9,5},{13,1},{2,14},{6,10},... | collective-permute-start | bytes 522248 | tf_op jit(solution)/shard_map/ppermute | solution.py:669
  57.3 8.9 %collective-permute-start.8 = (bf16[136,640]{1,0:T(8,128)(2,1)S(1)}, bf16[136,640]{1,0:T(8,128)(2,1)S(1)}, u32[]{:S(2)}, u32[]{:S(2)}) collective-permute-start(bf16[136,640]{1,0:T(8,128)(2,1)S(1)} %get-tuple-element.63), channel_id=1, source_target_pairs={{0,4},{4,0},{8,12},{12,8},{1,5},{5,1},{9,13},{13,9},{2,6},{6,2},{1... | collective-permute-start | bytes 522248 | tf_op jit(solution)/shard_map/ppermute | solution.py:669
  59.1 4.1 %collective-permute-start.20 = (bf16[192,128]{1,0:T(8,128)(2,1)S(1)}, bf16[192,128]{1,0:T(8,128)(2,1)S(1)}, u32[]{:S(2)}, u32[]{:S(2)}) collective-permute-start(bf16[192,128]{1,0:T(8,128)(2,1)S(1)} %get-tuple-element.82.refs_9_.own_e), channel_id=1, source_target_pairs={{0,1},{1,2},{2,3},{4,5},{5,6},{6,7},{8,9},{9,10},{10,11},{12,13},{... | collective-permute-start | bytes 147464 | tf_op jit(solution)/shard_map/ppermute | solution.py:711
  60.6 3.9 %collective-permute-start.19 = (bf16[192,128]{1,0:T(8,128)(2,1)S(1)}, bf16[192,128]{1,0:T(8,128)(2,1)S(1)}, u32[]{:S(2)}, u32[]{:S(2)}) collective-permute-start(bf16[192,128]{1,0:T(8,128)(2,1)S(1)} %get-tuple-element.83.refs_10_.own_w), channel_id=1, source_target_pairs={{1,0},{2,1},{3,2},{5,4},{6,5},{7,6},{9,8},{10,9},{11,10},{13,12},{... | collective-permute-start | bytes 147464 | tf_op jit(solution)/shard_map/ppermute | solution.py:710
  70.1 17.4 %all-to-all-start = ((bf16[32,40,128]{2,1,0:T(8,128)(2,1)}), bf16[32,40,128]{2,1,0:T(8,128)(2,1)S(1)}, u32[]{:S(2)}, u32[]{:S(2)}) async-start(bf16[32,40,128]{2,1,0:T(8,128)(2,1)} %get-tuple-element.87), calls=%async_computation | async-start | bytes 655360 | tf_op jit(solution)/shard_map/all_to_all | solution.py:723
  (14 other events, 106.2 us)

commit v9 on v7

--- a/solution.py
+++ b/solution.py
@@ -121,7 +121,7 @@
     wanted = jnp.zeros((8, cap), F32)
     for at, x in enumerate((0, 1, last, last - 1, 0, 0, last, last)):
         wanted = jnp.where(row == at, float(x), wanted)
-    group = 8
+    group = 16
 
     def owners(g, _):
         ds = [g * group + j for j in range(group)]
@@ -168,7 +168,7 @@
         send[...] = xs[m * n_gx : (m + 1) * n_gx].astype(BF16)
 
 
-def forward(flux, w, src, own, dst, grid, cap, parts=20):
+def forward(flux, w, src, own, dst, grid, cap, parts=8):
     n_sec, n_gx, n_gy = grid
     devices = n_sec * n_gx * n_gy
     total, width, _ = w.shape
@@ -561,7 +561,7 @@
             held[tracer, l] = update(c, tracers[tracer, l], halo, under, over, forcing(tracer, l))
         return 0
 
-    lax.fori_loop(0, levels, first_step, 0)
+    lax.fori_loop(0, levels, first_step, 0, unroll=4)
 
     def second_step(l, _):
         c = [weights[i, l] for i in range(5)]
@@ -573,7 +573,7 @@
         send(l).start()
         return 0
 
-    lax.fori_loop(0, levels, second_step, 0)
+    lax.fori_loop(0, levels, second_step, 0, unroll=4)
     for l in range(levels):
         send(l).wait()
 
@@ -622,7 +622,7 @@
     out[...] = both[:, :width] + both[:, width:]
 
 
-def backward(back, w, src, slots, blocks, parts=20):
+def backward(back, w, src, slots, blocks, parts=10):
     total, width, _ = w.shape
     devices, cap, _ = back.shape
     return pl.pallas_call(
@@ -638,7 +638,7 @@
             pltpu.SemaphoreType.DMA((parts + 1,)),
         ],
         out_shape=jax.ShapeDtypeStruct((blocks, width), F32),
-        compiler_params=kernel_params(58),
+        compiler_params=kernel_params(46),
         cost_estimate=pl.CostEstimate(flops=2 * total * 8 * width * width, bytes_accessed=total * width * width * 2, transcendentals=0),
         name="backward_remap",
     )(slots, src.reshape(1, total), back, w)
@@ -703,7 +703,7 @@
         functools.partial(surface_kernel, grid, chunk, levels),
         [((planes * n_gx, cap, width), BF16), ((5, height, width), F32), ((8, wide), F32)],
         "surface",
-        58,
+        24,
         1 << 22,
     )(*parts, tracers[0:1, 0:3], currents[:, 0:2], land_sea, *edges)
     returned = lax.all_to_all(back, EVERY, split_axis=0, concat_axis=0, tiled=True)

time: 94.7 us -> 89.7 us (0.947)
  Pallas kernels: 42.2 us -> 37.1 us
  waiting for transfers between devices: 16.6 us -> 18.8 us
  local copies, waits for them, and re-layouts: 3.51 us -> 1.44 us
    pallas_call x1, Pallas kernels: 12.6 us -> 10.8 us  [on_device(): kernel(stencil_kernel, [(tracers.shape, F32)], 'substeps', 58, 1 << 24, [...]
    pallas_call x1, Pallas kernels: 3.29 us -> 1.89 us  [on_device(): kernel(functools.partial(surface_kernel, grid, chunk, levels), [((planes...]
    pallas_call x1, Pallas kernels: 14.7 us -> 13.6 us  [forward(): pl.pallas_call(functools.partial(forward_kernel, parts, cap, grid), in_sp...]
  transfers between devices with their start and end apart: 15 -> 15, of which waited for: 4 -> 6; matrix products, arithmetic and copies ran while one was open for 2% -> 0% of each run, Pallas kernels for 15% -> 14%
where the time goes in v9:
time: 89.7 us; the launch traced here: 89.4 us
  Pallas kernels  37.1 us (41%)
  starting transfers between devices  31.2 us (35%)
  waiting for transfers between devices  18.8 us (21%)
  local copies, waits for them, and re-layouts  1.44 us (2%)
  between operations  0.93 us (1%)
    ppermute x10, waiting for transfers between devices, swapped(): return lax.ppermute(array, axes, [(i, i ^ step) for i in range(count)])  17.2 us
    ppermute x10, starting transfers between devices, swapped(): return lax.ppermute(array, axes, [(i, i ^ step) for i in range(count)])  14.5 us
    pallas_call x1, Pallas kernels, forward(): pl.pallas_call(functools.partial(forward_kernel, parts, cap, grid), in_sp...  13.6 us
    pallas_call x1, Pallas kernels, on_device(): kernel(stencil_kernel, [(tracers.shape, F32)], 'substeps', 58, 1 << 24, [...  10.8 us
    pallas_call x1, Pallas kernels, backward(): pl.pallas_call(functools.partial(backward_kernel, parts), in_specs=[ANY,...  8.4 us
    all_to_all x1, starting transfers between devices, on_device(): lax.all_to_all(back, EVERY, split_axis=0, concat_axis=0, tiled=True)  6.39 us
    ppermute x1, starting transfers between devices, on_device(): from_s = lax.ppermute(own_n, NORTH, to_north)  4.55 us
    ppermute x1, starting transfers between devices, on_device(): from_w = lax.ppermute(own_e, 'gy', to_east)  3.03 us
  transfers between devices with their start and end apart: 15, of which 6 were waited for; matrix products, arithmetic and copies ran while one was open for 0% of the time, Pallas kernels for 14%

profile of v9, /device:TPU:0, one launch (start us, length us, event | category | flops | bytes accessed | tf_op | source)
XLA Modules:
  0.0 89.4 jit_solution(2930093232135346518)
XLA Ops:
  0.6 0.0 copy-start
  0.6 0.0 copy-start.1
  0.7 0.0 copy-start.2
  0.7 13.6 %forward_remap.1 = (bf16[4,48,640]{2,1,0:T(8,128)(2,1)}, bf16[4,48,640]{2,1,0:T(8,128)(2,1)}, bf16[4,48,640]{2,1,0:T(8,128)(2,1)}, bf16[4,48,640]{2,1,0:T(8,128)...) custom-call(s32[640]{0:T(1024)} %src.1, ...), custom_call_target="tpu_custom_call" | custom-call | flops 167772160 | bytes 20971520 | tf_op jit(solution)/shard_map/forward_remap/pallas_call | solution.py:178
  14.3 0.5 collective-permute-start
  14.8 2.6 %collective-permute-start.1 = (bf16[4,48,640]{2,1,0:T(8,128)(2,1)}, bf16[4,48,640]{2,1,0:T(8,128)(2,1)S(1)}, u32[]{:S(2)}, u32[]{:S(2)}) collective-permute-start(bf16[4,48,640]{2,1,0:T(8,128)(2,1)} %get-tuple-element.38), channel_id=1, source_target_pairs={{0,2},{1,3},{2,0},{3,1},{16,18},{17,19},{18,16},{19,17},{4,6},{5,7... | collective-permute-start | bytes 737288 | tf_op jit(solution)/shard_map/ppermute | solution.py:666
  17.4 0.1 collective-permute-start.2
  17.4 1.8 %collective-permute-start.3 = (bf16[4,48,640]{2,1,0:T(8,128)(2,1)}, bf16[4,48,640]{2,1,0:T(8,128)(2,1)S(1)}, u32[]{:S(2)}, u32[]{:S(2)}) collective-permute-start(bf16[4,48,640]{2,1,0:T(8,128)(2,1)} %get-tuple-element.40), channel_id=1, source_target_pairs={{0,16},{1,17},{2,18},{3,19},{16,0},{17,1},{18,2},{19,3},{4,20},{5,... | collective-permute-start | bytes 737288 | tf_op jit(solution)/shard_map/ppermute | solution.py:666
  19.2 2.6 %collective-permute-start.5 = (bf16[4,48,640]{2,1,0:T(8,128)(2,1)}, bf16[4,48,640]{2,1,0:T(8,128)(2,1)S(1)}, u32[]{:S(2)}, u32[]{:S(2)}) collective-permute-start(bf16[4,48,640]{2,1,0:T(8,128)(2,1)} %get-tuple-element.42), channel_id=1, source_target_pairs={{0,18},{1,19},{2,16},{3,17},{16,2},{17,3},{18,0},{19,1},{4,22},{5,... | collective-permute-start | bytes 737288 | tf_op jit(solution)/shard_map/ppermute | solution.py:666
  21.8 2.6 %collective-permute-done.1.refs_2_ = bf16[4,48,640]{2,1,0:T(8,128)(2,1)S(1)} collective-permute-done((bf16[4,48,640]{2,1,0:T(8,128)(2,1)}, bf16[4,48,640]{2,1,0:T(8,128)(2,1)S(1)}, u32[]{:S(2)}, u32[]{:S(2)}) %collective-permute-start.1) | collective-permute-done | bytes 245792 | tf_op jit(solution)/shard_map/ppermute | solution.py:666
  24.4 1.7 %collective-permute-start.6 = (bf16[4,48,640]{2,1,0:T(8,128)(2,1)}, bf16[4,48,640]{2,1,0:T(8,128)(2,1)S(1)}, u32[]{:S(2)}, u32[]{:S(2)}) collective-permute-start(bf16[4,48,640]{2,1,0:T(8,128)(2,1)} %get-tuple-element.43), channel_id=1, source_target_pairs={{0,19},{1,18},{2,17},{3,16},{16,3},{17,2},{18,1},{19,0},{4,23},{5,... | collective-permute-start | bytes 737288 | tf_op jit(solution)/shard_map/ppermute | solution.py:666
  26.1 0.1 edge_rows.1
  26.2 3.0 %collective-permute-done.2.refs_3_ = bf16[4,48,640]{2,1,0:T(8,128)(2,1)S(1)} collective-permute-done((bf16[4,48,640]{2,1,0:T(8,128)(2,1)}, bf16[4,48,640]{2,1,0:T(8,128)(2,1)S(1)}, u32[]{:S(2)}, u32[]{:S(2)}) %collective-permute-start.2) | collective-permute-done | bytes 245792 | tf_op jit(solution)/shard_map/ppermute | solution.py:666
  29.2 1.3 %collective-permute-start.7 = (bf16[128,128]{1,0:T(8,128)(2,1)S(1)}, bf16[128,128]{1,0:T(8,128)(2,1)S(1)}, u32[]{:S(2)}, u32[]{:S(2)}) collective-permute-start(bf16[128,128]{1,0:T(8,128)(2,1)S(1)} %get-tuple-element.46.refs_8_.own_s), channel_id=1, source_target_pairs={{4,0},{8,4},{12,8},{16,12},{20,16},{24,20},{28,24},{5,1},{9,5},{13... | collective-permute-start | bytes 98312 | tf_op jit(solution)/shard_map/ppermute | solution.py:689
  30.5 4.5 %collective-permute-start.8 = (bf16[128,128]{1,0:T(8,128)(2,1)S(1)}, bf16[128,128]{1,0:T(8,128)(2,1)S(1)}, u32[]{:S(2)}, u32[]{:S(2)}) collective-permute-start(bf16[128,128]{1,0:T(8,128)(2,1)S(1)} %get-tuple-element.47.refs_7_.own_n), channel_id=1, source_target_pairs={{0,4},{4,8},{8,12},{12,16},{16,20},{20,24},{24,28},{1,5},{5,9},{9,... | collective-permute-start | bytes 98312 | tf_op jit(solution)/shard_map/ppermute | solution.py:690
  35.1 6.0 %collective-permute-done.4.refs_5_ = bf16[4,48,640]{2,1,0:T(8,128)(2,1)S(1)} collective-permute-done((bf16[4,48,640]{2,1,0:T(8,128)(2,1)}, bf16[4,48,640]{2,1,0:T(8,128)(2,1)S(1)}, u32[]{:S(2)}, u32[]{:S(2)}) %collective-permute-start.4) | collective-permute-done | bytes 245792 | tf_op jit(solution)/shard_map/ppermute | solution.py:666
  41.1 0.6 merge.1
  41.7 1.9 %collective-permute-start.9 = (bf16[136,640]{1,0:T(8,128)(2,1)S(1)}, bf16[136,640]{1,0:T(8,128)(2,1)S(1)}, u32[]{:S(2)}, u32[]{:S(2)}) collective-permute-start(bf16[136,640]{1,0:T(8,128)(2,1)S(1)} %get-tuple-element.57), channel_id=1, source_target_pairs={{0,4},{4,0},{8,12},{12,8},{1,5},{5,1},{9,13},{13,9},{2,6},{6,2},{1... | collective-permute-start | bytes 522248 | tf_op jit(solution)/shard_map/ppermute | solution.py:666
  43.6 3.3 %collective-permute-start.10 = (bf16[136,640]{1,0:T(8,128)(2,1)S(1)}, bf16[136,640]{1,0:T(8,128)(2,1)S(1)}, u32[]{:S(2)}, u32[]{:S(2)}) collective-permute-start(bf16[136,640]{1,0:T(8,128)(2,1)S(1)} %get-tuple-element.58), channel_id=1, source_target_pairs={{0,8},{4,12},{8,0},{12,4},{1,9},{5,13},{9,1},{13,5},{2,10},{6,14},... | collective-permute-start | bytes 522248 | tf_op jit(solution)/shard_map/ppermute | solution.py:666
  47.0 1.7 %edge_columns.1 = (bf16[192,128]{1,0:T(8,128)(2,1)S(1)}, bf16[192,128]{1,0:T(8,128)(2,1)S(1)}) custom-call(f32[2,16,128,128]{3,2,1,0:T(8,128)S(1)} %copy-done.1, f32[2,16,128,128]{3,2,1,0:T(8,128)S(1)} %copy-done, s32[128,128]{1,0:T(8,128)S(1)} %copy-done.2, bf16[128,128]{1,0:T(8,128)(2,1)S(1)} %collective-permute-done.7.from_n.refs_11_, ...), custom_call_target="tpu_custom_call" | custom-call | flops 4194304 | bytes 4194304 | tf_op jit(solution)/shard_map/edge_columns/pallas_call | solution.py:692
  48.7 0.0 copy-start.8
  48.7 1.4 %collective-permute-start.12 = (bf16[192,128]{1,0:T(8,128)(2,1)S(1)}, bf16[192,128]{1,0:T(8,128)(2,1)S(1)}, u32[]{:S(2)}, u32[]{:S(2)}) collective-permute-start(bf16[192,128]{1,0:T(8,128)(2,1)S(1)} %get-tuple-element.63.refs_10_.own_w), channel_id=1, source_target_pairs={{1,0},{2,1},{3,2},{5,4},{6,5},{7,6},{9,8},{10,9},{11,10},{13,12},{... | collective-permute-start | bytes 147464 | tf_op jit(solution)/shard_map/ppermute | solution.py:695
  50.1 3.0 %collective-permute-start.13 = (bf16[192,128]{1,0:T(8,128)(2,1)S(1)}, bf16[192,128]{1,0:T(8,128)(2,1)S(1)}, u32[]{:S(2)}, u32[]{:S(2)}) collective-permute-start(bf16[192,128]{1,0:T(8,128)(2,1)S(1)} %get-tuple-element.62.refs_9_.own_e), channel_id=1, source_target_pairs={{0,1},{1,2},{2,3},{4,5},{5,6},{6,7},{8,9},{9,10},{10,11},{12,13},{... | collective-permute-start | bytes 147464 | tf_op jit(solution)/shard_map/ppermute | solution.py:696
  53.2 0.8 collective-permute-done.13.refs_14_.from_w
  54.0 5.6 %collective-permute-done.10.refs_2_ = bf16[136,640]{1,0:T(8,128)(2,1)S(1)} collective-permute-done((bf16[136,640]{1,0:T(8,128)(2,1)S(1)}, bf16[136,640]{1,0:T(8,128)(2,1)S(1)}, u32[]{:S(2)}, u32[]{:S(2)}) %collective-permute-start.10) | collective-permute-done | bytes 174112 | tf_op jit(solution)/shard_map/ppermute | solution.py:666
  59.7 1.9 %surface.1 = (bf16[32,40,128]{2,1,0:T(8,128)(2,1)}, f32[5,128,128]{2,1,0:T(8,128)S(1)}, f32[8,640]{1,0:T(8,128)S(1)}) custom-call(f32[136,640]{1,0:T(8,128)S(1)} %get-tuple-element.56.refs_0_, bf16[136,640]{1,0:T(8,128)(2,1)S(1)} %collective-permute-done.9.refs_1_, bf16[136,640]{1,0:T(8,128)(2,1)S(1)} %collective-permute-done.10.refs_2_, ...), custom_call_target="tpu_custom_call" | custom-call | flops 4194304 | bytes 4194304 | tf_op jit(solution)/shard_map/surface/pallas_call | solution.py:702
  61.6 0.7 copy-done.3
  62.3 0.6 copy-done.13
  62.9 6.4 %all-to-all-start = ((bf16[32,40,128]{2,1,0:T(8,128)(2,1)}), bf16[32,40,128]{2,1,0:T(8,128)(2,1)S(1)}, u32[]{:S(2)}, u32[]{:S(2)}) async-start(bf16[32,40,128]{2,1,0:T(8,128)(2,1)} %get-tuple-element.67), calls=%async_computation | async-start | bytes 655360 | tf_op jit(solution)/shard_map/all_to_all | solution.py:709
  69.4 10.8 %substeps.1 = f32[2,16,128,128]{3,2,1,0:T(8,128)} custom-call(f32[2,16,128,128]{3,2,1,0:T(8,128)} %tracers_in.1, f32[2,16,128,128]{3,2,1,0:T(8,128)} %currents_in.1, s32[128,128]{1,0:T(8,128)} %land.5, f32[5,128,128]{2,1,0:T(8,128)} %copy-done.3, f32[8,640]{1,0:T(8,128)} %copy-done.13, bf16[128,128]{1,0:T(8,128)(2,1)} %copy-done.12, ...), custom_call_target="tpu_custom_call" | custom-call | flops 16777216 | bytes 16777216 | tf_op jit(solution)/shard_map/substeps/pallas_call | solution.py:712
  80.2 0.8 all-to-all-done.back
  81.0 8.4 %backward_remap.1 = f32[160,128]{1,0:T(8,128)} custom-call(s32[640]{0:T(1024)S(1)} %copy-done.14, s32[1,640]{1,0:T(1,128)S(1)} %reshape.19.src, bf16[32,40,128]{2,1,0:T(8,128)(2,1)S(1)} %all-to-all-done.back, bf16[640,128,128]{2,1,0:T(8,128)(2,1)} %w.3), custom_call_target="tpu_custom_call" | custom-call | flops 167772160 | bytes 20971520 | tf_op jit(solution)/shard_map/backward_remap/pallas_call | solution.py:628
  (40 shorter events, 0.1 us)
Async XLA Ops:
  0.6 25.5 %copy-start = (f32[2,16,128,128]{3,2,1,0:T(8,128)S(1)}, f32[2,16,128,128]{3,2,1,0:T(8,128)}, u32[]{:S(2)}) copy-start(f32[2,16,128,128]{3,2,1,0:T(8,128)} %currents_in.1) | copy-start | bytes 6291460
  0.6 25.5 %copy-start.1 = (f32[2,16,128,128]{3,2,1,0:T(8,128)S(1)}, f32[2,16,128,128]{3,2,1,0:T(8,128)}, u32[]{:S(2)}) copy-start(f32[2,16,128,128]{3,2,1,0:T(8,128)} %tracers_in.1) | copy-start | bytes 6291460
  0.7 25.5 %copy-start.2 = (s32[128,128]{1,0:T(8,128)S(1)}, s32[128,128]{1,0:T(8,128)}, u32[]{:S(2)}) copy-start(s32[128,128]{1,0:T(8,128)} %land.5) | copy-start | bytes 196612
  14.3 4.9 %collective-permute-start = (bf16[4,48,640]{2,1,0:T(8,128)(2,1)}, bf16[4,48,640]{2,1,0:T(8,128)(2,1)S(1)}, u32[]{:S(2)}, u32[]{:S(2)}) collective-permute-start(bf16[4,48,640]{2,1,0:T(8,128)(2,1)} %get-tuple-element.36), channel_id=1, source_target_pairs={{0,1},{1,0},{2,3},{3,2},{16,17},{17,16},{18,19},{19,18},{4,5},{5,4... | collective-permute-start | bytes 737288 | tf_op jit(solution)/shard_map/ppermute | solution.py:666
  14.8 9.6 %collective-permute-start.1 = (bf16[4,48,640]{2,1,0:T(8,128)(2,1)}, bf16[4,48,640]{2,1,0:T(8,128)(2,1)S(1)}, u32[]{:S(2)}, u32[]{:S(2)}) collective-permute-start(bf16[4,48,640]{2,1,0:T(8,128)(2,1)} %get-tuple-element.38), channel_id=1, source_target_pairs={{0,2},{1,3},{2,0},{3,1},{16,18},{17,19},{18,16},{19,17},{4,6},{5,7... | collective-permute-start | bytes 737288 | tf_op jit(solution)/shard_map/ppermute | solution.py:666
  17.4 11.9 %collective-permute-start.2 = (bf16[4,48,640]{2,1,0:T(8,128)(2,1)}, bf16[4,48,640]{2,1,0:T(8,128)(2,1)S(1)}, u32[]{:S(2)}, u32[]{:S(2)}) collective-permute-start(bf16[4,48,640]{2,1,0:T(8,128)(2,1)} %get-tuple-element.39), channel_id=1, source_target_pairs={{0,3},{1,2},{2,1},{3,0},{16,19},{17,18},{18,17},{19,16},{4,7},{5,6... | collective-permute-start | bytes 737288 | tf_op jit(solution)/shard_map/ppermute | solution.py:666
  17.4 13.1 %collective-permute-start.3 = (bf16[4,48,640]{2,1,0:T(8,128)(2,1)}, bf16[4,48,640]{2,1,0:T(8,128)(2,1)S(1)}, u32[]{:S(2)}, u32[]{:S(2)}) collective-permute-start(bf16[4,48,640]{2,1,0:T(8,128)(2,1)} %get-tuple-element.40), channel_id=1, source_target_pairs={{0,16},{1,17},{2,18},{3,19},{16,0},{17,1},{18,2},{19,3},{4,20},{5,... | collective-permute-start | bytes 737288 | tf_op jit(solution)/shard_map/ppermute | solution.py:666
  19.2 21.8 %collective-permute-start.4 = (bf16[4,48,640]{2,1,0:T(8,128)(2,1)}, bf16[4,48,640]{2,1,0:T(8,128)(2,1)S(1)}, u32[]{:S(2)}, u32[]{:S(2)}) collective-permute-start(bf16[4,48,640]{2,1,0:T(8,128)(2,1)} %get-tuple-element.41), channel_id=1, source_target_pairs={{0,17},{1,16},{2,19},{3,18},{16,1},{17,0},{18,3},{19,2},{4,21},{5,... | collective-permute-start | bytes 737288 | tf_op jit(solution)/shard_map/ppermute | solution.py:666
  19.2 21.8 %collective-permute-start.5 = (bf16[4,48,640]{2,1,0:T(8,128)(2,1)}, bf16[4,48,640]{2,1,0:T(8,128)(2,1)S(1)}, u32[]{:S(2)}, u32[]{:S(2)}) collective-permute-start(bf16[4,48,640]{2,1,0:T(8,128)(2,1)} %get-tuple-element.42), channel_id=1, source_target_pairs={{0,18},{1,19},{2,16},{3,17},{16,2},{17,3},{18,0},{19,1},{4,22},{5,... | collective-permute-start | bytes 737288 | tf_op jit(solution)/shard_map/ppermute | solution.py:666
  24.4 16.7 %collective-permute-start.6 = (bf16[4,48,640]{2,1,0:T(8,128)(2,1)}, bf16[4,48,640]{2,1,0:T(8,128)(2,1)S(1)}, u32[]{:S(2)}, u32[]{:S(2)}) collective-permute-start(bf16[4,48,640]{2,1,0:T(8,128)(2,1)} %get-tuple-element.43), channel_id=1, source_target_pairs={{0,19},{1,18},{2,17},{3,16},{16,3},{17,2},{18,1},{19,0},{4,23},{5,... | collective-permute-start | bytes 737288 | tf_op jit(solution)/shard_map/ppermute | solution.py:666
  26.1 15.0 %copy-start.6 = (bf16[4,48,640]{2,1,0:T(8,128)(2,1)S(1)}, bf16[4,48,640]{2,1,0:T(8,128)(2,1)}, u32[]{:S(2)}) copy-start(bf16[4,48,640]{2,1,0:T(8,128)(2,1)} %get-tuple-element.48.refs_0_) | copy-start | bytes 737284
  26.2 33.5 %copy-start.11 = (bf16[128,128]{1,0:T(8,128)(2,1)}, bf16[128,128]{1,0:T(8,128)(2,1)S(1)}, u32[]{:S(2)}) copy-start(bf16[128,128]{1,0:T(8,128)(2,1)S(1)} %get-tuple-element.46.refs_8_.own_s) | copy-start | bytes 98308
  26.2 33.5 %copy-start.12 = (bf16[128,128]{1,0:T(8,128)(2,1)}, bf16[128,128]{1,0:T(8,128)(2,1)S(1)}, u32[]{:S(2)}) copy-start(bf16[128,128]{1,0:T(8,128)(2,1)S(1)} %get-tuple-element.47.refs_7_.own_n) | copy-start | bytes 98308
  29.2 11.8 %collective-permute-start.7 = (bf16[128,128]{1,0:T(8,128)(2,1)S(1)}, bf16[128,128]{1,0:T(8,128)(2,1)S(1)}, u32[]{:S(2)}, u32[]{:S(2)}) collective-permute-start(bf16[128,128]{1,0:T(8,128)(2,1)S(1)} %get-tuple-element.46.refs_8_.own_s), channel_id=1, source_target_pairs={{4,0},{8,4},{12,8},{16,12},{20,16},{24,20},{28,24},{5,1},{9,5},{13... | collective-permute-start | bytes 98312 | tf_op jit(solution)/shard_map/ppermute | solution.py:689
  30.5 10.5 %collective-permute-start.8 = (bf16[128,128]{1,0:T(8,128)(2,1)S(1)}, bf16[128,128]{1,0:T(8,128)(2,1)S(1)}, u32[]{:S(2)}, u32[]{:S(2)}) collective-permute-start(bf16[128,128]{1,0:T(8,128)(2,1)S(1)} %get-tuple-element.47.refs_7_.own_n), channel_id=1, source_target_pairs={{0,4},{4,8},{8,12},{12,16},{16,20},{20,24},{24,28},{1,5},{5,9},{9,... | collective-permute-start | bytes 98312 | tf_op jit(solution)/shard_map/ppermute | solution.py:690
  41.0 18.7 %copy-start.4 = (bf16[128,128]{1,0:T(8,128)(2,1)}, bf16[128,128]{1,0:T(8,128)(2,1)S(1)}, u32[]{:S(2)}) copy-start(bf16[128,128]{1,0:T(8,128)(2,1)S(1)} %collective-permute-done.7.from_n.refs_11_) | copy-start | bytes 98308
  41.1 18.6 %copy-start.5 = (bf16[128,128]{1,0:T(8,128)(2,1)}, bf16[128,128]{1,0:T(8,128)(2,1)S(1)}, u32[]{:S(2)}) copy-start(bf16[128,128]{1,0:T(8,128)(2,1)S(1)} %collective-permute-done.8.from_s.refs_12_) | copy-start | bytes 98308
  41.7 12.3 %collective-permute-start.9 = (bf16[136,640]{1,0:T(8,128)(2,1)S(1)}, bf16[136,640]{1,0:T(8,128)(2,1)S(1)}, u32[]{:S(2)}, u32[]{:S(2)}) collective-permute-start(bf16[136,640]{1,0:T(8,128)(2,1)S(1)} %get-tuple-element.57), channel_id=1, source_target_pairs={{0,4},{4,0},{8,12},{12,8},{1,5},{5,1},{9,13},{13,9},{2,6},{6,2},{1... | collective-permute-start | bytes 522248 | tf_op jit(solution)/shard_map/ppermute | solution.py:666
  43.6 16.0 %collective-permute-start.10 = (bf16[136,640]{1,0:T(8,128)(2,1)S(1)}, bf16[136,640]{1,0:T(8,128)(2,1)S(1)}, u32[]{:S(2)}, u32[]{:S(2)}) collective-permute-start(bf16[136,640]{1,0:T(8,128)(2,1)S(1)} %get-tuple-element.58), channel_id=1, source_target_pairs={{0,8},{4,12},{8,0},{12,4},{1,9},{5,13},{9,1},{13,5},{2,10},{6,14},... | collective-permute-start | bytes 522248 | tf_op jit(solution)/shard_map/ppermute | solution.py:666
  47.0 12.7 %collective-permute-start.11 = (bf16[136,640]{1,0:T(8,128)(2,1)S(1)}, bf16[136,640]{1,0:T(8,128)(2,1)S(1)}, u32[]{:S(2)}, u32[]{:S(2)}) collective-permute-start(bf16[136,640]{1,0:T(8,128)(2,1)S(1)} %get-tuple-element.59), channel_id=1, source_target_pairs={{0,12},{4,8},{8,4},{12,0},{1,13},{5,9},{9,5},{13,1},{2,14},{6,10},... | collective-permute-start | bytes 522248 | tf_op jit(solution)/shard_map/ppermute | solution.py:666
  48.7 20.7 %copy-start.7 = (bf16[192,128]{1,0:T(8,128)(2,1)}, bf16[192,128]{1,0:T(8,128)(2,1)S(1)}, u32[]{:S(2)}) copy-start(bf16[192,128]{1,0:T(8,128)(2,1)S(1)} %get-tuple-element.63.refs_10_.own_w) | copy-start | bytes 147460
  48.7 20.7 %copy-start.8 = (bf16[192,128]{1,0:T(8,128)(2,1)}, bf16[192,128]{1,0:T(8,128)(2,1)S(1)}, u32[]{:S(2)}) copy-start(bf16[192,128]{1,0:T(8,128)(2,1)S(1)} %get-tuple-element.62.refs_9_.own_e) | copy-start | bytes 147460
  48.7 20.7 %copy-start.15 = (s32[640]{0:T(1024)S(1)}, s32[640]{0:T(1024)}, u32[]{:S(2)}) copy-start(s32[640]{0:T(1024)} %src.1) | copy-start | bytes 7684
  48.7 4.5 %collective-permute-start.12 = (bf16[192,128]{1,0:T(8,128)(2,1)S(1)}, bf16[192,128]{1,0:T(8,128)(2,1)S(1)}, u32[]{:S(2)}, u32[]{:S(2)}) collective-permute-start(bf16[192,128]{1,0:T(8,128)(2,1)S(1)} %get-tuple-element.63.refs_10_.own_w), channel_id=1, source_target_pairs={{1,0},{2,1},{3,2},{5,4},{6,5},{7,6},{9,8},{10,9},{11,10},{13,12},{... | collective-permute-start | bytes 147464 | tf_op jit(solution)/shard_map/ppermute | solution.py:695
  50.1 3.9 %collective-permute-start.13 = (bf16[192,128]{1,0:T(8,128)(2,1)S(1)}, bf16[192,128]{1,0:T(8,128)(2,1)S(1)}, u32[]{:S(2)}, u32[]{:S(2)}) collective-permute-start(bf16[192,128]{1,0:T(8,128)(2,1)S(1)} %get-tuple-element.62.refs_9_.own_e), channel_id=1, source_target_pairs={{0,1},{1,2},{2,3},{4,5},{5,6},{6,7},{8,9},{9,10},{10,11},{12,13},{... | collective-permute-start | bytes 147464 | tf_op jit(solution)/shard_map/ppermute | solution.py:696
  53.2 16.2 %copy-start.9 = (bf16[192,128]{1,0:T(8,128)(2,1)}, bf16[192,128]{1,0:T(8,128)(2,1)S(1)}, u32[]{:S(2)}) copy-start(bf16[192,128]{1,0:T(8,128)(2,1)S(1)} %collective-permute-done.12.refs_13_.from_e) | copy-start | bytes 147460
  54.0 15.4 %copy-start.10 = (bf16[192,128]{1,0:T(8,128)(2,1)}, bf16[192,128]{1,0:T(8,128)(2,1)S(1)}, u32[]{:S(2)}) copy-start(bf16[192,128]{1,0:T(8,128)(2,1)S(1)} %collective-permute-done.13.refs_14_.from_w) | copy-start | bytes 147460
  61.6 0.7 copy-start.3
  62.3 0.6 copy-start.13
  62.9 18.1 %all-to-all-start = ((bf16[32,40,128]{2,1,0:T(8,128)(2,1)}), bf16[32,40,128]{2,1,0:T(8,128)(2,1)S(1)}, u32[]{:S(2)}, u32[]{:S(2)}) async-start(bf16[32,40,128]{2,1,0:T(8,128)(2,1)} %get-tuple-element.67), calls=%async_computation | async-start | bytes 655360 | tf_op jit(solution)/shard_map/all_to_all | solution.py:709
  69.4 11.6 %copy-start.14 = (s32[640]{0:T(1024)S(1)}, s32[640]{0:T(1024)}, u32[]{:S(2)}) copy-start(s32[640]{0:T(1024)} %get-tuple-element.66.slots_in) | copy-start | bytes 7684

commit v10 on v9

--- a/solution.py
+++ b/solution.py
@@ -43,11 +43,12 @@
 def forward_kernel(parts, cap, grid, src, own, dst, flux, w, *refs):
     sends, (slots, held, mixed, acc, rows, xs, counts, renumbered, sems) = refs[:-9], refs[-9:]
     n_sec, n_gx, n_gy = grid
-    devices, chunk, wide = xs.shape
+    devices, _, wide = xs.shape
     total, width, _ = held.shape
     batch = total // parts
     fields = flux.shape[1]
-    first = chunk - 8
+    main = sends[0].shape[1] - 16
+    first = 8
     last = width - 1
 
     def copy(c):
@@ -123,14 +124,17 @@
         wanted = jnp.where(row == at, float(x), wanted)
     group = 16
 
-    def owners(g, _):
+    def owners(g):
         ds = [g * group + j for j in range(group)]
         five = []
         for d in ds:
             x = [acc[pl.ds(d * cap * fields + f, cap, stride=fields), :] for f in range(SENT)]
             x = jnp.concatenate(x, axis=1)
-            xs[d, 0:cap, :] = x
-            five.append(x.astype(BF16))
+            if cap > main:
+                xs[d, 0 : cap - main, :] = x[main:]
+            x = x.astype(BF16)
+            sends[d // n_gx][d % n_gx, 0:main, :] = x[:main]
+            five.append(x)
         where = [rows[pl.ds(pl.multiple_of(d * cap, 8), cap), :] for d in ds]
         hot = [(lane == r).astype(F32).astype(BF16) for r in where]
         flat = [jnp.sum(jnp.where(lane == sub, r, 0.0), axis=0, keepdims=True) for r in where]
@@ -139,8 +143,8 @@
         sides = [dot(e, h, NN) for e, h in zip(edge, hot)]
         ends = [dot((f[:, :cap] == wanted).astype(F32).astype(BF16), x, NN) for f, x in zip(flat, five)]
         for d, f, side, end in zip(ds, flat, sides, ends):
-            here = lax.div(d, n_gx) ^ plane
-            here = (lax.div(here, n_gy) * n_gx + (lax.rem(d, n_gx) ^ line)) * n_gy + lax.rem(here, n_gy)
+            here = (d // n_gx) ^ plane
+            here = (lax.div(here, n_gy) * n_gx + ((d % n_gx) ^ line)) * n_gy + lax.rem(here, n_gy)
 
             def at(offset):
                 return renumbered[lax.rem(here + offset + 2 * devices, devices)]
@@ -160,12 +164,12 @@
             xs[west_of, first + 4 : first + 6, 2 * width : 3 * width] = side[20:22]
             xs[east_of, first + 6 : first + 8, 2 * width : 3 * width] = side[22:24]
             xs[d, first + 1 : first + 2, 0:width] = f
-        return 0
-
-    lax.fori_loop(0, devices // group, owners, 0)
+
+    for g in range(devices // group):
+        owners(g)
 
     for m, send in enumerate(sends):
-        send[...] = xs[m * n_gx : (m + 1) * n_gx].astype(BF16)
+        send[:, main:, :] = xs[m * n_gx : (m + 1) * n_gx].astype(BF16)
 
 
 def forward(flux, w, src, own, dst, grid, cap, parts=8):
@@ -184,7 +188,7 @@
             pltpu.VMEM(flux.shape, BF16),
             pltpu.VMEM((devices * cap * fields, width), F32),
             pltpu.VMEM((devices * cap, width), F32),
-            pltpu.VMEM((devices, chunk, wide), F32),
+            pltpu.VMEM((devices, 16, wide), F32),
             pltpu.SMEM((devices,), jnp.int32),
             pltpu.SMEM((devices,), jnp.int32),
             pltpu.SemaphoreType.DMA((parts,)),
@@ -384,6 +388,13 @@
     return edge
 
 
+def owner_sums(height, width, parts):
+    sums = parts[0][...]
+    for part in parts[1:]:
+        sums = sums + part[...].astype(F32)
+    return [sums[:height, f * width : (f + 1) * width] for f in range(SENT)], sums[height : height + 8]
+
+
 def corrected_edges(levels, ext, stress_u, stress_v, near, far):
     height, width = stress_u.shape
     last = width - 1
@@ -415,21 +426,14 @@
     planes = n_sec * n_gy
     parts, refs = refs[:n_gx], refs[n_gx:]
     tracers, currents, land, own_n, own_s, own_e, own_w, from_n, from_s, from_e, from_w, *refs = refs
-    back, flux, rim = refs
+    (back,) = refs
     height, width = land.shape
     last = width - 1
     lane = iota((1, width), 1)
-    sums = parts[0][...]
-    for part in parts[1:]:
-        sums = sums + part[...].astype(F32)
-    sums, ext = sums[:height], sums[height : height + 8]
-    shortwave, heat, salt, stress_u, stress_v = [sums[:, f * width : (f + 1) * width] for f in range(SENT)]
+    (shortwave, heat, salt, stress_u, stress_v), ext = owner_sums(height, width, parts)
     wet = land[...].astype(F32)
     u0 = currents[0, 0] + 0.1 * stress_u
     v0 = currents[1, 0] + 0.1 * stress_v
-    flux[0], flux[1], flux[2], flux[3], flux[4] = shortwave, heat, salt, stress_u, stress_v
-    rim[...] = ext
-
     near, far = corrected_edges(levels, ext, stress_u, stress_v, (own_n, own_s, own_e, own_w), (from_n, from_s, from_e, from_w))
     far_n, far_s, far_e, far_w = far
     e_turned, w_turned = far_e[:width].T, far_w[:width].T
@@ -469,10 +473,10 @@
         where = part[height + 3 : height + 4, : planes * chunk].astype(F32)
         hot = (iota((height, planes * chunk), 0).astype(F32) == where).astype(F32)
         picked = dot(hot.T.astype(BF16), sst, NN).reshape(planes, chunk, width)
-        for m in range(planes):
+        for i, m in enumerate(swap_order(planes)):
             there = plane ^ m
             device = (lax.div(there, n_gy) * n_gx + (line ^ z)) * n_gy + lax.rem(there, n_gy)
-            back[device] = picked[m, : back.shape[1]].astype(BF16)
+            back[device] = picked[i, : back.shape[1]].astype(BF16)
 
 
 def rim_flux(ext, width):
@@ -487,10 +491,9 @@
     )
 
 
-def stencil_kernel(
-    tracers_in, currents_in, land, flux, rim, own_n, own_s, own_e, own_w, from_n, from_s, from_e, from_w,
-    result, tracers, currents, out, held, weights, edge_n, edge_s, line_n, line_s, depth, forced, passing, sems,
-):
+def stencil_kernel(n_gx, tracers_in, currents_in, land, *refs):
+    parts, edges, refs = refs[:n_gx], refs[n_gx : n_gx + 8], refs[n_gx + 8 :]
+    result, tracers, currents, out, held, weights, edge_n, edge_s, line_n, line_s, depth, forced, passing, sems = refs
     copies = [
         pltpu.make_async_copy(tracers_in, tracers, sems.at[0]),
         pltpu.make_async_copy(currents_in, currents, sems.at[1]),
@@ -505,9 +508,8 @@
     height, width = land.shape
     last = width - 1
     wet = land[...].astype(F32)
-    near, far = corrected_edges(
-        levels, rim[...], flux[3], flux[4], (own_n, own_s, own_e, own_w), (from_n, from_s, from_e, from_w)
-    )
+    (shortwave, heat, salt, stress_u, stress_v), ext = owner_sums(height, width, parts)
+    near, far = corrected_edges(levels, ext, stress_u, stress_v, edges[:4], edges[4:])
     far_n, far_s, far_e, far_w = far
     edge_n[...], edge_s[...] = far_n, far_s
     e_turned, w_turned = far_e[:width].T, far_w[:width].T
@@ -516,12 +518,12 @@
         wet_products(wet, far_n[at : at + 1], far_s[at : at + 1], column(e_turned, at, last), column(w_turned, at, 0))
     ):
         passing[i] = x
-    forced[0], forced[1], forced[2] = 0.3 * wet * flux[0], wet * flux[1], wet * flux[2]
+    forced[0], forced[1], forced[2] = 0.3 * wet * shortwave, wet * heat, wet * salt
     depth[...] = level_profile(levels, width)
     columns = []
     for tracer in range(2):
         lines = strips(
-            tracer, levels, near, far, rim_flux(rim[...], width)
+            tracer, levels, near, far, rim_flux(ext, width)
         )
         line_n[tracer * levels : (tracer + 1) * levels] = lines[0]
         line_s[tracer * levels : (tracer + 1) * levels] = lines[1]
@@ -542,8 +544,8 @@
 
     for copy in copies:
         copy.wait()
-    currents[0, 0] = currents[0, 0] + 0.1 * flux[3]
-    currents[1, 0] = currents[1, 0] + 0.1 * flux[4]
+    currents[0, 0] = currents[0, 0] + 0.1 * stress_u
+    currents[1, 0] = currents[1, 0] + 0.1 * stress_v
 
     def first_step(l, _):
         u, v = currents[0, l], currents[1, l]
@@ -662,6 +664,10 @@
     return forward_pairs, [(b, a) for a, b in forward_pairs]
 
 
+def swap_order(count):
+    return [0, count - 1, count - 2, 1] + list(range(count - 3, 1, -1))
+
+
 def swapped(array, axes, count, step):
     return lax.ppermute(array, axes, [(i, i ^ step) for i in range(count)])
 
@@ -676,13 +682,15 @@
 
     *sends, slots = forward(atm_flux, remap_weights, remap_src, remap_owner.reshape(1, total), remap_dst, grid, cap)
     chunk = sends[0].shape[1]
-    got = [sends[0]] + [swapped(sends[m], ("sec", "gy"), planes, m) for m in range(1, planes)]
+    order = swap_order(planes)
+    got = [sends[0]] + [swapped(sends[m], ("sec", "gy"), planes, m) for m in order[1:]]
+    early = order.index(1)
 
     side = (width, width)
     end = (7 * levels + 80, width)
     to_north, to_south = neighbours(NORTH)
     to_east, to_west = neighbours("gy")
-    got[1], tracers_there, currents_there = lax.optimization_barrier((got[1], tracers, currents))
+    got[early], tracers_there, currents_there = lax.optimization_barrier((got[early], tracers, currents))
     own_s, own_n = kernel(rows_kernel, [(side, BF16)] * 2, "edge_rows", 16, 1 << 20)(
         tracers_there.reshape(-1, width), currents_there.reshape(-1, width), land_sea
     )
@@ -699,9 +707,9 @@
     parts = [merged[0]] + [swapped(merged[m], "gx", n_gx, m) for m in range(1, n_gx)]
 
     edges = own_n, own_s, own_e, own_w, from_n, from_s, from_e, from_w
-    back, flux, rim = kernel(
+    (back,) = kernel(
         functools.partial(surface_kernel, grid, chunk, levels),
-        [((planes * n_gx, cap, width), BF16), ((5, height, width), F32), ((8, wide), F32)],
+        [((planes * n_gx, cap, width), BF16)],
         "surface",
         24,
         1 << 22,
@@ -710,7 +718,7 @@
 
     plane = (height, width)
     (tracers_out,) = kernel(
-        stencil_kernel,
+        functools.partial(stencil_kernel, n_gx),
         [(tracers.shape, F32)],
         "substeps",
         58,
@@ -730,9 +738,9 @@
             pltpu.VMEM((4,) + plane, F32),
             pltpu.SemaphoreType.DMA((2 + levels,)),
         ],
-        in_specs=[ANY, ANY] + [VMEM] * 11,
+        in_specs=[ANY, ANY] + [VMEM] * (n_gx + 9),
         out_specs=[ANY],
-    )(tracers, currents, land_sea, flux, rim, *edges)
+    )(tracers, currents, land_sea, *parts, *edges)
     return tracers_out, backward(returned, remap_weights, remap_src, slots, atm_flux.shape[0])
 
 

time: 89.7 us -> 87.6 us (0.977)
  local copies, waits for them, and re-layouts: 1.44 us -> 0.12 us
  starting transfers between devices: 31.2 us -> 30.3 us
    unnamed x32 -> x36, local copies, waits for them, and re-layouts: 1.4 us -> 0.08 us
    ppermute x10, starting transfers between devices: 14.5 us -> 13.6 us  [swapped(): return lax.ppermute(array, axes, [(i, i ^ step) for i in range(count)])]
  transfers between devices with their start and end apart: 15 -> 15, of which waited for: 6 -> 9; matrix products, arithmetic and copies ran while one was open for 0% -> 0% of each run, Pallas kernels for 14% -> 15%
where the time goes in v10:
time: 87.6 us; the launch traced here: 87.3 us
  Pallas kernels  37.4 us (43%)
  starting transfers between devices  30.3 us (35%)
  waiting for transfers between devices  18.5 us (21%)
  between operations  0.94 us (1%)
    ppermute x10, waiting for transfers between devices, swapped(): return lax.ppermute(array, axes, [(i, i ^ step) for i in range(count)])  17.3 us
    pallas_call x1, Pallas kernels, forward(): pl.pallas_call(functools.partial(forward_kernel, parts, cap, grid), in_sp...  13.6 us
    ppermute x10, starting transfers between devices, swapped(): return lax.ppermute(array, axes, [(i, i ^ step) for i in range(count)])  13.6 us
    pallas_call x1, Pallas kernels, on_device(): kernel(functools.partial(stencil_kernel, n_gx), [(tracers.shape, F32)], '...  11.1 us
    pallas_call x1, Pallas kernels, backward(): pl.pallas_call(functools.partial(backward_kernel, parts), in_specs=[ANY,...  8.4 us
    all_to_all x1, starting transfers between devices, on_device(): lax.all_to_all(back, EVERY, split_axis=0, concat_axis=0, tiled=True)  7.25 us
    ppermute x1, starting transfers between devices, on_device(): from_s = lax.ppermute(own_n, NORTH, to_north)  3.67 us
    ppermute x1, starting transfers between devices, on_device(): from_w = lax.ppermute(own_e, 'gy', to_east)  3.03 us
  transfers between devices with their start and end apart: 15, of which 9 were waited for; matrix products, arithmetic and copies ran while one was open for 0% of the time, Pallas kernels for 15%

profile of v10, /device:TPU:0, one launch (start us, length us, event | category | flops | bytes accessed | tf_op | source)
XLA Modules:
  0.0 87.3 jit_solution(4089547958246489105)
XLA Ops:
  0.7 0.0 copy-start.3
  0.7 13.6 %forward_remap.1 = (bf16[4,48,640]{2,1,0:T(8,128)(2,1)}, bf16[4,48,640]{2,1,0:T(8,128)(2,1)}, bf16[4,48,640]{2,1,0:T(8,128)(2,1)}, bf16[4,48,640]{2,1,0:T(8,128)...) custom-call(s32[640]{0:T(1024)} %src.1, ...), custom_call_target="tpu_custom_call" | custom-call | flops 167772160 | bytes 20971520 | tf_op jit(solution)/shard_map/forward_remap/pallas_call | solution.py:182
  14.3 0.5 collective-permute-start.2
  14.8 3.6 %collective-permute-start = (bf16[4,48,640]{2,1,0:T(8,128)(2,1)}, bf16[4,48,640]{2,1,0:T(8,128)(2,1)S(1)}, u32[]{:S(2)}, u32[]{:S(2)}) collective-permute-start(bf16[4,48,640]{2,1,0:T(8,128)(2,1)} %get-tuple-element.33), channel_id=1, source_target_pairs={{0,19},{1,18},{2,17},{3,16},{16,3},{17,2},{18,1},{19,0},{4,23},{5,... | collective-permute-start | bytes 737288 | tf_op jit(solution)/shard_map/ppermute | solution.py:672
  18.4 0.0 collective-permute-start.1
  18.5 1.3 %collective-permute-start.3 = (bf16[4,48,640]{2,1,0:T(8,128)(2,1)}, bf16[4,48,640]{2,1,0:T(8,128)(2,1)S(1)}, u32[]{:S(2)}, u32[]{:S(2)}) collective-permute-start(bf16[4,48,640]{2,1,0:T(8,128)(2,1)} %get-tuple-element.37), channel_id=1, source_target_pairs={{0,17},{1,16},{2,19},{3,18},{16,1},{17,0},{18,3},{19,2},{4,21},{5,... | collective-permute-start | bytes 737288 | tf_op jit(solution)/shard_map/ppermute | solution.py:672
  19.8 0.6 collective-permute-start.4
  20.4 1.4 %collective-permute-start.5 = (bf16[4,48,640]{2,1,0:T(8,128)(2,1)}, bf16[4,48,640]{2,1,0:T(8,128)(2,1)S(1)}, u32[]{:S(2)}, u32[]{:S(2)}) collective-permute-start(bf16[4,48,640]{2,1,0:T(8,128)(2,1)} %get-tuple-element.39), channel_id=1, source_target_pairs={{0,3},{1,2},{2,1},{3,0},{16,19},{17,18},{18,17},{19,16},{4,7},{5,6... | collective-permute-start | bytes 737288 | tf_op jit(solution)/shard_map/ppermute | solution.py:672
  21.8 3.2 %collective-permute-done.refs_1_ = bf16[4,48,640]{2,1,0:T(8,128)(2,1)S(1)} collective-permute-done((bf16[4,48,640]{2,1,0:T(8,128)(2,1)}, bf16[4,48,640]{2,1,0:T(8,128)(2,1)S(1)}, u32[]{:S(2)}, u32[]{:S(2)}) %collective-permute-start) | collective-permute-done | bytes 245792 | tf_op jit(solution)/shard_map/ppermute | solution.py:672
  25.1 1.2 %collective-permute-start.6 = (bf16[4,48,640]{2,1,0:T(8,128)(2,1)}, bf16[4,48,640]{2,1,0:T(8,128)(2,1)S(1)}, u32[]{:S(2)}, u32[]{:S(2)}) collective-permute-start(bf16[4,48,640]{2,1,0:T(8,128)(2,1)} %get-tuple-element.40), channel_id=1, source_target_pairs={{0,2},{1,3},{2,0},{3,1},{16,18},{17,19},{18,16},{19,17},{4,6},{5,7... | collective-permute-start | bytes 737288 | tf_op jit(solution)/shard_map/ppermute | solution.py:672
  26.3 0.1 edge_rows.1
  26.4 4.3 %collective-permute-done.1.refs_2_ = bf16[4,48,640]{2,1,0:T(8,128)(2,1)S(1)} collective-permute-done((bf16[4,48,640]{2,1,0:T(8,128)(2,1)}, bf16[4,48,640]{2,1,0:T(8,128)(2,1)S(1)}, u32[]{:S(2)}, u32[]{:S(2)}) %collective-permute-start.1) | collective-permute-done | bytes 245792 | tf_op jit(solution)/shard_map/ppermute | solution.py:672
  30.7 1.3 %collective-permute-start.7 = (bf16[128,128]{1,0:T(8,128)(2,1)S(1)}, bf16[128,128]{1,0:T(8,128)(2,1)S(1)}, u32[]{:S(2)}, u32[]{:S(2)}) collective-permute-start(bf16[128,128]{1,0:T(8,128)(2,1)S(1)} %get-tuple-element.43.refs_5_.refs_8_), channel_id=1, source_target_pairs={{4,0},{8,4},{12,8},{16,12},{20,16},{24,20},{28,24},{5,1},{9,5},{13... | collective-permute-start | bytes 98312 | tf_op jit(solution)/shard_map/ppermute | solution.py:697
  32.0 3.6 %collective-permute-done.3.refs_4_ = bf16[4,48,640]{2,1,0:T(8,128)(2,1)S(1)} collective-permute-done((bf16[4,48,640]{2,1,0:T(8,128)(2,1)}, bf16[4,48,640]{2,1,0:T(8,128)(2,1)S(1)}, u32[]{:S(2)}, u32[]{:S(2)}) %collective-permute-start.3) | collective-permute-done | bytes 245792 | tf_op jit(solution)/shard_map/ppermute | solution.py:672
  35.6 3.7 %collective-permute-start.8 = (bf16[128,128]{1,0:T(8,128)(2,1)S(1)}, bf16[128,128]{1,0:T(8,128)(2,1)S(1)}, u32[]{:S(2)}, u32[]{:S(2)}) collective-permute-start(bf16[128,128]{1,0:T(8,128)(2,1)S(1)} %get-tuple-element.44.refs_4_.refs_7_), channel_id=1, source_target_pairs={{0,4},{4,8},{8,12},{12,16},{16,20},{20,24},{24,28},{1,5},{5,9},{9,... | collective-permute-start | bytes 98312 | tf_op jit(solution)/shard_map/ppermute | solution.py:698
  39.3 1.6 %collective-permute-done.4.refs_5_ = bf16[4,48,640]{2,1,0:T(8,128)(2,1)S(1)} collective-permute-done((bf16[4,48,640]{2,1,0:T(8,128)(2,1)}, bf16[4,48,640]{2,1,0:T(8,128)(2,1)S(1)}, u32[]{:S(2)}, u32[]{:S(2)}) %collective-permute-start.4) | collective-permute-done | bytes 245792 | tf_op jit(solution)/shard_map/ppermute | solution.py:672
  40.9 0.3 collective-permute-done.6.refs_7_
  41.2 0.6 merge.1
  41.9 3.0 %collective-permute-start.10 = (bf16[136,640]{1,0:T(8,128)(2,1)S(1)}, bf16[136,640]{1,0:T(8,128)(2,1)S(1)}, u32[]{:S(2)}, u32[]{:S(2)}) collective-permute-start(bf16[136,640]{1,0:T(8,128)(2,1)S(1)} %get-tuple-element.55), channel_id=1, source_target_pairs={{0,8},{4,12},{8,0},{12,4},{1,9},{5,13},{9,1},{13,5},{2,10},{6,14},... | collective-permute-start | bytes 522248 | tf_op jit(solution)/shard_map/ppermute | solution.py:672
  44.9 1.3 %collective-permute-start.11 = (bf16[136,640]{1,0:T(8,128)(2,1)S(1)}, bf16[136,640]{1,0:T(8,128)(2,1)S(1)}, u32[]{:S(2)}, u32[]{:S(2)}) collective-permute-start(bf16[136,640]{1,0:T(8,128)(2,1)S(1)} %get-tuple-element.56), channel_id=1, source_target_pairs={{0,12},{4,8},{8,4},{12,0},{1,13},{5,9},{9,5},{13,1},{2,14},{6,10},... | collective-permute-start | bytes 522248 | tf_op jit(solution)/shard_map/ppermute | solution.py:672
  46.2 0.5 collective-permute-start.9
  46.7 1.7 %edge_columns.1 = (bf16[192,128]{1,0:T(8,128)(2,1)S(1)}, bf16[192,128]{1,0:T(8,128)(2,1)S(1)}) custom-call(f32[2,16,128,128]{3,2,1,0:T(8,128)S(1)} %copy-done.1, f32[2,16,128,128]{3,2,1,0:T(8,128)S(1)} %copy-done, s32[128,128]{1,0:T(8,128)S(1)} %copy-done.3, bf16[128,128]{1,0:T(8,128)(2,1)S(1)} %collective-permute-done.7.from_n.refs_8_.refs_11_, ...), custom_call_target="tpu_custom_call" | custom-call | flops 4194304 | bytes 4194304 | tf_op jit(solution)/shard_map/edge_columns/pallas_call | solution.py:700
  48.4 1.4 %collective-permute-start.12 = (bf16[192,128]{1,0:T(8,128)(2,1)S(1)}, bf16[192,128]{1,0:T(8,128)(2,1)S(1)}, u32[]{:S(2)}, u32[]{:S(2)}) collective-permute-start(bf16[192,128]{1,0:T(8,128)(2,1)S(1)} %get-tuple-element.60.refs_7_.refs_10_), channel_id=1, source_target_pairs={{1,0},{2,1},{3,2},{5,4},{6,5},{7,6},{9,8},{10,9},{11,10},{13,12},{... | collective-permute-start | bytes 147464 | tf_op jit(solution)/shard_map/ppermute | solution.py:703
  49.9 3.0 %collective-permute-start.13 = (bf16[192,128]{1,0:T(8,128)(2,1)S(1)}, bf16[192,128]{1,0:T(8,128)(2,1)S(1)}, u32[]{:S(2)}, u32[]{:S(2)}) collective-permute-start(bf16[192,128]{1,0:T(8,128)(2,1)S(1)} %get-tuple-element.59.refs_6_.refs_9_), channel_id=1, source_target_pairs={{0,1},{1,2},{2,3},{4,5},{5,6},{6,7},{8,9},{9,10},{10,11},{12,13},{... | collective-permute-start | bytes 147464 | tf_op jit(solution)/shard_map/ppermute | solution.py:704
  53.0 0.8 collective-permute-done.13.refs_11_.refs_14_
  53.8 3.9 %collective-permute-done.10.refs_2_ = bf16[136,640]{1,0:T(8,128)(2,1)S(1)} collective-permute-done((bf16[136,640]{1,0:T(8,128)(2,1)S(1)}, bf16[136,640]{1,0:T(8,128)(2,1)S(1)}, u32[]{:S(2)}, u32[]{:S(2)}) %collective-permute-start.10) | collective-permute-done | bytes 174112 | tf_op jit(solution)/shard_map/ppermute | solution.py:672
  57.7 0.3 collective-permute-done.9.refs_1_
  58.1 1.9 %surface.1 = bf16[32,40,128]{2,1,0:T(8,128)(2,1)} custom-call(f32[136,640]{1,0:T(8,128)S(1)} %get-tuple-element.53.refs_0_, bf16[136,640]{1,0:T(8,128)(2,1)S(1)} %collective-permute-done.9.refs_1_, bf16[136,640]{1,0:T(8,128)(2,1)S(1)} %collective-permute-done.10.refs_2_, bf16[136,640]{1,0:T(8,128)(2,1)S(1)} %collective-permute-done.11.refs_3_, ...), custom_call_target="tpu_custom_call" | custom-call | flops 4194304 | bytes 4194304 | tf_op jit(solution)/shard_map/surface/pallas_call | solution.py:710
  59.9 7.3 %all-to-all-start = ((bf16[32,40,128]{2,1,0:T(8,128)(2,1)}), bf16[32,40,128]{2,1,0:T(8,128)(2,1)S(1)}, u32[]{:S(2)}, u32[]{:S(2)}) async-start(bf16[32,40,128]{2,1,0:T(8,128)(2,1)} %surface.1), calls=%async_computation | async-start | bytes 655360 | tf_op jit(solution)/shard_map/all_to_all | solution.py:717
  67.3 11.1 %substeps.1 = f32[2,16,128,128]{3,2,1,0:T(8,128)} custom-call(f32[2,16,128,128]{3,2,1,0:T(8,128)} %tracers_in.1, f32[2,16,128,128]{3,2,1,0:T(8,128)} %currents_in.1, s32[128,128]{1,0:T(8,128)} %refs_6_.1, f32[136,640]{1,0:T(8,128)} %copy-done.2, bf16[136,640]{1,0:T(8,128)(2,1)} %copy-done.6, bf16[136,640]{1,0:T(8,128)(2,1)} %copy-done.4, ...), custom_call_target="tpu_custom_call" | custom-call | flops 16777216 | bytes 16777216 | tf_op jit(solution)/shard_map/substeps/pallas_call | solution.py:720
  78.4 0.5 all-to-all-done.back
  78.9 8.4 %backward_remap.1 = f32[160,128]{1,0:T(8,128)} custom-call(s32[640]{0:T(1024)S(1)} %copy-done.16, s32[1,640]{1,0:T(1,128)S(1)} %reshape.19.src, bf16[32,40,128]{2,1,0:T(8,128)(2,1)S(1)} %all-to-all-done.back, bf16[640,128,128]{2,1,0:T(8,128)(2,1)} %w.3), custom_call_target="tpu_custom_call" | custom-call | flops 167772160 | bytes 20971520 | tf_op jit(solution)/shard_map/backward_remap/pallas_call | solution.py:630
  (44 shorter events, 0.1 us)
Async XLA Ops:
  0.6 25.7 %copy-start = (f32[2,16,128,128]{3,2,1,0:T(8,128)S(1)}, f32[2,16,128,128]{3,2,1,0:T(8,128)}, u32[]{:S(2)}) copy-start(f32[2,16,128,128]{3,2,1,0:T(8,128)} %currents_in.1) | copy-start | bytes 6291460
  0.6 25.7 %copy-start.1 = (f32[2,16,128,128]{3,2,1,0:T(8,128)S(1)}, f32[2,16,128,128]{3,2,1,0:T(8,128)}, u32[]{:S(2)}) copy-start(f32[2,16,128,128]{3,2,1,0:T(8,128)} %tracers_in.1) | copy-start | bytes 6291460
  0.7 25.6 %copy-start.3 = (s32[128,128]{1,0:T(8,128)S(1)}, s32[128,128]{1,0:T(8,128)}, u32[]{:S(2)}) copy-start(s32[128,128]{1,0:T(8,128)} %refs_6_.1) | copy-start | bytes 196612
  14.3 6.1 %collective-permute-start.2 = (bf16[4,48,640]{2,1,0:T(8,128)(2,1)}, bf16[4,48,640]{2,1,0:T(8,128)(2,1)S(1)}, u32[]{:S(2)}, u32[]{:S(2)}) collective-permute-start(bf16[4,48,640]{2,1,0:T(8,128)(2,1)} %get-tuple-element.35), channel_id=1, source_target_pairs={{0,1},{1,0},{2,3},{3,2},{16,17},{17,16},{18,19},{19,18},{4,5},{5,4... | collective-permute-start | bytes 737288 | tf_op jit(solution)/shard_map/ppermute | solution.py:672
  14.8 10.2 %collective-permute-start = (bf16[4,48,640]{2,1,0:T(8,128)(2,1)}, bf16[4,48,640]{2,1,0:T(8,128)(2,1)S(1)}, u32[]{:S(2)}, u32[]{:S(2)}) collective-permute-start(bf16[4,48,640]{2,1,0:T(8,128)(2,1)} %get-tuple-element.33), channel_id=1, source_target_pairs={{0,19},{1,18},{2,17},{3,16},{16,3},{17,2},{18,1},{19,0},{4,23},{5,... | collective-permute-start | bytes 737288 | tf_op jit(solution)/shard_map/ppermute | solution.py:672
  18.4 12.3 %collective-permute-start.1 = (bf16[4,48,640]{2,1,0:T(8,128)(2,1)}, bf16[4,48,640]{2,1,0:T(8,128)(2,1)S(1)}, u32[]{:S(2)}, u32[]{:S(2)}) collective-permute-start(bf16[4,48,640]{2,1,0:T(8,128)(2,1)} %get-tuple-element.34), channel_id=1, source_target_pairs={{0,18},{1,19},{2,16},{3,17},{16,2},{17,3},{18,0},{19,1},{4,22},{5,... | collective-permute-start | bytes 737288 | tf_op jit(solution)/shard_map/ppermute | solution.py:672
  18.5 17.1 %collective-permute-start.3 = (bf16[4,48,640]{2,1,0:T(8,128)(2,1)}, bf16[4,48,640]{2,1,0:T(8,128)(2,1)S(1)}, u32[]{:S(2)}, u32[]{:S(2)}) collective-permute-start(bf16[4,48,640]{2,1,0:T(8,128)(2,1)} %get-tuple-element.37), channel_id=1, source_target_pairs={{0,17},{1,16},{2,19},{3,18},{16,1},{17,0},{18,3},{19,2},{4,21},{5,... | collective-permute-start | bytes 737288 | tf_op jit(solution)/shard_map/ppermute | solution.py:672
  19.8 21.1 %collective-permute-start.4 = (bf16[4,48,640]{2,1,0:T(8,128)(2,1)}, bf16[4,48,640]{2,1,0:T(8,128)(2,1)S(1)}, u32[]{:S(2)}, u32[]{:S(2)}) collective-permute-start(bf16[4,48,640]{2,1,0:T(8,128)(2,1)} %get-tuple-element.38), channel_id=1, source_target_pairs={{0,16},{1,17},{2,18},{3,19},{16,0},{17,1},{18,2},{19,3},{4,20},{5,... | collective-permute-start | bytes 737288 | tf_op jit(solution)/shard_map/ppermute | solution.py:672
  20.4 20.5 %collective-permute-start.5 = (bf16[4,48,640]{2,1,0:T(8,128)(2,1)}, bf16[4,48,640]{2,1,0:T(8,128)(2,1)S(1)}, u32[]{:S(2)}, u32[]{:S(2)}) collective-permute-start(bf16[4,48,640]{2,1,0:T(8,128)(2,1)} %get-tuple-element.39), channel_id=1, source_target_pairs={{0,3},{1,2},{2,1},{3,0},{16,19},{17,18},{18,17},{19,16},{4,7},{5,6... | collective-permute-start | bytes 737288 | tf_op jit(solution)/shard_map/ppermute | solution.py:672
  25.1 16.1 %collective-permute-start.6 = (bf16[4,48,640]{2,1,0:T(8,128)(2,1)}, bf16[4,48,640]{2,1,0:T(8,128)(2,1)S(1)}, u32[]{:S(2)}, u32[]{:S(2)}) collective-permute-start(bf16[4,48,640]{2,1,0:T(8,128)(2,1)} %get-tuple-element.40), channel_id=1, source_target_pairs={{0,2},{1,3},{2,0},{3,1},{16,18},{17,19},{18,16},{19,17},{4,6},{5,7... | collective-permute-start | bytes 737288 | tf_op jit(solution)/shard_map/ppermute | solution.py:672
  26.3 14.9 %copy-start.9 = (bf16[4,48,640]{2,1,0:T(8,128)(2,1)S(1)}, bf16[4,48,640]{2,1,0:T(8,128)(2,1)}, u32[]{:S(2)}) copy-start(bf16[4,48,640]{2,1,0:T(8,128)(2,1)} %get-tuple-element.45.refs_0_) | copy-start | bytes 737284
  26.4 31.6 %copy-start.14 = (bf16[128,128]{1,0:T(8,128)(2,1)}, bf16[128,128]{1,0:T(8,128)(2,1)S(1)}, u32[]{:S(2)}) copy-start(bf16[128,128]{1,0:T(8,128)(2,1)S(1)} %get-tuple-element.43.refs_5_.refs_8_) | copy-start | bytes 98308
  26.4 31.6 %copy-start.15 = (bf16[128,128]{1,0:T(8,128)(2,1)}, bf16[128,128]{1,0:T(8,128)(2,1)S(1)}, u32[]{:S(2)}) copy-start(bf16[128,128]{1,0:T(8,128)(2,1)S(1)} %get-tuple-element.44.refs_4_.refs_7_) | copy-start | bytes 98308
  30.7 10.5 %collective-permute-start.7 = (bf16[128,128]{1,0:T(8,128)(2,1)S(1)}, bf16[128,128]{1,0:T(8,128)(2,1)S(1)}, u32[]{:S(2)}, u32[]{:S(2)}) collective-permute-start(bf16[128,128]{1,0:T(8,128)(2,1)S(1)} %get-tuple-element.43.refs_5_.refs_8_), channel_id=1, source_target_pairs={{4,0},{8,4},{12,8},{16,12},{20,16},{24,20},{28,24},{5,1},{9,5},{13... | collective-permute-start | bytes 98312 | tf_op jit(solution)/shard_map/ppermute | solution.py:697
  35.6 5.6 %collective-permute-start.8 = (bf16[128,128]{1,0:T(8,128)(2,1)S(1)}, bf16[128,128]{1,0:T(8,128)(2,1)S(1)}, u32[]{:S(2)}, u32[]{:S(2)}) collective-permute-start(bf16[128,128]{1,0:T(8,128)(2,1)S(1)} %get-tuple-element.44.refs_4_.refs_7_), channel_id=1, source_target_pairs={{0,4},{4,8},{8,12},{12,16},{16,20},{20,24},{24,28},{1,5},{5,9},{9,... | collective-permute-start | bytes 98312 | tf_op jit(solution)/shard_map/ppermute | solution.py:698
  41.2 16.8 %copy-start.7 = (bf16[128,128]{1,0:T(8,128)(2,1)}, bf16[128,128]{1,0:T(8,128)(2,1)S(1)}, u32[]{:S(2)}) copy-start(bf16[128,128]{1,0:T(8,128)(2,1)S(1)} %collective-permute-done.7.from_n.refs_8_.refs_11_) | copy-start | bytes 98308
  41.2 16.8 %copy-start.8 = (bf16[128,128]{1,0:T(8,128)(2,1)}, bf16[128,128]{1,0:T(8,128)(2,1)S(1)}, u32[]{:S(2)}) copy-start(bf16[128,128]{1,0:T(8,128)(2,1)S(1)} %collective-permute-done.8.from_s.refs_9_.refs_12_) | copy-start | bytes 98308
  41.8 16.2 %copy-start.2 = (f32[136,640]{1,0:T(8,128)}, f32[136,640]{1,0:T(8,128)S(1)}, u32[]{:S(2)}) copy-start(f32[136,640]{1,0:T(8,128)S(1)} %get-tuple-element.53.refs_0_) | copy-start | bytes 1044484
  41.9 15.8 %collective-permute-start.10 = (bf16[136,640]{1,0:T(8,128)(2,1)S(1)}, bf16[136,640]{1,0:T(8,128)(2,1)S(1)}, u32[]{:S(2)}, u32[]{:S(2)}) collective-permute-start(bf16[136,640]{1,0:T(8,128)(2,1)S(1)} %get-tuple-element.55), channel_id=1, source_target_pairs={{0,8},{4,12},{8,0},{12,4},{1,9},{5,13},{9,1},{13,5},{2,10},{6,14},... | collective-permute-start | bytes 522248 | tf_op jit(solution)/shard_map/ppermute | solution.py:672
  44.9 12.8 %collective-permute-start.11 = (bf16[136,640]{1,0:T(8,128)(2,1)S(1)}, bf16[136,640]{1,0:T(8,128)(2,1)S(1)}, u32[]{:S(2)}, u32[]{:S(2)}) collective-permute-start(bf16[136,640]{1,0:T(8,128)(2,1)S(1)} %get-tuple-element.56), channel_id=1, source_target_pairs={{0,12},{4,8},{8,4},{12,0},{1,13},{5,9},{9,5},{13,1},{2,14},{6,10},... | collective-permute-start | bytes 522248 | tf_op jit(solution)/shard_map/ppermute | solution.py:672
  46.2 11.8 %collective-permute-start.9 = (bf16[136,640]{1,0:T(8,128)(2,1)S(1)}, bf16[136,640]{1,0:T(8,128)(2,1)S(1)}, u32[]{:S(2)}, u32[]{:S(2)}) collective-permute-start(bf16[136,640]{1,0:T(8,128)(2,1)S(1)} %get-tuple-element.54), channel_id=1, source_target_pairs={{0,4},{4,0},{8,12},{12,8},{1,5},{5,1},{9,13},{13,9},{2,6},{6,2},{1... | collective-permute-start | bytes 522248 | tf_op jit(solution)/shard_map/ppermute | solution.py:672
  48.4 18.8 %copy-start.10 = (bf16[192,128]{1,0:T(8,128)(2,1)}, bf16[192,128]{1,0:T(8,128)(2,1)S(1)}, u32[]{:S(2)}) copy-start(bf16[192,128]{1,0:T(8,128)(2,1)S(1)} %get-tuple-element.60.refs_7_.refs_10_) | copy-start | bytes 147460
  48.4 18.8 %copy-start.11 = (bf16[192,128]{1,0:T(8,128)(2,1)}, bf16[192,128]{1,0:T(8,128)(2,1)S(1)}, u32[]{:S(2)}) copy-start(bf16[192,128]{1,0:T(8,128)(2,1)S(1)} %get-tuple-element.59.refs_6_.refs_9_) | copy-start | bytes 147460
  48.4 18.8 %copy-start.17 = (s32[640]{0:T(1024)S(1)}, s32[640]{0:T(1024)}, u32[]{:S(2)}) copy-start(s32[640]{0:T(1024)} %src.1) | copy-start | bytes 7684
  48.4 4.5 %collective-permute-start.12 = (bf16[192,128]{1,0:T(8,128)(2,1)S(1)}, bf16[192,128]{1,0:T(8,128)(2,1)S(1)}, u32[]{:S(2)}, u32[]{:S(2)}) collective-permute-start(bf16[192,128]{1,0:T(8,128)(2,1)S(1)} %get-tuple-element.60.refs_7_.refs_10_), channel_id=1, source_target_pairs={{1,0},{2,1},{3,2},{5,4},{6,5},{7,6},{9,8},{10,9},{11,10},{13,12},{... | collective-permute-start | bytes 147464 | tf_op jit(solution)/shard_map/ppermute | solution.py:703
  49.9 3.9 %collective-permute-start.13 = (bf16[192,128]{1,0:T(8,128)(2,1)S(1)}, bf16[192,128]{1,0:T(8,128)(2,1)S(1)}, u32[]{:S(2)}, u32[]{:S(2)}) collective-permute-start(bf16[192,128]{1,0:T(8,128)(2,1)S(1)} %get-tuple-element.59.refs_6_.refs_9_), channel_id=1, source_target_pairs={{0,1},{1,2},{2,3},{4,5},{5,6},{6,7},{8,9},{9,10},{10,11},{12,13},{... | collective-permute-start | bytes 147464 | tf_op jit(solution)/shard_map/ppermute | solution.py:704
  53.0 14.3 %copy-start.12 = (bf16[192,128]{1,0:T(8,128)(2,1)}, bf16[192,128]{1,0:T(8,128)(2,1)S(1)}, u32[]{:S(2)}) copy-start(bf16[192,128]{1,0:T(8,128)(2,1)S(1)} %collective-permute-done.12.refs_10_.refs_13_) | copy-start | bytes 147460
  53.8 13.5 %copy-start.13 = (bf16[192,128]{1,0:T(8,128)(2,1)}, bf16[192,128]{1,0:T(8,128)(2,1)S(1)}, u32[]{:S(2)}) copy-start(bf16[192,128]{1,0:T(8,128)(2,1)S(1)} %collective-permute-done.13.refs_11_.refs_14_) | copy-start | bytes 147460
  57.7 9.6 %copy-start.4 = (bf16[136,640]{1,0:T(8,128)(2,1)}, bf16[136,640]{1,0:T(8,128)(2,1)S(1)}, u32[]{:S(2)}) copy-start(bf16[136,640]{1,0:T(8,128)(2,1)S(1)} %collective-permute-done.10.refs_2_) | copy-start | bytes 522244
  57.7 9.6 %copy-start.5 = (bf16[136,640]{1,0:T(8,128)(2,1)}, bf16[136,640]{1,0:T(8,128)(2,1)S(1)}, u32[]{:S(2)}) copy-start(bf16[136,640]{1,0:T(8,128)(2,1)S(1)} %collective-permute-done.11.refs_3_) | copy-start | bytes 522244
  59.9 19.0 %all-to-all-start = ((bf16[32,40,128]{2,1,0:T(8,128)(2,1)}), bf16[32,40,128]{2,1,0:T(8,128)(2,1)S(1)}, u32[]{:S(2)}, u32[]{:S(2)}) async-start(bf16[32,40,128]{2,1,0:T(8,128)(2,1)} %surface.1), calls=%async_computation | async-start | bytes 655360 | tf_op jit(solution)/shard_map/all_to_all | solution.py:717
  67.3 11.6 %copy-start.16 = (s32[640]{0:T(1024)S(1)}, s32[640]{0:T(1024)}, u32[]{:S(2)}) copy-start(s32[640]{0:T(1024)} %get-tuple-element.61.slots_in) | copy-start | bytes 7684
  (1 other events, 9.3 us)

commit v11 on v10

--- a/solution.py
+++ b/solution.py
@@ -40,8 +40,8 @@
 ANY = pl.BlockSpec(memory_space=pl.ANY)
 
 
-def forward_kernel(parts, cap, grid, src, own, dst, flux, w, *refs):
-    sends, (slots, held, mixed, acc, rows, xs, counts, renumbered, sems) = refs[:-9], refs[-9:]
+def forward_kernel(parts, cap, grid, src_in, own_in, dst_in, flux_in, w, *refs):
+    sends, (slots, held, mixed, acc, rows, xs, counts, renumbered, sems, src, own, dst, flux) = refs[:-13], refs[-13:]
     n_sec, n_gx, n_gy = grid
     devices, _, wide = xs.shape
     total, width, _ = held.shape
@@ -54,6 +54,10 @@
     def copy(c):
         return pltpu.make_async_copy(w.at[pl.ds(c * batch, batch)], held.at[pl.ds(c * batch, batch)], sems.at[c])
 
+    small = [(src_in, src), (own_in, own), (dst_in, dst), (flux_in, flux)]
+    small = [pltpu.make_async_copy(there, here, sems.at[parts + i]) for i, (there, here) in enumerate(small)]
+    for load in small:
+        load.start()
     for c in range(parts):
         copy(c).start()
 
@@ -74,6 +78,8 @@
     rows[...] = jnp.full_like(rows, 255.0)
     acc[...] = jnp.zeros_like(acc)
     xs[...] = jnp.zeros_like(xs)
+    for load in small:
+        load.wait()
     full = flux[...].astype(F32)
     one = [full[:, f : f + 1] for f in range(fields)]
     heat = 0.2 * (one[1] + one[2] + one[3]) - 0.15 * one[5]
@@ -181,7 +187,7 @@
     wide = SENT * width
     return pl.pallas_call(
         functools.partial(forward_kernel, parts, cap, grid),
-        in_specs=[SMEM, SMEM, SMEM, VMEM, ANY],
+        in_specs=[ANY] * 5,
         out_specs=[VMEM] * (n_sec * n_gy) + [SMEM],
         scratch_shapes=[
             pltpu.VMEM(w.shape, BF16),
@@ -191,7 +197,11 @@
             pltpu.VMEM((devices, 16, wide), F32),
             pltpu.SMEM((devices,), jnp.int32),
             pltpu.SMEM((devices,), jnp.int32),
-            pltpu.SemaphoreType.DMA((parts,)),
+            pltpu.SemaphoreType.DMA((parts + 4,)),
+            pltpu.SMEM(src.shape, jnp.int32),
+            pltpu.SMEM(own.shape, jnp.int32),
+            pltpu.SMEM(dst.shape, jnp.int32),
+            pltpu.VMEM(flux.shape, BF16),
         ],
         out_shape=[jax.ShapeDtypeStruct((n_gx, chunk, wide), BF16)] * (n_sec * n_gy) + [jax.ShapeDtypeStruct((total,), jnp.int32)],
         compiler_params=kernel_params(58),
@@ -491,19 +501,20 @@
     )
 
 
-def stencil_kernel(n_gx, tracers_in, currents_in, land, *refs):
-    parts, edges, refs = refs[:n_gx], refs[n_gx : n_gx + 8], refs[n_gx + 8 :]
-    result, tracers, currents, out, held, weights, edge_n, edge_s, line_n, line_s, depth, forced, passing, sems = refs
-    copies = [
-        pltpu.make_async_copy(tracers_in, tracers, sems.at[0]),
-        pltpu.make_async_copy(currents_in, currents, sems.at[1]),
-    ]
+def stencil_kernel(n_gx, *refs):
+    count = n_gx + 11
+    given, result, here, refs = refs[:count], refs[count], refs[count + 1 : 2 * count + 1], refs[2 * count + 1 :]
+    out, held, weights, edge_n, edge_s, line_n, line_s, depth, forced, passing, sems = refs
+    parts, edges, (land, tracers, currents) = here[:n_gx], here[n_gx : n_gx + 8], here[n_gx + 8 :]
+    copies = [pltpu.make_async_copy(x, y, sems.at[i]) for i, (x, y) in enumerate(zip(given, here))]
     for copy in copies:
         copy.start()
+    for copy in copies[:-2]:
+        copy.wait()
     levels = tracers.shape[1]
 
     def send(l):
-        return pltpu.make_async_copy(out.at[:, l], result.at[:, l], sems.at[2 + l])
+        return pltpu.make_async_copy(out.at[:, l], result.at[:, l], sems.at[count + l])
 
     height, width = land.shape
     last = width - 1
@@ -542,7 +553,7 @@
             return forced[0] * depth[pl.ds(l, 1), :] + top * forced[1]
         return top * forced[2]
 
-    for copy in copies:
+    for copy in copies[-2:]:
         copy.wait()
     currents[0, 0] = currents[0, 0] + 0.1 * stress_u
     currents[1, 0] = currents[1, 0] + 0.1 * stress_v
@@ -563,7 +574,7 @@
             held[tracer, l] = update(c, tracers[tracer, l], halo, under, over, forcing(tracer, l))
         return 0
 
-    lax.fori_loop(0, levels, first_step, 0, unroll=4)
+    lax.fori_loop(0, levels, first_step, 0, unroll=8)
 
     def second_step(l, _):
         c = [weights[i, l] for i in range(5)]
@@ -575,12 +586,12 @@
         send(l).start()
         return 0
 
-    lax.fori_loop(0, levels, second_step, 0, unroll=4)
+    lax.fori_loop(0, levels, second_step, 0, unroll=8)
     for l in range(levels):
         send(l).wait()
 
 
-def backward_kernel(parts, slots_in, src, back, w, out, held, wide, picked, terms, slots, sems):
+def backward_kernel(parts, slots_in, src_in, back, w, out, held, wide, picked, terms, slots, src, sems):
     total, width = terms.shape
     blocks = out.shape[0]
     batch = total // parts
@@ -589,7 +600,9 @@
         return pltpu.make_async_copy(w.at[pl.ds(c * batch, batch)], held.at[pl.ds(c * batch, batch)], sems.at[c])
 
     slots_copy = pltpu.make_async_copy(slots_in, slots, sems.at[parts])
+    src_copy = pltpu.make_async_copy(src_in, src, sems.at[parts + 1])
     slots_copy.start()
+    src_copy.start()
     for c in range(parts):
         copy(c).start()
     slots_copy.wait()
@@ -616,6 +629,7 @@
         return 0
 
     lax.fori_loop(0, parts, work, 0)
+    src_copy.wait()
     hot = (iota((blocks, total), 0) == src[...]).astype(F32).astype(BF16)
     value = terms[...]
     high = value.astype(BF16)
@@ -629,7 +643,7 @@
     devices, cap, _ = back.shape
     return pl.pallas_call(
         functools.partial(backward_kernel, parts),
-        in_specs=[ANY, VMEM, VMEM, ANY],
+        in_specs=[ANY, ANY, VMEM, ANY],
         out_specs=VMEM,
         scratch_shapes=[
             pltpu.VMEM(w.shape, BF16),
@@ -637,7 +651,8 @@
             pltpu.VMEM((total, width), F32),
             pltpu.VMEM((total, width), F32),
             pltpu.SMEM((total,), jnp.int32),
-            pltpu.SemaphoreType.DMA((parts + 1,)),
+            pltpu.VMEM((1, total), jnp.int32),
+            pltpu.SemaphoreType.DMA((parts + 2,)),
         ],
         out_shape=jax.ShapeDtypeStruct((blocks, width), F32),
         compiler_params=kernel_params(46),
@@ -717,15 +732,15 @@
     returned = lax.all_to_all(back, EVERY, split_axis=0, concat_axis=0, tiled=True)
 
     plane = (height, width)
+    given = (*parts, *edges, land_sea, tracers, currents)
     (tracers_out,) = kernel(
         functools.partial(stencil_kernel, n_gx),
         [(tracers.shape, F32)],
         "substeps",
         58,
         1 << 24,
-        [
-            pltpu.VMEM(tracers.shape, F32),
-            pltpu.VMEM(currents.shape, F32),
+        [pltpu.VMEM(x.shape, x.dtype) for x in given]
+        + [
             pltpu.VMEM(tracers.shape, F32),
             pltpu.VMEM(tracers.shape, F32),
             pltpu.VMEM((5, levels) + plane, F32),
@@ -736,11 +751,11 @@
             pltpu.VMEM((levels, width), F32),
             pltpu.VMEM((3,) + plane, F32),
             pltpu.VMEM((4,) + plane, F32),
-            pltpu.SemaphoreType.DMA((2 + levels,)),
+            pltpu.SemaphoreType.DMA((len(given) + levels,)),
         ],
-        in_specs=[ANY, ANY] + [VMEM] * (n_gx + 9),
+        in_specs=[ANY] * len(given),
         out_specs=[ANY],
-    )(tracers, currents, land_sea, *parts, *edges)
+    )(*given)
     return tracers_out, backward(returned, remap_weights, remap_src, slots, atm_flux.shape[0])
 
 

time: 87.6 us -> 86.6 us (0.989)
  Pallas kernels: 37.4 us -> 35.5 us
  waiting for transfers between devices: 18.5 us -> 19.5 us
    pallas_call x1, Pallas kernels: 13.6 us -> 12.6 us  [forward(): pl.pallas_call(functools.partial(forward_kernel, parts, cap, grid), in_sp...]
    pallas_call x1, Pallas kernels: 11.1 us -> 10.2 us  [on_device(): kernel(functools.partial(stencil_kernel, n_gx), [(tracers.shape, F32)], '...]
    all_to_all x1, waiting for transfers between devices: 0.47 us -> 1.42 us  [on_device(): lax.all_to_all(back, EVERY, split_axis=0, concat_axis=0, tiled=True)]
  transfers between devices with their start and end apart: 15 -> 15, of which waited for: 9 -> 9; matrix products, arithmetic and copies ran while one was open for 0% -> 0% of each run, Pallas kernels for 15% -> 14%
where the time goes in v11:
time: 86.6 us; the launch traced here: 86.3 us
  Pallas kernels  35.5 us (41%)
  starting transfers between devices  30.2 us (35%)
  waiting for transfers between devices  19.5 us (23%)
  between operations  0.94 us (1%)
    ppermute x10, waiting for transfers between devices, swapped(): return lax.ppermute(array, axes, [(i, i ^ step) for i in range(count)])  17.3 us
    ppermute x10, starting transfers between devices, swapped(): return lax.ppermute(array, axes, [(i, i ^ step) for i in range(count)])  13.6 us
    pallas_call x1, Pallas kernels, forward(): pl.pallas_call(functools.partial(forward_kernel, parts, cap, grid), in_sp...  12.6 us
    pallas_call x1, Pallas kernels, on_device(): kernel(functools.partial(stencil_kernel, n_gx), [(tracers.shape, F32)], '...  10.2 us
    pallas_call x1, Pallas kernels, backward(): pl.pallas_call(functools.partial(backward_kernel, parts), in_specs=[ANY,...  8.42 us
    all_to_all x1, starting transfers between devices, on_device(): lax.all_to_all(back, EVERY, split_axis=0, concat_axis=0, tiled=True)  7.23 us
    ppermute x1, starting transfers between devices, on_device(): from_s = lax.ppermute(own_n, NORTH, to_north)  3.67 us
    ppermute x1, starting transfers between devices, on_device(): from_w = lax.ppermute(own_e, 'gy', to_east)  3.03 us
  transfers between devices with their start and end apart: 15, of which 9 were waited for; matrix products, arithmetic and copies ran while one was open for 0% of the time, Pallas kernels for 14%

profile of v11, /device:TPU:0, one launch (start us, length us, event | category | flops | bytes accessed | tf_op | source)
XLA Modules:
  0.0 86.3 jit_solution(12080337217490737957)
XLA Ops:
  0.7 0.0 copy-start.3
  0.7 12.6 %forward_remap.1 = (bf16[4,48,640]{2,1,0:T(8,128)(2,1)}, bf16[4,48,640]{2,1,0:T(8,128)(2,1)}, bf16[4,48,640]{2,1,0:T(8,128)(2,1)}, bf16[4,48,640]{2,1,0:T(8,128)...) custom-call(s32[640]{0:T(1024)} %src_in.1, ...), custom_call_target="tpu_custom_call" | custom-call | flops 167772160 | bytes 20971520 | tf_op jit(solution)/shard_map/forward_remap/pallas_call | solution.py:188
  13.3 0.5 collective-permute-start.2
  13.8 3.6 %collective-permute-start = (bf16[4,48,640]{2,1,0:T(8,128)(2,1)}, bf16[4,48,640]{2,1,0:T(8,128)(2,1)S(1)}, u32[]{:S(2)}, u32[]{:S(2)}) collective-permute-start(bf16[4,48,640]{2,1,0:T(8,128)(2,1)} %get-tuple-element.33), channel_id=1, source_target_pairs={{0,19},{1,18},{2,17},{3,16},{16,3},{17,2},{18,1},{19,0},{4,23},{5,... | collective-permute-start | bytes 737288 | tf_op jit(solution)/shard_map/ppermute | solution.py:687
  17.4 0.0 collective-permute-start.1
  17.4 1.3 %collective-permute-start.3 = (bf16[4,48,640]{2,1,0:T(8,128)(2,1)}, bf16[4,48,640]{2,1,0:T(8,128)(2,1)S(1)}, u32[]{:S(2)}, u32[]{:S(2)}) collective-permute-start(bf16[4,48,640]{2,1,0:T(8,128)(2,1)} %get-tuple-element.37), channel_id=1, source_target_pairs={{0,17},{1,16},{2,19},{3,18},{16,1},{17,0},{18,3},{19,2},{4,21},{5,... | collective-permute-start | bytes 737288 | tf_op jit(solution)/shard_map/ppermute | solution.py:687
  18.8 0.6 collective-permute-start.4
  19.4 1.4 %collective-permute-start.5 = (bf16[4,48,640]{2,1,0:T(8,128)(2,1)}, bf16[4,48,640]{2,1,0:T(8,128)(2,1)S(1)}, u32[]{:S(2)}, u32[]{:S(2)}) collective-permute-start(bf16[4,48,640]{2,1,0:T(8,128)(2,1)} %get-tuple-element.39), channel_id=1, source_target_pairs={{0,3},{1,2},{2,1},{3,0},{16,19},{17,18},{18,17},{19,16},{4,7},{5,6... | collective-permute-start | bytes 737288 | tf_op jit(solution)/shard_map/ppermute | solution.py:687
  20.8 3.2 %collective-permute-done.refs_1_ = bf16[4,48,640]{2,1,0:T(8,128)(2,1)S(1)} collective-permute-done((bf16[4,48,640]{2,1,0:T(8,128)(2,1)}, bf16[4,48,640]{2,1,0:T(8,128)(2,1)S(1)}, u32[]{:S(2)}, u32[]{:S(2)}) %collective-permute-start) | collective-permute-done | bytes 245792 | tf_op jit(solution)/shard_map/ppermute | solution.py:687
  24.0 1.2 %collective-permute-start.6 = (bf16[4,48,640]{2,1,0:T(8,128)(2,1)}, bf16[4,48,640]{2,1,0:T(8,128)(2,1)S(1)}, u32[]{:S(2)}, u32[]{:S(2)}) collective-permute-start(bf16[4,48,640]{2,1,0:T(8,128)(2,1)} %get-tuple-element.40), channel_id=1, source_target_pairs={{0,2},{1,3},{2,0},{3,1},{16,18},{17,19},{18,16},{19,17},{4,6},{5,7... | collective-permute-start | bytes 737288 | tf_op jit(solution)/shard_map/ppermute | solution.py:687
  25.3 0.1 edge_rows.1
  25.4 4.3 %collective-permute-done.1.refs_2_ = bf16[4,48,640]{2,1,0:T(8,128)(2,1)S(1)} collective-permute-done((bf16[4,48,640]{2,1,0:T(8,128)(2,1)}, bf16[4,48,640]{2,1,0:T(8,128)(2,1)S(1)}, u32[]{:S(2)}, u32[]{:S(2)}) %collective-permute-start.1) | collective-permute-done | bytes 245792 | tf_op jit(solution)/shard_map/ppermute | solution.py:687
  29.7 1.3 %collective-permute-start.7 = (bf16[128,128]{1,0:T(8,128)(2,1)S(1)}, bf16[128,128]{1,0:T(8,128)(2,1)S(1)}, u32[]{:S(2)}, u32[]{:S(2)}) collective-permute-start(bf16[128,128]{1,0:T(8,128)(2,1)S(1)} %get-tuple-element.43.refs_5_.refs_8_), channel_id=1, source_target_pairs={{4,0},{8,4},{12,8},{16,12},{20,16},{24,20},{28,24},{5,1},{9,5},{13... | collective-permute-start | bytes 98312 | tf_op jit(solution)/shard_map/ppermute | solution.py:712
  30.9 3.6 %collective-permute-done.3.refs_4_ = bf16[4,48,640]{2,1,0:T(8,128)(2,1)S(1)} collective-permute-done((bf16[4,48,640]{2,1,0:T(8,128)(2,1)}, bf16[4,48,640]{2,1,0:T(8,128)(2,1)S(1)}, u32[]{:S(2)}, u32[]{:S(2)}) %collective-permute-start.3) | collective-permute-done | bytes 245792 | tf_op jit(solution)/shard_map/ppermute | solution.py:687
  34.6 3.7 %collective-permute-start.8 = (bf16[128,128]{1,0:T(8,128)(2,1)S(1)}, bf16[128,128]{1,0:T(8,128)(2,1)S(1)}, u32[]{:S(2)}, u32[]{:S(2)}) collective-permute-start(bf16[128,128]{1,0:T(8,128)(2,1)S(1)} %get-tuple-element.44.refs_4_.refs_7_), channel_id=1, source_target_pairs={{0,4},{4,8},{8,12},{12,16},{16,20},{20,24},{24,28},{1,5},{5,9},{9,... | collective-permute-start | bytes 98312 | tf_op jit(solution)/shard_map/ppermute | solution.py:713
  38.2 1.6 %collective-permute-done.4.refs_5_ = bf16[4,48,640]{2,1,0:T(8,128)(2,1)S(1)} collective-permute-done((bf16[4,48,640]{2,1,0:T(8,128)(2,1)}, bf16[4,48,640]{2,1,0:T(8,128)(2,1)S(1)}, u32[]{:S(2)}, u32[]{:S(2)}) %collective-permute-start.4) | collective-permute-done | bytes 245792 | tf_op jit(solution)/shard_map/ppermute | solution.py:687
  39.9 0.3 collective-permute-done.6.refs_7_
  40.2 0.6 merge.1
  40.8 3.0 %collective-permute-start.10 = (bf16[136,640]{1,0:T(8,128)(2,1)S(1)}, bf16[136,640]{1,0:T(8,128)(2,1)S(1)}, u32[]{:S(2)}, u32[]{:S(2)}) collective-permute-start(bf16[136,640]{1,0:T(8,128)(2,1)S(1)} %get-tuple-element.55), channel_id=1, source_target_pairs={{0,8},{4,12},{8,0},{12,4},{1,9},{5,13},{9,1},{13,5},{2,10},{6,14},... | collective-permute-start | bytes 522248 | tf_op jit(solution)/shard_map/ppermute | solution.py:687
  43.9 1.3 %collective-permute-start.11 = (bf16[136,640]{1,0:T(8,128)(2,1)S(1)}, bf16[136,640]{1,0:T(8,128)(2,1)S(1)}, u32[]{:S(2)}, u32[]{:S(2)}) collective-permute-start(bf16[136,640]{1,0:T(8,128)(2,1)S(1)} %get-tuple-element.56), channel_id=1, source_target_pairs={{0,12},{4,8},{8,4},{12,0},{1,13},{5,9},{9,5},{13,1},{2,14},{6,10},... | collective-permute-start | bytes 522248 | tf_op jit(solution)/shard_map/ppermute | solution.py:687
  45.2 0.5 collective-permute-start.9
  45.7 1.7 %edge_columns.1 = (bf16[192,128]{1,0:T(8,128)(2,1)S(1)}, bf16[192,128]{1,0:T(8,128)(2,1)S(1)}) custom-call(f32[2,16,128,128]{3,2,1,0:T(8,128)S(1)} %copy-done.1, f32[2,16,128,128]{3,2,1,0:T(8,128)S(1)} %copy-done, s32[128,128]{1,0:T(8,128)S(1)} %copy-done.3, bf16[128,128]{1,0:T(8,128)(2,1)S(1)} %collective-permute-done.7.from_n.refs_8_.refs_11_, ...), custom_call_target="tpu_custom_call" | custom-call | flops 4194304 | bytes 4194304 | tf_op jit(solution)/shard_map/edge_columns/pallas_call | solution.py:715
  47.4 1.4 %collective-permute-start.12 = (bf16[192,128]{1,0:T(8,128)(2,1)S(1)}, bf16[192,128]{1,0:T(8,128)(2,1)S(1)}, u32[]{:S(2)}, u32[]{:S(2)}) collective-permute-start(bf16[192,128]{1,0:T(8,128)(2,1)S(1)} %get-tuple-element.60.refs_7_.refs_10_), channel_id=1, source_target_pairs={{1,0},{2,1},{3,2},{5,4},{6,5},{7,6},{9,8},{10,9},{11,10},{13,12},{... | collective-permute-start | bytes 147464 | tf_op jit(solution)/shard_map/ppermute | solution.py:718
  48.8 3.0 %collective-permute-start.13 = (bf16[192,128]{1,0:T(8,128)(2,1)S(1)}, bf16[192,128]{1,0:T(8,128)(2,1)S(1)}, u32[]{:S(2)}, u32[]{:S(2)}) collective-permute-start(bf16[192,128]{1,0:T(8,128)(2,1)S(1)} %get-tuple-element.59.refs_6_.refs_9_), channel_id=1, source_target_pairs={{0,1},{1,2},{2,3},{4,5},{5,6},{6,7},{8,9},{9,10},{10,11},{12,13},{... | collective-permute-start | bytes 147464 | tf_op jit(solution)/shard_map/ppermute | solution.py:719
  51.9 0.8 collective-permute-done.13.refs_11_.refs_14_
  52.7 3.9 %collective-permute-done.10.refs_2_ = bf16[136,640]{1,0:T(8,128)(2,1)S(1)} collective-permute-done((bf16[136,640]{1,0:T(8,128)(2,1)S(1)}, bf16[136,640]{1,0:T(8,128)(2,1)S(1)}, u32[]{:S(2)}, u32[]{:S(2)}) %collective-permute-start.10) | collective-permute-done | bytes 174112 | tf_op jit(solution)/shard_map/ppermute | solution.py:687
  56.7 0.3 collective-permute-done.9.refs_1_
  57.0 1.9 %surface.1 = bf16[32,40,128]{2,1,0:T(8,128)(2,1)} custom-call(f32[136,640]{1,0:T(8,128)S(1)} %get-tuple-element.53.refs_0_, bf16[136,640]{1,0:T(8,128)(2,1)S(1)} %collective-permute-done.9.refs_1_, bf16[136,640]{1,0:T(8,128)(2,1)S(1)} %collective-permute-done.10.refs_2_, bf16[136,640]{1,0:T(8,128)(2,1)S(1)} %collective-permute-done.11.refs_3_, ...), custom_call_target="tpu_custom_call" | custom-call | flops 4194304 | bytes 4194304 | tf_op jit(solution)/shard_map/surface/pallas_call | solution.py:725
  58.9 7.2 %all-to-all-start = ((bf16[32,40,128]{2,1,0:T(8,128)(2,1)}), bf16[32,40,128]{2,1,0:T(8,128)(2,1)S(1)}, u32[]{:S(2)}, u32[]{:S(2)}) async-start(bf16[32,40,128]{2,1,0:T(8,128)(2,1)} %surface.1), calls=%async_computation | async-start | bytes 655360 | tf_op jit(solution)/shard_map/all_to_all | solution.py:732
  66.2 10.2 %substeps.1 = f32[2,16,128,128]{3,2,1,0:T(8,128)} custom-call(f32[136,640]{1,0:T(8,128)} %copy-done.2, bf16[136,640]{1,0:T(8,128)(2,1)} %copy-done.6, bf16[136,640]{1,0:T(8,128)(2,1)} %copy-done.4, bf16[136,640]{1,0:T(8,128)(2,1)} %copy-done.5, bf16[128,128]{1,0:T(8,128)(2,1)} %copy-done.15, bf16[128,128]{1,0:T(8,128)(2,1)} %copy-done.14, ...), custom_call_target="tpu_custom_call" | custom-call | flops 16777216 | bytes 16777216 | tf_op jit(solution)/shard_map/substeps/pallas_call | solution.py:736
  76.4 1.4 %all-to-all-done.back = bf16[32,40,128]{2,1,0:T(8,128)(2,1)S(1)} async-done(((bf16[32,40,128]{2,1,0:T(8,128)(2,1)}), bf16[32,40,128]{2,1,0:T(8,128)(2,1)S(1)}, u32[]{:S(2)}, u32[]{:S(2)}) %all-to-all-start) | async-done | bytes 327712 | tf_op jit(solution)/shard_map/all_to_all | solution.py:732
  77.8 8.4 %backward_remap.1 = f32[160,128]{1,0:T(8,128)} custom-call(s32[640]{0:T(1024)S(1)} %copy-done.16, s32[1,640]{1,0:T(1,128)S(1)} %reshape.19.src_in, bf16[32,40,128]{2,1,0:T(8,128)(2,1)S(1)} %all-to-all-done.back, bf16[640,128,128]{2,1,0:T(8,128)(2,1)} %w.3), custom_call_target="tpu_custom_call" | custom-call | flops 167772160 | bytes 20971520 | tf_op jit(solution)/shard_map/backward_remap/pallas_call | solution.py:644
  (44 shorter events, 0.1 us)
Async XLA Ops:
  0.6 24.6 %copy-start = (f32[2,16,128,128]{3,2,1,0:T(8,128)S(1)}, f32[2,16,128,128]{3,2,1,0:T(8,128)}, u32[]{:S(2)}) copy-start(f32[2,16,128,128]{3,2,1,0:T(8,128)} %refs_14_.1) | copy-start | bytes 6291460
  0.6 24.6 %copy-start.1 = (f32[2,16,128,128]{3,2,1,0:T(8,128)S(1)}, f32[2,16,128,128]{3,2,1,0:T(8,128)}, u32[]{:S(2)}) copy-start(f32[2,16,128,128]{3,2,1,0:T(8,128)} %refs_13_.1) | copy-start | bytes 6291460
  0.7 24.6 %copy-start.3 = (s32[128,128]{1,0:T(8,128)S(1)}, s32[128,128]{1,0:T(8,128)}, u32[]{:S(2)}) copy-start(s32[128,128]{1,0:T(8,128)} %refs_6_.1) | copy-start | bytes 196612
  13.3 6.1 %collective-permute-start.2 = (bf16[4,48,640]{2,1,0:T(8,128)(2,1)}, bf16[4,48,640]{2,1,0:T(8,128)(2,1)S(1)}, u32[]{:S(2)}, u32[]{:S(2)}) collective-permute-start(bf16[4,48,640]{2,1,0:T(8,128)(2,1)} %get-tuple-element.35), channel_id=1, source_target_pairs={{0,1},{1,0},{2,3},{3,2},{16,17},{17,16},{18,19},{19,18},{4,5},{5,4... | collective-permute-start | bytes 737288 | tf_op jit(solution)/shard_map/ppermute | solution.py:687
  13.8 10.2 %collective-permute-start = (bf16[4,48,640]{2,1,0:T(8,128)(2,1)}, bf16[4,48,640]{2,1,0:T(8,128)(2,1)S(1)}, u32[]{:S(2)}, u32[]{:S(2)}) collective-permute-start(bf16[4,48,640]{2,1,0:T(8,128)(2,1)} %get-tuple-element.33), channel_id=1, source_target_pairs={{0,19},{1,18},{2,17},{3,16},{16,3},{17,2},{18,1},{19,0},{4,23},{5,... | collective-permute-start | bytes 737288 | tf_op jit(solution)/shard_map/ppermute | solution.py:687
  17.4 12.3 %collective-permute-start.1 = (bf16[4,48,640]{2,1,0:T(8,128)(2,1)}, bf16[4,48,640]{2,1,0:T(8,128)(2,1)S(1)}, u32[]{:S(2)}, u32[]{:S(2)}) collective-permute-start(bf16[4,48,640]{2,1,0:T(8,128)(2,1)} %get-tuple-element.34), channel_id=1, source_target_pairs={{0,18},{1,19},{2,16},{3,17},{16,2},{17,3},{18,0},{19,1},{4,22},{5,... | collective-permute-start | bytes 737288 | tf_op jit(solution)/shard_map/ppermute | solution.py:687
  17.4 17.1 %collective-permute-start.3 = (bf16[4,48,640]{2,1,0:T(8,128)(2,1)}, bf16[4,48,640]{2,1,0:T(8,128)(2,1)S(1)}, u32[]{:S(2)}, u32[]{:S(2)}) collective-permute-start(bf16[4,48,640]{2,1,0:T(8,128)(2,1)} %get-tuple-element.37), channel_id=1, source_target_pairs={{0,17},{1,16},{2,19},{3,18},{16,1},{17,0},{18,3},{19,2},{4,21},{5,... | collective-permute-start | bytes 737288 | tf_op jit(solution)/shard_map/ppermute | solution.py:687
  18.8 21.1 %collective-permute-start.4 = (bf16[4,48,640]{2,1,0:T(8,128)(2,1)}, bf16[4,48,640]{2,1,0:T(8,128)(2,1)S(1)}, u32[]{:S(2)}, u32[]{:S(2)}) collective-permute-start(bf16[4,48,640]{2,1,0:T(8,128)(2,1)} %get-tuple-element.38), channel_id=1, source_target_pairs={{0,16},{1,17},{2,18},{3,19},{16,0},{17,1},{18,2},{19,3},{4,20},{5,... | collective-permute-start | bytes 737288 | tf_op jit(solution)/shard_map/ppermute | solution.py:687
  19.4 20.5 %collective-permute-start.5 = (bf16[4,48,640]{2,1,0:T(8,128)(2,1)}, bf16[4,48,640]{2,1,0:T(8,128)(2,1)S(1)}, u32[]{:S(2)}, u32[]{:S(2)}) collective-permute-start(bf16[4,48,640]{2,1,0:T(8,128)(2,1)} %get-tuple-element.39), channel_id=1, source_target_pairs={{0,3},{1,2},{2,1},{3,0},{16,19},{17,18},{18,17},{19,16},{4,7},{5,6... | collective-permute-start | bytes 737288 | tf_op jit(solution)/shard_map/ppermute | solution.py:687
  24.0 16.1 %collective-permute-start.6 = (bf16[4,48,640]{2,1,0:T(8,128)(2,1)}, bf16[4,48,640]{2,1,0:T(8,128)(2,1)S(1)}, u32[]{:S(2)}, u32[]{:S(2)}) collective-permute-start(bf16[4,48,640]{2,1,0:T(8,128)(2,1)} %get-tuple-element.40), channel_id=1, source_target_pairs={{0,2},{1,3},{2,0},{3,1},{16,18},{17,19},{18,16},{19,17},{4,6},{5,7... | collective-permute-start | bytes 737288 | tf_op jit(solution)/shard_map/ppermute | solution.py:687
  25.3 14.9 %copy-start.9 = (bf16[4,48,640]{2,1,0:T(8,128)(2,1)S(1)}, bf16[4,48,640]{2,1,0:T(8,128)(2,1)}, u32[]{:S(2)}) copy-start(bf16[4,48,640]{2,1,0:T(8,128)(2,1)} %get-tuple-element.45.refs_0_) | copy-start | bytes 737284
  25.4 31.6 %copy-start.14 = (bf16[128,128]{1,0:T(8,128)(2,1)}, bf16[128,128]{1,0:T(8,128)(2,1)S(1)}, u32[]{:S(2)}) copy-start(bf16[128,128]{1,0:T(8,128)(2,1)S(1)} %get-tuple-element.43.refs_5_.refs_8_) | copy-start | bytes 98308
  25.4 31.6 %copy-start.15 = (bf16[128,128]{1,0:T(8,128)(2,1)}, bf16[128,128]{1,0:T(8,128)(2,1)S(1)}, u32[]{:S(2)}) copy-start(bf16[128,128]{1,0:T(8,128)(2,1)S(1)} %get-tuple-element.44.refs_4_.refs_7_) | copy-start | bytes 98308
  29.7 10.5 %collective-permute-start.7 = (bf16[128,128]{1,0:T(8,128)(2,1)S(1)}, bf16[128,128]{1,0:T(8,128)(2,1)S(1)}, u32[]{:S(2)}, u32[]{:S(2)}) collective-permute-start(bf16[128,128]{1,0:T(8,128)(2,1)S(1)} %get-tuple-element.43.refs_5_.refs_8_), channel_id=1, source_target_pairs={{4,0},{8,4},{12,8},{16,12},{20,16},{24,20},{28,24},{5,1},{9,5},{13... | collective-permute-start | bytes 98312 | tf_op jit(solution)/shard_map/ppermute | solution.py:712
  34.6 5.6 %collective-permute-start.8 = (bf16[128,128]{1,0:T(8,128)(2,1)S(1)}, bf16[128,128]{1,0:T(8,128)(2,1)S(1)}, u32[]{:S(2)}, u32[]{:S(2)}) collective-permute-start(bf16[128,128]{1,0:T(8,128)(2,1)S(1)} %get-tuple-element.44.refs_4_.refs_7_), channel_id=1, source_target_pairs={{0,4},{4,8},{8,12},{12,16},{16,20},{20,24},{24,28},{1,5},{5,9},{9,... | collective-permute-start | bytes 98312 | tf_op jit(solution)/shard_map/ppermute | solution.py:713
  40.2 16.8 %copy-start.7 = (bf16[128,128]{1,0:T(8,128)(2,1)}, bf16[128,128]{1,0:T(8,128)(2,1)S(1)}, u32[]{:S(2)}) copy-start(bf16[128,128]{1,0:T(8,128)(2,1)S(1)} %collective-permute-done.7.from_n.refs_8_.refs_11_) | copy-start | bytes 98308
  40.2 16.8 %copy-start.8 = (bf16[128,128]{1,0:T(8,128)(2,1)}, bf16[128,128]{1,0:T(8,128)(2,1)S(1)}, u32[]{:S(2)}) copy-start(bf16[128,128]{1,0:T(8,128)(2,1)S(1)} %collective-permute-done.8.from_s.refs_9_.refs_12_) | copy-start | bytes 98308
  40.8 16.2 %copy-start.2 = (f32[136,640]{1,0:T(8,128)}, f32[136,640]{1,0:T(8,128)S(1)}, u32[]{:S(2)}) copy-start(f32[136,640]{1,0:T(8,128)S(1)} %get-tuple-element.53.refs_0_) | copy-start | bytes 1044484
  40.8 15.8 %collective-permute-start.10 = (bf16[136,640]{1,0:T(8,128)(2,1)S(1)}, bf16[136,640]{1,0:T(8,128)(2,1)S(1)}, u32[]{:S(2)}, u32[]{:S(2)}) collective-permute-start(bf16[136,640]{1,0:T(8,128)(2,1)S(1)} %get-tuple-element.55), channel_id=1, source_target_pairs={{0,8},{4,12},{8,0},{12,4},{1,9},{5,13},{9,1},{13,5},{2,10},{6,14},... | collective-permute-start | bytes 522248 | tf_op jit(solution)/shard_map/ppermute | solution.py:687
  43.9 12.8 %collective-permute-start.11 = (bf16[136,640]{1,0:T(8,128)(2,1)S(1)}, bf16[136,640]{1,0:T(8,128)(2,1)S(1)}, u32[]{:S(2)}, u32[]{:S(2)}) collective-permute-start(bf16[136,640]{1,0:T(8,128)(2,1)S(1)} %get-tuple-element.56), channel_id=1, source_target_pairs={{0,12},{4,8},{8,4},{12,0},{1,13},{5,9},{9,5},{13,1},{2,14},{6,10},... | collective-permute-start | bytes 522248 | tf_op jit(solution)/shard_map/ppermute | solution.py:687
  45.2 11.8 %collective-permute-start.9 = (bf16[136,640]{1,0:T(8,128)(2,1)S(1)}, bf16[136,640]{1,0:T(8,128)(2,1)S(1)}, u32[]{:S(2)}, u32[]{:S(2)}) collective-permute-start(bf16[136,640]{1,0:T(8,128)(2,1)S(1)} %get-tuple-element.54), channel_id=1, source_target_pairs={{0,4},{4,0},{8,12},{12,8},{1,5},{5,1},{9,13},{13,9},{2,6},{6,2},{1... | collective-permute-start | bytes 522248 | tf_op jit(solution)/shard_map/ppermute | solution.py:687
  47.4 18.8 %copy-start.10 = (bf16[192,128]{1,0:T(8,128)(2,1)}, bf16[192,128]{1,0:T(8,128)(2,1)S(1)}, u32[]{:S(2)}) copy-start(bf16[192,128]{1,0:T(8,128)(2,1)S(1)} %get-tuple-element.60.refs_7_.refs_10_) | copy-start | bytes 147460
  47.4 18.8 %copy-start.11 = (bf16[192,128]{1,0:T(8,128)(2,1)}, bf16[192,128]{1,0:T(8,128)(2,1)S(1)}, u32[]{:S(2)}) copy-start(bf16[192,128]{1,0:T(8,128)(2,1)S(1)} %get-tuple-element.59.refs_6_.refs_9_) | copy-start | bytes 147460
  47.4 18.8 %copy-start.17 = (s32[640]{0:T(1024)S(1)}, s32[640]{0:T(1024)}, u32[]{:S(2)}) copy-start(s32[640]{0:T(1024)} %src_in.1) | copy-start | bytes 7684
  47.4 4.5 %collective-permute-start.12 = (bf16[192,128]{1,0:T(8,128)(2,1)S(1)}, bf16[192,128]{1,0:T(8,128)(2,1)S(1)}, u32[]{:S(2)}, u32[]{:S(2)}) collective-permute-start(bf16[192,128]{1,0:T(8,128)(2,1)S(1)} %get-tuple-element.60.refs_7_.refs_10_), channel_id=1, source_target_pairs={{1,0},{2,1},{3,2},{5,4},{6,5},{7,6},{9,8},{10,9},{11,10},{13,12},{... | collective-permute-start | bytes 147464 | tf_op jit(solution)/shard_map/ppermute | solution.py:718
  48.8 3.9 %collective-permute-start.13 = (bf16[192,128]{1,0:T(8,128)(2,1)S(1)}, bf16[192,128]{1,0:T(8,128)(2,1)S(1)}, u32[]{:S(2)}, u32[]{:S(2)}) collective-permute-start(bf16[192,128]{1,0:T(8,128)(2,1)S(1)} %get-tuple-element.59.refs_6_.refs_9_), channel_id=1, source_target_pairs={{0,1},{1,2},{2,3},{4,5},{5,6},{6,7},{8,9},{9,10},{10,11},{12,13},{... | collective-permute-start | bytes 147464 | tf_op jit(solution)/shard_map/ppermute | solution.py:719
  51.9 14.2 %copy-start.12 = (bf16[192,128]{1,0:T(8,128)(2,1)}, bf16[192,128]{1,0:T(8,128)(2,1)S(1)}, u32[]{:S(2)}) copy-start(bf16[192,128]{1,0:T(8,128)(2,1)S(1)} %collective-permute-done.12.refs_10_.refs_13_) | copy-start | bytes 147460
  52.7 13.5 %copy-start.13 = (bf16[192,128]{1,0:T(8,128)(2,1)}, bf16[192,128]{1,0:T(8,128)(2,1)S(1)}, u32[]{:S(2)}) copy-start(bf16[192,128]{1,0:T(8,128)(2,1)S(1)} %collective-permute-done.13.refs_11_.refs_14_) | copy-start | bytes 147460
  56.6 9.6 %copy-start.4 = (bf16[136,640]{1,0:T(8,128)(2,1)}, bf16[136,640]{1,0:T(8,128)(2,1)S(1)}, u32[]{:S(2)}) copy-start(bf16[136,640]{1,0:T(8,128)(2,1)S(1)} %collective-permute-done.10.refs_2_) | copy-start | bytes 522244
  56.7 9.6 %copy-start.5 = (bf16[136,640]{1,0:T(8,128)(2,1)}, bf16[136,640]{1,0:T(8,128)(2,1)S(1)}, u32[]{:S(2)}) copy-start(bf16[136,640]{1,0:T(8,128)(2,1)S(1)} %collective-permute-done.11.refs_3_) | copy-start | bytes 522244
  58.9 18.9 %all-to-all-start = ((bf16[32,40,128]{2,1,0:T(8,128)(2,1)}), bf16[32,40,128]{2,1,0:T(8,128)(2,1)S(1)}, u32[]{:S(2)}, u32[]{:S(2)}) async-start(bf16[32,40,128]{2,1,0:T(8,128)(2,1)} %surface.1), calls=%async_computation | async-start | bytes 655360 | tf_op jit(solution)/shard_map/all_to_all | solution.py:732
  66.2 11.6 %copy-start.16 = (s32[640]{0:T(1024)S(1)}, s32[640]{0:T(1024)}, u32[]{:S(2)}) copy-start(s32[640]{0:T(1024)} %get-tuple-element.61.slots_in) | copy-start | bytes 7684
  (1 other events, 9.2 us)

commit v12 on v11

--- a/solution.py
+++ b/solution.py
@@ -40,6 +40,36 @@
 ANY = pl.BlockSpec(memory_space=pl.ANY)
 
 
+def place_of(device, grid):
+    n_sec, n_gx, n_gy = grid
+    x, y = lax.div(device, n_gy), lax.rem(device, n_gy)
+    gx = lax.rem(x, n_gx)
+    return (lax.div(x, n_gx) * (n_gx // 2) + lax.rem(gx, n_gx // 2)) * n_gy + y, lax.div(gx, n_gx // 2)
+
+
+def device_at(index, half, grid):
+    n_sec, n_gx, n_gy = grid
+    x = lax.div(index, n_gy)
+    gx = half * (n_gx // 2) + lax.rem(x, n_gx // 2)
+    return (lax.div(x, n_gx // 2) * n_gx + gx) * n_gy + lax.rem(index, n_gy)
+
+
+def this_device(grid):
+    n_sec, n_gx, n_gy = grid
+    return (lax.axis_index("sec") * n_gx + lax.axis_index("gx")) * n_gy + lax.axis_index("gy")
+
+
+def swap_order(count):
+    return [0, count - 1, count - 2, 1] + list(range(count - 3, 1, -1))
+
+
+def swapped(array, grid, index, half):
+    n_sec, n_gx, n_gy = grid
+    x = index // n_gy
+    bits = (x // (n_gx // 2) * n_gx + half * (n_gx // 2) + x % (n_gx // 2)) * n_gy + index % n_gy
+    return lax.ppermute(array, EVERY, [(i, i ^ bits) for i in range(n_sec * n_gx * n_gy)])
+
+
 def forward_kernel(parts, cap, grid, src_in, own_in, dst_in, flux_in, w, *refs):
     sends, (slots, held, mixed, acc, rows, xs, counts, renumbered, sems, src, own, dst, flux) = refs[:-13], refs[-13:]
     n_sec, n_gx, n_gy = grid
@@ -61,13 +91,11 @@
     for c in range(parts):
         copy(c).start()
 
-    plane = lax.axis_index("sec") * n_gy + lax.axis_index("gy")
-    line = lax.axis_index("gx")
+    index, half = place_of(this_device(grid), grid)
 
     def renumber(owner):
-        x = lax.div(owner, n_gy)
-        there = lax.div(x, n_gx) * n_gy + lax.rem(owner, n_gy)
-        return (there ^ plane) * n_gx + (lax.rem(x, n_gx) ^ line)
+        index_there, half_there = place_of(owner, grid)
+        return (index_there ^ index) * 2 + (half_there ^ half)
 
     def clear(o, _):
         counts[o] = 0
@@ -139,7 +167,7 @@
             if cap > main:
                 xs[d, 0 : cap - main, :] = x[main:]
             x = x.astype(BF16)
-            sends[d // n_gx][d % n_gx, 0:main, :] = x[:main]
+            sends[d // 2][d % 2, 0:main, :] = x[:main]
             five.append(x)
         where = [rows[pl.ds(pl.multiple_of(d * cap, 8), cap), :] for d in ds]
         hot = [(lane == r).astype(F32).astype(BF16) for r in where]
@@ -149,8 +177,7 @@
         sides = [dot(e, h, NN) for e, h in zip(edge, hot)]
         ends = [dot((f[:, :cap] == wanted).astype(F32).astype(BF16), x, NN) for f, x in zip(flat, five)]
         for d, f, side, end in zip(ds, flat, sides, ends):
-            here = (d // n_gx) ^ plane
-            here = (lax.div(here, n_gy) * n_gx + ((d % n_gx) ^ line)) * n_gy + lax.rem(here, n_gy)
+            here = device_at((d // 2) ^ index, (d % 2) ^ half, grid)
 
             def at(offset):
                 return renumbered[lax.rem(here + offset + 2 * devices, devices)]
@@ -175,7 +202,7 @@
         owners(g)
 
     for m, send in enumerate(sends):
-        send[:, main:, :] = xs[m * n_gx : (m + 1) * n_gx].astype(BF16)
+        send[:, main:, :] = xs[2 * m : 2 * m + 2].astype(BF16)
 
 
 def forward(flux, w, src, own, dst, grid, cap, parts=8):
@@ -188,7 +215,7 @@
     return pl.pallas_call(
         functools.partial(forward_kernel, parts, cap, grid),
         in_specs=[ANY] * 5,
-        out_specs=[VMEM] * (n_sec * n_gy) + [SMEM],
+        out_specs=[VMEM] * (devices // 2) + [SMEM],
         scratch_shapes=[
             pltpu.VMEM(w.shape, BF16),
             pltpu.VMEM(flux.shape, BF16),
@@ -203,7 +230,7 @@
             pltpu.SMEM(dst.shape, jnp.int32),
             pltpu.VMEM(flux.shape, BF16),
         ],
-        out_shape=[jax.ShapeDtypeStruct((n_gx, chunk, wide), BF16)] * (n_sec * n_gy) + [jax.ShapeDtypeStruct((total,), jnp.int32)],
+        out_shape=[jax.ShapeDtypeStruct((2, chunk, wide), BF16)] * (devices // 2) + [jax.ShapeDtypeStruct((total,), jnp.int32)],
         compiler_params=kernel_params(58),
         cost_estimate=pl.CostEstimate(flops=2 * total * 8 * width * width, bytes_accessed=total * width * width * 2, transcendentals=0),
         name="forward_remap",
@@ -213,7 +240,8 @@
 def merge_kernel(n_sources, *refs):
     sources, outs = refs[:n_sources], refs[n_sources:]
     chunk = sources[0].shape[1]
-    height = outs[0].shape[0] - 8
+    height, wide = outs[0].shape
+    height -= 16
     first = chunk - 8
     count = n_sources * chunk
     for z, out in enumerate(outs):
@@ -226,9 +254,10 @@
         where = jnp.concatenate(where, axis=1)
         hot = (iota((height, count), 0).astype(F32) == where).astype(F32).astype(BF16)
         sums = dot(hot, jnp.concatenate([source[z] for source in sources], axis=0), NN)
-        row3 = jnp.concatenate([where, ext[3:4, count:]], axis=1)
-        ext = jnp.where(iota((8, 1), 0) == 3, row3, ext)
-        out[...] = jnp.concatenate([sums, ext], axis=0).astype(out.dtype)
+        where = jnp.concatenate([where, jnp.zeros((1, up(count, wide) - count), F32)], axis=1)
+        where = [where[:, at : at + wide] for at in range(0, count, wide)]
+        blank = jnp.zeros((8 - len(where), wide), F32)
+        out[...] = jnp.concatenate([sums, ext, *where, blank], axis=0).astype(out.dtype)
 
 
 def rows_kernel(tracers, currents, land, south, north):
@@ -432,9 +461,8 @@
 
 
 def surface_kernel(grid, chunk, levels, *refs):
-    n_sec, n_gx, n_gy = grid
-    planes = n_sec * n_gy
-    parts, refs = refs[:n_gx], refs[n_gx:]
+    group = grid[0] * grid[1] * grid[2] // 2
+    parts, refs = refs[:2], refs[2:]
     tracers, currents, land, own_n, own_s, own_e, own_w, from_n, from_s, from_e, from_w, *refs = refs
     (back,) = refs
     height, width = land.shape
@@ -477,16 +505,15 @@
     halo = lines[0][0:1], lines[1][0:1], column(sides, 0, last), column(sides, 8, 0)
     t0 = horizontal(c0, t0, halo) + mix * (t1 - t0) + warm * profile[0:1] + wet * heat
     sst = t0.astype(BF16)
-    plane = lax.axis_index("sec") * n_gy + lax.axis_index("gy")
-    line = lax.axis_index("gx")
+    index, half = place_of(this_device(grid), grid)
     for z, part in enumerate(parts):
-        where = part[height + 3 : height + 4, : planes * chunk].astype(F32)
-        hot = (iota((height, planes * chunk), 0).astype(F32) == where).astype(F32)
-        picked = dot(hot.T.astype(BF16), sst, NN).reshape(planes, chunk, width)
-        for i, m in enumerate(swap_order(planes)):
-            there = plane ^ m
-            device = (lax.div(there, n_gy) * n_gx + (line ^ z)) * n_gy + lax.rem(there, n_gy)
-            back[device] = picked[i, : back.shape[1]].astype(BF16)
+        rows = part[height + 8 :].astype(F32)
+        where = [rows[r : r + 1] for r in range(up(group * chunk, rows.shape[1]) // rows.shape[1])]
+        where = jnp.concatenate(where, axis=1)[:, : group * chunk]
+        hot = (iota((height, group * chunk), 0).astype(F32) == where).astype(F32)
+        picked = dot(hot.T.astype(BF16), sst, NN).reshape(group, chunk, width)
+        for i, m in enumerate(swap_order(group)):
+            back[device_at(index ^ m, half ^ z, grid)] = picked[i, : back.shape[1]].astype(BF16)
 
 
 def rim_flux(ext, width):
@@ -501,11 +528,11 @@
     )
 
 
-def stencil_kernel(n_gx, *refs):
-    count = n_gx + 11
+def stencil_kernel(*refs):
+    count = 13
     given, result, here, refs = refs[:count], refs[count], refs[count + 1 : 2 * count + 1], refs[2 * count + 1 :]
     out, held, weights, edge_n, edge_s, line_n, line_s, depth, forced, passing, sems = refs
-    parts, edges, (land, tracers, currents) = here[:n_gx], here[n_gx : n_gx + 8], here[n_gx + 8 :]
+    parts, edges, (land, tracers, currents) = here[:2], here[2:10], here[10:]
     copies = [pltpu.make_async_copy(x, y, sems.at[i]) for i, (x, y) in enumerate(zip(given, here))]
     for copy in copies:
         copy.start()
@@ -679,26 +706,19 @@
     return forward_pairs, [(b, a) for a, b in forward_pairs]
 
 
-def swap_order(count):
-    return [0, count - 1, count - 2, 1] + list(range(count - 3, 1, -1))
-
-
-def swapped(array, axes, count, step):
-    return lax.ppermute(array, axes, [(i, i ^ step) for i in range(count)])
-
-
 def on_device(atm_flux, remap_weights, remap_src, remap_dst, remap_owner, tracers, currents, land_sea):
     grid = n_sec, n_gx, n_gy = [lax.axis_size(axis) for axis in EVERY]
-    planes = n_sec * n_gy
+    devices = n_sec * n_gx * n_gy
+    group = devices // 2
     total, width, _ = remap_weights.shape
     _, levels, height, _ = tracers.shape
-    cap = up(2 * total // (planes * n_gx), 8)
+    cap = up(2 * total // devices, 8)
     wide = SENT * width
 
     *sends, slots = forward(atm_flux, remap_weights, remap_src, remap_owner.reshape(1, total), remap_dst, grid, cap)
     chunk = sends[0].shape[1]
-    order = swap_order(planes)
-    got = [sends[0]] + [swapped(sends[m], ("sec", "gy"), planes, m) for m in order[1:]]
+    order = swap_order(group)
+    got = [sends[0]] + [swapped(sends[m], grid, m, 0) for m in order[1:]]
     early = order.index(1)
 
     side = (width, width)
@@ -717,14 +737,14 @@
     )
     from_e = lax.ppermute(own_w, "gy", to_west)
     from_w = lax.ppermute(own_e, "gy", to_east)
-    part = (height + 8, wide)
-    merged = kernel(functools.partial(merge_kernel, planes), [(part, F32)] + [(part, BF16)] * (n_gx - 1), "merge", 24, 1 << 22)(*got)
-    parts = [merged[0]] + [swapped(merged[m], "gx", n_gx, m) for m in range(1, n_gx)]
+    part = (height + 16, wide)
+    merged = kernel(functools.partial(merge_kernel, group), [(part, F32), (part, BF16)], "merge", 24, 1 << 22)(*got)
+    parts = [merged[0], swapped(merged[1], grid, 0, 1)]
 
     edges = own_n, own_s, own_e, own_w, from_n, from_s, from_e, from_w
     (back,) = kernel(
         functools.partial(surface_kernel, grid, chunk, levels),
-        [((planes * n_gx, cap, width), BF16)],
+        [((devices, cap, width), BF16)],
         "surface",
         24,
         1 << 22,
@@ -734,7 +754,7 @@
     plane = (height, width)
     given = (*parts, *edges, land_sea, tracers, currents)
     (tracers_out,) = kernel(
-        functools.partial(stencil_kernel, n_gx),
+        stencil_kernel,
         [(tracers.shape, F32)],
         "substeps",
         58,

time: 86.6 us -> 92.8 us (1.072)
  starting transfers between devices: 30.2 us -> 40.2 us
  waiting for transfers between devices: 19.5 us -> 14.7 us
    ppermute x10 -> x16, starting transfers between devices: 13.6 us -> 20.8 us  [swapped(): lax.ppermute(array, EVERY, [(i, i ^ bits) for i in range(n_sec * n_gx * n...]
    ppermute x10 -> x16, waiting for transfers between devices: 17.3 us -> 12.9 us  [swapped(): lax.ppermute(array, EVERY, [(i, i ^ bits) for i in range(n_sec * n_gx * n...]
    all_to_all x1, starting transfers between devices: 7.23 us -> 8.79 us  [on_device(): lax.all_to_all(back, EVERY, split_axis=0, concat_axis=0, tiled=True)]
    ppermute x1, starting transfers between devices: 3.67 us -> 4.81 us  [on_device(): from_s = lax.ppermute(own_n, NORTH, to_north)]
    all_to_all x1, waiting for transfers between devices: 1.42 us -> 0.3 us  [on_device(): lax.all_to_all(back, EVERY, split_axis=0, concat_axis=0, tiled=True)]
  transfers between devices with their start and end apart: 15 -> 21, of which waited for: 9 -> 11; matrix products, arithmetic and copies ran while one was open for 0% -> 0% of each run, Pallas kernels for 14% -> 14%
where the time goes in v12:
time: 92.8 us; the launch traced here: 92.5 us
  starting transfers between devices  40.2 us (43%)
  Pallas kernels  36.4 us (39%)
  waiting for transfers between devices  14.7 us (16%)
  between operations  1.09 us (1%)
    ppermute x16, starting transfers between devices, swapped(): lax.ppermute(array, EVERY, [(i, i ^ bits) for i in range(n_sec * n_gx * n...  20.8 us
    ppermute x16, waiting for transfers between devices, swapped(): lax.ppermute(array, EVERY, [(i, i ^ bits) for i in range(n_sec * n_gx * n...  12.9 us
    pallas_call x1, Pallas kernels, forward(): pl.pallas_call(functools.partial(forward_kernel, parts, cap, grid), in_sp...  12.7 us
    pallas_call x1, Pallas kernels, on_device(): kernel(stencil_kernel, [(tracers.shape, F32)], 'substeps', 58, 1 << 24, [...  11.1 us
    all_to_all x1, starting transfers between devices, on_device(): lax.all_to_all(back, EVERY, split_axis=0, concat_axis=0, tiled=True)  8.79 us
    pallas_call x1, Pallas kernels, backward(): pl.pallas_call(functools.partial(backward_kernel, parts), in_specs=[ANY,...  8.41 us
    ppermute x1, starting transfers between devices, on_device(): from_s = lax.ppermute(own_n, NORTH, to_north)  4.81 us
    ppermute x1, starting transfers between devices, on_device(): from_w = lax.ppermute(own_e, 'gy', to_east)  3.03 us
  transfers between devices with their start and end apart: 21, of which 11 were waited for; matrix products, arithmetic and copies ran while one was open for 0% of the time, Pallas kernels for 14%

profile of v12, /device:TPU:0, one launch (start us, length us, event | category | flops | bytes accessed | tf_op | source)
XLA Modules:
  0.0 92.5 jit_solution(6389127974565139560)
XLA Ops:
  0.7 12.7 %forward_remap.1 = (bf16[2,48,640]{2,1,0:T(8,128)(2,1)}, bf16[2,48,640]{2,1,0:T(8,128)(2,1)}, bf16[2,48,640]{2,1,0:T(8,128)(2,1)}, bf16[2,48,640]{2,1,0:T(8,128)...) custom-call(s32[640]{0:T(1024)} %src_in.1, ...), custom_call_target="tpu_custom_call" | custom-call | flops 167772160 | bytes 20971520 | tf_op jit(solution)/shard_map/forward_remap/pallas_call | solution.py:215
  13.9 4.6 %collective-permute-start = (bf16[2,48,640]{2,1,0:T(8,128)(2,1)}, bf16[2,48,640]{2,1,0:T(8,128)(2,1)S(1)}, u32[]{:S(2)}, u32[]{:S(2)}) collective-permute-start(bf16[2,48,640]{2,1,0:T(8,128)(2,1)} %get-tuple-element.47), channel_id=1, source_target_pairs={{0,23},{1,22},{2,21},{3,20},{4,19},{5,18},{6,17},{7,16},{8,31},{9,... | collective-permute-start | bytes 368648 | tf_op jit(solution)/shard_map/ppermute | solution.py:70
  18.5 2.8 %collective-permute-start.10 = (bf16[2,48,640]{2,1,0:T(8,128)(2,1)}, bf16[2,48,640]{2,1,0:T(8,128)(2,1)S(1)}, u32[]{:S(2)}, u32[]{:S(2)}) collective-permute-start(bf16[2,48,640]{2,1,0:T(8,128)(2,1)} %get-tuple-element.58), channel_id=1, source_target_pairs={{0,6},{1,7},{2,4},{3,5},{4,2},{5,3},{6,0},{7,1},{8,14},{9,15},{10,... | collective-permute-start | bytes 368648 | tf_op jit(solution)/shard_map/ppermute | solution.py:70
  21.3 1.1 %collective-permute-start.12 = (bf16[2,48,640]{2,1,0:T(8,128)(2,1)}, bf16[2,48,640]{2,1,0:T(8,128)(2,1)S(1)}, u32[]{:S(2)}, u32[]{:S(2)}) collective-permute-start(bf16[2,48,640]{2,1,0:T(8,128)(2,1)} %get-tuple-element.60), channel_id=1, source_target_pairs={{0,4},{1,5},{2,6},{3,7},{4,0},{5,1},{6,2},{7,3},{8,12},{9,13},{10,... | collective-permute-start | bytes 368648 | tf_op jit(solution)/shard_map/ppermute | solution.py:70
  22.5 1.4 %collective-permute-start.13 = (bf16[2,48,640]{2,1,0:T(8,128)(2,1)}, bf16[2,48,640]{2,1,0:T(8,128)(2,1)S(1)}, u32[]{:S(2)}, u32[]{:S(2)}) collective-permute-start(bf16[2,48,640]{2,1,0:T(8,128)(2,1)} %get-tuple-element.61), channel_id=1, source_target_pairs={{0,3},{1,2},{2,1},{3,0},{4,7},{5,6},{6,5},{7,4},{8,11},{9,10},{10,... | collective-permute-start | bytes 368648 | tf_op jit(solution)/shard_map/ppermute | solution.py:70
  23.8 2.8 %collective-permute-done.1.refs_2_ = bf16[2,48,640]{2,1,0:T(8,128)(2,1)S(1)} collective-permute-done((bf16[2,48,640]{2,1,0:T(8,128)(2,1)}, bf16[2,48,640]{2,1,0:T(8,128)(2,1)S(1)}, u32[]{:S(2)}, u32[]{:S(2)}) %collective-permute-start.1) | collective-permute-done | bytes 122912 | tf_op jit(solution)/shard_map/ppermute | solution.py:70
  26.7 0.5 collective-permute-start.14
  27.2 1.2 %collective-permute-done.10.refs_11_ = bf16[2,48,640]{2,1,0:T(8,128)(2,1)S(1)} collective-permute-done((bf16[2,48,640]{2,1,0:T(8,128)(2,1)}, bf16[2,48,640]{2,1,0:T(8,128)(2,1)S(1)}, u32[]{:S(2)}, u32[]{:S(2)}) %collective-permute-start.10) | collective-permute-done | bytes 122912 | tf_op jit(solution)/shard_map/ppermute | solution.py:70
  28.6 1.8 %collective-permute-done.11.refs_12_ = bf16[2,48,640]{2,1,0:T(8,128)(2,1)S(1)} collective-permute-done((bf16[2,48,640]{2,1,0:T(8,128)(2,1)}, bf16[2,48,640]{2,1,0:T(8,128)(2,1)S(1)}, u32[]{:S(2)}, u32[]{:S(2)}) %collective-permute-start.11) | collective-permute-done | bytes 122912 | tf_op jit(solution)/shard_map/ppermute | solution.py:70
  30.4 1.1 %collective-permute-start.4 = (bf16[2,48,640]{2,1,0:T(8,128)(2,1)}, bf16[2,48,640]{2,1,0:T(8,128)(2,1)S(1)}, u32[]{:S(2)}, u32[]{:S(2)}) collective-permute-start(bf16[2,48,640]{2,1,0:T(8,128)(2,1)} %get-tuple-element.52), channel_id=1, source_target_pairs={{0,20},{1,21},{2,22},{3,23},{4,16},{5,17},{6,18},{7,19},{8,28},{9,... | collective-permute-start | bytes 368648 | tf_op jit(solution)/shard_map/ppermute | solution.py:70
  31.5 2.3 %collective-permute-done.12.refs_13_ = bf16[2,48,640]{2,1,0:T(8,128)(2,1)S(1)} collective-permute-done((bf16[2,48,640]{2,1,0:T(8,128)(2,1)}, bf16[2,48,640]{2,1,0:T(8,128)(2,1)S(1)}, u32[]{:S(2)}, u32[]{:S(2)}) %collective-permute-start.12) | collective-permute-done | bytes 122912 | tf_op jit(solution)/shard_map/ppermute | solution.py:70
  33.8 1.5 %collective-permute-start.6 = (bf16[2,48,640]{2,1,0:T(8,128)(2,1)}, bf16[2,48,640]{2,1,0:T(8,128)(2,1)S(1)}, u32[]{:S(2)}, u32[]{:S(2)}) collective-permute-start(bf16[2,48,640]{2,1,0:T(8,128)(2,1)} %get-tuple-element.54), channel_id=1, source_target_pairs={{0,18},{1,19},{2,16},{3,17},{4,22},{5,23},{6,20},{7,21},{8,26},{9,... | collective-permute-start | bytes 368648 | tf_op jit(solution)/shard_map/ppermute | solution.py:70
  35.3 1.2 %collective-permute-start.7 = (bf16[2,48,640]{2,1,0:T(8,128)(2,1)}, bf16[2,48,640]{2,1,0:T(8,128)(2,1)S(1)}, u32[]{:S(2)}, u32[]{:S(2)}) collective-permute-start(bf16[2,48,640]{2,1,0:T(8,128)(2,1)} %get-tuple-element.55), channel_id=1, source_target_pairs={{0,17},{1,16},{2,19},{3,18},{4,21},{5,20},{6,23},{7,22},{8,25},{9,... | collective-permute-start | bytes 368648 | tf_op jit(solution)/shard_map/ppermute | solution.py:70
  36.6 1.7 %collective-permute-start.8 = (bf16[2,48,640]{2,1,0:T(8,128)(2,1)}, bf16[2,48,640]{2,1,0:T(8,128)(2,1)S(1)}, u32[]{:S(2)}, u32[]{:S(2)}) collective-permute-start(bf16[2,48,640]{2,1,0:T(8,128)(2,1)} %get-tuple-element.56), channel_id=1, source_target_pairs={{0,16},{1,17},{2,18},{3,19},{4,20},{5,21},{6,22},{7,23},{8,24},{9,... | collective-permute-start | bytes 368648 | tf_op jit(solution)/shard_map/ppermute | solution.py:70
  38.2 1.6 %collective-permute-done.4.refs_5_ = bf16[2,48,640]{2,1,0:T(8,128)(2,1)S(1)} collective-permute-done((bf16[2,48,640]{2,1,0:T(8,128)(2,1)}, bf16[2,48,640]{2,1,0:T(8,128)(2,1)S(1)}, u32[]{:S(2)}, u32[]{:S(2)}) %collective-permute-start.4) | collective-permute-done | bytes 122912 | tf_op jit(solution)/shard_map/ppermute | solution.py:70
  39.9 1.0 %collective-permute-start.9 = (bf16[2,48,640]{2,1,0:T(8,128)(2,1)}, bf16[2,48,640]{2,1,0:T(8,128)(2,1)S(1)}, u32[]{:S(2)}, u32[]{:S(2)}) collective-permute-start(bf16[2,48,640]{2,1,0:T(8,128)(2,1)} %get-tuple-element.57), channel_id=1, source_target_pairs={{0,7},{1,6},{2,5},{3,4},{4,3},{5,2},{6,1},{7,0},{8,15},{9,14},{10,... | collective-permute-start | bytes 368648 | tf_op jit(solution)/shard_map/ppermute | solution.py:70
  41.0 1.0 %collective-permute-done.5.refs_6_ = bf16[2,48,640]{2,1,0:T(8,128)(2,1)S(1)} collective-permute-done((bf16[2,48,640]{2,1,0:T(8,128)(2,1)}, bf16[2,48,640]{2,1,0:T(8,128)(2,1)S(1)}, u32[]{:S(2)}, u32[]{:S(2)}) %collective-permute-start.5) | collective-permute-done | bytes 122912 | tf_op jit(solution)/shard_map/ppermute | solution.py:70
  42.0 1.3 %collective-permute-start.15 = (bf16[128,128]{1,0:T(8,128)(2,1)S(1)}, bf16[128,128]{1,0:T(8,128)(2,1)S(1)}, u32[]{:S(2)}, u32[]{:S(2)}) collective-permute-start(bf16[128,128]{1,0:T(8,128)(2,1)S(1)} %get-tuple-element.65.refs_3_.refs_6_), channel_id=1, source_target_pairs={{4,0},{8,4},{12,8},{16,12},{20,16},{24,20},{28,24},{5,1},{9,5},{13... | collective-permute-start | bytes 98312 | tf_op jit(solution)/shard_map/ppermute | solution.py:732
  43.3 4.8 %collective-permute-start.16 = (bf16[128,128]{1,0:T(8,128)(2,1)S(1)}, bf16[128,128]{1,0:T(8,128)(2,1)S(1)}, u32[]{:S(2)}, u32[]{:S(2)}) collective-permute-start(bf16[128,128]{1,0:T(8,128)(2,1)S(1)} %get-tuple-element.66.refs_2_.refs_5_), channel_id=1, source_target_pairs={{0,4},{4,8},{8,12},{12,16},{16,20},{20,24},{24,28},{1,5},{5,9},{9,... | collective-permute-start | bytes 98312 | tf_op jit(solution)/shard_map/ppermute | solution.py:733
  48.1 0.8 collective-permute-done.8.refs_9_
  49.0 0.7 collective-permute-done.16.from_s.refs_7_.refs_10_
  49.7 0.5 merge.1
  50.2 3.1 %collective-permute-start.17 = (bf16[144,640]{1,0:T(8,128)(2,1)S(1)}, bf16[144,640]{1,0:T(8,128)(2,1)S(1)}, u32[]{:S(2)}, u32[]{:S(2)}) collective-permute-start(bf16[144,640]{1,0:T(8,128)(2,1)S(1)} %get-tuple-element.84), channel_id=1, source_target_pairs={{0,8},{1,9},{2,10},{3,11},{4,12},{5,13},{6,14},{7,15},{8,0},{9,1},... | collective-permute-start | bytes 552968 | tf_op jit(solution)/shard_map/ppermute | solution.py:70
  53.4 1.7 %edge_columns.1 = (bf16[192,128]{1,0:T(8,128)(2,1)S(1)}, bf16[192,128]{1,0:T(8,128)(2,1)S(1)}) custom-call(f32[2,16,128,128]{3,2,1,0:T(8,128)S(1)} %copy-done.1, f32[2,16,128,128]{3,2,1,0:T(8,128)S(1)} %copy-done, s32[128,128]{1,0:T(8,128)S(1)} %copy-done.3, bf16[128,128]{1,0:T(8,128)(2,1)S(1)} %collective-permute-done.15.from_n.refs_6_.refs_9_, ...), custom_call_target="tpu_custom_call" | custom-call | flops 4194304 | bytes 4194304 | tf_op jit(solution)/shard_map/edge_columns/pallas_call | solution.py:735
  55.1 1.4 %collective-permute-start.18 = (bf16[192,128]{1,0:T(8,128)(2,1)S(1)}, bf16[192,128]{1,0:T(8,128)(2,1)S(1)}, u32[]{:S(2)}, u32[]{:S(2)}) collective-permute-start(bf16[192,128]{1,0:T(8,128)(2,1)S(1)} %get-tuple-element.88.refs_5_.refs_8_), channel_id=1, source_target_pairs={{1,0},{2,1},{3,2},{5,4},{6,5},{7,6},{9,8},{10,9},{11,10},{13,12},{... | collective-permute-start | bytes 147464 | tf_op jit(solution)/shard_map/ppermute | solution.py:738
  56.5 3.0 %collective-permute-start.19 = (bf16[192,128]{1,0:T(8,128)(2,1)S(1)}, bf16[192,128]{1,0:T(8,128)(2,1)S(1)}, u32[]{:S(2)}, u32[]{:S(2)}) collective-permute-start(bf16[192,128]{1,0:T(8,128)(2,1)S(1)} %get-tuple-element.87.refs_4_.refs_7_), channel_id=1, source_target_pairs={{0,1},{1,2},{2,3},{4,5},{5,6},{6,7},{8,9},{9,10},{10,11},{12,13},{... | collective-permute-start | bytes 147464 | tf_op jit(solution)/shard_map/ppermute | solution.py:739
  59.6 0.8 collective-permute-done.19.refs_9_.refs_12_
  60.4 1.3 %collective-permute-done.17.refs_1_ = bf16[144,640]{1,0:T(8,128)(2,1)S(1)} collective-permute-done((bf16[144,640]{1,0:T(8,128)(2,1)S(1)}, bf16[144,640]{1,0:T(8,128)(2,1)S(1)}, u32[]{:S(2)}, u32[]{:S(2)}) %collective-permute-start.17) | collective-permute-done | bytes 184352 | tf_op jit(solution)/shard_map/ppermute | solution.py:70
  61.8 1.9 %surface.1 = bf16[32,40,128]{2,1,0:T(8,128)(2,1)} custom-call(f32[144,640]{1,0:T(8,128)S(1)} %get-tuple-element.83.refs_0_, bf16[144,640]{1,0:T(8,128)(2,1)S(1)} %collective-permute-done.17.refs_1_, f32[1,3,128,128]{3,2,1,0:T(8,128)S(1)} %slice.6.refs_2_, f32[2,2,128,128]{3,2,1,0:T(8,128)S(1)} %slice.7.refs_3_, s32[128,128]{1,0:T(8,128)S(1)} %copy-done.3, ...), custom_call_target="tpu_custom_call" | custom-call | flops 4194304 | bytes 4194304 | tf_op jit(solution)/shard_map/surface/pallas_call | solution.py:745
  63.6 8.8 %all-to-all-start = ((bf16[32,40,128]{2,1,0:T(8,128)(2,1)}), bf16[32,40,128]{2,1,0:T(8,128)(2,1)S(1)}, u32[]{:S(2)}, u32[]{:S(2)}) async-start(bf16[32,40,128]{2,1,0:T(8,128)(2,1)} %surface.1), calls=%async_computation | async-start | bytes 655360 | tf_op jit(solution)/shard_map/all_to_all | solution.py:752
  72.5 11.1 %substeps.1 = f32[2,16,128,128]{3,2,1,0:T(8,128)} custom-call(f32[144,640]{1,0:T(8,128)} %copy-done.2, bf16[144,640]{1,0:T(8,128)(2,1)} %copy-done.4, bf16[128,128]{1,0:T(8,128)(2,1)} %copy-done.12, bf16[128,128]{1,0:T(8,128)(2,1)} %copy-done.11, bf16[192,128]{1,0:T(8,128)(2,1)} %copy-done.8, bf16[192,128]{1,0:T(8,128)(2,1)} %copy-done.7, ...), custom_call_target="tpu_custom_call" | custom-call | flops 16777216 | bytes 16777216 | tf_op jit(solution)/shard_map/substeps/pallas_call | solution.py:756
  83.9 8.4 %backward_remap.1 = f32[160,128]{1,0:T(8,128)} custom-call(s32[640]{0:T(1024)S(1)} %copy-done.14, s32[1,640]{1,0:T(1,128)S(1)} %reshape.19.src_in, bf16[32,40,128]{2,1,0:T(8,128)(2,1)S(1)} %all-to-all-done.back, bf16[640,128,128]{2,1,0:T(8,128)(2,1)} %w.3), custom_call_target="tpu_custom_call" | custom-call | flops 167772160 | bytes 20971520 | tf_op jit(solution)/shard_map/backward_remap/pallas_call | solution.py:671
  (52 shorter events, 1.3 us)
Async XLA Ops:
  0.6 40.2 %copy-start = (f32[2,16,128,128]{3,2,1,0:T(8,128)S(1)}, f32[2,16,128,128]{3,2,1,0:T(8,128)}, u32[]{:S(2)}) copy-start(f32[2,16,128,128]{3,2,1,0:T(8,128)} %refs_12_.1) | copy-start | bytes 6291460
  0.6 40.2 %copy-start.1 = (f32[2,16,128,128]{3,2,1,0:T(8,128)S(1)}, f32[2,16,128,128]{3,2,1,0:T(8,128)}, u32[]{:S(2)}) copy-start(f32[2,16,128,128]{3,2,1,0:T(8,128)} %refs_11_.1) | copy-start | bytes 6291460
  0.7 40.2 %copy-start.3 = (s32[128,128]{1,0:T(8,128)S(1)}, s32[128,128]{1,0:T(8,128)}, u32[]{:S(2)}) copy-start(s32[128,128]{1,0:T(8,128)} %refs_4_.1) | copy-start | bytes 196612
  13.4 8.0 %collective-permute-start.2 = (bf16[2,48,640]{2,1,0:T(8,128)(2,1)}, bf16[2,48,640]{2,1,0:T(8,128)(2,1)S(1)}, u32[]{:S(2)}, u32[]{:S(2)}) collective-permute-start(bf16[2,48,640]{2,1,0:T(8,128)(2,1)} %get-tuple-element.49), channel_id=1, source_target_pairs={{0,1},{1,0},{2,3},{3,2},{4,5},{5,4},{6,7},{7,6},{8,9},{9,8},{10,11... | collective-permute-start | bytes 368648 | tf_op jit(solution)/shard_map/ppermute | solution.py:70
  13.9 8.6 %collective-permute-start = (bf16[2,48,640]{2,1,0:T(8,128)(2,1)}, bf16[2,48,640]{2,1,0:T(8,128)(2,1)S(1)}, u32[]{:S(2)}, u32[]{:S(2)}) collective-permute-start(bf16[2,48,640]{2,1,0:T(8,128)(2,1)} %get-tuple-element.47), channel_id=1, source_target_pairs={{0,23},{1,22},{2,21},{3,20},{4,19},{5,18},{6,17},{7,16},{8,31},{9,... | collective-permute-start | bytes 368648 | tf_op jit(solution)/shard_map/ppermute | solution.py:70
  18.5 8.2 %collective-permute-start.1 = (bf16[2,48,640]{2,1,0:T(8,128)(2,1)}, bf16[2,48,640]{2,1,0:T(8,128)(2,1)S(1)}, u32[]{:S(2)}, u32[]{:S(2)}) collective-permute-start(bf16[2,48,640]{2,1,0:T(8,128)(2,1)} %get-tuple-element.48), channel_id=1, source_target_pairs={{0,22},{1,23},{2,20},{3,21},{4,18},{5,19},{6,16},{7,17},{8,30},{9,... | collective-permute-start | bytes 368648 | tf_op jit(solution)/shard_map/ppermute | solution.py:70
  18.5 9.9 %collective-permute-start.10 = (bf16[2,48,640]{2,1,0:T(8,128)(2,1)}, bf16[2,48,640]{2,1,0:T(8,128)(2,1)S(1)}, u32[]{:S(2)}, u32[]{:S(2)}) collective-permute-start(bf16[2,48,640]{2,1,0:T(8,128)(2,1)} %get-tuple-element.58), channel_id=1, source_target_pairs={{0,6},{1,7},{2,4},{3,5},{4,2},{5,3},{6,0},{7,1},{8,14},{9,15},{10,... | collective-permute-start | bytes 368648 | tf_op jit(solution)/shard_map/ppermute | solution.py:70
  21.3 9.1 %collective-permute-start.11 = (bf16[2,48,640]{2,1,0:T(8,128)(2,1)}, bf16[2,48,640]{2,1,0:T(8,128)(2,1)S(1)}, u32[]{:S(2)}, u32[]{:S(2)}) collective-permute-start(bf16[2,48,640]{2,1,0:T(8,128)(2,1)} %get-tuple-element.59), channel_id=1, source_target_pairs={{0,5},{1,4},{2,7},{3,6},{4,1},{5,0},{6,3},{7,2},{8,13},{9,12},{10,... | collective-permute-start | bytes 368648 | tf_op jit(solution)/shard_map/ppermute | solution.py:70
  21.3 12.5 %collective-permute-start.12 = (bf16[2,48,640]{2,1,0:T(8,128)(2,1)}, bf16[2,48,640]{2,1,0:T(8,128)(2,1)S(1)}, u32[]{:S(2)}, u32[]{:S(2)}) collective-permute-start(bf16[2,48,640]{2,1,0:T(8,128)(2,1)} %get-tuple-element.60), channel_id=1, source_target_pairs={{0,4},{1,5},{2,6},{3,7},{4,0},{5,1},{6,2},{7,3},{8,12},{9,13},{10,... | collective-permute-start | bytes 368648 | tf_op jit(solution)/shard_map/ppermute | solution.py:70
  22.5 11.3 %collective-permute-start.13 = (bf16[2,48,640]{2,1,0:T(8,128)(2,1)}, bf16[2,48,640]{2,1,0:T(8,128)(2,1)S(1)}, u32[]{:S(2)}, u32[]{:S(2)}) collective-permute-start(bf16[2,48,640]{2,1,0:T(8,128)(2,1)} %get-tuple-element.61), channel_id=1, source_target_pairs={{0,3},{1,2},{2,1},{3,0},{4,7},{5,6},{6,5},{7,4},{8,11},{9,10},{10,... | collective-permute-start | bytes 368648 | tf_op jit(solution)/shard_map/ppermute | solution.py:70
  26.7 8.7 %collective-permute-start.14 = (bf16[2,48,640]{2,1,0:T(8,128)(2,1)}, bf16[2,48,640]{2,1,0:T(8,128)(2,1)S(1)}, u32[]{:S(2)}, u32[]{:S(2)}) collective-permute-start(bf16[2,48,640]{2,1,0:T(8,128)(2,1)} %get-tuple-element.62), channel_id=1, source_target_pairs={{0,2},{1,3},{2,0},{3,1},{4,6},{5,7},{6,4},{7,5},{8,10},{9,11},{10,... | collective-permute-start | bytes 368648 | tf_op jit(solution)/shard_map/ppermute | solution.py:70
  28.4 8.2 %collective-permute-start.3 = (bf16[2,48,640]{2,1,0:T(8,128)(2,1)}, bf16[2,48,640]{2,1,0:T(8,128)(2,1)S(1)}, u32[]{:S(2)}, u32[]{:S(2)}) collective-permute-start(bf16[2,48,640]{2,1,0:T(8,128)(2,1)} %get-tuple-element.51), channel_id=1, source_target_pairs={{0,21},{1,20},{2,23},{3,22},{4,17},{5,16},{6,19},{7,18},{8,29},{9,... | collective-permute-start | bytes 368648 | tf_op jit(solution)/shard_map/ppermute | solution.py:70
  30.4 9.5 %collective-permute-start.4 = (bf16[2,48,640]{2,1,0:T(8,128)(2,1)}, bf16[2,48,640]{2,1,0:T(8,128)(2,1)S(1)}, u32[]{:S(2)}, u32[]{:S(2)}) collective-permute-start(bf16[2,48,640]{2,1,0:T(8,128)(2,1)} %get-tuple-element.52), channel_id=1, source_target_pairs={{0,20},{1,21},{2,22},{3,23},{4,16},{5,17},{6,18},{7,19},{8,28},{9,... | collective-permute-start | bytes 368648 | tf_op jit(solution)/shard_map/ppermute | solution.py:70
  33.8 8.2 %collective-permute-start.5 = (bf16[2,48,640]{2,1,0:T(8,128)(2,1)}, bf16[2,48,640]{2,1,0:T(8,128)(2,1)S(1)}, u32[]{:S(2)}, u32[]{:S(2)}) collective-permute-start(bf16[2,48,640]{2,1,0:T(8,128)(2,1)} %get-tuple-element.53), channel_id=1, source_target_pairs={{0,19},{1,18},{2,17},{3,16},{4,23},{5,22},{6,21},{7,20},{8,27},{9,... | collective-permute-start | bytes 368648 | tf_op jit(solution)/shard_map/ppermute | solution.py:70
  33.8 9.4 %collective-permute-start.6 = (bf16[2,48,640]{2,1,0:T(8,128)(2,1)}, bf16[2,48,640]{2,1,0:T(8,128)(2,1)S(1)}, u32[]{:S(2)}, u32[]{:S(2)}) collective-permute-start(bf16[2,48,640]{2,1,0:T(8,128)(2,1)} %get-tuple-element.54), channel_id=1, source_target_pairs={{0,18},{1,19},{2,16},{3,17},{4,22},{5,23},{6,20},{7,21},{8,26},{9,... | collective-permute-start | bytes 368648 | tf_op jit(solution)/shard_map/ppermute | solution.py:70
  35.3 12.8 %collective-permute-start.7 = (bf16[2,48,640]{2,1,0:T(8,128)(2,1)}, bf16[2,48,640]{2,1,0:T(8,128)(2,1)S(1)}, u32[]{:S(2)}, u32[]{:S(2)}) collective-permute-start(bf16[2,48,640]{2,1,0:T(8,128)(2,1)} %get-tuple-element.55), channel_id=1, source_target_pairs={{0,17},{1,16},{2,19},{3,18},{4,21},{5,20},{6,23},{7,22},{8,25},{9,... | collective-permute-start | bytes 368648 | tf_op jit(solution)/shard_map/ppermute | solution.py:70
  36.6 12.4 %collective-permute-start.8 = (bf16[2,48,640]{2,1,0:T(8,128)(2,1)}, bf16[2,48,640]{2,1,0:T(8,128)(2,1)S(1)}, u32[]{:S(2)}, u32[]{:S(2)}) collective-permute-start(bf16[2,48,640]{2,1,0:T(8,128)(2,1)} %get-tuple-element.56), channel_id=1, source_target_pairs={{0,16},{1,17},{2,18},{3,19},{4,20},{5,21},{6,22},{7,23},{8,24},{9,... | collective-permute-start | bytes 368648 | tf_op jit(solution)/shard_map/ppermute | solution.py:70
  39.9 9.1 %collective-permute-start.9 = (bf16[2,48,640]{2,1,0:T(8,128)(2,1)}, bf16[2,48,640]{2,1,0:T(8,128)(2,1)S(1)}, u32[]{:S(2)}, u32[]{:S(2)}) collective-permute-start(bf16[2,48,640]{2,1,0:T(8,128)(2,1)} %get-tuple-element.57), channel_id=1, source_target_pairs={{0,7},{1,6},{2,5},{3,4},{4,3},{5,2},{6,1},{7,0},{8,15},{9,14},{10,... | collective-permute-start | bytes 368648 | tf_op jit(solution)/shard_map/ppermute | solution.py:70
  40.9 20.8 %copy-start.11 = (bf16[128,128]{1,0:T(8,128)(2,1)}, bf16[128,128]{1,0:T(8,128)(2,1)S(1)}, u32[]{:S(2)}) copy-start(bf16[128,128]{1,0:T(8,128)(2,1)S(1)} %get-tuple-element.65.refs_3_.refs_6_) | copy-start | bytes 98308
  41.0 20.8 %copy-start.12 = (bf16[128,128]{1,0:T(8,128)(2,1)}, bf16[128,128]{1,0:T(8,128)(2,1)S(1)}, u32[]{:S(2)}) copy-start(bf16[128,128]{1,0:T(8,128)(2,1)S(1)} %get-tuple-element.66.refs_2_.refs_5_) | copy-start | bytes 98308
  42.0 7.0 %collective-permute-start.15 = (bf16[128,128]{1,0:T(8,128)(2,1)S(1)}, bf16[128,128]{1,0:T(8,128)(2,1)S(1)}, u32[]{:S(2)}, u32[]{:S(2)}) collective-permute-start(bf16[128,128]{1,0:T(8,128)(2,1)S(1)} %get-tuple-element.65.refs_3_.refs_6_), channel_id=1, source_target_pairs={{4,0},{8,4},{12,8},{16,12},{20,16},{24,20},{28,24},{5,1},{9,5},{13... | collective-permute-start | bytes 98312 | tf_op jit(solution)/shard_map/ppermute | solution.py:732
  43.3 6.4 %collective-permute-start.16 = (bf16[128,128]{1,0:T(8,128)(2,1)S(1)}, bf16[128,128]{1,0:T(8,128)(2,1)S(1)}, u32[]{:S(2)}, u32[]{:S(2)}) collective-permute-start(bf16[128,128]{1,0:T(8,128)(2,1)S(1)} %get-tuple-element.66.refs_2_.refs_5_), channel_id=1, source_target_pairs={{0,4},{4,8},{8,12},{12,16},{16,20},{20,24},{24,28},{1,5},{5,9},{9,... | collective-permute-start | bytes 98312 | tf_op jit(solution)/shard_map/ppermute | solution.py:733
  49.0 12.8 %copy-start.5 = (bf16[128,128]{1,0:T(8,128)(2,1)}, bf16[128,128]{1,0:T(8,128)(2,1)S(1)}, u32[]{:S(2)}) copy-start(bf16[128,128]{1,0:T(8,128)(2,1)S(1)} %collective-permute-done.15.from_n.refs_6_.refs_9_) | copy-start | bytes 98308
  49.7 12.1 %copy-start.6 = (bf16[128,128]{1,0:T(8,128)(2,1)}, bf16[128,128]{1,0:T(8,128)(2,1)S(1)}, u32[]{:S(2)}) copy-start(bf16[128,128]{1,0:T(8,128)(2,1)S(1)} %collective-permute-done.16.from_s.refs_7_.refs_10_) | copy-start | bytes 98308
  50.2 11.5 %collective-permute-start.17 = (bf16[144,640]{1,0:T(8,128)(2,1)S(1)}, bf16[144,640]{1,0:T(8,128)(2,1)S(1)}, u32[]{:S(2)}, u32[]{:S(2)}) collective-permute-start(bf16[144,640]{1,0:T(8,128)(2,1)S(1)} %get-tuple-element.84), channel_id=1, source_target_pairs={{0,8},{1,9},{2,10},{3,11},{4,12},{5,13},{6,14},{7,15},{8,0},{9,1},... | collective-permute-start | bytes 552968 | tf_op jit(solution)/shard_map/ppermute | solution.py:70
  55.1 17.4 %copy-start.7 = (bf16[192,128]{1,0:T(8,128)(2,1)}, bf16[192,128]{1,0:T(8,128)(2,1)S(1)}, u32[]{:S(2)}) copy-start(bf16[192,128]{1,0:T(8,128)(2,1)S(1)} %get-tuple-element.88.refs_5_.refs_8_) | copy-start | bytes 147460
  55.1 17.4 %copy-start.8 = (bf16[192,128]{1,0:T(8,128)(2,1)}, bf16[192,128]{1,0:T(8,128)(2,1)S(1)}, u32[]{:S(2)}) copy-start(bf16[192,128]{1,0:T(8,128)(2,1)S(1)} %get-tuple-element.87.refs_4_.refs_7_) | copy-start | bytes 147460
  55.1 17.3 %copy-start.15 = (s32[640]{0:T(1024)S(1)}, s32[640]{0:T(1024)}, u32[]{:S(2)}) copy-start(s32[640]{0:T(1024)} %src_in.1) | copy-start | bytes 7684
  55.1 4.5 %collective-permute-start.18 = (bf16[192,128]{1,0:T(8,128)(2,1)S(1)}, bf16[192,128]{1,0:T(8,128)(2,1)S(1)}, u32[]{:S(2)}, u32[]{:S(2)}) collective-permute-start(bf16[192,128]{1,0:T(8,128)(2,1)S(1)} %get-tuple-element.88.refs_5_.refs_8_), channel_id=1, source_target_pairs={{1,0},{2,1},{3,2},{5,4},{6,5},{7,6},{9,8},{10,9},{11,10},{13,12},{... | collective-permute-start | bytes 147464 | tf_op jit(solution)/shard_map/ppermute | solution.py:738
  56.5 3.9 %collective-permute-start.19 = (bf16[192,128]{1,0:T(8,128)(2,1)S(1)}, bf16[192,128]{1,0:T(8,128)(2,1)S(1)}, u32[]{:S(2)}, u32[]{:S(2)}) collective-permute-start(bf16[192,128]{1,0:T(8,128)(2,1)S(1)} %get-tuple-element.87.refs_4_.refs_7_), channel_id=1, source_target_pairs={{0,1},{1,2},{2,3},{4,5},{5,6},{6,7},{8,9},{9,10},{10,11},{12,13},{... | collective-permute-start | bytes 147464 | tf_op jit(solution)/shard_map/ppermute | solution.py:739
  59.6 12.8 %copy-start.9 = (bf16[192,128]{1,0:T(8,128)(2,1)}, bf16[192,128]{1,0:T(8,128)(2,1)S(1)}, u32[]{:S(2)}) copy-start(bf16[192,128]{1,0:T(8,128)(2,1)S(1)} %collective-permute-done.18.refs_8_.refs_11_) | copy-start | bytes 147460
  63.6 20.3 %all-to-all-start = ((bf16[32,40,128]{2,1,0:T(8,128)(2,1)}), bf16[32,40,128]{2,1,0:T(8,128)(2,1)S(1)}, u32[]{:S(2)}, u32[]{:S(2)}) async-start(bf16[32,40,128]{2,1,0:T(8,128)(2,1)} %surface.1), calls=%async_computation | async-start | bytes 655360 | tf_op jit(solution)/shard_map/all_to_all | solution.py:752
  (5 other events, 54.6 us)

commit v13 on v11

--- a/solution.py
+++ b/solution.py
@@ -212,6 +212,8 @@
 
 def merge_kernel(n_sources, *refs):
     sources, outs = refs[:n_sources], refs[n_sources:]
+    outs, salts = outs[: len(outs) // 2], outs[len(outs) // 2 :]
+    width = salts[0].shape[1]
     chunk = sources[0].shape[1]
     height = outs[0].shape[0] - 8
     first = chunk - 8
@@ -226,9 +228,17 @@
         where = jnp.concatenate(where, axis=1)
         hot = (iota((height, count), 0).astype(F32) == where).astype(F32).astype(BF16)
         sums = dot(hot, jnp.concatenate([source[z] for source in sources], axis=0), NN)
-        row3 = jnp.concatenate([where, ext[3:4, count:]], axis=1)
-        ext = jnp.where(iota((8, 1), 0) == 3, row3, ext)
-        out[...] = jnp.concatenate([sums, ext], axis=0).astype(out.dtype)
+        both = jnp.concatenate([sums, ext], axis=0)
+        salts[z][...] = both[:, 2 * width : 3 * width].astype(salts[z].dtype)
+        if count < 4 * width:
+            where = jnp.concatenate([where, jnp.zeros((1, 4 * width - count), F32)], axis=1)
+        salt = ext[:, 2 * width : 3 * width]
+        row1 = jnp.concatenate([salt[5:6], salt[7:8], where[:, 3 * width :], ext[1:2, 4 * width :]], axis=1)
+        row3 = jnp.concatenate([where[:, : 3 * width], ext[3:4, 4 * width :]], axis=1)
+        both = jnp.concatenate([both[:, : 2 * width], both[:, 3 * width :]], axis=1)
+        ext, row = both[height:], iota((8, 1), 0)
+        ext = jnp.where(row == 1, row1, jnp.where(row == 3, row3, ext))
+        out[...] = jnp.concatenate([both[:height], ext], axis=0).astype(out.dtype)
 
 
 def rows_kernel(tracers, currents, land, south, north):
@@ -398,11 +408,21 @@
     return edge
 
 
-def owner_sums(height, width, parts):
-    sums = parts[0][...]
+def added(parts):
+    total = parts[0][...]
     for part in parts[1:]:
-        sums = sums + part[...].astype(F32)
-    return [sums[:height, f * width : (f + 1) * width] for f in range(SENT)], sums[height : height + 8]
+        total = total + part[...].astype(F32)
+    return total
+
+
+def owner_sums(height, width, parts, salts=None):
+    sums = added(parts)
+    salt = jnp.zeros((height + 8, width), F32) if salts is None else added(salts)
+    ext, row = sums[height:], iota((8, 1), 0)
+    third = jnp.where(row == 5, ext[1:2, :width], jnp.where(row == 7, ext[1:2, width : 2 * width], salt[height:]))
+    shortwave, heat, stress_u, stress_v = [sums[:height, f * width : (f + 1) * width] for f in range(4)]
+    ext = jnp.concatenate([ext[:, : 2 * width], third, ext[:, 2 * width :]], axis=1)
+    return (shortwave, heat, salt[:height], stress_u, stress_v), ext
 
 
 def corrected_edges(levels, ext, stress_u, stress_v, near, far):
@@ -480,7 +500,8 @@
     plane = lax.axis_index("sec") * n_gy + lax.axis_index("gy")
     line = lax.axis_index("gx")
     for z, part in enumerate(parts):
-        where = part[height + 3 : height + 4, : planes * chunk].astype(F32)
+        rows = part[height:].astype(F32)
+        where = jnp.concatenate([rows[3:4, : 3 * width], rows[1:2, 2 * width : 3 * width]], axis=1)[:, : planes * chunk]
         hot = (iota((height, planes * chunk), 0).astype(F32) == where).astype(F32)
         picked = dot(hot.T.astype(BF16), sst, NN).reshape(planes, chunk, width)
         for i, m in enumerate(swap_order(planes)):
@@ -502,10 +523,11 @@
 
 
 def stencil_kernel(n_gx, *refs):
-    count = n_gx + 11
+    count = 2 * n_gx + 11
     given, result, here, refs = refs[:count], refs[count], refs[count + 1 : 2 * count + 1], refs[2 * count + 1 :]
     out, held, weights, edge_n, edge_s, line_n, line_s, depth, forced, passing, sems = refs
-    parts, edges, (land, tracers, currents) = here[:n_gx], here[n_gx : n_gx + 8], here[n_gx + 8 :]
+    parts, salts, edges = here[:n_gx], here[n_gx : 2 * n_gx], here[2 * n_gx : 2 * n_gx + 8]
+    land, tracers, currents = here[2 * n_gx + 8 :]
     copies = [pltpu.make_async_copy(x, y, sems.at[i]) for i, (x, y) in enumerate(zip(given, here))]
     for copy in copies:
         copy.start()
@@ -519,7 +541,7 @@
     height, width = land.shape
     last = width - 1
     wet = land[...].astype(F32)
-    (shortwave, heat, salt, stress_u, stress_v), ext = owner_sums(height, width, parts)
+    (shortwave, heat, salt, stress_u, stress_v), ext = owner_sums(height, width, parts, salts)
     near, far = corrected_edges(levels, ext, stress_u, stress_v, edges[:4], edges[4:])
     far_n, far_s, far_e, far_w = far
     edge_n[...], edge_s[...] = far_n, far_s
@@ -717,9 +739,12 @@
     )
     from_e = lax.ppermute(own_w, "gy", to_west)
     from_w = lax.ppermute(own_e, "gy", to_east)
-    part = (height + 8, wide)
-    merged = kernel(functools.partial(merge_kernel, planes), [(part, F32)] + [(part, BF16)] * (n_gx - 1), "merge", 24, 1 << 22)(*got)
-    parts = [merged[0]] + [swapped(merged[m], "gx", n_gx, m) for m in range(1, n_gx)]
+    outs = [((height + 8, x), dtype) for x in (4 * width, width) for dtype in [F32] + [BF16] * (n_gx - 1)]
+    merged = kernel(functools.partial(merge_kernel, planes), outs, "merge", 24, 1 << 22)(*got)
+    parts, salts = merged[:n_gx], merged[n_gx:]
+    parts = [parts[0]] + [swapped(parts[m], "gx", n_gx, m) for m in range(1, n_gx)]
+    salts, from_e, from_w = lax.optimization_barrier((salts, from_e, from_w))
+    salts = [salts[0]] + [swapped(salts[m], "gx", n_gx, m) for m in range(1, n_gx)]
 
     edges = own_n, own_s, own_e, own_w, from_n, from_s, from_e, from_w
     (back,) = kernel(
@@ -732,7 +757,7 @@
     returned = lax.all_to_all(back, EVERY, split_axis=0, concat_axis=0, tiled=True)
 
     plane = (height, width)
-    given = (*parts, *edges, land_sea, tracers, currents)
+    given = (*parts, *salts, *edges, land_sea, tracers, currents)
     (tracers_out,) = kernel(
         functools.partial(stencil_kernel, n_gx),
         [(tracers.shape, F32)],

time: 86.6 us -> 96.8 us (1.12)
  waiting for transfers between devices: 19.5 us -> 24.6 us
  starting transfers between devices: 30.2 us -> 34.1 us
  local copies, waits for them, and re-layouts: 0.12 us -> 1.26 us
    ppermute x10 -> x13, waiting for transfers between devices: 17.3 us -> 23.8 us  [swapped(): return lax.ppermute(array, axes, [(i, i ^ step) for i in range(count)])]
    ppermute x10 -> x13, starting transfers between devices: 13.6 us -> 18.1 us  [swapped(): return lax.ppermute(array, axes, [(i, i ^ step) for i in range(count)])]
    all_to_all x1, waiting for transfers between devices: 1.42 us -> 0.01 us  [on_device(): lax.all_to_all(back, EVERY, split_axis=0, concat_axis=0, tiled=True)]
    unnamed x36 -> x44, local copies, waits for them, and re-layouts: 0.08 us -> 1.22 us
  transfers between devices with their start and end apart: 15 -> 18, of which waited for: 9 -> 10; matrix products, arithmetic and copies ran while one was open for 0% -> 0% of each run, Pallas kernels for 14% -> 12%
where the time goes in v13:
time: 96.8 us; the launch traced here: 96.5 us
  Pallas kernels  35.5 us (37%)
  starting transfers between devices  34.1 us (35%)
  waiting for transfers between devices  24.6 us (25%)
  local copies, waits for them, and re-layouts  1.26 us (1%)
  between operations  1.12 us (1%)
    ppermute x13, waiting for transfers between devices, swapped(): return lax.ppermute(array, axes, [(i, i ^ step) for i in range(count)])  23.8 us
    ppermute x13, starting transfers between devices, swapped(): return lax.ppermute(array, axes, [(i, i ^ step) for i in range(count)])  18.1 us
    pallas_call x1, Pallas kernels, forward(): pl.pallas_call(functools.partial(forward_kernel, parts, cap, grid), in_sp...  12.6 us
    pallas_call x1, Pallas kernels, on_device(): kernel(functools.partial(stencil_kernel, n_gx), [(tracers.shape, F32)], '...  10.2 us
    pallas_call x1, Pallas kernels, backward(): pl.pallas_call(functools.partial(backward_kernel, parts), in_specs=[ANY,...  8.42 us
    all_to_all x1, starting transfers between devices, on_device(): lax.all_to_all(back, EVERY, split_axis=0, concat_axis=0, tiled=True)  6.63 us
    ppermute x1, starting transfers between devices, on_device(): from_s = lax.ppermute(own_n, NORTH, to_north)  3.68 us
    ppermute x1, starting transfers between devices, on_device(): from_w = lax.ppermute(own_e, 'gy', to_east)  3.03 us
  transfers between devices with their start and end apart: 18, of which 10 were waited for; matrix products, arithmetic and copies ran while one was open for 0% of the time, Pallas kernels for 12%

profile of v13, /device:TPU:0, one launch (start us, length us, event | category | flops | bytes accessed | tf_op | source)
XLA Modules:
  0.0 96.5 jit_solution(8960520280119955693)
XLA Ops:
  0.7 12.6 %forward_remap.1 = (bf16[4,48,640]{2,1,0:T(8,128)(2,1)}, bf16[4,48,640]{2,1,0:T(8,128)(2,1)}, bf16[4,48,640]{2,1,0:T(8,128)(2,1)}, bf16[4,48,640]{2,1,0:T(8,128)...) custom-call(s32[640]{0:T(1024)} %src_in.1, ...), custom_call_target="tpu_custom_call" | custom-call | flops 167772160 | bytes 20971520 | tf_op jit(solution)/shard_map/forward_remap/pallas_call | solution.py:188
  13.3 0.5 collective-permute-start.2
  13.8 3.6 %collective-permute-start = (bf16[4,48,640]{2,1,0:T(8,128)(2,1)}, bf16[4,48,640]{2,1,0:T(8,128)(2,1)S(1)}, u32[]{:S(2)}, u32[]{:S(2)}) collective-permute-start(bf16[4,48,640]{2,1,0:T(8,128)(2,1)} %get-tuple-element.43), channel_id=1, source_target_pairs={{0,19},{1,18},{2,17},{3,16},{16,3},{17,2},{18,1},{19,0},{4,23},{5,... | collective-permute-start | bytes 737288 | tf_op jit(solution)/shard_map/ppermute | solution.py:709
  17.4 1.3 %collective-permute-start.3 = (bf16[4,48,640]{2,1,0:T(8,128)(2,1)}, bf16[4,48,640]{2,1,0:T(8,128)(2,1)S(1)}, u32[]{:S(2)}, u32[]{:S(2)}) collective-permute-start(bf16[4,48,640]{2,1,0:T(8,128)(2,1)} %get-tuple-element.47), channel_id=1, source_target_pairs={{0,17},{1,16},{2,19},{3,18},{16,1},{17,0},{18,3},{19,2},{4,21},{5,... | collective-permute-start | bytes 737288 | tf_op jit(solution)/shard_map/ppermute | solution.py:709
  18.7 0.6 collective-permute-start.4
  19.4 1.4 %collective-permute-start.5 = (bf16[4,48,640]{2,1,0:T(8,128)(2,1)}, bf16[4,48,640]{2,1,0:T(8,128)(2,1)S(1)}, u32[]{:S(2)}, u32[]{:S(2)}) collective-permute-start(bf16[4,48,640]{2,1,0:T(8,128)(2,1)} %get-tuple-element.49), channel_id=1, source_target_pairs={{0,3},{1,2},{2,1},{3,0},{16,19},{17,18},{18,17},{19,16},{4,7},{5,6... | collective-permute-start | bytes 737288 | tf_op jit(solution)/shard_map/ppermute | solution.py:709
  20.8 3.2 %collective-permute-done.refs_1_ = bf16[4,48,640]{2,1,0:T(8,128)(2,1)S(1)} collective-permute-done((bf16[4,48,640]{2,1,0:T(8,128)(2,1)}, bf16[4,48,640]{2,1,0:T(8,128)(2,1)S(1)}, u32[]{:S(2)}, u32[]{:S(2)}) %collective-permute-start) | collective-permute-done | bytes 245792 | tf_op jit(solution)/shard_map/ppermute | solution.py:709
  24.0 1.2 %collective-permute-start.6 = (bf16[4,48,640]{2,1,0:T(8,128)(2,1)}, bf16[4,48,640]{2,1,0:T(8,128)(2,1)S(1)}, u32[]{:S(2)}, u32[]{:S(2)}) collective-permute-start(bf16[4,48,640]{2,1,0:T(8,128)(2,1)} %get-tuple-element.50), channel_id=1, source_target_pairs={{0,2},{1,3},{2,0},{3,1},{16,18},{17,19},{18,16},{19,17},{4,6},{5,7... | collective-permute-start | bytes 737288 | tf_op jit(solution)/shard_map/ppermute | solution.py:709
  25.4 4.3 %collective-permute-done.1.refs_2_ = bf16[4,48,640]{2,1,0:T(8,128)(2,1)S(1)} collective-permute-done((bf16[4,48,640]{2,1,0:T(8,128)(2,1)}, bf16[4,48,640]{2,1,0:T(8,128)(2,1)S(1)}, u32[]{:S(2)}, u32[]{:S(2)}) %collective-permute-start.1) | collective-permute-done | bytes 245792 | tf_op jit(solution)/shard_map/ppermute | solution.py:709
  29.6 1.3 %collective-permute-start.7 = (bf16[128,128]{1,0:T(8,128)(2,1)S(1)}, bf16[128,128]{1,0:T(8,128)(2,1)S(1)}, u32[]{:S(2)}, u32[]{:S(2)}) collective-permute-start(bf16[128,128]{1,0:T(8,128)(2,1)S(1)} %get-tuple-element.53.refs_9_.refs_8_), channel_id=1, source_target_pairs={{4,0},{8,4},{12,8},{16,12},{20,16},{24,20},{28,24},{5,1},{9,5},{13... | collective-permute-start | bytes 98312 | tf_op jit(solution)/shard_map/ppermute | solution.py:734
  30.9 3.6 %collective-permute-done.3.refs_4_ = bf16[4,48,640]{2,1,0:T(8,128)(2,1)S(1)} collective-permute-done((bf16[4,48,640]{2,1,0:T(8,128)(2,1)}, bf16[4,48,640]{2,1,0:T(8,128)(2,1)S(1)}, u32[]{:S(2)}, u32[]{:S(2)}) %collective-permute-start.3) | collective-permute-done | bytes 245792 | tf_op jit(solution)/shard_map/ppermute | solution.py:709
  34.5 3.7 %collective-permute-start.8 = (bf16[128,128]{1,0:T(8,128)(2,1)S(1)}, bf16[128,128]{1,0:T(8,128)(2,1)S(1)}, u32[]{:S(2)}, u32[]{:S(2)}) collective-permute-start(bf16[128,128]{1,0:T(8,128)(2,1)S(1)} %get-tuple-element.54.refs_8_.refs_7_), channel_id=1, source_target_pairs={{0,4},{4,8},{8,12},{12,16},{16,20},{20,24},{24,28},{1,5},{5,9},{9,... | collective-permute-start | bytes 98312 | tf_op jit(solution)/shard_map/ppermute | solution.py:735
  38.2 1.6 %collective-permute-done.4.refs_5_ = bf16[4,48,640]{2,1,0:T(8,128)(2,1)S(1)} collective-permute-done((bf16[4,48,640]{2,1,0:T(8,128)(2,1)}, bf16[4,48,640]{2,1,0:T(8,128)(2,1)S(1)}, u32[]{:S(2)}, u32[]{:S(2)}) %collective-permute-start.4) | collective-permute-done | bytes 245792 | tf_op jit(solution)/shard_map/ppermute | solution.py:709
  40.2 0.6 merge.1
  40.8 3.0 %collective-permute-start.10 = (bf16[136,512]{1,0:T(8,128)(2,1)S(1)}, bf16[136,512]{1,0:T(8,128)(2,1)S(1)}, u32[]{:S(2)}, u32[]{:S(2)}) collective-permute-start(bf16[136,512]{1,0:T(8,128)(2,1)S(1)} %get-tuple-element.65), channel_id=1, source_target_pairs={{0,8},{4,12},{8,0},{12,4},{1,9},{5,13},{9,1},{13,5},{2,10},{6,14},... | collective-permute-start | bytes 417800 | tf_op jit(solution)/shard_map/ppermute | solution.py:709
  43.9 1.4 %collective-permute-start.11 = (bf16[136,512]{1,0:T(8,128)(2,1)S(1)}, bf16[136,512]{1,0:T(8,128)(2,1)S(1)}, u32[]{:S(2)}, u32[]{:S(2)}) collective-permute-start(bf16[136,512]{1,0:T(8,128)(2,1)S(1)} %get-tuple-element.66), channel_id=1, source_target_pairs={{0,12},{4,8},{8,4},{12,0},{1,13},{5,9},{9,5},{13,1},{2,14},{6,10},... | collective-permute-start | bytes 417800 | tf_op jit(solution)/shard_map/ppermute | solution.py:709
  45.2 0.5 collective-permute-start.9
  45.7 1.7 %edge_columns.1 = (bf16[192,128]{1,0:T(8,128)(2,1)S(1)}, bf16[192,128]{1,0:T(8,128)(2,1)S(1)}) custom-call(f32[2,16,128,128]{3,2,1,0:T(8,128)S(1)} %copy-done.1, f32[2,16,128,128]{3,2,1,0:T(8,128)S(1)} %copy-done, s32[128,128]{1,0:T(8,128)S(1)} %copy-done.3, bf16[128,128]{1,0:T(8,128)(2,1)S(1)} %collective-permute-done.7.from_n.refs_12_.refs_11_, ...), custom_call_target="tpu_custom_call" | custom-call | flops 4194304 | bytes 4194304 | tf_op jit(solution)/shard_map/edge_columns/pallas_call | solution.py:737
  47.4 1.4 %collective-permute-start.12 = (bf16[192,128]{1,0:T(8,128)(2,1)S(1)}, bf16[192,128]{1,0:T(8,128)(2,1)S(1)}, u32[]{:S(2)}, u32[]{:S(2)}) collective-permute-start(bf16[192,128]{1,0:T(8,128)(2,1)S(1)} %get-tuple-element.73.refs_11_.refs_10_), channel_id=1, source_target_pairs={{1,0},{2,1},{3,2},{5,4},{6,5},{7,6},{9,8},{10,9},{11,10},{13,12},{... | collective-permute-start | bytes 147464 | tf_op jit(solution)/shard_map/ppermute | solution.py:740
  48.9 3.0 %collective-permute-start.13 = (bf16[192,128]{1,0:T(8,128)(2,1)S(1)}, bf16[192,128]{1,0:T(8,128)(2,1)S(1)}, u32[]{:S(2)}, u32[]{:S(2)}) collective-permute-start(bf16[192,128]{1,0:T(8,128)(2,1)S(1)} %get-tuple-element.74.refs_10_.refs_9_), channel_id=1, source_target_pairs={{0,1},{1,2},{2,3},{4,5},{5,6},{6,7},{8,9},{9,10},{10,11},{12,13},{... | collective-permute-start | bytes 147464 | tf_op jit(solution)/shard_map/ppermute | solution.py:741
  52.0 0.8 collective-permute-done.13.refs_15_.refs_14_
  52.8 1.7 %collective-permute-done.10.refs_2_ = bf16[136,512]{1,0:T(8,128)(2,1)S(1)} collective-permute-done((bf16[136,512]{1,0:T(8,128)(2,1)S(1)}, bf16[136,512]{1,0:T(8,128)(2,1)S(1)}, u32[]{:S(2)}, u32[]{:S(2)}) %collective-permute-start.10) | collective-permute-done | bytes 139296 | tf_op jit(solution)/shard_map/ppermute | solution.py:709
  54.8 1.9 %surface.1 = bf16[32,40,128]{2,1,0:T(8,128)(2,1)} custom-call(f32[136,512]{1,0:T(8,128)S(1)} %get-tuple-element.63.refs_0_, bf16[136,512]{1,0:T(8,128)(2,1)S(1)} %collective-permute-done.9.refs_1_, bf16[136,512]{1,0:T(8,128)(2,1)S(1)} %collective-permute-done.10.refs_2_, bf16[136,512]{1,0:T(8,128)(2,1)S(1)} %collective-permute-done.11.refs_3_, ...), custom_call_target="tpu_custom_call" | custom-call | flops 4194304 | bytes 4194304 | tf_op jit(solution)/shard_map/surface/pallas_call | solution.py:750
  56.7 6.6 %all-to-all-start = ((bf16[32,40,128]{2,1,0:T(8,128)(2,1)}), bf16[32,40,128]{2,1,0:T(8,128)(2,1)S(1)}, u32[]{:S(2)}, u32[]{:S(2)}) async-start(bf16[32,40,128]{2,1,0:T(8,128)(2,1)} %surface.1), calls=%async_computation | async-start | bytes 655360 | tf_op jit(solution)/shard_map/all_to_all | solution.py:757
  63.3 1.7 %collective-permute-start.14 = (bf16[136,128]{1,0:T(8,128)(2,1)S(1)}, bf16[136,128]{1,0:T(8,128)(2,1)S(1)}, u32[]{:S(2)}, u32[]{:S(2)}) collective-permute-start(bf16[136,128]{1,0:T(8,128)(2,1)S(1)} %get-tuple-element.76), channel_id=1, source_target_pairs={{0,4},{4,0},{8,12},{12,8},{1,5},{5,1},{9,13},{13,9},{2,6},{6,2},{1... | collective-permute-start | bytes 104456 | tf_op jit(solution)/shard_map/ppermute | solution.py:709
  65.0 2.4 %collective-permute-start.15 = (bf16[136,128]{1,0:T(8,128)(2,1)S(1)}, bf16[136,128]{1,0:T(8,128)(2,1)S(1)}, u32[]{:S(2)}, u32[]{:S(2)}) collective-permute-start(bf16[136,128]{1,0:T(8,128)(2,1)S(1)} %get-tuple-element.77), channel_id=1, source_target_pairs={{0,8},{4,12},{8,0},{12,4},{1,9},{5,13},{9,1},{13,5},{2,10},{6,14},... | collective-permute-start | bytes 104456 | tf_op jit(solution)/shard_map/ppermute | solution.py:709
  67.8 2.5 %collective-permute-done.14.refs_5_ = bf16[136,128]{1,0:T(8,128)(2,1)S(1)} collective-permute-done((bf16[136,128]{1,0:T(8,128)(2,1)S(1)}, bf16[136,128]{1,0:T(8,128)(2,1)S(1)}, u32[]{:S(2)}, u32[]{:S(2)}) %collective-permute-start.14) | collective-permute-done | bytes 34848 | tf_op jit(solution)/shard_map/ppermute | solution.py:709
  70.3 6.2 %collective-permute-done.15.refs_6_ = bf16[136,128]{1,0:T(8,128)(2,1)S(1)} collective-permute-done((bf16[136,128]{1,0:T(8,128)(2,1)S(1)}, bf16[136,128]{1,0:T(8,128)(2,1)S(1)}, u32[]{:S(2)}, u32[]{:S(2)}) %collective-permute-start.15) | collective-permute-done | bytes 34848 | tf_op jit(solution)/shard_map/ppermute | solution.py:709
  76.6 0.5 copy-done.19
  77.1 0.6 copy-done.20
  77.7 10.2 %substeps.1 = f32[2,16,128,128]{3,2,1,0:T(8,128)} custom-call(f32[136,512]{1,0:T(8,128)} %copy-done.2, bf16[136,512]{1,0:T(8,128)(2,1)} %copy-done.6, bf16[136,512]{1,0:T(8,128)(2,1)} %copy-done.4, bf16[136,512]{1,0:T(8,128)(2,1)} %copy-done.5, f32[136,128]{1,0:T(8,128)} %copy-done.16, bf16[136,128]{1,0:T(8,128)(2,1)} %copy-done.18, ...), custom_call_target="tpu_custom_call" | custom-call | flops 16777216 | bytes 16777216 | tf_op jit(solution)/shard_map/substeps/pallas_call | solution.py:761
  88.0 8.4 %backward_remap.1 = f32[160,128]{1,0:T(8,128)} custom-call(s32[640]{0:T(1024)S(1)} %copy-done.17, s32[1,640]{1,0:T(1,128)S(1)} %reshape.19.src_in, bf16[32,40,128]{2,1,0:T(8,128)(2,1)S(1)} %all-to-all-done.back, bf16[640,128,128]{2,1,0:T(8,128)(2,1)} %w.3), custom_call_target="tpu_custom_call" | custom-call | flops 167772160 | bytes 20971520 | tf_op jit(solution)/shard_map/backward_remap/pallas_call | solution.py:666
  (58 shorter events, 1.2 us)
Async XLA Ops:
  0.6 24.6 %copy-start = (f32[2,16,128,128]{3,2,1,0:T(8,128)S(1)}, f32[2,16,128,128]{3,2,1,0:T(8,128)}, u32[]{:S(2)}) copy-start(f32[2,16,128,128]{3,2,1,0:T(8,128)} %refs_18_.1) | copy-start | bytes 6291460
  0.6 24.6 %copy-start.1 = (f32[2,16,128,128]{3,2,1,0:T(8,128)S(1)}, f32[2,16,128,128]{3,2,1,0:T(8,128)}, u32[]{:S(2)}) copy-start(f32[2,16,128,128]{3,2,1,0:T(8,128)} %refs_17_.1) | copy-start | bytes 6291460
  0.7 24.6 %copy-start.3 = (s32[128,128]{1,0:T(8,128)S(1)}, s32[128,128]{1,0:T(8,128)}, u32[]{:S(2)}) copy-start(s32[128,128]{1,0:T(8,128)} %refs_6_.1) | copy-start | bytes 196612
  13.3 6.1 %collective-permute-start.2 = (bf16[4,48,640]{2,1,0:T(8,128)(2,1)}, bf16[4,48,640]{2,1,0:T(8,128)(2,1)S(1)}, u32[]{:S(2)}, u32[]{:S(2)}) collective-permute-start(bf16[4,48,640]{2,1,0:T(8,128)(2,1)} %get-tuple-element.45), channel_id=1, source_target_pairs={{0,1},{1,0},{2,3},{3,2},{16,17},{17,16},{18,19},{19,18},{4,5},{5,4... | collective-permute-start | bytes 737288 | tf_op jit(solution)/shard_map/ppermute | solution.py:709
  13.8 10.2 %collective-permute-start = (bf16[4,48,640]{2,1,0:T(8,128)(2,1)}, bf16[4,48,640]{2,1,0:T(8,128)(2,1)S(1)}, u32[]{:S(2)}, u32[]{:S(2)}) collective-permute-start(bf16[4,48,640]{2,1,0:T(8,128)(2,1)} %get-tuple-element.43), channel_id=1, source_target_pairs={{0,19},{1,18},{2,17},{3,16},{16,3},{17,2},{18,1},{19,0},{4,23},{5,... | collective-permute-start | bytes 737288 | tf_op jit(solution)/shard_map/ppermute | solution.py:709
  17.4 12.3 %collective-permute-start.1 = (bf16[4,48,640]{2,1,0:T(8,128)(2,1)}, bf16[4,48,640]{2,1,0:T(8,128)(2,1)S(1)}, u32[]{:S(2)}, u32[]{:S(2)}) collective-permute-start(bf16[4,48,640]{2,1,0:T(8,128)(2,1)} %get-tuple-element.44), channel_id=1, source_target_pairs={{0,18},{1,19},{2,16},{3,17},{16,2},{17,3},{18,0},{19,1},{4,22},{5,... | collective-permute-start | bytes 737288 | tf_op jit(solution)/shard_map/ppermute | solution.py:709
  17.4 17.1 %collective-permute-start.3 = (bf16[4,48,640]{2,1,0:T(8,128)(2,1)}, bf16[4,48,640]{2,1,0:T(8,128)(2,1)S(1)}, u32[]{:S(2)}, u32[]{:S(2)}) collective-permute-start(bf16[4,48,640]{2,1,0:T(8,128)(2,1)} %get-tuple-element.47), channel_id=1, source_target_pairs={{0,17},{1,16},{2,19},{3,18},{16,1},{17,0},{18,3},{19,2},{4,21},{5,... | collective-permute-start | bytes 737288 | tf_op jit(solution)/shard_map/ppermute | solution.py:709
  18.7 21.1 %collective-permute-start.4 = (bf16[4,48,640]{2,1,0:T(8,128)(2,1)}, bf16[4,48,640]{2,1,0:T(8,128)(2,1)S(1)}, u32[]{:S(2)}, u32[]{:S(2)}) collective-permute-start(bf16[4,48,640]{2,1,0:T(8,128)(2,1)} %get-tuple-element.48), channel_id=1, source_target_pairs={{0,16},{1,17},{2,18},{3,19},{16,0},{17,1},{18,2},{19,3},{4,20},{5,... | collective-permute-start | bytes 737288 | tf_op jit(solution)/shard_map/ppermute | solution.py:709
  19.4 20.5 %collective-permute-start.5 = (bf16[4,48,640]{2,1,0:T(8,128)(2,1)}, bf16[4,48,640]{2,1,0:T(8,128)(2,1)S(1)}, u32[]{:S(2)}, u32[]{:S(2)}) collective-permute-start(bf16[4,48,640]{2,1,0:T(8,128)(2,1)} %get-tuple-element.49), channel_id=1, source_target_pairs={{0,3},{1,2},{2,1},{3,0},{16,19},{17,18},{18,17},{19,16},{4,7},{5,6... | collective-permute-start | bytes 737288 | tf_op jit(solution)/shard_map/ppermute | solution.py:709
  24.0 16.1 %collective-permute-start.6 = (bf16[4,48,640]{2,1,0:T(8,128)(2,1)}, bf16[4,48,640]{2,1,0:T(8,128)(2,1)S(1)}, u32[]{:S(2)}, u32[]{:S(2)}) collective-permute-start(bf16[4,48,640]{2,1,0:T(8,128)(2,1)} %get-tuple-element.50), channel_id=1, source_target_pairs={{0,2},{1,3},{2,0},{3,1},{16,18},{17,19},{18,16},{19,17},{4,6},{5,7... | collective-permute-start | bytes 737288 | tf_op jit(solution)/shard_map/ppermute | solution.py:709
  25.3 29.4 %copy-start.14 = (bf16[128,128]{1,0:T(8,128)(2,1)}, bf16[128,128]{1,0:T(8,128)(2,1)S(1)}, u32[]{:S(2)}) copy-start(bf16[128,128]{1,0:T(8,128)(2,1)S(1)} %get-tuple-element.53.refs_9_.refs_8_) | copy-start | bytes 98308
  25.3 29.4 %copy-start.15 = (bf16[128,128]{1,0:T(8,128)(2,1)}, bf16[128,128]{1,0:T(8,128)(2,1)S(1)}, u32[]{:S(2)}) copy-start(bf16[128,128]{1,0:T(8,128)(2,1)S(1)} %get-tuple-element.54.refs_8_.refs_7_) | copy-start | bytes 98308
  29.6 10.5 %collective-permute-start.7 = (bf16[128,128]{1,0:T(8,128)(2,1)S(1)}, bf16[128,128]{1,0:T(8,128)(2,1)S(1)}, u32[]{:S(2)}, u32[]{:S(2)}) collective-permute-start(bf16[128,128]{1,0:T(8,128)(2,1)S(1)} %get-tuple-element.53.refs_9_.refs_8_), channel_id=1, source_target_pairs={{4,0},{8,4},{12,8},{16,12},{20,16},{24,20},{28,24},{5,1},{9,5},{13... | collective-permute-start | bytes 98312 | tf_op jit(solution)/shard_map/ppermute | solution.py:734
  34.5 5.6 %collective-permute-start.8 = (bf16[128,128]{1,0:T(8,128)(2,1)S(1)}, bf16[128,128]{1,0:T(8,128)(2,1)S(1)}, u32[]{:S(2)}, u32[]{:S(2)}) collective-permute-start(bf16[128,128]{1,0:T(8,128)(2,1)S(1)} %get-tuple-element.54.refs_8_.refs_7_), channel_id=1, source_target_pairs={{0,4},{4,8},{8,12},{12,16},{16,20},{20,24},{24,28},{1,5},{5,9},{9,... | collective-permute-start | bytes 98312 | tf_op jit(solution)/shard_map/ppermute | solution.py:735
  40.8 13.6 %collective-permute-start.10 = (bf16[136,512]{1,0:T(8,128)(2,1)S(1)}, bf16[136,512]{1,0:T(8,128)(2,1)S(1)}, u32[]{:S(2)}, u32[]{:S(2)}) collective-permute-start(bf16[136,512]{1,0:T(8,128)(2,1)S(1)} %get-tuple-element.65), channel_id=1, source_target_pairs={{0,8},{4,12},{8,0},{12,4},{1,9},{5,13},{9,1},{13,5},{2,10},{6,14},... | collective-permute-start | bytes 417800 | tf_op jit(solution)/shard_map/ppermute | solution.py:709
  43.9 10.5 %collective-permute-start.11 = (bf16[136,512]{1,0:T(8,128)(2,1)S(1)}, bf16[136,512]{1,0:T(8,128)(2,1)S(1)}, u32[]{:S(2)}, u32[]{:S(2)}) collective-permute-start(bf16[136,512]{1,0:T(8,128)(2,1)S(1)} %get-tuple-element.66), channel_id=1, source_target_pairs={{0,12},{4,8},{8,4},{12,0},{1,13},{5,9},{9,5},{13,1},{2,14},{6,10},... | collective-permute-start | bytes 417800 | tf_op jit(solution)/shard_map/ppermute | solution.py:709
  45.2 9.5 %collective-permute-start.9 = (bf16[136,512]{1,0:T(8,128)(2,1)S(1)}, bf16[136,512]{1,0:T(8,128)(2,1)S(1)}, u32[]{:S(2)}, u32[]{:S(2)}) collective-permute-start(bf16[136,512]{1,0:T(8,128)(2,1)S(1)} %get-tuple-element.64), channel_id=1, source_target_pairs={{0,4},{4,0},{8,12},{12,8},{1,5},{5,1},{9,13},{13,9},{2,6},{6,2},{1... | collective-permute-start | bytes 417800 | tf_op jit(solution)/shard_map/ppermute | solution.py:709
  47.4 29.1 %copy-start.10 = (bf16[192,128]{1,0:T(8,128)(2,1)}, bf16[192,128]{1,0:T(8,128)(2,1)S(1)}, u32[]{:S(2)}) copy-start(bf16[192,128]{1,0:T(8,128)(2,1)S(1)} %get-tuple-element.73.refs_11_.refs_10_) | copy-start | bytes 147460
  47.4 29.1 %copy-start.11 = (bf16[192,128]{1,0:T(8,128)(2,1)}, bf16[192,128]{1,0:T(8,128)(2,1)S(1)}, u32[]{:S(2)}) copy-start(bf16[192,128]{1,0:T(8,128)(2,1)S(1)} %get-tuple-element.74.refs_10_.refs_9_) | copy-start | bytes 147460
  47.4 20.3 %copy-start.21 = (s32[640]{0:T(1024)S(1)}, s32[640]{0:T(1024)}, u32[]{:S(2)}) copy-start(s32[640]{0:T(1024)} %src_in.1) | copy-start | bytes 7684
  47.4 4.5 %collective-permute-start.12 = (bf16[192,128]{1,0:T(8,128)(2,1)S(1)}, bf16[192,128]{1,0:T(8,128)(2,1)S(1)}, u32[]{:S(2)}, u32[]{:S(2)}) collective-permute-start(bf16[192,128]{1,0:T(8,128)(2,1)S(1)} %get-tuple-element.73.refs_11_.refs_10_), channel_id=1, source_target_pairs={{1,0},{2,1},{3,2},{5,4},{6,5},{7,6},{9,8},{10,9},{11,10},{13,12},{... | collective-permute-start | bytes 147464 | tf_op jit(solution)/shard_map/ppermute | solution.py:740
  48.9 3.9 %collective-permute-start.13 = (bf16[192,128]{1,0:T(8,128)(2,1)S(1)}, bf16[192,128]{1,0:T(8,128)(2,1)S(1)}, u32[]{:S(2)}, u32[]{:S(2)}) collective-permute-start(bf16[192,128]{1,0:T(8,128)(2,1)S(1)} %get-tuple-element.74.refs_10_.refs_9_), channel_id=1, source_target_pairs={{0,1},{1,2},{2,3},{4,5},{5,6},{6,7},{8,9},{9,10},{10,11},{12,13},{... | collective-permute-start | bytes 147464 | tf_op jit(solution)/shard_map/ppermute | solution.py:741
  52.0 24.6 %copy-start.12 = (bf16[192,128]{1,0:T(8,128)(2,1)}, bf16[192,128]{1,0:T(8,128)(2,1)S(1)}, u32[]{:S(2)}) copy-start(bf16[192,128]{1,0:T(8,128)(2,1)S(1)} %collective-permute-done.12.refs_14_.refs_13_) | copy-start | bytes 147460
  52.8 23.8 %copy-start.13 = (bf16[192,128]{1,0:T(8,128)(2,1)}, bf16[192,128]{1,0:T(8,128)(2,1)S(1)}, u32[]{:S(2)}) copy-start(bf16[192,128]{1,0:T(8,128)(2,1)S(1)} %collective-permute-done.13.refs_15_.refs_14_) | copy-start | bytes 147460
  54.4 22.2 %copy-start.4 = (bf16[136,512]{1,0:T(8,128)(2,1)}, bf16[136,512]{1,0:T(8,128)(2,1)S(1)}, u32[]{:S(2)}) copy-start(bf16[136,512]{1,0:T(8,128)(2,1)S(1)} %collective-permute-done.10.refs_2_) | copy-start | bytes 417796
  54.4 22.2 %copy-start.5 = (bf16[136,512]{1,0:T(8,128)(2,1)}, bf16[136,512]{1,0:T(8,128)(2,1)S(1)}, u32[]{:S(2)}) copy-start(bf16[136,512]{1,0:T(8,128)(2,1)S(1)} %collective-permute-done.11.refs_3_) | copy-start | bytes 417796
  54.8 21.8 %copy-start.6 = (bf16[136,512]{1,0:T(8,128)(2,1)}, bf16[136,512]{1,0:T(8,128)(2,1)S(1)}, u32[]{:S(2)}) copy-start(bf16[136,512]{1,0:T(8,128)(2,1)S(1)} %collective-permute-done.9.refs_1_) | copy-start | bytes 417796
  56.7 31.3 %all-to-all-start = ((bf16[32,40,128]{2,1,0:T(8,128)(2,1)}), bf16[32,40,128]{2,1,0:T(8,128)(2,1)S(1)}, u32[]{:S(2)}, u32[]{:S(2)}) async-start(bf16[32,40,128]{2,1,0:T(8,128)(2,1)} %surface.1), calls=%async_computation | async-start | bytes 655360 | tf_op jit(solution)/shard_map/all_to_all | solution.py:757
  63.3 7.0 %collective-permute-start.14 = (bf16[136,128]{1,0:T(8,128)(2,1)S(1)}, bf16[136,128]{1,0:T(8,128)(2,1)S(1)}, u32[]{:S(2)}, u32[]{:S(2)}) collective-permute-start(bf16[136,128]{1,0:T(8,128)(2,1)S(1)} %get-tuple-element.76), channel_id=1, source_target_pairs={{0,4},{4,0},{8,12},{12,8},{1,5},{5,1},{9,13},{13,9},{2,6},{6,2},{1... | collective-permute-start | bytes 104456 | tf_op jit(solution)/shard_map/ppermute | solution.py:709
  65.0 11.6 %collective-permute-start.15 = (bf16[136,128]{1,0:T(8,128)(2,1)S(1)}, bf16[136,128]{1,0:T(8,128)(2,1)S(1)}, u32[]{:S(2)}, u32[]{:S(2)}) collective-permute-start(bf16[136,128]{1,0:T(8,128)(2,1)S(1)} %get-tuple-element.77), channel_id=1, source_target_pairs={{0,8},{4,12},{8,0},{12,4},{1,9},{5,13},{9,1},{13,5},{2,10},{6,14},... | collective-permute-start | bytes 104456 | tf_op jit(solution)/shard_map/ppermute | solution.py:709
  67.4 9.1 %collective-permute-start.16 = (bf16[136,128]{1,0:T(8,128)(2,1)S(1)}, bf16[136,128]{1,0:T(8,128)(2,1)S(1)}, u32[]{:S(2)}, u32[]{:S(2)}) collective-permute-start(bf16[136,128]{1,0:T(8,128)(2,1)S(1)} %get-tuple-element.78), channel_id=1, source_target_pairs={{0,12},{4,8},{8,4},{12,0},{1,13},{5,9},{9,5},{13,1},{2,14},{6,10},... | collective-permute-start | bytes 104456 | tf_op jit(solution)/shard_map/ppermute | solution.py:709
  67.8 20.2 %copy-start.17 = (s32[640]{0:T(1024)S(1)}, s32[640]{0:T(1024)}, u32[]{:S(2)}) copy-start(s32[640]{0:T(1024)} %get-tuple-element.81.slots_in) | copy-start | bytes 7684
  (8 other events, 72.2 us)

commit v14 on v13

--- a/solution.py
+++ b/solution.py
@@ -660,7 +660,7 @@
     out[...] = both[:, :width] + both[:, width:]
 
 
-def backward(back, w, src, slots, blocks, parts=10):
+def backward(back, w, src, slots, blocks, parts=20):
     total, width, _ = w.shape
     devices, cap, _ = back.shape
     return pl.pallas_call(
@@ -754,6 +754,7 @@
         24,
         1 << 22,
     )(*parts, tracers[0:1, 0:3], currents[:, 0:2], land_sea, *edges)
+    back, salts = lax.optimization_barrier((back, salts))
     returned = lax.all_to_all(back, EVERY, split_axis=0, concat_axis=0, tiled=True)
 
     plane = (height, width)

time: 96.8 us -> 90.5 us (0.935)
  waiting for transfers between devices: 24.6 us -> 21 us
  starting transfers between devices: 34.1 us -> 32.6 us
  local copies, waits for them, and re-layouts: 1.26 us -> 0.14 us
    ppermute x13, waiting for transfers between devices: 23.8 us -> 16.3 us  [swapped(): return lax.ppermute(array, axes, [(i, i ^ step) for i in range(count)])]
    ppermute x1, waiting for transfers between devices: 0.01 us -> 3.36 us  [on_device(): from_e = lax.ppermute(own_w, 'gy', to_west)]
    ppermute x1, starting transfers between devices: 3.03 us -> 1.58 us  [on_device(): from_w = lax.ppermute(own_e, 'gy', to_east)]
    all_to_all x1, waiting for transfers between devices: 0.01 us -> 1.36 us  [on_device(): lax.all_to_all(back, EVERY, split_axis=0, concat_axis=0, tiled=True)]
    unnamed x44, local copies, waits for them, and re-layouts: 1.22 us -> 0.1 us
  transfers between devices with their start and end apart: 18 -> 18, of which waited for: 10 -> 9; matrix products, arithmetic and copies ran while one was open for 0% -> 0% of each run, Pallas kernels for 12% -> 15%
where the time goes in v14:
time: 90.5 us; the launch traced here: 90.2 us
  Pallas kernels  35.4 us (39%)
  starting transfers between devices  32.6 us (36%)
  waiting for transfers between devices  21 us (23%)
  between operations  1.04 us (1%)
    ppermute x13, starting transfers between devices, swapped(): return lax.ppermute(array, axes, [(i, i ^ step) for i in range(count)])  17.8 us
    ppermute x13, waiting for transfers between devices, swapped(): return lax.ppermute(array, axes, [(i, i ^ step) for i in range(count)])  16.3 us
    pallas_call x1, Pallas kernels, forward(): pl.pallas_call(functools.partial(forward_kernel, parts, cap, grid), in_sp...  12.6 us
    pallas_call x1, Pallas kernels, on_device(): kernel(functools.partial(stencil_kernel, n_gx), [(tracers.shape, F32)], '...  10.2 us
    pallas_call x1, Pallas kernels, backward(): pl.pallas_call(functools.partial(backward_kernel, parts), in_specs=[ANY,...  8.3 us
    all_to_all x1, starting transfers between devices, on_device(): lax.all_to_all(back, EVERY, split_axis=0, concat_axis=0, tiled=True)  6.41 us
    ppermute x1, starting transfers between devices, on_device(): from_s = lax.ppermute(own_n, NORTH, to_north)  4.26 us
    ppermute x1, waiting for transfers between devices, on_device(): from_e = lax.ppermute(own_w, 'gy', to_west)  3.36 us
  transfers between devices with their start and end apart: 18, of which 9 were waited for; matrix products, arithmetic and copies ran while one was open for 0% of the time, Pallas kernels for 15%

profile of v14, /device:TPU:0, one launch (start us, length us, event | category | flops | bytes accessed | tf_op | source)
XLA Modules:
  0.0 90.2 jit_solution(16559527342549419941)
XLA Ops:
  0.7 12.6 %forward_remap.1 = (bf16[4,48,640]{2,1,0:T(8,128)(2,1)}, bf16[4,48,640]{2,1,0:T(8,128)(2,1)}, bf16[4,48,640]{2,1,0:T(8,128)(2,1)}, bf16[4,48,640]{2,1,0:T(8,128)...) custom-call(s32[640]{0:T(1024)} %src_in.1, ...), custom_call_target="tpu_custom_call" | custom-call | flops 167772160 | bytes 20971520 | tf_op jit(solution)/shard_map/forward_remap/pallas_call | solution.py:188
  13.3 3.4 %collective-permute-start = (bf16[4,48,640]{2,1,0:T(8,128)(2,1)}, bf16[4,48,640]{2,1,0:T(8,128)(2,1)S(1)}, u32[]{:S(2)}, u32[]{:S(2)}) collective-permute-start(bf16[4,48,640]{2,1,0:T(8,128)(2,1)} %get-tuple-element.48), channel_id=1, source_target_pairs={{0,19},{1,18},{2,17},{3,16},{16,3},{17,2},{18,1},{19,0},{4,23},{5,... | collective-permute-start | bytes 737288 | tf_op jit(solution)/shard_map/ppermute | solution.py:709
  16.7 0.7 collective-permute-start.2
  17.3 0.0 collective-permute-start.1
  17.4 1.3 %collective-permute-start.3 = (bf16[4,48,640]{2,1,0:T(8,128)(2,1)}, bf16[4,48,640]{2,1,0:T(8,128)(2,1)S(1)}, u32[]{:S(2)}, u32[]{:S(2)}) collective-permute-start(bf16[4,48,640]{2,1,0:T(8,128)(2,1)} %get-tuple-element.52), channel_id=1, source_target_pairs={{0,17},{1,16},{2,19},{3,18},{16,1},{17,0},{18,3},{19,2},{4,21},{5,... | collective-permute-start | bytes 737288 | tf_op jit(solution)/shard_map/ppermute | solution.py:709
  18.7 0.7 collective-permute-start.4
  19.4 4.0 %collective-permute-done.refs_1_ = bf16[4,48,640]{2,1,0:T(8,128)(2,1)S(1)} collective-permute-done((bf16[4,48,640]{2,1,0:T(8,128)(2,1)}, bf16[4,48,640]{2,1,0:T(8,128)(2,1)S(1)}, u32[]{:S(2)}, u32[]{:S(2)}) %collective-permute-start) | collective-permute-done | bytes 245792 | tf_op jit(solution)/shard_map/ppermute | solution.py:709
  23.4 2.0 %collective-permute-start.5 = (bf16[4,48,640]{2,1,0:T(8,128)(2,1)}, bf16[4,48,640]{2,1,0:T(8,128)(2,1)S(1)}, u32[]{:S(2)}, u32[]{:S(2)}) collective-permute-start(bf16[4,48,640]{2,1,0:T(8,128)(2,1)} %get-tuple-element.54), channel_id=1, source_target_pairs={{0,3},{1,2},{2,1},{3,0},{16,19},{17,18},{18,17},{19,16},{4,7},{5,6... | collective-permute-start | bytes 737288 | tf_op jit(solution)/shard_map/ppermute | solution.py:709
  25.4 0.4 collective-permute-start.6
  25.8 0.1 edge_rows.1
  25.9 3.1 %collective-permute-done.1.refs_2_ = bf16[4,48,640]{2,1,0:T(8,128)(2,1)S(1)} collective-permute-done((bf16[4,48,640]{2,1,0:T(8,128)(2,1)}, bf16[4,48,640]{2,1,0:T(8,128)(2,1)S(1)}, u32[]{:S(2)}, u32[]{:S(2)}) %collective-permute-start.1) | collective-permute-done | bytes 245792 | tf_op jit(solution)/shard_map/ppermute | solution.py:709
  29.0 1.3 %collective-permute-start.7 = (bf16[128,128]{1,0:T(8,128)(2,1)S(1)}, bf16[128,128]{1,0:T(8,128)(2,1)S(1)}, u32[]{:S(2)}, u32[]{:S(2)}) collective-permute-start(bf16[128,128]{1,0:T(8,128)(2,1)S(1)} %get-tuple-element.58.refs_8_.refs_9_), channel_id=1, source_target_pairs={{4,0},{8,4},{12,8},{16,12},{20,16},{24,20},{28,24},{5,1},{9,5},{13... | collective-permute-start | bytes 98312 | tf_op jit(solution)/shard_map/ppermute | solution.py:734
  30.2 3.6 %collective-permute-done.3.refs_4_ = bf16[4,48,640]{2,1,0:T(8,128)(2,1)S(1)} collective-permute-done((bf16[4,48,640]{2,1,0:T(8,128)(2,1)}, bf16[4,48,640]{2,1,0:T(8,128)(2,1)S(1)}, u32[]{:S(2)}, u32[]{:S(2)}) %collective-permute-start.3) | collective-permute-done | bytes 245792 | tf_op jit(solution)/shard_map/ppermute | solution.py:709
  33.9 4.3 %collective-permute-start.8 = (bf16[128,128]{1,0:T(8,128)(2,1)S(1)}, bf16[128,128]{1,0:T(8,128)(2,1)S(1)}, u32[]{:S(2)}, u32[]{:S(2)}) collective-permute-start(bf16[128,128]{1,0:T(8,128)(2,1)S(1)} %get-tuple-element.59.refs_7_.refs_8_), channel_id=1, source_target_pairs={{0,4},{4,8},{8,12},{12,16},{16,20},{20,24},{24,28},{1,5},{5,9},{9,... | collective-permute-start | bytes 98312 | tf_op jit(solution)/shard_map/ppermute | solution.py:735
  38.1 1.0 %collective-permute-done.4.refs_5_ = bf16[4,48,640]{2,1,0:T(8,128)(2,1)S(1)} collective-permute-done((bf16[4,48,640]{2,1,0:T(8,128)(2,1)}, bf16[4,48,640]{2,1,0:T(8,128)(2,1)S(1)}, u32[]{:S(2)}, u32[]{:S(2)}) %collective-permute-start.4) | collective-permute-done | bytes 245792 | tf_op jit(solution)/shard_map/ppermute | solution.py:709
  39.2 0.8 collective-permute-done.6.refs_7_
  40.1 0.6 merge.1
  40.7 2.0 %collective-permute-start.9 = (bf16[136,512]{1,0:T(8,128)(2,1)S(1)}, bf16[136,512]{1,0:T(8,128)(2,1)S(1)}, u32[]{:S(2)}, u32[]{:S(2)}) collective-permute-start(bf16[136,512]{1,0:T(8,128)(2,1)S(1)} %get-tuple-element.69), channel_id=1, source_target_pairs={{0,4},{4,0},{8,12},{12,8},{1,5},{5,1},{9,13},{13,9},{2,6},{6,2},{1... | collective-permute-start | bytes 417800 | tf_op jit(solution)/shard_map/ppermute | solution.py:709
  42.8 2.8 %collective-permute-start.10 = (bf16[136,512]{1,0:T(8,128)(2,1)S(1)}, bf16[136,512]{1,0:T(8,128)(2,1)S(1)}, u32[]{:S(2)}, u32[]{:S(2)}) collective-permute-start(bf16[136,512]{1,0:T(8,128)(2,1)S(1)} %get-tuple-element.70), channel_id=1, source_target_pairs={{0,8},{4,12},{8,0},{12,4},{1,9},{5,13},{9,1},{13,5},{2,10},{6,14},... | collective-permute-start | bytes 417800 | tf_op jit(solution)/shard_map/ppermute | solution.py:709
  45.6 1.7 %edge_columns.1 = (bf16[192,128]{1,0:T(8,128)(2,1)S(1)}, bf16[192,128]{1,0:T(8,128)(2,1)S(1)}) custom-call(f32[2,16,128,128]{3,2,1,0:T(8,128)S(1)} %copy-done.1, f32[2,16,128,128]{3,2,1,0:T(8,128)S(1)} %copy-done, s32[128,128]{1,0:T(8,128)S(1)} %copy-done.3, bf16[128,128]{1,0:T(8,128)(2,1)S(1)} %collective-permute-done.7.from_n.refs_11_.refs_12_, ...), custom_call_target="tpu_custom_call" | custom-call | flops 4194304 | bytes 4194304 | tf_op jit(solution)/shard_map/edge_columns/pallas_call | solution.py:737
  47.3 1.6 %collective-permute-start.13 = (bf16[192,128]{1,0:T(8,128)(2,1)S(1)}, bf16[192,128]{1,0:T(8,128)(2,1)S(1)}, u32[]{:S(2)}, u32[]{:S(2)}) collective-permute-start(bf16[192,128]{1,0:T(8,128)(2,1)S(1)} %get-tuple-element.74.refs_9_.refs_10_), channel_id=1, source_target_pairs={{0,1},{1,2},{2,3},{4,5},{5,6},{6,7},{8,9},{9,10},{10,11},{12,13},{... | collective-permute-start | bytes 147464 | tf_op jit(solution)/shard_map/ppermute | solution.py:741
  48.9 1.3 %collective-permute-start.12 = (bf16[192,128]{1,0:T(8,128)(2,1)S(1)}, bf16[192,128]{1,0:T(8,128)(2,1)S(1)}, u32[]{:S(2)}, u32[]{:S(2)}) collective-permute-start(bf16[192,128]{1,0:T(8,128)(2,1)S(1)} %get-tuple-element.75.refs_10_.refs_11_), channel_id=1, source_target_pairs={{1,0},{2,1},{3,2},{5,4},{6,5},{7,6},{9,8},{10,9},{11,10},{13,12},{... | collective-permute-start | bytes 147464 | tf_op jit(solution)/shard_map/ppermute | solution.py:740
  50.3 3.4 %collective-permute-done.12.refs_13_.refs_14_ = bf16[192,128]{1,0:T(8,128)(2,1)S(1)} collective-permute-done((bf16[192,128]{1,0:T(8,128)(2,1)S(1)}, bf16[192,128]{1,0:T(8,128)(2,1)S(1)}, u32[]{:S(2)}, u32[]{:S(2)}) %collective-permute-start.12) | collective-permute-done | bytes 49184 | tf_op jit(solution)/shard_map/ppermute | solution.py:740
  53.6 0.7 collective-permute-start.14
  54.3 3.7 %collective-permute-start.15 = (bf16[136,128]{1,0:T(8,128)(2,1)S(1)}, bf16[136,128]{1,0:T(8,128)(2,1)S(1)}, u32[]{:S(2)}, u32[]{:S(2)}) collective-permute-start(bf16[136,128]{1,0:T(8,128)(2,1)S(1)} %get-tuple-element.84), channel_id=1, source_target_pairs={{0,8},{4,12},{8,0},{12,4},{1,9},{5,13},{9,1},{13,5},{2,10},{6,14},... | collective-permute-start | bytes 104456 | tf_op jit(solution)/shard_map/ppermute | solution.py:709
  58.2 1.9 %surface.1 = bf16[32,40,128]{2,1,0:T(8,128)(2,1)} custom-call(f32[136,512]{1,0:T(8,128)S(1)} %get-tuple-element.68.refs_0_, bf16[136,512]{1,0:T(8,128)(2,1)S(1)} %collective-permute-done.9.refs_1_, bf16[136,512]{1,0:T(8,128)(2,1)S(1)} %collective-permute-done.10.refs_2_, bf16[136,512]{1,0:T(8,128)(2,1)S(1)} %collective-permute-done.11.refs_3_, ...), custom_call_target="tpu_custom_call" | custom-call | flops 4194304 | bytes 4194304 | tf_op jit(solution)/shard_map/surface/pallas_call | solution.py:750
  60.0 0.3 collective-permute-done.15.refs_6_
  60.3 3.5 %collective-permute-done.16.refs_7_ = bf16[136,128]{1,0:T(8,128)(2,1)S(1)} collective-permute-done((bf16[136,128]{1,0:T(8,128)(2,1)S(1)}, bf16[136,128]{1,0:T(8,128)(2,1)S(1)}, u32[]{:S(2)}, u32[]{:S(2)}) %collective-permute-start.16) | collective-permute-done | bytes 34848 | tf_op jit(solution)/shard_map/ppermute | solution.py:709
  63.8 6.4 %all-to-all-start = ((bf16[32,40,128]{2,1,0:T(8,128)(2,1)}), bf16[32,40,128]{2,1,0:T(8,128)(2,1)S(1)}, u32[]{:S(2)}, u32[]{:S(2)}) async-start(bf16[32,40,128]{2,1,0:T(8,128)(2,1)} %surface.1), calls=%async_computation | async-start | bytes 655360 | tf_op jit(solution)/shard_map/all_to_all | solution.py:758
  70.3 10.2 %substeps.1 = f32[2,16,128,128]{3,2,1,0:T(8,128)} custom-call(f32[136,512]{1,0:T(8,128)} %copy-done.2, bf16[136,512]{1,0:T(8,128)(2,1)} %copy-done.4, bf16[136,512]{1,0:T(8,128)(2,1)} %copy-done.5, bf16[136,512]{1,0:T(8,128)(2,1)} %copy-done.6, f32[136,128]{1,0:T(8,128)} %copy-done.16, bf16[136,128]{1,0:T(8,128)(2,1)} %copy-done.18, ...), custom_call_target="tpu_custom_call" | custom-call | flops 16777216 | bytes 16777216 | tf_op jit(solution)/shard_map/substeps/pallas_call | solution.py:762
  80.5 1.4 %all-to-all-done.back = bf16[32,40,128]{2,1,0:T(8,128)(2,1)S(1)} async-done(((bf16[32,40,128]{2,1,0:T(8,128)(2,1)}), bf16[32,40,128]{2,1,0:T(8,128)(2,1)S(1)}, u32[]{:S(2)}, u32[]{:S(2)}) %all-to-all-start) | async-done | bytes 327712 | tf_op jit(solution)/shard_map/all_to_all | solution.py:758
  81.9 8.3 %backward_remap.1 = f32[160,128]{1,0:T(8,128)} custom-call(s32[640]{0:T(1024)S(1)} %copy-done.17, s32[1,640]{1,0:T(1,128)S(1)} %reshape.19.src_in, bf16[32,40,128]{2,1,0:T(8,128)(2,1)S(1)} %all-to-all-done.back, bf16[640,128,128]{2,1,0:T(8,128)(2,1)} %w.3), custom_call_target="tpu_custom_call" | custom-call | flops 167772160 | bytes 20971520 | tf_op jit(solution)/shard_map/backward_remap/pallas_call | solution.py:666
  (58 shorter events, 0.2 us)
Async XLA Ops:
  0.6 25.2 %copy-start = (f32[2,16,128,128]{3,2,1,0:T(8,128)S(1)}, f32[2,16,128,128]{3,2,1,0:T(8,128)}, u32[]{:S(2)}) copy-start(f32[2,16,128,128]{3,2,1,0:T(8,128)} %refs_18_.1) | copy-start | bytes 6291460
  0.6 25.1 %copy-start.1 = (f32[2,16,128,128]{3,2,1,0:T(8,128)S(1)}, f32[2,16,128,128]{3,2,1,0:T(8,128)}, u32[]{:S(2)}) copy-start(f32[2,16,128,128]{3,2,1,0:T(8,128)} %refs_17_.1) | copy-start | bytes 6291460
  0.7 25.1 %copy-start.3 = (s32[128,128]{1,0:T(8,128)S(1)}, s32[128,128]{1,0:T(8,128)}, u32[]{:S(2)}) copy-start(s32[128,128]{1,0:T(8,128)} %refs_16_.1) | copy-start | bytes 196612
  13.3 10.1 %collective-permute-start = (bf16[4,48,640]{2,1,0:T(8,128)(2,1)}, bf16[4,48,640]{2,1,0:T(8,128)(2,1)S(1)}, u32[]{:S(2)}, u32[]{:S(2)}) collective-permute-start(bf16[4,48,640]{2,1,0:T(8,128)(2,1)} %get-tuple-element.48), channel_id=1, source_target_pairs={{0,19},{1,18},{2,17},{3,16},{16,3},{17,2},{18,1},{19,0},{4,23},{5,... | collective-permute-start | bytes 737288 | tf_op jit(solution)/shard_map/ppermute | solution.py:709
  16.7 8.7 %collective-permute-start.2 = (bf16[4,48,640]{2,1,0:T(8,128)(2,1)}, bf16[4,48,640]{2,1,0:T(8,128)(2,1)S(1)}, u32[]{:S(2)}, u32[]{:S(2)}) collective-permute-start(bf16[4,48,640]{2,1,0:T(8,128)(2,1)} %get-tuple-element.50), channel_id=1, source_target_pairs={{0,1},{1,0},{2,3},{3,2},{16,17},{17,16},{18,19},{19,18},{4,5},{5,4... | collective-permute-start | bytes 737288 | tf_op jit(solution)/shard_map/ppermute | solution.py:709
  17.3 11.6 %collective-permute-start.1 = (bf16[4,48,640]{2,1,0:T(8,128)(2,1)}, bf16[4,48,640]{2,1,0:T(8,128)(2,1)S(1)}, u32[]{:S(2)}, u32[]{:S(2)}) collective-permute-start(bf16[4,48,640]{2,1,0:T(8,128)(2,1)} %get-tuple-element.49), channel_id=1, source_target_pairs={{0,18},{1,19},{2,16},{3,17},{16,2},{17,3},{18,0},{19,1},{4,22},{5,... | collective-permute-start | bytes 737288 | tf_op jit(solution)/shard_map/ppermute | solution.py:709
  17.4 16.5 %collective-permute-start.3 = (bf16[4,48,640]{2,1,0:T(8,128)(2,1)}, bf16[4,48,640]{2,1,0:T(8,128)(2,1)S(1)}, u32[]{:S(2)}, u32[]{:S(2)}) collective-permute-start(bf16[4,48,640]{2,1,0:T(8,128)(2,1)} %get-tuple-element.52), channel_id=1, source_target_pairs={{0,17},{1,16},{2,19},{3,18},{16,1},{17,0},{18,3},{19,2},{4,21},{5,... | collective-permute-start | bytes 737288 | tf_op jit(solution)/shard_map/ppermute | solution.py:709
  18.7 20.5 %collective-permute-start.4 = (bf16[4,48,640]{2,1,0:T(8,128)(2,1)}, bf16[4,48,640]{2,1,0:T(8,128)(2,1)S(1)}, u32[]{:S(2)}, u32[]{:S(2)}) collective-permute-start(bf16[4,48,640]{2,1,0:T(8,128)(2,1)} %get-tuple-element.53), channel_id=1, source_target_pairs={{0,16},{1,17},{2,18},{3,19},{16,0},{17,1},{18,2},{19,3},{4,20},{5,... | collective-permute-start | bytes 737288 | tf_op jit(solution)/shard_map/ppermute | solution.py:709
  23.4 15.8 %collective-permute-start.5 = (bf16[4,48,640]{2,1,0:T(8,128)(2,1)}, bf16[4,48,640]{2,1,0:T(8,128)(2,1)S(1)}, u32[]{:S(2)}, u32[]{:S(2)}) collective-permute-start(bf16[4,48,640]{2,1,0:T(8,128)(2,1)} %get-tuple-element.54), channel_id=1, source_target_pairs={{0,3},{1,2},{2,1},{3,0},{16,19},{17,18},{18,17},{19,16},{4,7},{5,6... | collective-permute-start | bytes 737288 | tf_op jit(solution)/shard_map/ppermute | solution.py:709
  25.4 14.7 %collective-permute-start.6 = (bf16[4,48,640]{2,1,0:T(8,128)(2,1)}, bf16[4,48,640]{2,1,0:T(8,128)(2,1)S(1)}, u32[]{:S(2)}, u32[]{:S(2)}) collective-permute-start(bf16[4,48,640]{2,1,0:T(8,128)(2,1)} %get-tuple-element.55), channel_id=1, source_target_pairs={{0,2},{1,3},{2,0},{3,1},{16,18},{17,19},{18,16},{19,17},{4,6},{5,7... | collective-permute-start | bytes 737288 | tf_op jit(solution)/shard_map/ppermute | solution.py:709
  25.8 14.3 %copy-start.9 = (bf16[4,48,640]{2,1,0:T(8,128)(2,1)S(1)}, bf16[4,48,640]{2,1,0:T(8,128)(2,1)}, u32[]{:S(2)}) copy-start(bf16[4,48,640]{2,1,0:T(8,128)(2,1)} %get-tuple-element.60.refs_0_) | copy-start | bytes 737284
  25.9 32.2 %copy-start.14 = (bf16[128,128]{1,0:T(8,128)(2,1)}, bf16[128,128]{1,0:T(8,128)(2,1)S(1)}, u32[]{:S(2)}) copy-start(bf16[128,128]{1,0:T(8,128)(2,1)S(1)} %get-tuple-element.58.refs_8_.refs_9_) | copy-start | bytes 98308
  25.9 32.2 %copy-start.15 = (bf16[128,128]{1,0:T(8,128)(2,1)}, bf16[128,128]{1,0:T(8,128)(2,1)S(1)}, u32[]{:S(2)}) copy-start(bf16[128,128]{1,0:T(8,128)(2,1)S(1)} %get-tuple-element.59.refs_7_.refs_8_) | copy-start | bytes 98308
  29.0 11.1 %collective-permute-start.7 = (bf16[128,128]{1,0:T(8,128)(2,1)S(1)}, bf16[128,128]{1,0:T(8,128)(2,1)S(1)}, u32[]{:S(2)}, u32[]{:S(2)}) collective-permute-start(bf16[128,128]{1,0:T(8,128)(2,1)S(1)} %get-tuple-element.58.refs_8_.refs_9_), channel_id=1, source_target_pairs={{4,0},{8,4},{12,8},{16,12},{20,16},{24,20},{28,24},{5,1},{9,5},{13... | collective-permute-start | bytes 98312 | tf_op jit(solution)/shard_map/ppermute | solution.py:734
  33.9 6.2 %collective-permute-start.8 = (bf16[128,128]{1,0:T(8,128)(2,1)S(1)}, bf16[128,128]{1,0:T(8,128)(2,1)S(1)}, u32[]{:S(2)}, u32[]{:S(2)}) collective-permute-start(bf16[128,128]{1,0:T(8,128)(2,1)S(1)} %get-tuple-element.59.refs_7_.refs_8_), channel_id=1, source_target_pairs={{0,4},{4,8},{8,12},{12,16},{16,20},{20,24},{24,28},{1,5},{5,9},{9,... | collective-permute-start | bytes 98312 | tf_op jit(solution)/shard_map/ppermute | solution.py:735
  40.1 18.1 %copy-start.7 = (bf16[128,128]{1,0:T(8,128)(2,1)}, bf16[128,128]{1,0:T(8,128)(2,1)S(1)}, u32[]{:S(2)}) copy-start(bf16[128,128]{1,0:T(8,128)(2,1)S(1)} %collective-permute-done.7.from_n.refs_11_.refs_12_) | copy-start | bytes 98308
  40.1 18.1 %copy-start.8 = (bf16[128,128]{1,0:T(8,128)(2,1)}, bf16[128,128]{1,0:T(8,128)(2,1)S(1)}, u32[]{:S(2)}) copy-start(bf16[128,128]{1,0:T(8,128)(2,1)S(1)} %collective-permute-done.8.from_s.refs_12_.refs_13_) | copy-start | bytes 98308
  40.7 17.4 %copy-start.2 = (f32[136,512]{1,0:T(8,128)}, f32[136,512]{1,0:T(8,128)S(1)}, u32[]{:S(2)}) copy-start(f32[136,512]{1,0:T(8,128)S(1)} %get-tuple-element.68.refs_0_) | copy-start | bytes 835588
  40.7 17.3 %collective-permute-start.9 = (bf16[136,512]{1,0:T(8,128)(2,1)S(1)}, bf16[136,512]{1,0:T(8,128)(2,1)S(1)}, u32[]{:S(2)}, u32[]{:S(2)}) collective-permute-start(bf16[136,512]{1,0:T(8,128)(2,1)S(1)} %get-tuple-element.69), channel_id=1, source_target_pairs={{0,4},{4,0},{8,12},{12,8},{1,5},{5,1},{9,13},{13,9},{2,6},{6,2},{1... | collective-permute-start | bytes 417800 | tf_op jit(solution)/shard_map/ppermute | solution.py:709
  42.8 15.3 %collective-permute-start.10 = (bf16[136,512]{1,0:T(8,128)(2,1)S(1)}, bf16[136,512]{1,0:T(8,128)(2,1)S(1)}, u32[]{:S(2)}, u32[]{:S(2)}) collective-permute-start(bf16[136,512]{1,0:T(8,128)(2,1)S(1)} %get-tuple-element.70), channel_id=1, source_target_pairs={{0,8},{4,12},{8,0},{12,4},{1,9},{5,13},{9,1},{13,5},{2,10},{6,14},... | collective-permute-start | bytes 417800 | tf_op jit(solution)/shard_map/ppermute | solution.py:709
  45.6 12.5 %collective-permute-start.11 = (bf16[136,512]{1,0:T(8,128)(2,1)S(1)}, bf16[136,512]{1,0:T(8,128)(2,1)S(1)}, u32[]{:S(2)}, u32[]{:S(2)}) collective-permute-start(bf16[136,512]{1,0:T(8,128)(2,1)S(1)} %get-tuple-element.71), channel_id=1, source_target_pairs={{0,12},{4,8},{8,4},{12,0},{1,13},{5,9},{9,5},{13,1},{2,14},{6,10},... | collective-permute-start | bytes 417800 | tf_op jit(solution)/shard_map/ppermute | solution.py:709
  47.3 22.9 %copy-start.10 = (bf16[192,128]{1,0:T(8,128)(2,1)}, bf16[192,128]{1,0:T(8,128)(2,1)S(1)}, u32[]{:S(2)}) copy-start(bf16[192,128]{1,0:T(8,128)(2,1)S(1)} %get-tuple-element.75.refs_10_.refs_11_) | copy-start | bytes 147460
  47.3 22.9 %copy-start.11 = (bf16[192,128]{1,0:T(8,128)(2,1)}, bf16[192,128]{1,0:T(8,128)(2,1)S(1)}, u32[]{:S(2)}) copy-start(bf16[192,128]{1,0:T(8,128)(2,1)S(1)} %get-tuple-element.74.refs_9_.refs_10_) | copy-start | bytes 147460
  47.3 22.8 %copy-start.21 = (s32[640]{0:T(1024)S(1)}, s32[640]{0:T(1024)}, u32[]{:S(2)}) copy-start(s32[640]{0:T(1024)} %src_in.1) | copy-start | bytes 7684
  47.3 2.9 %collective-permute-start.13 = (bf16[192,128]{1,0:T(8,128)(2,1)S(1)}, bf16[192,128]{1,0:T(8,128)(2,1)S(1)}, u32[]{:S(2)}, u32[]{:S(2)}) collective-permute-start(bf16[192,128]{1,0:T(8,128)(2,1)S(1)} %get-tuple-element.74.refs_9_.refs_10_), channel_id=1, source_target_pairs={{0,1},{1,2},{2,3},{4,5},{5,6},{6,7},{8,9},{9,10},{10,11},{12,13},{... | collective-permute-start | bytes 147464 | tf_op jit(solution)/shard_map/ppermute | solution.py:741
  48.9 4.7 %collective-permute-start.12 = (bf16[192,128]{1,0:T(8,128)(2,1)S(1)}, bf16[192,128]{1,0:T(8,128)(2,1)S(1)}, u32[]{:S(2)}, u32[]{:S(2)}) collective-permute-start(bf16[192,128]{1,0:T(8,128)(2,1)S(1)} %get-tuple-element.75.refs_10_.refs_11_), channel_id=1, source_target_pairs={{1,0},{2,1},{3,2},{5,4},{6,5},{7,6},{9,8},{10,9},{11,10},{13,12},{... | collective-permute-start | bytes 147464 | tf_op jit(solution)/shard_map/ppermute | solution.py:740
  50.2 20.0 %copy-start.12 = (bf16[192,128]{1,0:T(8,128)(2,1)}, bf16[192,128]{1,0:T(8,128)(2,1)S(1)}, u32[]{:S(2)}) copy-start(bf16[192,128]{1,0:T(8,128)(2,1)S(1)} %collective-permute-done.13.refs_14_.refs_15_) | copy-start | bytes 147460
  53.6 16.6 %copy-start.13 = (bf16[192,128]{1,0:T(8,128)(2,1)}, bf16[192,128]{1,0:T(8,128)(2,1)S(1)}, u32[]{:S(2)}) copy-start(bf16[192,128]{1,0:T(8,128)(2,1)S(1)} %collective-permute-done.12.refs_13_.refs_14_) | copy-start | bytes 147460
  53.6 6.4 %collective-permute-start.14 = (bf16[136,128]{1,0:T(8,128)(2,1)S(1)}, bf16[136,128]{1,0:T(8,128)(2,1)S(1)}, u32[]{:S(2)}, u32[]{:S(2)}) collective-permute-start(bf16[136,128]{1,0:T(8,128)(2,1)S(1)} %get-tuple-element.83), channel_id=1, source_target_pairs={{0,4},{4,0},{8,12},{12,8},{1,5},{5,1},{9,13},{13,9},{2,6},{6,2},{1... | collective-permute-start | bytes 104456 | tf_op jit(solution)/shard_map/ppermute | solution.py:709
  54.3 6.0 %collective-permute-start.15 = (bf16[136,128]{1,0:T(8,128)(2,1)S(1)}, bf16[136,128]{1,0:T(8,128)(2,1)S(1)}, u32[]{:S(2)}, u32[]{:S(2)}) collective-permute-start(bf16[136,128]{1,0:T(8,128)(2,1)S(1)} %get-tuple-element.84), channel_id=1, source_target_pairs={{0,8},{4,12},{8,0},{12,4},{1,9},{5,13},{9,1},{13,5},{2,10},{6,14},... | collective-permute-start | bytes 104456 | tf_op jit(solution)/shard_map/ppermute | solution.py:709
  58.0 5.7 %collective-permute-start.16 = (bf16[136,128]{1,0:T(8,128)(2,1)S(1)}, bf16[136,128]{1,0:T(8,128)(2,1)S(1)}, u32[]{:S(2)}, u32[]{:S(2)}) collective-permute-start(bf16[136,128]{1,0:T(8,128)(2,1)S(1)} %get-tuple-element.85), channel_id=1, source_target_pairs={{0,12},{4,8},{8,4},{12,0},{1,13},{5,9},{9,5},{13,1},{2,14},{6,10},... | collective-permute-start | bytes 104456 | tf_op jit(solution)/shard_map/ppermute | solution.py:709
  63.8 18.1 %all-to-all-start = ((bf16[32,40,128]{2,1,0:T(8,128)(2,1)}), bf16[32,40,128]{2,1,0:T(8,128)(2,1)S(1)}, u32[]{:S(2)}, u32[]{:S(2)}) async-start(bf16[32,40,128]{2,1,0:T(8,128)(2,1)} %surface.1), calls=%async_computation | async-start | bytes 655360 | tf_op jit(solution)/shard_map/all_to_all | solution.py:758
  (8 other events, 81.4 us)

commit v15 on v11

--- a/solution.py
+++ b/solution.py
@@ -214,13 +214,12 @@
     sources, outs = refs[:n_sources], refs[n_sources:]
     chunk = sources[0].shape[1]
     height = outs[0].shape[0] - 8
-    first = chunk - 8
     count = n_sources * chunk
     for z, out in enumerate(outs):
         ext = None
         where = []
         for source in sources:
-            piece = source[z, first:chunk, :].astype(F32)
+            piece = source[z, chunk - 16 : chunk, :].astype(F32)[8:]
             where.append(piece[1:2, :chunk])
             ext = piece if ext is None else ext + piece
         where = jnp.concatenate(where, axis=1)
@@ -480,7 +479,7 @@
     plane = lax.axis_index("sec") * n_gy + lax.axis_index("gy")
     line = lax.axis_index("gx")
     for z, part in enumerate(parts):
-        where = part[height + 3 : height + 4, : planes * chunk].astype(F32)
+        where = part[...].astype(F32)[height + 3 : height + 4, : planes * chunk]
         hot = (iota((height, planes * chunk), 0).astype(F32) == where).astype(F32)
         picked = dot(hot.T.astype(BF16), sst, NN).reshape(planes, chunk, width)
         for i, m in enumerate(swap_order(planes)):
@@ -638,7 +637,7 @@
     out[...] = both[:, :width] + both[:, width:]
 
 
-def backward(back, w, src, slots, blocks, parts=10):
+def backward(back, w, src, slots, blocks, parts=20):
     total, width, _ = w.shape
     devices, cap, _ = back.shape
     return pl.pallas_call(

time: 86.6 us -> 86.4 us (level)
  no operation moved by 1% of the time
where the time goes in v15:
time: 86.4 us; the launch traced here: 86.1 us
  Pallas kernels  35.4 us (41%)
  starting transfers between devices  30.2 us (35%)
  waiting for transfers between devices  19.5 us (23%)
  between operations  0.94 us (1%)
    ppermute x10, waiting for transfers between devices, swapped(): return lax.ppermute(array, axes, [(i, i ^ step) for i in range(count)])  17.3 us
    ppermute x10, starting transfers between devices, swapped(): return lax.ppermute(array, axes, [(i, i ^ step) for i in range(count)])  13.6 us
    pallas_call x1, Pallas kernels, forward(): pl.pallas_call(functools.partial(forward_kernel, parts, cap, grid), in_sp...  12.6 us
    pallas_call x1, Pallas kernels, on_device(): kernel(functools.partial(stencil_kernel, n_gx), [(tracers.shape, F32)], '...  10.2 us
    pallas_call x1, Pallas kernels, backward(): pl.pallas_call(functools.partial(backward_kernel, parts), in_specs=[ANY,...  8.3 us
    all_to_all x1, starting transfers between devices, on_device(): lax.all_to_all(back, EVERY, split_axis=0, concat_axis=0, tiled=True)  7.15 us
    ppermute x1, starting transfers between devices, on_device(): from_s = lax.ppermute(own_n, NORTH, to_north)  3.68 us
    ppermute x1, starting transfers between devices, on_device(): from_w = lax.ppermute(own_e, 'gy', to_east)  3.03 us
  transfers between devices with their start and end apart: 15, of which 9 were waited for; matrix products, arithmetic and copies ran while one was open for 0% of the time, Pallas kernels for 14%

profile of v15, /device:TPU:0, one launch (start us, length us, event | category | flops | bytes accessed | tf_op | source)
XLA Modules:
  0.0 86.1 jit_solution(11044714262891704902)
XLA Ops:
  0.6 0.0 copy-start
  0.7 12.6 %forward_remap.1 = (bf16[4,48,640]{2,1,0:T(8,128)(2,1)}, bf16[4,48,640]{2,1,0:T(8,128)(2,1)}, bf16[4,48,640]{2,1,0:T(8,128)(2,1)}, bf16[4,48,640]{2,1,0:T(8,128)...) custom-call(s32[640]{0:T(1024)} %src_in.1, ...), custom_call_target="tpu_custom_call" | custom-call | flops 167772160 | bytes 20971520 | tf_op jit(solution)/shard_map/forward_remap/pallas_call | solution.py:188
  13.3 0.5 collective-permute-start.2
  13.8 3.6 %collective-permute-start = (bf16[4,48,640]{2,1,0:T(8,128)(2,1)}, bf16[4,48,640]{2,1,0:T(8,128)(2,1)S(1)}, u32[]{:S(2)}, u32[]{:S(2)}) collective-permute-start(bf16[4,48,640]{2,1,0:T(8,128)(2,1)} %get-tuple-element.33), channel_id=1, source_target_pairs={{0,19},{1,18},{2,17},{3,16},{16,3},{17,2},{18,1},{19,0},{4,23},{5,... | collective-permute-start | bytes 737288 | tf_op jit(solution)/shard_map/ppermute | solution.py:686
  17.4 0.0 collective-permute-start.1
  17.4 1.3 %collective-permute-start.3 = (bf16[4,48,640]{2,1,0:T(8,128)(2,1)}, bf16[4,48,640]{2,1,0:T(8,128)(2,1)S(1)}, u32[]{:S(2)}, u32[]{:S(2)}) collective-permute-start(bf16[4,48,640]{2,1,0:T(8,128)(2,1)} %get-tuple-element.37), channel_id=1, source_target_pairs={{0,17},{1,16},{2,19},{3,18},{16,1},{17,0},{18,3},{19,2},{4,21},{5,... | collective-permute-start | bytes 737288 | tf_op jit(solution)/shard_map/ppermute | solution.py:686
  18.8 0.6 collective-permute-start.4
  19.4 1.4 %collective-permute-start.5 = (bf16[4,48,640]{2,1,0:T(8,128)(2,1)}, bf16[4,48,640]{2,1,0:T(8,128)(2,1)S(1)}, u32[]{:S(2)}, u32[]{:S(2)}) collective-permute-start(bf16[4,48,640]{2,1,0:T(8,128)(2,1)} %get-tuple-element.39), channel_id=1, source_target_pairs={{0,3},{1,2},{2,1},{3,0},{16,19},{17,18},{18,17},{19,16},{4,7},{5,6... | collective-permute-start | bytes 737288 | tf_op jit(solution)/shard_map/ppermute | solution.py:686
  20.8 3.2 %collective-permute-done.refs_1_ = bf16[4,48,640]{2,1,0:T(8,128)(2,1)S(1)} collective-permute-done((bf16[4,48,640]{2,1,0:T(8,128)(2,1)}, bf16[4,48,640]{2,1,0:T(8,128)(2,1)S(1)}, u32[]{:S(2)}, u32[]{:S(2)}) %collective-permute-start) | collective-permute-done | bytes 245792 | tf_op jit(solution)/shard_map/ppermute | solution.py:686
  24.0 1.2 %collective-permute-start.6 = (bf16[4,48,640]{2,1,0:T(8,128)(2,1)}, bf16[4,48,640]{2,1,0:T(8,128)(2,1)S(1)}, u32[]{:S(2)}, u32[]{:S(2)}) collective-permute-start(bf16[4,48,640]{2,1,0:T(8,128)(2,1)} %get-tuple-element.40), channel_id=1, source_target_pairs={{0,2},{1,3},{2,0},{3,1},{16,18},{17,19},{18,16},{19,17},{4,6},{5,7... | collective-permute-start | bytes 737288 | tf_op jit(solution)/shard_map/ppermute | solution.py:686
  25.3 0.1 edge_rows.1
  25.4 4.3 %collective-permute-done.1.refs_2_ = bf16[4,48,640]{2,1,0:T(8,128)(2,1)S(1)} collective-permute-done((bf16[4,48,640]{2,1,0:T(8,128)(2,1)}, bf16[4,48,640]{2,1,0:T(8,128)(2,1)S(1)}, u32[]{:S(2)}, u32[]{:S(2)}) %collective-permute-start.1) | collective-permute-done | bytes 245792 | tf_op jit(solution)/shard_map/ppermute | solution.py:686
  29.7 1.3 %collective-permute-start.7 = (bf16[128,128]{1,0:T(8,128)(2,1)S(1)}, bf16[128,128]{1,0:T(8,128)(2,1)S(1)}, u32[]{:S(2)}, u32[]{:S(2)}) collective-permute-start(bf16[128,128]{1,0:T(8,128)(2,1)S(1)} %get-tuple-element.43.refs_5_.refs_8_), channel_id=1, source_target_pairs={{4,0},{8,4},{12,8},{16,12},{20,16},{24,20},{28,24},{5,1},{9,5},{13... | collective-permute-start | bytes 98312 | tf_op jit(solution)/shard_map/ppermute | solution.py:711
  30.9 3.6 %collective-permute-done.3.refs_4_ = bf16[4,48,640]{2,1,0:T(8,128)(2,1)S(1)} collective-permute-done((bf16[4,48,640]{2,1,0:T(8,128)(2,1)}, bf16[4,48,640]{2,1,0:T(8,128)(2,1)S(1)}, u32[]{:S(2)}, u32[]{:S(2)}) %collective-permute-start.3) | collective-permute-done | bytes 245792 | tf_op jit(solution)/shard_map/ppermute | solution.py:686
  34.6 3.7 %collective-permute-start.8 = (bf16[128,128]{1,0:T(8,128)(2,1)S(1)}, bf16[128,128]{1,0:T(8,128)(2,1)S(1)}, u32[]{:S(2)}, u32[]{:S(2)}) collective-permute-start(bf16[128,128]{1,0:T(8,128)(2,1)S(1)} %get-tuple-element.44.refs_4_.refs_7_), channel_id=1, source_target_pairs={{0,4},{4,8},{8,12},{12,16},{16,20},{20,24},{24,28},{1,5},{5,9},{9,... | collective-permute-start | bytes 98312 | tf_op jit(solution)/shard_map/ppermute | solution.py:712
  38.3 1.6 %collective-permute-done.4.refs_5_ = bf16[4,48,640]{2,1,0:T(8,128)(2,1)S(1)} collective-permute-done((bf16[4,48,640]{2,1,0:T(8,128)(2,1)}, bf16[4,48,640]{2,1,0:T(8,128)(2,1)S(1)}, u32[]{:S(2)}, u32[]{:S(2)}) %collective-permute-start.4) | collective-permute-done | bytes 245792 | tf_op jit(solution)/shard_map/ppermute | solution.py:686
  39.9 0.3 collective-permute-done.6.refs_7_
  40.2 0.6 merge.1
  40.8 3.1 %collective-permute-start.10 = (bf16[136,640]{1,0:T(8,128)(2,1)S(1)}, bf16[136,640]{1,0:T(8,128)(2,1)S(1)}, u32[]{:S(2)}, u32[]{:S(2)}) collective-permute-start(bf16[136,640]{1,0:T(8,128)(2,1)S(1)} %get-tuple-element.55), channel_id=1, source_target_pairs={{0,8},{4,12},{8,0},{12,4},{1,9},{5,13},{9,1},{13,5},{2,10},{6,14},... | collective-permute-start | bytes 522248 | tf_op jit(solution)/shard_map/ppermute | solution.py:686
  43.9 1.4 %collective-permute-start.11 = (bf16[136,640]{1,0:T(8,128)(2,1)S(1)}, bf16[136,640]{1,0:T(8,128)(2,1)S(1)}, u32[]{:S(2)}, u32[]{:S(2)}) collective-permute-start(bf16[136,640]{1,0:T(8,128)(2,1)S(1)} %get-tuple-element.56), channel_id=1, source_target_pairs={{0,12},{4,8},{8,4},{12,0},{1,13},{5,9},{9,5},{13,1},{2,14},{6,10},... | collective-permute-start | bytes 522248 | tf_op jit(solution)/shard_map/ppermute | solution.py:686
  45.2 0.5 collective-permute-start.9
  45.7 1.7 %edge_columns.1 = (bf16[192,128]{1,0:T(8,128)(2,1)S(1)}, bf16[192,128]{1,0:T(8,128)(2,1)S(1)}) custom-call(f32[2,16,128,128]{3,2,1,0:T(8,128)S(1)} %copy-done.1, f32[2,16,128,128]{3,2,1,0:T(8,128)S(1)} %copy-done, s32[128,128]{1,0:T(8,128)S(1)} %copy-done.3, bf16[128,128]{1,0:T(8,128)(2,1)S(1)} %collective-permute-done.7.from_n.refs_8_.refs_11_, ...), custom_call_target="tpu_custom_call" | custom-call | flops 4194304 | bytes 4194304 | tf_op jit(solution)/shard_map/edge_columns/pallas_call | solution.py:714
  47.4 1.4 %collective-permute-start.12 = (bf16[192,128]{1,0:T(8,128)(2,1)S(1)}, bf16[192,128]{1,0:T(8,128)(2,1)S(1)}, u32[]{:S(2)}, u32[]{:S(2)}) collective-permute-start(bf16[192,128]{1,0:T(8,128)(2,1)S(1)} %get-tuple-element.60.refs_7_.refs_10_), channel_id=1, source_target_pairs={{1,0},{2,1},{3,2},{5,4},{6,5},{7,6},{9,8},{10,9},{11,10},{13,12},{... | collective-permute-start | bytes 147464 | tf_op jit(solution)/shard_map/ppermute | solution.py:717
  48.8 3.0 %collective-permute-start.13 = (bf16[192,128]{1,0:T(8,128)(2,1)S(1)}, bf16[192,128]{1,0:T(8,128)(2,1)S(1)}, u32[]{:S(2)}, u32[]{:S(2)}) collective-permute-start(bf16[192,128]{1,0:T(8,128)(2,1)S(1)} %get-tuple-element.59.refs_6_.refs_9_), channel_id=1, source_target_pairs={{0,1},{1,2},{2,3},{4,5},{5,6},{6,7},{8,9},{9,10},{10,11},{12,13},{... | collective-permute-start | bytes 147464 | tf_op jit(solution)/shard_map/ppermute | solution.py:718
  51.9 0.8 collective-permute-done.13.refs_11_.refs_14_
  52.7 3.9 %collective-permute-done.10.refs_2_ = bf16[136,640]{1,0:T(8,128)(2,1)S(1)} collective-permute-done((bf16[136,640]{1,0:T(8,128)(2,1)S(1)}, bf16[136,640]{1,0:T(8,128)(2,1)S(1)}, u32[]{:S(2)}, u32[]{:S(2)}) %collective-permute-start.10) | collective-permute-done | bytes 174112 | tf_op jit(solution)/shard_map/ppermute | solution.py:686
  56.7 0.4 collective-permute-done.9.refs_1_
  57.1 1.9 %surface.1 = bf16[32,40,128]{2,1,0:T(8,128)(2,1)} custom-call(f32[136,640]{1,0:T(8,128)S(1)} %get-tuple-element.53.refs_0_, bf16[136,640]{1,0:T(8,128)(2,1)S(1)} %collective-permute-done.9.refs_1_, bf16[136,640]{1,0:T(8,128)(2,1)S(1)} %collective-permute-done.10.refs_2_, bf16[136,640]{1,0:T(8,128)(2,1)S(1)} %collective-permute-done.11.refs_3_, ...), custom_call_target="tpu_custom_call" | custom-call | flops 4194304 | bytes 4194304 | tf_op jit(solution)/shard_map/surface/pallas_call | solution.py:724
  59.0 7.2 %all-to-all-start = ((bf16[32,40,128]{2,1,0:T(8,128)(2,1)}), bf16[32,40,128]{2,1,0:T(8,128)(2,1)S(1)}, u32[]{:S(2)}, u32[]{:S(2)}) async-start(bf16[32,40,128]{2,1,0:T(8,128)(2,1)} %surface.1), calls=%async_computation | async-start | bytes 655360 | tf_op jit(solution)/shard_map/all_to_all | solution.py:731
  66.2 10.2 %substeps.1 = f32[2,16,128,128]{3,2,1,0:T(8,128)} custom-call(f32[136,640]{1,0:T(8,128)} %copy-done.2, bf16[136,640]{1,0:T(8,128)(2,1)} %copy-done.6, bf16[136,640]{1,0:T(8,128)(2,1)} %copy-done.4, bf16[136,640]{1,0:T(8,128)(2,1)} %copy-done.5, bf16[128,128]{1,0:T(8,128)(2,1)} %copy-done.15, bf16[128,128]{1,0:T(8,128)(2,1)} %copy-done.14, ...), custom_call_target="tpu_custom_call" | custom-call | flops 16777216 | bytes 16777216 | tf_op jit(solution)/shard_map/substeps/pallas_call | solution.py:735
  76.4 1.4 %all-to-all-done.back = bf16[32,40,128]{2,1,0:T(8,128)(2,1)S(1)} async-done(((bf16[32,40,128]{2,1,0:T(8,128)(2,1)}), bf16[32,40,128]{2,1,0:T(8,128)(2,1)S(1)}, u32[]{:S(2)}, u32[]{:S(2)}) %all-to-all-start) | async-done | bytes 327712 | tf_op jit(solution)/shard_map/all_to_all | solution.py:731
  77.8 8.3 %backward_remap.1 = f32[160,128]{1,0:T(8,128)} custom-call(s32[640]{0:T(1024)S(1)} %copy-done.16, s32[1,640]{1,0:T(1,128)S(1)} %reshape.19.src_in, bf16[32,40,128]{2,1,0:T(8,128)(2,1)S(1)} %all-to-all-done.back, bf16[640,128,128]{2,1,0:T(8,128)(2,1)} %w.3), custom_call_target="tpu_custom_call" | custom-call | flops 167772160 | bytes 20971520 | tf_op jit(solution)/shard_map/backward_remap/pallas_call | solution.py:643
  (44 shorter events, 0.1 us)
Async XLA Ops:
  0.6 24.6 %copy-start = (f32[2,16,128,128]{3,2,1,0:T(8,128)S(1)}, f32[2,16,128,128]{3,2,1,0:T(8,128)}, u32[]{:S(2)}) copy-start(f32[2,16,128,128]{3,2,1,0:T(8,128)} %refs_14_.1) | copy-start | bytes 6291460
  0.6 24.6 %copy-start.1 = (f32[2,16,128,128]{3,2,1,0:T(8,128)S(1)}, f32[2,16,128,128]{3,2,1,0:T(8,128)}, u32[]{:S(2)}) copy-start(f32[2,16,128,128]{3,2,1,0:T(8,128)} %refs_13_.1) | copy-start | bytes 6291460
  0.7 24.6 %copy-start.3 = (s32[128,128]{1,0:T(8,128)S(1)}, s32[128,128]{1,0:T(8,128)}, u32[]{:S(2)}) copy-start(s32[128,128]{1,0:T(8,128)} %refs_6_.1) | copy-start | bytes 196612
  13.3 6.1 %collective-permute-start.2 = (bf16[4,48,640]{2,1,0:T(8,128)(2,1)}, bf16[4,48,640]{2,1,0:T(8,128)(2,1)S(1)}, u32[]{:S(2)}, u32[]{:S(2)}) collective-permute-start(bf16[4,48,640]{2,1,0:T(8,128)(2,1)} %get-tuple-element.35), channel_id=1, source_target_pairs={{0,1},{1,0},{2,3},{3,2},{16,17},{17,16},{18,19},{19,18},{4,5},{5,4... | collective-permute-start | bytes 737288 | tf_op jit(solution)/shard_map/ppermute | solution.py:686
  13.8 10.2 %collective-permute-start = (bf16[4,48,640]{2,1,0:T(8,128)(2,1)}, bf16[4,48,640]{2,1,0:T(8,128)(2,1)S(1)}, u32[]{:S(2)}, u32[]{:S(2)}) collective-permute-start(bf16[4,48,640]{2,1,0:T(8,128)(2,1)} %get-tuple-element.33), channel_id=1, source_target_pairs={{0,19},{1,18},{2,17},{3,16},{16,3},{17,2},{18,1},{19,0},{4,23},{5,... | collective-permute-start | bytes 737288 | tf_op jit(solution)/shard_map/ppermute | solution.py:686
  17.4 12.3 %collective-permute-start.1 = (bf16[4,48,640]{2,1,0:T(8,128)(2,1)}, bf16[4,48,640]{2,1,0:T(8,128)(2,1)S(1)}, u32[]{:S(2)}, u32[]{:S(2)}) collective-permute-start(bf16[4,48,640]{2,1,0:T(8,128)(2,1)} %get-tuple-element.34), channel_id=1, source_target_pairs={{0,18},{1,19},{2,16},{3,17},{16,2},{17,3},{18,0},{19,1},{4,22},{5,... | collective-permute-start | bytes 737288 | tf_op jit(solution)/shard_map/ppermute | solution.py:686
  17.4 17.1 %collective-permute-start.3 = (bf16[4,48,640]{2,1,0:T(8,128)(2,1)}, bf16[4,48,640]{2,1,0:T(8,128)(2,1)S(1)}, u32[]{:S(2)}, u32[]{:S(2)}) collective-permute-start(bf16[4,48,640]{2,1,0:T(8,128)(2,1)} %get-tuple-element.37), channel_id=1, source_target_pairs={{0,17},{1,16},{2,19},{3,18},{16,1},{17,0},{18,3},{19,2},{4,21},{5,... | collective-permute-start | bytes 737288 | tf_op jit(solution)/shard_map/ppermute | solution.py:686
  18.8 21.1 %collective-permute-start.4 = (bf16[4,48,640]{2,1,0:T(8,128)(2,1)}, bf16[4,48,640]{2,1,0:T(8,128)(2,1)S(1)}, u32[]{:S(2)}, u32[]{:S(2)}) collective-permute-start(bf16[4,48,640]{2,1,0:T(8,128)(2,1)} %get-tuple-element.38), channel_id=1, source_target_pairs={{0,16},{1,17},{2,18},{3,19},{16,0},{17,1},{18,2},{19,3},{4,20},{5,... | collective-permute-start | bytes 737288 | tf_op jit(solution)/shard_map/ppermute | solution.py:686
  19.4 20.5 %collective-permute-start.5 = (bf16[4,48,640]{2,1,0:T(8,128)(2,1)}, bf16[4,48,640]{2,1,0:T(8,128)(2,1)S(1)}, u32[]{:S(2)}, u32[]{:S(2)}) collective-permute-start(bf16[4,48,640]{2,1,0:T(8,128)(2,1)} %get-tuple-element.39), channel_id=1, source_target_pairs={{0,3},{1,2},{2,1},{3,0},{16,19},{17,18},{18,17},{19,16},{4,7},{5,6... | collective-permute-start | bytes 737288 | tf_op jit(solution)/shard_map/ppermute | solution.py:686
  24.0 16.1 %collective-permute-start.6 = (bf16[4,48,640]{2,1,0:T(8,128)(2,1)}, bf16[4,48,640]{2,1,0:T(8,128)(2,1)S(1)}, u32[]{:S(2)}, u32[]{:S(2)}) collective-permute-start(bf16[4,48,640]{2,1,0:T(8,128)(2,1)} %get-tuple-element.40), channel_id=1, source_target_pairs={{0,2},{1,3},{2,0},{3,1},{16,18},{17,19},{18,16},{19,17},{4,6},{5,7... | collective-permute-start | bytes 737288 | tf_op jit(solution)/shard_map/ppermute | solution.py:686
  25.3 14.9 %copy-start.9 = (bf16[4,48,640]{2,1,0:T(8,128)(2,1)S(1)}, bf16[4,48,640]{2,1,0:T(8,128)(2,1)}, u32[]{:S(2)}) copy-start(bf16[4,48,640]{2,1,0:T(8,128)(2,1)} %get-tuple-element.45.refs_0_) | copy-start | bytes 737284
  25.4 31.7 %copy-start.14 = (bf16[128,128]{1,0:T(8,128)(2,1)}, bf16[128,128]{1,0:T(8,128)(2,1)S(1)}, u32[]{:S(2)}) copy-start(bf16[128,128]{1,0:T(8,128)(2,1)S(1)} %get-tuple-element.43.refs_5_.refs_8_) | copy-start | bytes 98308
  25.4 31.7 %copy-start.15 = (bf16[128,128]{1,0:T(8,128)(2,1)}, bf16[128,128]{1,0:T(8,128)(2,1)S(1)}, u32[]{:S(2)}) copy-start(bf16[128,128]{1,0:T(8,128)(2,1)S(1)} %get-tuple-element.44.refs_4_.refs_7_) | copy-start | bytes 98308
  29.7 10.5 %collective-permute-start.7 = (bf16[128,128]{1,0:T(8,128)(2,1)S(1)}, bf16[128,128]{1,0:T(8,128)(2,1)S(1)}, u32[]{:S(2)}, u32[]{:S(2)}) collective-permute-start(bf16[128,128]{1,0:T(8,128)(2,1)S(1)} %get-tuple-element.43.refs_5_.refs_8_), channel_id=1, source_target_pairs={{4,0},{8,4},{12,8},{16,12},{20,16},{24,20},{28,24},{5,1},{9,5},{13... | collective-permute-start | bytes 98312 | tf_op jit(solution)/shard_map/ppermute | solution.py:711
  34.6 5.6 %collective-permute-start.8 = (bf16[128,128]{1,0:T(8,128)(2,1)S(1)}, bf16[128,128]{1,0:T(8,128)(2,1)S(1)}, u32[]{:S(2)}, u32[]{:S(2)}) collective-permute-start(bf16[128,128]{1,0:T(8,128)(2,1)S(1)} %get-tuple-element.44.refs_4_.refs_7_), channel_id=1, source_target_pairs={{0,4},{4,8},{8,12},{12,16},{16,20},{20,24},{24,28},{1,5},{5,9},{9,... | collective-permute-start | bytes 98312 | tf_op jit(solution)/shard_map/ppermute | solution.py:712
  40.1 16.9 %copy-start.7 = (bf16[128,128]{1,0:T(8,128)(2,1)}, bf16[128,128]{1,0:T(8,128)(2,1)S(1)}, u32[]{:S(2)}) copy-start(bf16[128,128]{1,0:T(8,128)(2,1)S(1)} %collective-permute-done.7.from_n.refs_8_.refs_11_) | copy-start | bytes 98308
  40.2 16.9 %copy-start.8 = (bf16[128,128]{1,0:T(8,128)(2,1)}, bf16[128,128]{1,0:T(8,128)(2,1)S(1)}, u32[]{:S(2)}) copy-start(bf16[128,128]{1,0:T(8,128)(2,1)S(1)} %collective-permute-done.8.from_s.refs_9_.refs_12_) | copy-start | bytes 98308
  40.8 16.3 %copy-start.2 = (f32[136,640]{1,0:T(8,128)}, f32[136,640]{1,0:T(8,128)S(1)}, u32[]{:S(2)}) copy-start(f32[136,640]{1,0:T(8,128)S(1)} %get-tuple-element.53.refs_0_) | copy-start | bytes 1044484
  40.8 15.8 %collective-permute-start.10 = (bf16[136,640]{1,0:T(8,128)(2,1)S(1)}, bf16[136,640]{1,0:T(8,128)(2,1)S(1)}, u32[]{:S(2)}, u32[]{:S(2)}) collective-permute-start(bf16[136,640]{1,0:T(8,128)(2,1)S(1)} %get-tuple-element.55), channel_id=1, source_target_pairs={{0,8},{4,12},{8,0},{12,4},{1,9},{5,13},{9,1},{13,5},{2,10},{6,14},... | collective-permute-start | bytes 522248 | tf_op jit(solution)/shard_map/ppermute | solution.py:686
  43.9 12.8 %collective-permute-start.11 = (bf16[136,640]{1,0:T(8,128)(2,1)S(1)}, bf16[136,640]{1,0:T(8,128)(2,1)S(1)}, u32[]{:S(2)}, u32[]{:S(2)}) collective-permute-start(bf16[136,640]{1,0:T(8,128)(2,1)S(1)} %get-tuple-element.56), channel_id=1, source_target_pairs={{0,12},{4,8},{8,4},{12,0},{1,13},{5,9},{9,5},{13,1},{2,14},{6,10},... | collective-permute-start | bytes 522248 | tf_op jit(solution)/shard_map/ppermute | solution.py:686
  45.2 11.8 %collective-permute-start.9 = (bf16[136,640]{1,0:T(8,128)(2,1)S(1)}, bf16[136,640]{1,0:T(8,128)(2,1)S(1)}, u32[]{:S(2)}, u32[]{:S(2)}) collective-permute-start(bf16[136,640]{1,0:T(8,128)(2,1)S(1)} %get-tuple-element.54), channel_id=1, source_target_pairs={{0,4},{4,0},{8,12},{12,8},{1,5},{5,1},{9,13},{13,9},{2,6},{6,2},{1... | collective-permute-start | bytes 522248 | tf_op jit(solution)/shard_map/ppermute | solution.py:686
  47.4 18.8 %copy-start.10 = (bf16[192,128]{1,0:T(8,128)(2,1)}, bf16[192,128]{1,0:T(8,128)(2,1)S(1)}, u32[]{:S(2)}) copy-start(bf16[192,128]{1,0:T(8,128)(2,1)S(1)} %get-tuple-element.60.refs_7_.refs_10_) | copy-start | bytes 147460
  47.4 18.8 %copy-start.11 = (bf16[192,128]{1,0:T(8,128)(2,1)}, bf16[192,128]{1,0:T(8,128)(2,1)S(1)}, u32[]{:S(2)}) copy-start(bf16[192,128]{1,0:T(8,128)(2,1)S(1)} %get-tuple-element.59.refs_6_.refs_9_) | copy-start | bytes 147460
  47.4 18.7 %copy-start.17 = (s32[640]{0:T(1024)S(1)}, s32[640]{0:T(1024)}, u32[]{:S(2)}) copy-start(s32[640]{0:T(1024)} %src_in.1) | copy-start | bytes 7684
  47.4 4.5 %collective-permute-start.12 = (bf16[192,128]{1,0:T(8,128)(2,1)S(1)}, bf16[192,128]{1,0:T(8,128)(2,1)S(1)}, u32[]{:S(2)}, u32[]{:S(2)}) collective-permute-start(bf16[192,128]{1,0:T(8,128)(2,1)S(1)} %get-tuple-element.60.refs_7_.refs_10_), channel_id=1, source_target_pairs={{1,0},{2,1},{3,2},{5,4},{6,5},{7,6},{9,8},{10,9},{11,10},{13,12},{... | collective-permute-start | bytes 147464 | tf_op jit(solution)/shard_map/ppermute | solution.py:717
  48.8 3.9 %collective-permute-start.13 = (bf16[192,128]{1,0:T(8,128)(2,1)S(1)}, bf16[192,128]{1,0:T(8,128)(2,1)S(1)}, u32[]{:S(2)}, u32[]{:S(2)}) collective-permute-start(bf16[192,128]{1,0:T(8,128)(2,1)S(1)} %get-tuple-element.59.refs_6_.refs_9_), channel_id=1, source_target_pairs={{0,1},{1,2},{2,3},{4,5},{5,6},{6,7},{8,9},{9,10},{10,11},{12,13},{... | collective-permute-start | bytes 147464 | tf_op jit(solution)/shard_map/ppermute | solution.py:718
  51.9 14.2 %copy-start.12 = (bf16[192,128]{1,0:T(8,128)(2,1)}, bf16[192,128]{1,0:T(8,128)(2,1)S(1)}, u32[]{:S(2)}) copy-start(bf16[192,128]{1,0:T(8,128)(2,1)S(1)} %collective-permute-done.12.refs_10_.refs_13_) | copy-start | bytes 147460
  52.7 13.4 %copy-start.13 = (bf16[192,128]{1,0:T(8,128)(2,1)}, bf16[192,128]{1,0:T(8,128)(2,1)S(1)}, u32[]{:S(2)}) copy-start(bf16[192,128]{1,0:T(8,128)(2,1)S(1)} %collective-permute-done.13.refs_11_.refs_14_) | copy-start | bytes 147460
  56.7 9.5 %copy-start.4 = (bf16[136,640]{1,0:T(8,128)(2,1)}, bf16[136,640]{1,0:T(8,128)(2,1)S(1)}, u32[]{:S(2)}) copy-start(bf16[136,640]{1,0:T(8,128)(2,1)S(1)} %collective-permute-done.10.refs_2_) | copy-start | bytes 522244
  56.7 9.5 %copy-start.5 = (bf16[136,640]{1,0:T(8,128)(2,1)}, bf16[136,640]{1,0:T(8,128)(2,1)S(1)}, u32[]{:S(2)}) copy-start(bf16[136,640]{1,0:T(8,128)(2,1)S(1)} %collective-permute-done.11.refs_3_) | copy-start | bytes 522244
  59.0 18.9 %all-to-all-start = ((bf16[32,40,128]{2,1,0:T(8,128)(2,1)}), bf16[32,40,128]{2,1,0:T(8,128)(2,1)S(1)}, u32[]{:S(2)}, u32[]{:S(2)}) async-start(bf16[32,40,128]{2,1,0:T(8,128)(2,1)} %surface.1), calls=%async_computation | async-start | bytes 655360 | tf_op jit(solution)/shard_map/all_to_all | solution.py:731
  66.2 11.6 %copy-start.16 = (s32[640]{0:T(1024)S(1)}, s32[640]{0:T(1024)}, u32[]{:S(2)}) copy-start(s32[640]{0:T(1024)} %get-tuple-element.61.slots_in) | copy-start | bytes 7684
  (1 other events, 9.2 us)
